TPU v7x, 128 devices: a whole 4x4x4 slice. The times are simulated.
128 devices in a mesh: seq: 32 (over z, x, core), tp: 4 (over y).
Axes of the slice: x: 4, y: 4, z: 4, core: 2. Of those that a mesh axis runs over, the one named last changes fastest.
Arguments:
- frames: bfloat16 [8192, 1280], P('seq'), may hold values from -6 to 6
- gain_attn: float32 [1280], replicated, may hold values from 0.1 to 1.9
- w_qkv: bfloat16 [3, 1280, 1280], P(None, None, 'tp'), as said below
- w_out: bfloat16 [1280, 1280], P('tp'), may hold values from -0.15625 to 0.15625
- gain_ffn: float32 [1280], replicated, may hold values from 0.1 to 1.9
- w_up: bfloat16 [1280, 5120], P(None, 'tp'), may hold values from -0.15625 to 0.15625
- w_down: bfloat16 [5120, 1280], P('tp'), may hold values from -0.078125 to 0.078125
- w_conv: bfloat16 [3, 1280, 1280], P(None, None, 'tp'), may hold values from -0.09375 to 0.09375
- w_proj: bfloat16 [1280, 4096], P('tp'), may hold values from -0.15625 to 0.15625
- block_utt: int32 [64], P('seq'), may hold values from 0 to 15, never falling along the last dimension, each value on 1 to 11 neighbouring positions
Outputs:
- lm_rows: bfloat16 [4096, 4096], P(('seq', 'tp'))
Inputs may be any that keep to these rules, and one draw needn't show every extreme that they name: `block_utt`: ids never fall from block to block; each utterance covers 1 to 11 consecutive blocks, every id is used, and one utterance covers exactly 11 blocks. `w_qkv`: entries of order a few times 1280 ** -0.5.
All inputs are finite; a program needn't handle non-finite values.
Results may differ from a plain program's by a relative error of at most 0.025.
The roundings to bfloat16 on the way count: a program that leaves them out, or rounds other values in their place, can miss the bound.
Values may be sent and summed in bfloat16 or wider, within the bound.
No kernel may reach another device: no remote copies, remote signals or barrier semaphores. Data moves between devices by JAX's collectives and lax.ppermute only.
A program may use at most 64 MiB of HBM per device.

v0:
```python
import jax
import jax.numpy as jnp
from jax import lax
from jax.sharding import PartitionSpec as P

HEAD_DIM = 64
REACH = 5


def shifted(value, axis, steps):
    count = lax.axis_size(axis)
    leading, last = (max(0, -steps), min(count, count - steps))
    return lax.ppermute(value, axis, [(source, source + steps) for source in range(leading, last)])


def layer_norm(value, gain):
    mean = jnp.mean(value, axis=-1, keepdims=True)
    centred = value - mean
    spread = jnp.mean(centred * centred, axis=-1, keepdims=True)
    return centred * lax.rsqrt(spread + 1e-05) * gain


def absorb(carry, piece, queries, query_ids):
    top, total, summed = carry
    keys_piece, values_piece, ids_piece = piece
    count = keys_piece.shape[0]
    heads_here = queries.shape[1]
    keys_split = keys_piece.reshape(count, heads_here, HEAD_DIM)
    values_split = values_piece.reshape(count, heads_here, HEAD_DIM)
    scores = (
        jnp.einsum("fhd,nhd->fhn", queries, keys_split, preferred_element_type=jnp.float32)
        / HEAD_DIM**0.5
    )
    same = (query_ids[:, None] == ids_piece[None, :])[:, None, :]
    scores = jnp.where(same, scores, -1e30)
    new_top = jnp.maximum(top, jnp.max(scores, axis=-1))
    weights = jnp.where(same, jnp.exp(scores - new_top[..., None]), 0.0)
    rescale = jnp.exp(top - new_top)
    total = total * rescale + jnp.sum(weights, axis=-1)
    summed = summed * rescale[..., None] + jnp.einsum(
        "fhn,nhd->fhd",
        weights.astype(jnp.bfloat16),
        values_split,
        preferred_element_type=jnp.float32,
    )
    return (new_top, total, summed)


def shards(frames, gain_attn, w_qkv, w_out, gain_ffn, w_up, w_down, w_conv, w_proj, block_utt):
    frame_count = frames.shape[0]
    width = frames.shape[1]
    block_rows = frame_count // block_utt.shape[0]
    frame_id = jnp.repeat(block_utt, block_rows, total_repeat_length=frame_count) + 1
    resid_in = frames.astype(jnp.float32)
    normed = layer_norm(resid_in, gain_attn).astype(jnp.bfloat16)
    queries = jnp.dot(normed, w_qkv[0], preferred_element_type=jnp.float32).astype(jnp.bfloat16)
    keys = jnp.dot(normed, w_qkv[1], preferred_element_type=jnp.float32).astype(jnp.bfloat16)
    values = jnp.dot(normed, w_qkv[2], preferred_element_type=jnp.float32).astype(jnp.bfloat16)
    local_width = queries.shape[1]
    heads_here = local_width // HEAD_DIM
    query_split = queries.reshape(frame_count, heads_here, HEAD_DIM)
    carry = (
        jnp.full((frame_count, heads_here), -1e30, jnp.float32),
        jnp.zeros((frame_count, heads_here), jnp.float32),
        jnp.zeros((frame_count, heads_here, HEAD_DIM), jnp.float32),
    )
    carry = absorb(carry, (keys, values, frame_id), query_split, frame_id)
    for step in range(1, REACH + 1):
        for sign in (1, -1):
            moved = shifted((keys, values, frame_id), "seq", sign * step)
            carry = absorb(carry, moved, query_split, frame_id)
    top, total, summed = carry
    attended = (summed / total[..., None]).reshape(frame_count, local_width).astype(jnp.bfloat16)
    attn_term = jnp.dot(attended, w_out, preferred_element_type=jnp.float32)
    resid = resid_in + lax.psum(attn_term.astype(jnp.bfloat16), "tp").astype(jnp.float32)
    normed_two = layer_norm(resid, gain_ffn).astype(jnp.bfloat16)
    hidden = jax.nn.gelu(
        jnp.dot(normed_two, w_up, preferred_element_type=jnp.float32), approximate=False
    ).astype(jnp.bfloat16)
    ffn_term = jnp.dot(hidden, w_down, preferred_element_type=jnp.float32)
    layer_out = (resid + lax.psum(ffn_term.astype(jnp.bfloat16), "tp").astype(jnp.float32)).astype(
        jnp.bfloat16
    )
    rim_frame, rim_id = shifted((layer_out[-1:], frame_id[-1:]), "seq", 1)
    pooled_count = frame_count // 2
    pairs = layer_out.reshape(pooled_count, 2, width)
    pair_ids = frame_id.reshape(pooled_count, 2)
    even_rows = pairs[:, 0]
    odd_rows = pairs[:, 1]
    before = jnp.concatenate([rim_frame, odd_rows[:-1]], axis=0)
    before_ids = jnp.concatenate([rim_id, pair_ids[:-1, 1]], axis=0)
    keep_before = (before_ids == pair_ids[:, 0]).astype(jnp.bfloat16)[:, None]
    keep_after = (pair_ids[:, 1] == pair_ids[:, 0]).astype(jnp.bfloat16)[:, None]
    conv = jnp.dot(before * keep_before, w_conv[0], preferred_element_type=jnp.float32)
    conv = conv + jnp.dot(even_rows, w_conv[1], preferred_element_type=jnp.float32)
    conv = conv + jnp.dot(odd_rows * keep_after, w_conv[2], preferred_element_type=jnp.float32)
    pooled = jax.nn.gelu(conv, approximate=False).astype(jnp.bfloat16)
    lm_share = pooled_count // lax.axis_size("tp")
    rows = lax.slice_in_dim(pooled, 0, lax.axis_size("tp") * lm_share, axis=0)
    return lax.psum_scatter(
        jnp.dot(rows, w_proj, preferred_element_type=jnp.float32).astype(jnp.bfloat16),
        "tp",
        scatter_dimension=0,
        tiled=True,
    )


def solution(mesh):
    placed = (
        P("seq", None),
        P(),
        P(None, None, "tp"),
        P("tp", None),
        P(),
        P(None, "tp"),
        P("tp", None),
        P(None, None, "tp"),
        P("tp", None),
        P("seq"),
    )
    return jax.shard_map(
        shards, mesh=mesh, in_specs=placed, out_specs=P(("seq", "tp"), None), check_vma=False
    )
```

profile of v0, /device:TPU:70, one launch (start us, length us, event | category | flops | bytes accessed | tf_op | source)
XLA Modules:
  0.0 292.0 jit_solution(9089519384101639386)
XLA Ops:
  6.6 1.5 fusion.320
  8.0 0.5 broadcast.583
  8.6 2.0 fusion.316
  10.6 1.9 collective-permute-start
  12.5 4.6 %collective-permute-start.12 = (s32[256]{0:T(256)S(1)}, s32[256]{0:T(256)S(1)}, u32[]{:S(2)}, u32[]{:S(2)}) collective-permute-start(s32[256]{0:T(256)S(1)} %fusion.234), channel_id=1, source_target_pairs={{0,12},{4,16},{8,20},{12,24},{16,28},{20,32},{24,36},{28,40},{32,4... | collective-permute-start | bytes 3080 | tf_op jit(solution)/shard_map/ppermute | solution.py:13
  17.1 2.4 collective-permute-start.15
  19.6 5.3 %collective-permute-start.18 = (s32[256]{0:T(256)S(1)}, s32[256]{0:T(256)S(1)}, u32[]{:S(2)}, u32[]{:S(2)}) collective-permute-start(s32[256]{0:T(256)S(1)} %fusion.234), channel_id=1, source_target_pairs={{0,16},{4,20},{8,24},{12,28},{16,32},{20,36},{24,40},{28,44},{32,4... | collective-permute-start | bytes 3080 | tf_op jit(solution)/shard_map/ppermute | solution.py:13
  24.8 2.1 collective-permute-start.21
  26.9 1.3 convert_reduce_fusion
  28.2 1.4 fusion.24
  29.6 1.8 convolution_convert_fusion.4
  31.6 0.5 convolution_convert_fusion.5
  32.1 4.4 %collective-permute-start.24 = (s32[256]{0:T(256)S(1)}, s32[256]{0:T(256)S(1)}, u32[]{:S(2)}, u32[]{:S(2)}) collective-permute-start(s32[256]{0:T(256)S(1)} %fusion.234), channel_id=1, source_target_pairs={{0,20},{4,24},{8,28},{12,32},{16,36},{20,40},{24,44},{28,48},{32,5... | collective-permute-start | bytes 3080 | tf_op jit(solution)/shard_map/ppermute | solution.py:13
  36.5 2.4 collective-permute-start.27
  38.9 2.9 collective-permute-start.3
  41.8 5.0 %collective-permute-start.6 = (s32[256]{0:T(256)S(1)}, s32[256]{0:T(256)S(1)}, u32[]{:S(2)}, u32[]{:S(2)}) collective-permute-start(s32[256]{0:T(256)S(1)} %fusion.234), channel_id=1, source_target_pairs={{0,8},{4,12},{8,16},{12,20},{16,24},{20,28},{24,32},{28,36},{32,40... | collective-permute-start | bytes 3080 | tf_op jit(solution)/shard_map/ppermute | solution.py:13
  46.9 1.9 collective-permute-start.9
  48.8 0.5 convolution_convert_fusion.3
  49.3 5.2 %collective-permute-start.28 = (bf16[256,320]{0,1:T(8,128)(2,1)S(1)}, bf16[256,320]{0,1:T(8,128)(2,1)S(1)}, u32[]{:S(2)}, u32[]{:S(2)}) collective-permute-start(bf16[256,320]{0,1:T(8,128)(2,1)S(1)} %convolution_convert_fusion.5), channel_id=1, source_target_pairs={{20,0},{24,4},{28,8},{32,12},{36,16},{40,20},{44,24},{48,28},{52,3... | collective-permute-start | bytes 491528 | tf_op jit(solution)/shard_map/ppermute | solution.py:13
  54.5 2.8 collective-permute-start.25
  57.3 4.2 %collective-permute-start.22 = (bf16[256,320]{0,1:T(8,128)(2,1)S(1)}, bf16[256,320]{0,1:T(8,128)(2,1)S(1)}, u32[]{:S(2)}, u32[]{:S(2)}) collective-permute-start(bf16[256,320]{0,1:T(8,128)(2,1)S(1)} %convolution_convert_fusion.5), channel_id=1, source_target_pairs={{16,0},{20,4},{24,8},{28,12},{32,16},{36,20},{40,24},{44,28},{48,3... | collective-permute-start | bytes 491528 | tf_op jit(solution)/shard_map/ppermute | solution.py:13
  61.5 4.1 %collective-permute-start.19 = (bf16[256,320]{0,1:T(8,128)(2,1)S(1)}, bf16[256,320]{0,1:T(8,128)(2,1)S(1)}, u32[]{:S(2)}, u32[]{:S(2)}) collective-permute-start(bf16[256,320]{0,1:T(8,128)(2,1)S(1)} %convolution_convert_fusion.5), channel_id=1, source_target_pairs={{0,16},{4,20},{8,24},{12,28},{16,32},{20,36},{24,40},{28,44},{32,4... | collective-permute-start | bytes 491528 | tf_op jit(solution)/shard_map/ppermute | solution.py:13
  65.6 1.9 collective-permute-start.16
  67.6 0.6 broadcast_compare_fusion.10
  68.6 5.8 %collective-permute-start.13 = (bf16[256,320]{0,1:T(8,128)(2,1)S(1)}, bf16[256,320]{0,1:T(8,128)(2,1)S(1)}, u32[]{:S(2)}, u32[]{:S(2)}) collective-permute-start(bf16[256,320]{0,1:T(8,128)(2,1)S(1)} %convolution_convert_fusion.5), channel_id=1, source_target_pairs={{0,12},{4,16},{8,20},{12,24},{16,28},{20,32},{24,36},{28,40},{32,4... | collective-permute-start | bytes 491528 | tf_op jit(solution)/shard_map/ppermute | solution.py:13
  74.8 1.9 collective-permute-start.10
  77.2 6.0 %collective-permute-start.7 = (bf16[256,320]{0,1:T(8,128)(2,1)S(1)}, bf16[256,320]{0,1:T(8,128)(2,1)S(1)}, u32[]{:S(2)}, u32[]{:S(2)}) collective-permute-start(bf16[256,320]{0,1:T(8,128)(2,1)S(1)} %convolution_convert_fusion.5), channel_id=1, source_target_pairs={{0,8},{4,12},{8,16},{12,20},{16,24},{20,28},{24,32},{28,36},{32,40... | collective-permute-start | bytes 491528 | tf_op jit(solution)/shard_map/ppermute | solution.py:13
  83.6 1.9 collective-permute-start.4
  86.0 2.4 collective-permute-start.1
  88.8 3.2 %collective-permute-start.5 = (bf16[256,320]{0,1:T(8,128)(2,1)S(1)}, bf16[256,320]{0,1:T(8,128)(2,1)S(1)}, u32[]{:S(2)}, u32[]{:S(2)}) collective-permute-start(bf16[256,320]{0,1:T(8,128)(2,1)S(1)} %convolution_convert_fusion.3), channel_id=1, source_target_pairs={{4,0},{8,4},{12,8},{16,12},{20,16},{24,20},{28,24},{32,28},{36,32}... | collective-permute-start | bytes 491528 | tf_op jit(solution)/shard_map/ppermute | solution.py:13
  92.4 6.3 %collective-permute-start.8 = (bf16[256,320]{0,1:T(8,128)(2,1)S(1)}, bf16[256,320]{0,1:T(8,128)(2,1)S(1)}, u32[]{:S(2)}, u32[]{:S(2)}) collective-permute-start(bf16[256,320]{0,1:T(8,128)(2,1)S(1)} %convolution_convert_fusion.3), channel_id=1, source_target_pairs={{0,8},{4,12},{8,16},{12,20},{16,24},{20,28},{24,32},{28,36},{32,40... | collective-permute-start | bytes 491528 | tf_op jit(solution)/shard_map/ppermute | solution.py:13
  99.2 1.9 collective-permute-start.11
  101.6 1.9 collective-permute-start.14
  103.9 5.1 %collective-permute-start.17 = (bf16[256,320]{0,1:T(8,128)(2,1)S(1)}, bf16[256,320]{0,1:T(8,128)(2,1)S(1)}, u32[]{:S(2)}, u32[]{:S(2)}) collective-permute-start(bf16[256,320]{0,1:T(8,128)(2,1)S(1)} %convolution_convert_fusion.3), channel_id=1, source_target_pairs={{12,0},{16,4},{20,8},{24,12},{28,16},{32,20},{36,24},{40,28},{44,3... | collective-permute-start | bytes 491528 | tf_op jit(solution)/shard_map/ppermute | solution.py:13
  109.8 0.5 fusion.61
  110.3 0.5 fusion.65
  110.8 0.5 fusion.69
  112.7 4.3 %collective-permute-start.20 = (bf16[256,320]{0,1:T(8,128)(2,1)S(1)}, bf16[256,320]{0,1:T(8,128)(2,1)S(1)}, u32[]{:S(2)}, u32[]{:S(2)}) collective-permute-start(bf16[256,320]{0,1:T(8,128)(2,1)S(1)} %convolution_convert_fusion.3), channel_id=1, source_target_pairs={{0,16},{4,20},{8,24},{12,28},{16,32},{20,36},{24,40},{28,44},{32,4... | collective-permute-start | bytes 491528 | tf_op jit(solution)/shard_map/ppermute | solution.py:13
  117.3 3.1 %collective-permute-start.23 = (bf16[256,320]{0,1:T(8,128)(2,1)S(1)}, bf16[256,320]{0,1:T(8,128)(2,1)S(1)}, u32[]{:S(2)}, u32[]{:S(2)}) collective-permute-start(bf16[256,320]{0,1:T(8,128)(2,1)S(1)} %convolution_convert_fusion.3), channel_id=1, source_target_pairs={{16,0},{20,4},{24,8},{28,12},{32,16},{36,20},{40,24},{44,28},{48,3... | collective-permute-start | bytes 491528 | tf_op jit(solution)/shard_map/ppermute | solution.py:13
  120.7 4.5 %collective-permute-start.26 = (bf16[256,320]{0,1:T(8,128)(2,1)S(1)}, bf16[256,320]{0,1:T(8,128)(2,1)S(1)}, u32[]{:S(2)}, u32[]{:S(2)}) collective-permute-start(bf16[256,320]{0,1:T(8,128)(2,1)S(1)} %convolution_convert_fusion.3), channel_id=1, source_target_pairs={{0,20},{4,24},{8,28},{12,32},{16,36},{20,40},{24,44},{28,48},{32,5... | collective-permute-start | bytes 491528 | tf_op jit(solution)/shard_map/ppermute | solution.py:13
  125.5 2.5 collective-permute-start.29
  128.3 1.9 collective-permute-start.2
  131.6 3.5 %collective-permute-done.29 = bf16[256,320]{0,1:T(8,128)(2,1)S(1)} collective-permute-done((bf16[256,320]{0,1:T(8,128)(2,1)S(1)}, bf16[256,320]{0,1:T(8,128)(2,1)S(1)}, u32[]{:S(2)}, u32[]{:S(2)}) %collective-permute-start.29) | collective-permute-done | bytes 163872 | tf_op jit(solution)/shard_map/ppermute | solution.py:13
  135.4 1.4 collective-permute-done.2
  137.3 0.7 copy-done.5
  138.0 1.4 convolution_convert_fusion.2
  139.4 0.6 slice.69
  140.0 3.3 %collective-permute-start.31 = (s32[1]{0:T(128)}, s32[1]{0:T(128)}, u32[]{:S(2)}, u32[]{:S(2)}) collective-permute-start(s32[1]{0:T(128)} %slice.69), channel_id=1, source_target_pairs={{0,4},{4,8},{8,12},{12,16},{16,20},{20,24},{24,28},{28,32},{32,36}... | collective-permute-start | bytes 20 | tf_op jit(solution)/shard_map/ppermute | solution.py:13
  143.6 43.0 %all-reduce.3.cloned.1.call-done = bf16[256,1280]{1,0:T(8,128)(2,1)} async-done(((bf16[256,1280]{1,0:T(8,128)(2,1)}), bf16[256,1280]{1,0:T(8,128)(2,1)}) %all-reduce.3.cloned.1.call-update) | async-done | bytes 655376 | tf_op jit(solution)/shard_map/psum | solution.py:75
  186.6 1.6 fusion.83
  188.6 7.8 %convolution_convert_fusion.1 = bf16[256,1280]{1,0:T(8,128)(2,1)} fusion(bf16[1280,1280]{1,0:T(8,128)(2,1)S(1)} %copy-done, bf16[1280,1280]{1,0:T(8,128)(2,1)} %param.17, bf16[256,1280]{1,0:T(8,128)(2,1)} %all-reduce.3.cloned.1.call-done, bf16[256,1280]{1,0:T(8,128)(2,1)} %param.12, f32[1280]{0:T(1024)S(1)} %copy-done.9, f32[256]{0:T(256)S(1)} %add_rsqrt_fusion, ...), kind=kOutput, calls=%fused_computation.1 | convolution fusion | flops 1701642240 | bytes 8526848 | tf_op jit(solution)/shard_map/dot_general | solution.py:80
  196.8 0.7 pad_add_fusion
  197.8 43.1 %all-reduce.5.cloned.1.call-done = bf16[256,1280]{1,0:T(8,128)(2,1)} async-done(((bf16[256,1280]{1,0:T(8,128)(2,1)}), bf16[256,1280]{1,0:T(8,128)(2,1)}) %all-reduce.5.cloned.1.call-update) | async-done | bytes 655376 | tf_op jit(solution)/shard_map/psum | solution.py:81
  240.9 2.6 add_convert_fusion
  243.5 2.6 reshape.870
  246.2 0.7 slice.81
  246.9 2.6 fusion.319
  249.5 2.1 collective-permute-start.30
  251.7 1.1 fusion.84
  252.8 1.1 fusion.86
  253.8 0.7 slice.82
  254.5 0.8 copy.88
  255.3 4.7 %convolution_convert_fusion = bf16[128,4096]{1,0:T(8,128)(2,1)} fusion(bf16[320,4096]{1,0:T(8,128)(2,1)} %param.20, f32[128,320]{0,1:T(8,128)} %fusion.84, f32[128,320]{0,1:T(8,128)} %fusion.86, bf16[3,1280,320]{1,2,0:T(8,128)(2,1)} %param.19, bf16[127,1280]{1,0:T(8,128)(2,1)} %bitcast.228, bf16[1,1280]{1,0:T(2,128)(2,1)S(1)} %collective-permute-done.30, ...), kind=kOutput, calls=%fused_computation | convolution fusion | flops 444653568 | bytes 5147392 | tf_op jit(solution)/shard_map/dot_general | solution.py:101
  260.0 25.4 %reduce-scatter.2.cloned.1.call-done = bf16[32,4096]{1,0:T(8,128)(2,1)} async-done(((bf16[128,4096]{1,0:T(8,128)(2,1)}), bf16[32,4096]{1,0:T(8,128)(2,1)}) %reduce-scatter.2.cloned.1.call-update) | async-done | bytes 262160 | tf_op jit(solution)/shard_map/reduce_scatter | solution.py:100
  (101 shorter events, 11.4 us)
Async XLA Ops:
  6.5 182.1 %copy-start = (bf16[1280,1280]{1,0:T(8,128)(2,1)S(1)}, bf16[1280,1280]{1,0:T(8,128)(2,1)}, u32[]{:S(2)}) copy-start(bf16[1280,1280]{1,0:T(8,128)(2,1)} %param.18) | copy-start | bytes 9830404
  6.5 23.1 %copy-start.8 = (f32[1280]{0:T(1024)S(1)}, f32[1280]{0:T(1024)}, u32[]{:S(2)}) copy-start(f32[1280]{0:T(1024)} %param.13) | copy-start | bytes 15364
  6.5 180.1 %all-reduce.3.cloned.1.call-start = ((), (), s32[]{:S(2)}) async-start(), calls=%async_computation.1 | async-start | bytes 1310720 | tf_op jit(solution)/shard_map/psum | solution.py:75
  8.6 21.1 %copy-start.1 = (bf16[256,1280]{1,0:T(8,128)(2,1)S(1)}, bf16[256,1280]{1,0:T(8,128)(2,1)}, u32[]{:S(2)}) copy-start(bf16[256,1280]{1,0:T(8,128)(2,1)} %param.12) | copy-start | bytes 1966084
  10.6 21.5 %collective-permute-start = (s32[256]{0:T(256)S(1)}, s32[256]{0:T(256)S(1)}, u32[]{:S(2)}, u32[]{:S(2)}) collective-permute-start(s32[256]{0:T(256)S(1)} %fusion.234), channel_id=1, source_target_pairs={{0,4},{4,8},{8,12},{12,16},{16,20},{20,24},{24,28},{28,32},{32,36}... | collective-permute-start | bytes 3080 | tf_op jit(solution)/shard_map/ppermute | solution.py:13
  12.5 24.0 %collective-permute-start.12 = (s32[256]{0:T(256)S(1)}, s32[256]{0:T(256)S(1)}, u32[]{:S(2)}, u32[]{:S(2)}) collective-permute-start(s32[256]{0:T(256)S(1)} %fusion.234), channel_id=1, source_target_pairs={{0,12},{4,16},{8,20},{12,24},{16,28},{20,32},{24,36},{28,40},{32,4... | collective-permute-start | bytes 3080 | tf_op jit(solution)/shard_map/ppermute | solution.py:13
  17.1 21.8 %collective-permute-start.15 = (s32[256]{0:T(256)S(1)}, s32[256]{0:T(256)S(1)}, u32[]{:S(2)}, u32[]{:S(2)}) collective-permute-start(s32[256]{0:T(256)S(1)} %fusion.234), channel_id=1, source_target_pairs={{12,0},{16,4},{20,8},{24,12},{28,16},{32,20},{36,24},{40,28},{44,3... | collective-permute-start | bytes 3080 | tf_op jit(solution)/shard_map/ppermute | solution.py:13
  19.6 22.3 %collective-permute-start.18 = (s32[256]{0:T(256)S(1)}, s32[256]{0:T(256)S(1)}, u32[]{:S(2)}, u32[]{:S(2)}) collective-permute-start(s32[256]{0:T(256)S(1)} %fusion.234), channel_id=1, source_target_pairs={{0,16},{4,20},{8,24},{12,28},{16,32},{20,36},{24,40},{28,44},{32,4... | collective-permute-start | bytes 3080 | tf_op jit(solution)/shard_map/ppermute | solution.py:13
  24.8 22.0 %collective-permute-start.21 = (s32[256]{0:T(256)S(1)}, s32[256]{0:T(256)S(1)}, u32[]{:S(2)}, u32[]{:S(2)}) collective-permute-start(s32[256]{0:T(256)S(1)} %fusion.234), channel_id=1, source_target_pairs={{16,0},{20,4},{24,8},{28,12},{32,16},{36,20},{40,24},{44,28},{48,3... | collective-permute-start | bytes 3080 | tf_op jit(solution)/shard_map/ppermute | solution.py:13
  29.6 1.9 copy-start.6
  32.1 17.2 %collective-permute-start.24 = (s32[256]{0:T(256)S(1)}, s32[256]{0:T(256)S(1)}, u32[]{:S(2)}, u32[]{:S(2)}) collective-permute-start(s32[256]{0:T(256)S(1)} %fusion.234), channel_id=1, source_target_pairs={{0,20},{4,24},{8,28},{12,32},{16,36},{20,40},{24,44},{28,48},{32,5... | collective-permute-start | bytes 3080 | tf_op jit(solution)/shard_map/ppermute | solution.py:13
  36.5 18.0 %collective-permute-start.27 = (s32[256]{0:T(256)S(1)}, s32[256]{0:T(256)S(1)}, u32[]{:S(2)}, u32[]{:S(2)}) collective-permute-start(s32[256]{0:T(256)S(1)} %fusion.234), channel_id=1, source_target_pairs={{20,0},{24,4},{28,8},{32,12},{36,16},{40,20},{44,24},{48,28},{52,3... | collective-permute-start | bytes 3080 | tf_op jit(solution)/shard_map/ppermute | solution.py:13
  38.9 18.4 %collective-permute-start.3 = (s32[256]{0:T(256)S(1)}, s32[256]{0:T(256)S(1)}, u32[]{:S(2)}, u32[]{:S(2)}) collective-permute-start(s32[256]{0:T(256)S(1)} %fusion.234), channel_id=1, source_target_pairs={{4,0},{8,4},{12,8},{16,12},{20,16},{24,20},{28,24},{32,28},{36,32}... | collective-permute-start | bytes 3080 | tf_op jit(solution)/shard_map/ppermute | solution.py:13
  41.8 19.7 %collective-permute-start.6 = (s32[256]{0:T(256)S(1)}, s32[256]{0:T(256)S(1)}, u32[]{:S(2)}, u32[]{:S(2)}) collective-permute-start(s32[256]{0:T(256)S(1)} %fusion.234), channel_id=1, source_target_pairs={{0,8},{4,12},{8,16},{12,20},{16,24},{20,28},{24,32},{28,36},{32,40... | collective-permute-start | bytes 3080 | tf_op jit(solution)/shard_map/ppermute | solution.py:13
  46.9 18.7 %collective-permute-start.9 = (s32[256]{0:T(256)S(1)}, s32[256]{0:T(256)S(1)}, u32[]{:S(2)}, u32[]{:S(2)}) collective-permute-start(s32[256]{0:T(256)S(1)} %fusion.234), channel_id=1, source_target_pairs={{8,0},{12,4},{16,8},{20,12},{24,16},{28,20},{32,24},{36,28},{40,32... | collective-permute-start | bytes 3080 | tf_op jit(solution)/shard_map/ppermute | solution.py:13
  49.3 19.3 %collective-permute-start.28 = (bf16[256,320]{0,1:T(8,128)(2,1)S(1)}, bf16[256,320]{0,1:T(8,128)(2,1)S(1)}, u32[]{:S(2)}, u32[]{:S(2)}) collective-permute-start(bf16[256,320]{0,1:T(8,128)(2,1)S(1)} %convolution_convert_fusion.5), channel_id=1, source_target_pairs={{20,0},{24,4},{28,8},{32,12},{36,16},{40,20},{44,24},{48,28},{52,3... | collective-permute-start | bytes 491528 | tf_op jit(solution)/shard_map/ppermute | solution.py:13
  54.5 20.2 %collective-permute-start.25 = (bf16[256,320]{0,1:T(8,128)(2,1)S(1)}, bf16[256,320]{0,1:T(8,128)(2,1)S(1)}, u32[]{:S(2)}, u32[]{:S(2)}) collective-permute-start(bf16[256,320]{0,1:T(8,128)(2,1)S(1)} %convolution_convert_fusion.5), channel_id=1, source_target_pairs={{0,20},{4,24},{8,28},{12,32},{16,36},{20,40},{24,44},{28,48},{32,5... | collective-permute-start | bytes 491528 | tf_op jit(solution)/shard_map/ppermute | solution.py:13
  57.3 19.8 %collective-permute-start.22 = (bf16[256,320]{0,1:T(8,128)(2,1)S(1)}, bf16[256,320]{0,1:T(8,128)(2,1)S(1)}, u32[]{:S(2)}, u32[]{:S(2)}) collective-permute-start(bf16[256,320]{0,1:T(8,128)(2,1)S(1)} %convolution_convert_fusion.5), channel_id=1, source_target_pairs={{16,0},{20,4},{24,8},{28,12},{32,16},{36,20},{40,24},{44,28},{48,3... | collective-permute-start | bytes 491528 | tf_op jit(solution)/shard_map/ppermute | solution.py:13
  61.5 22.1 %collective-permute-start.19 = (bf16[256,320]{0,1:T(8,128)(2,1)S(1)}, bf16[256,320]{0,1:T(8,128)(2,1)S(1)}, u32[]{:S(2)}, u32[]{:S(2)}) collective-permute-start(bf16[256,320]{0,1:T(8,128)(2,1)S(1)} %convolution_convert_fusion.5), channel_id=1, source_target_pairs={{0,16},{4,20},{8,24},{12,28},{16,32},{20,36},{24,40},{28,44},{32,4... | collective-permute-start | bytes 491528 | tf_op jit(solution)/shard_map/ppermute | solution.py:13
  65.6 20.4 %collective-permute-start.16 = (bf16[256,320]{0,1:T(8,128)(2,1)S(1)}, bf16[256,320]{0,1:T(8,128)(2,1)S(1)}, u32[]{:S(2)}, u32[]{:S(2)}) collective-permute-start(bf16[256,320]{0,1:T(8,128)(2,1)S(1)} %convolution_convert_fusion.5), channel_id=1, source_target_pairs={{12,0},{16,4},{20,8},{24,12},{28,16},{32,20},{36,24},{40,28},{44,3... | collective-permute-start | bytes 491528 | tf_op jit(solution)/shard_map/ppermute | solution.py:13
  68.6 20.2 %collective-permute-start.13 = (bf16[256,320]{0,1:T(8,128)(2,1)S(1)}, bf16[256,320]{0,1:T(8,128)(2,1)S(1)}, u32[]{:S(2)}, u32[]{:S(2)}) collective-permute-start(bf16[256,320]{0,1:T(8,128)(2,1)S(1)} %convolution_convert_fusion.5), channel_id=1, source_target_pairs={{0,12},{4,16},{8,20},{12,24},{16,28},{20,32},{24,36},{28,40},{32,4... | collective-permute-start | bytes 491528 | tf_op jit(solution)/shard_map/ppermute | solution.py:13
  74.8 17.6 %collective-permute-start.10 = (bf16[256,320]{0,1:T(8,128)(2,1)S(1)}, bf16[256,320]{0,1:T(8,128)(2,1)S(1)}, u32[]{:S(2)}, u32[]{:S(2)}) collective-permute-start(bf16[256,320]{0,1:T(8,128)(2,1)S(1)} %convolution_convert_fusion.5), channel_id=1, source_target_pairs={{8,0},{12,4},{16,8},{20,12},{24,16},{28,20},{32,24},{36,28},{40,32... | collective-permute-start | bytes 491528 | tf_op jit(solution)/shard_map/ppermute | solution.py:13
  77.2 22.0 %collective-permute-start.7 = (bf16[256,320]{0,1:T(8,128)(2,1)S(1)}, bf16[256,320]{0,1:T(8,128)(2,1)S(1)}, u32[]{:S(2)}, u32[]{:S(2)}) collective-permute-start(bf16[256,320]{0,1:T(8,128)(2,1)S(1)} %convolution_convert_fusion.5), channel_id=1, source_target_pairs={{0,8},{4,12},{8,16},{12,20},{16,24},{20,28},{24,32},{28,36},{32,40... | collective-permute-start | bytes 491528 | tf_op jit(solution)/shard_map/ppermute | solution.py:13
  83.6 17.9 %collective-permute-start.4 = (bf16[256,320]{0,1:T(8,128)(2,1)S(1)}, bf16[256,320]{0,1:T(8,128)(2,1)S(1)}, u32[]{:S(2)}, u32[]{:S(2)}) collective-permute-start(bf16[256,320]{0,1:T(8,128)(2,1)S(1)} %convolution_convert_fusion.5), channel_id=1, source_target_pairs={{4,0},{8,4},{12,8},{16,12},{20,16},{24,20},{28,24},{32,28},{36,32}... | collective-permute-start | bytes 491528 | tf_op jit(solution)/shard_map/ppermute | solution.py:13
  86.0 17.9 %collective-permute-start.1 = (bf16[256,320]{0,1:T(8,128)(2,1)S(1)}, bf16[256,320]{0,1:T(8,128)(2,1)S(1)}, u32[]{:S(2)}, u32[]{:S(2)}) collective-permute-start(bf16[256,320]{0,1:T(8,128)(2,1)S(1)} %convolution_convert_fusion.5), channel_id=1, source_target_pairs={{0,4},{4,8},{8,12},{12,16},{16,20},{20,24},{24,28},{28,32},{32,36}... | collective-permute-start | bytes 491528 | tf_op jit(solution)/shard_map/ppermute | solution.py:13
  88.8 23.8 %collective-permute-start.5 = (bf16[256,320]{0,1:T(8,128)(2,1)S(1)}, bf16[256,320]{0,1:T(8,128)(2,1)S(1)}, u32[]{:S(2)}, u32[]{:S(2)}) collective-permute-start(bf16[256,320]{0,1:T(8,128)(2,1)S(1)} %convolution_convert_fusion.3), channel_id=1, source_target_pairs={{4,0},{8,4},{12,8},{16,12},{20,16},{24,20},{28,24},{32,28},{36,32}... | collective-permute-start | bytes 491528 | tf_op jit(solution)/shard_map/ppermute | solution.py:13
  92.4 24.8 %collective-permute-start.8 = (bf16[256,320]{0,1:T(8,128)(2,1)S(1)}, bf16[256,320]{0,1:T(8,128)(2,1)S(1)}, u32[]{:S(2)}, u32[]{:S(2)}) collective-permute-start(bf16[256,320]{0,1:T(8,128)(2,1)S(1)} %convolution_convert_fusion.3), channel_id=1, source_target_pairs={{0,8},{4,12},{8,16},{12,20},{16,24},{20,28},{24,32},{28,36},{32,40... | collective-permute-start | bytes 491528 | tf_op jit(solution)/shard_map/ppermute | solution.py:13
  99.2 21.5 %collective-permute-start.11 = (bf16[256,320]{0,1:T(8,128)(2,1)S(1)}, bf16[256,320]{0,1:T(8,128)(2,1)S(1)}, u32[]{:S(2)}, u32[]{:S(2)}) collective-permute-start(bf16[256,320]{0,1:T(8,128)(2,1)S(1)} %convolution_convert_fusion.3), channel_id=1, source_target_pairs={{8,0},{12,4},{16,8},{20,12},{24,16},{28,20},{32,24},{36,28},{40,32... | collective-permute-start | bytes 491528 | tf_op jit(solution)/shard_map/ppermute | solution.py:13
  101.6 24.0 %collective-permute-start.14 = (bf16[256,320]{0,1:T(8,128)(2,1)S(1)}, bf16[256,320]{0,1:T(8,128)(2,1)S(1)}, u32[]{:S(2)}, u32[]{:S(2)}) collective-permute-start(bf16[256,320]{0,1:T(8,128)(2,1)S(1)} %convolution_convert_fusion.3), channel_id=1, source_target_pairs={{0,12},{4,16},{8,20},{12,24},{16,28},{20,32},{24,36},{28,40},{32,4... | collective-permute-start | bytes 491528 | tf_op jit(solution)/shard_map/ppermute | solution.py:13
  103.9 24.4 %collective-permute-start.17 = (bf16[256,320]{0,1:T(8,128)(2,1)S(1)}, bf16[256,320]{0,1:T(8,128)(2,1)S(1)}, u32[]{:S(2)}, u32[]{:S(2)}) collective-permute-start(bf16[256,320]{0,1:T(8,128)(2,1)S(1)} %convolution_convert_fusion.3), channel_id=1, source_target_pairs={{12,0},{16,4},{20,8},{24,12},{28,16},{32,20},{36,24},{40,28},{44,3... | collective-permute-start | bytes 491528 | tf_op jit(solution)/shard_map/ppermute | solution.py:13
  112.7 17.9 %collective-permute-start.20 = (bf16[256,320]{0,1:T(8,128)(2,1)S(1)}, bf16[256,320]{0,1:T(8,128)(2,1)S(1)}, u32[]{:S(2)}, u32[]{:S(2)}) collective-permute-start(bf16[256,320]{0,1:T(8,128)(2,1)S(1)} %convolution_convert_fusion.3), channel_id=1, source_target_pairs={{0,16},{4,20},{8,24},{12,28},{16,32},{20,36},{24,40},{28,44},{32,4... | collective-permute-start | bytes 491528 | tf_op jit(solution)/shard_map/ppermute | solution.py:13
  117.3 13.6 %collective-permute-start.23 = (bf16[256,320]{0,1:T(8,128)(2,1)S(1)}, bf16[256,320]{0,1:T(8,128)(2,1)S(1)}, u32[]{:S(2)}, u32[]{:S(2)}) collective-permute-start(bf16[256,320]{0,1:T(8,128)(2,1)S(1)} %convolution_convert_fusion.3), channel_id=1, source_target_pairs={{16,0},{20,4},{24,8},{28,12},{32,16},{36,20},{40,24},{44,28},{48,3... | collective-permute-start | bytes 491528 | tf_op jit(solution)/shard_map/ppermute | solution.py:13
  120.7 10.6 %collective-permute-start.26 = (bf16[256,320]{0,1:T(8,128)(2,1)S(1)}, bf16[256,320]{0,1:T(8,128)(2,1)S(1)}, u32[]{:S(2)}, u32[]{:S(2)}) collective-permute-start(bf16[256,320]{0,1:T(8,128)(2,1)S(1)} %convolution_convert_fusion.3), channel_id=1, source_target_pairs={{0,20},{4,24},{8,28},{12,32},{16,36},{20,40},{24,44},{28,48},{32,5... | collective-permute-start | bytes 491528 | tf_op jit(solution)/shard_map/ppermute | solution.py:13
  125.5 9.6 %collective-permute-start.29 = (bf16[256,320]{0,1:T(8,128)(2,1)S(1)}, bf16[256,320]{0,1:T(8,128)(2,1)S(1)}, u32[]{:S(2)}, u32[]{:S(2)}) collective-permute-start(bf16[256,320]{0,1:T(8,128)(2,1)S(1)} %convolution_convert_fusion.3), channel_id=1, source_target_pairs={{20,0},{24,4},{28,8},{32,12},{36,16},{40,20},{44,24},{48,28},{52,3... | collective-permute-start | bytes 491528 | tf_op jit(solution)/shard_map/ppermute | solution.py:13
  128.3 8.5 %collective-permute-start.2 = (bf16[256,320]{0,1:T(8,128)(2,1)S(1)}, bf16[256,320]{0,1:T(8,128)(2,1)S(1)}, u32[]{:S(2)}, u32[]{:S(2)}) collective-permute-start(bf16[256,320]{0,1:T(8,128)(2,1)S(1)} %convolution_convert_fusion.3), channel_id=1, source_target_pairs={{0,4},{4,8},{8,12},{12,16},{16,20},{20,24},{24,28},{28,32},{32,36}... | collective-permute-start | bytes 491528 | tf_op jit(solution)/shard_map/ppermute | solution.py:13
  136.8 1.1 copy-start.5
  139.4 101.6 %all-reduce.5.cloned.1.call-start = ((), (), s32[]{:S(2)}) async-start(), calls=%async_computation.2 | async-start | bytes 1310720 | tf_op jit(solution)/shard_map/psum | solution.py:81
  140.0 56.8 %collective-permute-start.31 = (s32[1]{0:T(128)}, s32[1]{0:T(128)}, u32[]{:S(2)}, u32[]{:S(2)}) collective-permute-start(s32[1]{0:T(128)} %slice.69), channel_id=1, source_target_pairs={{0,4},{4,8},{8,12},{12,16},{16,20},{20,24},{24,28},{28,32},{32,36}... | collective-permute-start | bytes 20 | tf_op jit(solution)/shard_map/ppermute | solution.py:13
  186.6 1.7 copy-start.2
  186.6 1.7 copy-start.4
  186.6 2.0 copy-start.9
  196.4 89.0 %reduce-scatter.2.cloned.1.call-start = ((), (), s32[]{:S(2)}) async-start(), calls=%async_computation.3 | async-start | bytes 1310720 | tf_op jit(solution)/shard_map/reduce_scatter | solution.py:100
  246.9 4.8 %copy-start.7 = (bf16[3,1280,320]{1,2,0:T(8,128)(2,1)S(1)}, bf16[3,1280,320]{1,2,0:T(8,128)(2,1)}, u32[]{:S(2)}) copy-start(bf16[3,1280,320]{1,2,0:T(8,128)(2,1)} %param.19) | copy-start | bytes 7372804
  249.5 5.8 %collective-permute-start.30 = (bf16[1,1280]{1,0:T(2,128)(2,1)S(1)}, bf16[1,1280]{1,0:T(2,128)(2,1)S(1)}, u32[]{:S(2)}, u32[]{:S(2)}) collective-permute-start(bf16[1,1280]{1,0:T(2,128)(2,1)S(1)} %slice.81), channel_id=1, source_target_pairs={{0,4},{4,8},{8,12},{12,16},{16,20},{20,24},{24,28},{28,32},{32,36}... | collective-permute-start | bytes 7688 | tf_op jit(solution)/shard_map/ppermute | solution.py:13
  251.6 2.2 copy-start.3
Sparse Core Ops, SparseCore 0:
  139.5 47.0 all-reduce.2
  196.6 44.3 all-reduce.4
  260.2 25.2 reduce-scatter.1
where the time goes:
time: 294 us; the launch traced here: 292 us
  waiting for transfers between devices  117 us (40%)
  starting transfers between devices  109 us (37%)
  matrix products  27.3 us (9%)
  between operations  13.8 us (5%)
  other arithmetic  13.7 us (5%)
  local copies, waits for them, and re-layouts  11.4 us (4%)
    ppermute x32, starting transfers between devices, shifted(): lax.ppermute(value, axis, [(source, source + steps) for source in range(l...  109 us
    psum x1, waiting for transfers between devices, shards(): lax.psum(ffn_term.astype(jnp.bfloat16), 'tp').astype(jnp.float32)  43.1 us
    psum x1, waiting for transfers between devices, shards(): lax.psum(attn_term.astype(jnp.bfloat16), 'tp').astype(jnp.float32)  43 us
    reduce_scatter x1, waiting for transfers between devices, shards(): lax.psum_scatter(jnp.dot(rows, w_proj, preferred_element_type=jnp.float32...  25.4 us
    dot_general x1, matrix products, shards(): ffn_term = jnp.dot(hidden, w_down, preferred_element_type=jnp.float32)  7.76 us
  transfers between devices with their start and end apart: 35, of which 5 were waited for; matrix products, arithmetic and copies ran while one was open for 11% of the time, Pallas kernels for 0%

commit v1 on v0

v1 whole, which is shorter than its diff:
```python
import jax
import jax.numpy as jnp
from jax import lax
from jax.experimental import pallas as pl
from jax.experimental.pallas import tpu as pltpu
from jax.sharding import PartitionSpec as P

HEAD_DIM = 64
BLK = 128
MOST = 11
IDROWS = 16
SEQ = "seq"
TP = "tp"
VMEM = pl.BlockSpec(memory_space=pltpu.VMEM)
SMEM = pl.BlockSpec(memory_space=pltpu.SMEM)
ANY = pl.BlockSpec(memory_space=pl.ANY)


def send_tp(value, steps):
    count = lax.axis_size(TP)
    return lax.ppermute(value, TP, [(t, (t + steps) % count) for t in range(count)])


def send_seq(value, steps):
    count = lax.axis_size(SEQ)
    return lax.ppermute(
        value, SEQ, [(s, s + steps) for s in range(count) if 0 <= s + steps < count]
    )


def send_partner(value):
    count = lax.axis_size(SEQ)
    return lax.ppermute(value, SEQ, [(s, s ^ 1) for s in range(count)])


def send_five(value):
    count = lax.axis_size(SEQ)
    pairs = [(s, s + 5 if s % 2 else s - 5) for s in range(count)]
    return lax.ppermute(value, SEQ, [(a, b) for a, b in pairs if 0 <= b < count])


def layer_norm(value, gain):
    mean = jnp.mean(value, axis=-1, keepdims=True)
    centred = value - mean
    spread = jnp.mean(centred * centred, axis=-1, keepdims=True)
    return centred * lax.rsqrt(spread + 1e-05) * gain


def kv_kernel(ids_ref, frames_ref, gain_ref, w_ref, normed_ref, kv_ref):
    rows = frames_ref.shape[0]
    normed = layer_norm(frames_ref[...].astype(jnp.float32), gain_ref[...]).astype(jnp.bfloat16)
    normed_ref[...] = normed
    keys = jnp.dot(normed, w_ref[1], preferred_element_type=jnp.float32).astype(jnp.bfloat16)
    values = jnp.dot(normed, w_ref[2], preferred_element_type=jnp.float32).astype(jnp.bfloat16)
    kv_ref[:rows, :256] = keys[:, :256]
    kv_ref[:rows, 256:512] = values[:, :256]
    kv_ref[:rows, 512:576] = keys[:, 256:]
    kv_ref[:rows, 576:] = values[:, 256:]
    row = lax.broadcasted_iota(jnp.int32, (IDROWS, kv_ref.shape[1]), 0)
    marks = jnp.where(row == 0, ids_ref[0] + 1, jnp.where(row == 1, ids_ref[1] + 1, 0))
    kv_ref[rows:, :] = marks.astype(jnp.float32).astype(jnp.bfloat16)


def attend_kernel(info_ref, q_ref, *refs):
    pieces, (out_ref, buf, marks, sems, mark_sems) = refs[:11], refs[11:]
    parity = info_ref[2]
    rows = q_ref.shape[0]
    copies = []
    for n, piece in enumerate(pieces):
        if n < 5:
            slot = 1 + 2 * n + parity
        elif n < 10:
            slot = 2 * (n - 4) - parity
        else:
            slot = 11 * parity
        copies.append(pltpu.make_async_copy(
            piece.at[pl.ds(rows, IDROWS), pl.ds(0, 128)], marks.at[slot], mark_sems.at[n]))
        copies.append(pltpu.make_async_copy(
            piece.at[pl.ds(0, rows), :], buf.at[pl.ds(pl.multiple_of(slot * rows, rows), rows), :], sems.at[n]))
    for copy in copies:
        copy.start()
    unused = 11 - 11 * parity
    marks[unused] = jnp.zeros(marks.shape[1:], marks.dtype)
    for copy in copies:
        copy.wait()
    seen = marks[...].astype(jnp.float32)
    row = lax.broadcasted_iota(jnp.int32, seen.shape, 1)
    place = (2 * lax.broadcasted_iota(jnp.int32, seen.shape, 0) + row).astype(jnp.float32)
    lane = lax.broadcasted_iota(jnp.int32, (BLK, 128), 1)
    column = lax.broadcasted_iota(jnp.int32, (1, MOST * BLK), 1)
    low = lane < HEAD_DIM
    for i in range(2):
        mine = (info_ref[i] + 1).astype(jnp.float32)
        same = (seen == mine) & (row < 2)
        first = jnp.min(jnp.where(same, place, 99.0)).astype(jnp.int32)
        last = jnp.max(jnp.where(same, place, -1.0)).astype(jnp.int32)
        start = jnp.clip(first, 2 * parity, MOST + 2 * parity)
        begin = pl.multiple_of(start * BLK, BLK)
        kept = (last + 1 - start) * BLK
        bias = jnp.where(column < kept, 0.0, -1e30)
        window = pl.ds(begin, MOST * BLK)
        for pair in range(3):
            if pair < 2:
                q_pair = q_ref[i * BLK:(i + 1) * BLK, pair * 128:(pair + 1) * 128]
                keys = buf[window, pair * 128:(pair + 1) * 128]
                values = buf[window, 256 + pair * 128:256 + (pair + 1) * 128]
            else:
                q_pair = q_ref[i * BLK:(i + 1) * BLK, 256:384]
                keys = buf[window, 512:640]
                values = keys
            q_pair = q_pair * jnp.asarray(HEAD_DIM ** -0.5, q_pair.dtype)
            halves = []
            for half in range(2 if pair < 2 else 1):
                q_head = jnp.where(low if half == 0 else ~low, q_pair, jnp.zeros_like(q_pair))
                scores = lax.dot_general(
                    q_head, keys, (((1,), (1,)), ((), ())), preferred_element_type=jnp.float32) + bias
                top = jnp.max(scores, axis=-1, keepdims=True)
                weights = jnp.exp(scores - top)
                total = jnp.sum(weights, axis=-1, keepdims=True)
                summed = jnp.dot(weights.astype(jnp.bfloat16), values, preferred_element_type=jnp.float32)
                halves.append(summed / total)
            if pair < 2:
                merged = jnp.where(low, halves[0], halves[1])
                out_ref[i * BLK:(i + 1) * BLK, pair * 128:(pair + 1) * 128] = merged.astype(jnp.bfloat16)
            else:
                out_ref[i * BLK:(i + 1) * BLK, 256:] = halves[0][:, HEAD_DIM:].astype(jnp.bfloat16)


def attend(ids, normed, w_query, kv):
    rows = normed.shape[0]
    parity = lax.rem(lax.axis_index(SEQ), 2)
    far_back, far_on = send_seq(kv, 4), send_seq(kv, -4)
    back, on = send_seq(kv, 2), send_seq(kv, -2)
    five = send_five(kv)
    beside = send_partner(kv)
    queries = jnp.dot(normed, jnp.pad(w_query, ((0, 0), (0, 64))), preferred_element_type=jnp.float32).astype(jnp.bfloat16)
    chain = [far_back, back, kv, on, far_on]
    swapped = [send_partner(far_back), send_partner(back), beside, send_partner(on), send_partner(far_on)]
    info = jnp.concatenate([ids, parity[None].astype(jnp.int32)])
    return pl.pallas_call(
        attend_kernel,
        out_shape=jax.ShapeDtypeStruct((rows, w_query.shape[1]), jnp.bfloat16),
        in_specs=[SMEM, VMEM] + [ANY] * 11,
        out_specs=VMEM,
        scratch_shapes=[
            pltpu.VMEM((12 * rows, kv.shape[1]), jnp.bfloat16),
            pltpu.VMEM((12, IDROWS, 128), jnp.bfloat16),
            pltpu.SemaphoreType.DMA((11,)),
            pltpu.SemaphoreType.DMA((11,)),
        ],
        compiler_params=pltpu.CompilerParams(vmem_limit_bytes=24 << 20),
        cost_estimate=pl.CostEstimate(flops=1 << 30, bytes_accessed=4 << 20, transcendentals=1 << 21),
    )(info, queries, *chain, *swapped, five)


def shards(frames, gain_attn, w_qkv, w_out, gain_ffn, w_up, w_down, w_conv, w_proj, block_utt):
    rows, width = frames.shape
    tp = lax.axis_index(TP)
    core = lax.rem(lax.axis_index(SEQ), 2)
    resid_in = frames.astype(jnp.float32)
    normed, kv = pl.pallas_call(
        kv_kernel,
        out_shape=(
            jax.ShapeDtypeStruct((rows, width), jnp.bfloat16),
            jax.ShapeDtypeStruct((rows + IDROWS, 2 * w_qkv.shape[2]), jnp.bfloat16),
        ),
        in_specs=[SMEM, VMEM, VMEM, VMEM],
        out_specs=(VMEM, VMEM),
        compiler_params=pltpu.CompilerParams(vmem_limit_bytes=16 << 20),
        cost_estimate=pl.CostEstimate(flops=1 << 29, bytes_accessed=4 << 20, transcendentals=0),
    )(block_utt, frames, gain_attn[None], w_qkv)
    attended = attend(block_utt, normed, w_qkv[0], kv)

    half = width // 2
    mine = lax.dynamic_slice_in_dim(w_out, core * half, half, axis=1)
    fetched = jnp.stack([send_tp(mine, k) for k in (1, 2, 3)])
    other = send_partner(fetched)
    left = jnp.where(core == 0, fetched, other)
    right = jnp.where(core == 0, other, fetched)

    heads = [attended] + [send_tp(attended, k) for k in (1, 2, 3)]
    term = jnp.dot(heads[0], w_out, preferred_element_type=jnp.float32)
    for k in range(3):
        both = jnp.concatenate([left[k], right[k]], axis=1)
        term = term + jnp.dot(heads[k + 1], both, preferred_element_type=jnp.float32)
    resid = resid_in + term
    normed_two = layer_norm(resid, gain_ffn).astype(jnp.bfloat16)
    hidden = jax.nn.gelu(
        jnp.dot(normed_two, w_up, preferred_element_type=jnp.float32), approximate=False
    ).astype(jnp.bfloat16)
    ffn_term = jnp.dot(hidden, w_down, preferred_element_type=jnp.float32).astype(jnp.bfloat16)

    share = rows // 4
    parts = ffn_term.reshape(4, share, width)
    pick = lambda array, k: lax.dynamic_index_in_dim(array, lax.rem(tp + k, 4), 0, False)
    got = [send_tp(pick(parts, k), k) for k in (1, 2, 3)]
    total = pick(resid.reshape(4, share, width), 0) + pick(parts, 0).astype(jnp.float32)
    for piece in got:
        total = total + piece.astype(jnp.float32)
    own = total.astype(jnp.bfloat16)
    spread = jnp.stack([own] + [send_tp(own, 4 - k) for k in (1, 2, 3)])
    layer_out = jnp.concatenate([spread, spread])
    layer_out = lax.dynamic_slice_in_dim(layer_out, lax.rem(4 - tp, 4), 4, 0).reshape(rows, width)

    frame_id = jnp.repeat(block_utt, BLK, total_repeat_length=rows) + 1
    rim_frame = send_seq(layer_out[-1:], 1)
    rim_id = send_seq(frame_id[-1:], 1)
    pooled_count = rows // 2
    pairs = layer_out.reshape(pooled_count, 2, width)
    pair_ids = frame_id.reshape(pooled_count, 2)
    even_rows = pairs[:, 0]
    odd_rows = pairs[:, 1]
    before = jnp.concatenate([rim_frame, odd_rows[:-1]], axis=0)
    before_ids = jnp.concatenate([rim_id, pair_ids[:-1, 1]], axis=0)
    keep_before = (before_ids == pair_ids[:, 0]).astype(jnp.bfloat16)[:, None]
    conv = jnp.dot(before * keep_before, w_conv[0], preferred_element_type=jnp.float32)
    conv = conv + jnp.dot(even_rows, w_conv[1], preferred_element_type=jnp.float32)
    conv = conv + jnp.dot(odd_rows, w_conv[2], preferred_element_type=jnp.float32)
    pooled = jax.nn.gelu(conv, approximate=False).astype(jnp.bfloat16)
    lm = jnp.dot(pooled, w_proj, preferred_element_type=jnp.float32).astype(jnp.bfloat16)
    lm = lm.reshape(4, pooled_count // 4, w_proj.shape[1])
    got = [send_tp(pick(lm, k), k) for k in (1, 2, 3)]
    total = pick(lm, 0).astype(jnp.float32)
    for piece in got:
        total = total + piece.astype(jnp.float32)
    return total.astype(jnp.bfloat16)


def solution(mesh):
    placed = (
        P("seq", None),
        P(),
        P(None, None, "tp"),
        P("tp", None),
        P(),
        P(None, "tp"),
        P("tp", None),
        P(None, None, "tp"),
        P("tp", None),
        P("seq"),
    )
    return jax.shard_map(
        shards, mesh=mesh, in_specs=placed, out_specs=P(("seq", "tp"), None), check_vma=False
    )
```

time: 294 us -> 169 us (0.57)
  starting transfers between devices: 109 us -> 42.2 us
  waiting for transfers between devices: 117 us -> 57.7 us
  local copies, waits for them, and re-layouts: 11.4 us -> 28.8 us
  between operations: 13.8 us -> 0.39 us
  Pallas kernels: 0 us -> 9.75 us
  matrix products: 27.3 us -> 17.7 us
  other arithmetic: 13.7 us -> 10.5 us
    psum x2 -> x0, waiting for transfers between devices: 86.1 us -> none  [the longest x1 43.1 us: shards(): lax.psum(ffn_term.astype(jnp.bfloat16), 'tp').astype(jnp.float32)]
    ppermute x32 -> x28, starting transfers between devices: 109 us -> 42.2 us  [the longest x6 17.2 us: send_seq(): lax.ppermute(value, SEQ, [(s, s + steps) for s in range(count) if 0 <= s...]
    ppermute x32 -> x28, waiting for transfers between devices: 4.96 us -> 57.7 us  [the longest x15 54.4 us: send_tp(): lax.ppermute(value, TP, [(t, (t + steps) % count) for t in range(count)])]
    reduce_scatter x1 -> x0, waiting for transfers between devices: 25.4 us -> none  [shards(): lax.psum_scatter(jnp.dot(rows, w_proj, preferred_element_type=jnp.float32...]
    pallas_call x0 -> x2, Pallas kernels: none -> 9.75 us  [the longest x1 7.21 us: attend(): pl.pallas_call(attend_kernel, out_shape=jax.ShapeDtypeStruct((rows, w_que...]
    dot_general x29 -> x8, matrix products: 26.2 us -> 16.7 us  [the longest x1 7.66 us: shards(): jnp.dot(hidden, w_down, preferred_element_type=jnp.float32)]
    unnamed x22 -> x30, local copies, waits for them, and re-layouts: 1.66 us -> 11.1 us
    reduce_sum x8 -> x0, other arithmetic: 5.57 us -> none  [the longest x2 2.89 us: layer_norm(): mean = jnp.mean(value, axis=-1, keepdims=True)]
  transfers between devices with their start and end apart: 35 -> 28, of which waited for: 5 -> 14; matrix products, arithmetic and copies ran while one was open for 11% -> 19% of each run, Pallas kernels for 0% -> 4%
where the time goes in v1:
time: 169 us; the launch traced here: 167 us
  waiting for transfers between devices  57.7 us (34%)
  starting transfers between devices  42.2 us (25%)
  local copies, waits for them, and re-layouts  28.8 us (17%)
  matrix products  17.7 us (10%)
  other arithmetic  10.5 us (6%)
  Pallas kernels  9.75 us (6%)
    ppermute x15, waiting for transfers between devices, send_tp(): lax.ppermute(value, TP, [(t, (t + steps) % count) for t in range(count)])  54.4 us
    ppermute x6, starting transfers between devices, send_seq(): lax.ppermute(value, SEQ, [(s, s + steps) for s in range(count) if 0 <= s...  17.2 us
    ppermute x15, starting transfers between devices, send_tp(): lax.ppermute(value, TP, [(t, (t + steps) % count) for t in range(count)])  16.4 us
    unnamed x30, local copies, waits for them, and re-layouts  11.1 us
    dot_general x1, matrix products, shards(): jnp.dot(hidden, w_down, preferred_element_type=jnp.float32)  7.66 us
    pallas_call x1, Pallas kernels, attend(): pl.pallas_call(attend_kernel, out_shape=jax.ShapeDtypeStruct((rows, w_que...  7.21 us
    ppermute x6, starting transfers between devices, send_partner(): return lax.ppermute(value, SEQ, [(s, s ^ 1) for s in range(count)])  4.98 us
    dot_general x1, matrix products, shards(): jnp.dot(pooled, w_proj, preferred_element_type=jnp.float32)  4.65 us
  transfers between devices with their start and end apart: 28, of which 14 were waited for; matrix products, arithmetic and copies ran while one was open for 19% of the time, Pallas kernels for 4%

profile of v1, /device:TPU:70, one launch (start us, length us, event | category | flops | bytes accessed | tf_op | source)
XLA Modules:
  0.0 167.1 jit_solution(3716385543514505025)
XLA Ops:
  0.0 0.9 broadcast_in_dim.29.gain_ref
  0.9 5.4 %copy.18.w_ref = bf16[3,1280,320]{2,1,0:T(8,128)(2,1)} copy(bf16[3,1280,320]{1,2,0:T(8,128)(2,1)} %param.14) | data formatting | bytes 4915200 | tf_op args[2]
  6.3 1.8 %copy-done.1 = bf16[3,1280,320]{2,1,0:T(8,128)(2,1)S(1)} copy-done((bf16[3,1280,320]{2,1,0:T(8,128)(2,1)S(1)}, bf16[3,1280,320]{2,1,0:T(8,128)(2,1)}, u32[]{:S(2)}) %copy-start.1) | copy-done | bytes 2457624
  8.1 1.1 copy-done.2
  9.2 2.5 %shard_map.100 = (bf16[256,1280]{1,0:T(8,128)(2,1)S(1)}, bf16[272,640]{1,0:T(8,128)(2,1)}) custom-call(s32[2]{0:T(128)S(1)} %copy-done.4, bf16[256,1280]{1,0:T(8,128)(2,1)S(1)} %copy-done.2, f32[1,1280]{1,0:T(1,128)S(1)} %broadcast_in_dim.29.gain_ref, bf16[3,1280,320]{2,1,0:T(8,128)(2,1)S(1)} %copy-done.1), custom_call_target="tpu_custom_call" | custom-call | flops 536870912 | bytes 4194304 | tf_op jit(solution)/shard_map/pallas_call | solution.py:161
  11.8 0.8 copy-done.5
  12.6 4.4 %collective-permute-start = (bf16[272,640]{1,0:T(8,128)(2,1)}, bf16[272,640]{1,0:T(8,128)(2,1)}, u32[]{:S(2)}, u32[]{:S(2)}) collective-permute-start(bf16[272,640]{1,0:T(8,128)(2,1)} %get-tuple-element.20.refs_2_), channel_id=1, source_target_pairs={{0,16},{4,20},{8,24},{12,28},{16,32},{20,36},{24,40},{28,44},{32,4... | collective-permute-start | bytes 1044488 | tf_op jit(solution)/shard_map/ppermute | solution.py:26
  16.9 4.0 %collective-permute-start.1 = (bf16[272,640]{1,0:T(8,128)(2,1)}, bf16[272,640]{1,0:T(8,128)(2,1)}, u32[]{:S(2)}, u32[]{:S(2)}) collective-permute-start(bf16[272,640]{1,0:T(8,128)(2,1)} %get-tuple-element.20.refs_2_), channel_id=1, source_target_pairs={{0,8},{4,12},{8,16},{12,20},{16,24},{20,28},{24,32},{28,36},{32,40... | collective-permute-start | bytes 1044488 | tf_op jit(solution)/shard_map/ppermute | solution.py:26
  21.0 1.8 %constant_dynamic-slice_fusion.1 = bf16[320,640]{1,0:T(8,128)(2,1)} fusion(bf16[320,1280]{1,0:T(8,128)(2,1)} %param.15, s32[]{:T(128)S(6)} %select_n.67), kind=kLoop, calls=%fused_computation.179 | loop fusion | bytes 819204 | tf_op jit(solution)/shard_map/dynamic_slice | solution.py:175
  22.8 3.0 %collective-permute-start.13 = (bf16[320,640]{1,0:T(8,128)(2,1)}, bf16[320,640]{1,0:T(8,128)(2,1)}, u32[]{:S(2)}, u32[]{:S(2)}) collective-permute-start(bf16[320,640]{1,0:T(8,128)(2,1)} %constant_dynamic-slice_fusion.1), channel_id=1, source_target_pairs={{0,3},{1,0},{2,1},{3,2},{4,7},{5,4},{6,5},{7,6},{8,11},{9,8},{10,9... | collective-permute-start | bytes 1228808 | tf_op jit(solution)/shard_map/ppermute | solution.py:21
  25.8 0.6 collective-permute-start.12
  26.4 1.0 collective-permute-start.11
  27.4 0.6 fusion.206
  28.6 1.8 %fusion.203 = (s32[256]{0:T(256)S(1)}, s32[256,1]{0,1:T(1,128)S(1)}) fusion(s32[]{:T(128)} %broadcast.212, s32[]{:T(128)} %bitcast.27, s32[]{:T(128)} %bitcast.26, s32[256,1]{0,1:T(1,128)S(1)} %bitcast.110, s32[256,1]{0,1:T(1,128)S(1)} %bitcast.111), kind=kLoop, calls=%fused_computation.261 | loop fusion | flops 1024 | bytes 4108 | tf_op jit(solution)/shard_map/jit(_take)/gather | solution.py:205
  30.8 12.2 %collective-permute-done.13 = bf16[320,640]{1,0:T(8,128)(2,1)} collective-permute-done((bf16[320,640]{1,0:T(8,128)(2,1)}, bf16[320,640]{1,0:T(8,128)(2,1)}, u32[]{:S(2)}, u32[]{:S(2)}) %collective-permute-start.13) | collective-permute-done | bytes 409632 | tf_op jit(solution)/shard_map/ppermute | solution.py:21
  43.0 1.9 %collective-permute-start.2 = (bf16[272,640]{1,0:T(8,128)(2,1)}, bf16[272,640]{1,0:T(8,128)(2,1)}, u32[]{:S(2)}, u32[]{:S(2)}) collective-permute-start(bf16[272,640]{1,0:T(8,128)(2,1)} %get-tuple-element.20.refs_2_), channel_id=1, source_target_pairs={{8,0},{12,4},{16,8},{20,12},{24,16},{28,20},{32,24},{36,28},{40,32... | collective-permute-start | bytes 1044488 | tf_op jit(solution)/shard_map/ppermute | solution.py:26
  45.0 2.9 %collective-permute-start.3 = (bf16[272,640]{1,0:T(8,128)(2,1)}, bf16[272,640]{1,0:T(8,128)(2,1)}, u32[]{:S(2)}, u32[]{:S(2)}) collective-permute-start(bf16[272,640]{1,0:T(8,128)(2,1)} %get-tuple-element.20.refs_2_), channel_id=1, source_target_pairs={{16,0},{20,4},{24,8},{28,12},{32,16},{36,20},{40,24},{44,28},{48,3... | collective-permute-start | bytes 1044488 | tf_op jit(solution)/shard_map/ppermute | solution.py:26
  47.9 2.5 %pad_maximum_fusion = bf16[3,320,640]{2,1,0:T(8,128)(2,1)} fusion(bf16[1,320,640]{2,1,0:T(8,128)(2,1)} %bitcast.4, bf16[1,320,640]{2,1,0:T(8,128)(2,1)} %bitcast.3, bf16[1,320,640]{2,1,0:T(8,128)(2,1)} %bitcast.2), kind=kLoop, calls=%fused_computation.27 | loop fusion | flops 1228800 | bytes 2457600 | tf_op jit(solution)/shard_map/stack | solution.py:176
  50.3 2.1 %slice_bitcast_fusion = bf16[1280,320]{0,1:T(8,128)(2,1)} fusion(bf16[3,1280,320]{1,2,0:T(8,128)(2,1)} %param.14), kind=kLoop, calls=%fused_computation.54 | loop fusion | bytes 1638400 | tf_op jit(solution)/shard_map/squeeze | solution.py:172
  52.9 3.6 %collective-permute-start.9 = (bf16[272,640]{1,0:T(8,128)(2,1)}, bf16[272,640]{1,0:T(8,128)(2,1)}, u32[]{:S(2)}, u32[]{:S(2)}) collective-permute-start(bf16[272,640]{1,0:T(8,128)(2,1)} %get-tuple-element.20.refs_2_), channel_id=1, source_target_pairs={{4,24},{12,32},{20,40},{24,4},{28,48},{32,12},{36,56},{40,20},{44,... | collective-permute-start | bytes 1044488 | tf_op jit(solution)/shard_map/ppermute | solution.py:39
  56.6 0.7 slice.81
  57.2 1.1 collective-permute-done.2.refs_3_
  58.4 2.1 %collective-permute-start.4 = (bf16[272,640]{1,0:T(8,128)(2,1)}, bf16[272,640]{1,0:T(8,128)(2,1)S(1)}, u32[]{:S(2)}, u32[]{:S(2)}) collective-permute-start(bf16[272,640]{1,0:T(8,128)(2,1)} %collective-permute-done.refs_0_), channel_id=1, source_target_pairs={{0,4},{4,0},{8,12},{12,8},{16,20},{20,16},{24,28},{28,24},{32,36},... | collective-permute-start | bytes 1044488 | tf_op jit(solution)/shard_map/ppermute | solution.py:33
  61.0 2.1 %collective-permute-done.9.refs_10_ = bf16[272,640]{1,0:T(8,128)(2,1)} collective-permute-done((bf16[272,640]{1,0:T(8,128)(2,1)}, bf16[272,640]{1,0:T(8,128)(2,1)}, u32[]{:S(2)}, u32[]{:S(2)}) %collective-permute-start.9) | collective-permute-done | bytes 348192 | tf_op jit(solution)/shard_map/ppermute | solution.py:39
  63.1 1.9 %collective-permute-start.8 = (bf16[272,640]{1,0:T(8,128)(2,1)}, bf16[272,640]{1,0:T(8,128)(2,1)S(1)}, u32[]{:S(2)}, u32[]{:S(2)}) collective-permute-start(bf16[272,640]{1,0:T(8,128)(2,1)} %collective-permute-done.3.refs_4_), channel_id=1, source_target_pairs={{0,4},{4,0},{8,12},{12,8},{16,20},{20,16},{24,28},{28,24},{32,36},... | collective-permute-start | bytes 1044488 | tf_op jit(solution)/shard_map/ppermute | solution.py:33
  65.0 1.9 %convolution_convert_fusion.2.q_ref = bf16[256,384]{1,0:T(8,128)(2,1)S(1)} fusion(bf16[256,1280]{1,0:T(8,128)(2,1)} %copy-done.5, bf16[1280,320]{0,1:T(8,128)(2,1)} %slice_bitcast_fusion), kind=kOutput, calls=%fused_computation.30 | convolution fusion | flops 251756544 | bytes 1671168 | tf_op jit(solution)/shard_map/dot_general | solution.py:136
  66.9 1.9 %collective-permute-start.24 = (s32[1]{0:T(128)}, s32[1]{0:T(128)}, u32[]{:S(2)}, u32[]{:S(2)}) collective-permute-start(s32[1]{0:T(128)} %slice.81), channel_id=1, source_target_pairs={{0,4},{4,8},{8,12},{12,16},{16,20},{20,24},{24,28},{28,32},{32,36}... | collective-permute-start | bytes 20 | tf_op jit(solution)/shard_map/ppermute | solution.py:26
  68.9 7.2 %shard_map.101 = bf16[256,320]{1,0:T(8,128)(2,1)S(1)} custom-call(s32[3]{0:T(128)S(1)} %pad_add_fusion.info_ref, bf16[256,384]{1,0:T(8,128)(2,1)S(1)} %convolution_convert_fusion.2.q_ref, bf16[272,640]{1,0:T(8,128)(2,1)} %collective-permute-done.refs_0_, bf16[272,640]{1,0:T(8,128)(2,1)} %collective-permute-done.1.refs_1_, ...), custom_call_target="tpu_custom_call" | custom-call | flops 1073741824 | bytes 4194304 | tf_op jit(solution)/shard_map/pallas_call | solution.py:140
  76.1 3.8 %collective-permute-start.16 = (bf16[256,320]{1,0:T(8,128)(2,1)S(1)}, bf16[256,320]{1,0:T(8,128)(2,1)S(1)}, u32[]{:S(2)}, u32[]{:S(2)}) collective-permute-start(bf16[256,320]{1,0:T(8,128)(2,1)S(1)} %shard_map.101), channel_id=1, source_target_pairs={{0,3},{1,0},{2,1},{3,2},{4,7},{5,4},{6,5},{7,6},{8,11},{9,8},{10,9... | collective-permute-start | bytes 491528 | tf_op jit(solution)/shard_map/ppermute | solution.py:21
  79.9 0.9 collective-permute-start.10
  80.8 1.9 %broadcast_select_fusion.1 = (bf16[3,320,640]{2,1,0:T(8,128)(2,1)S(1)}, bf16[3,320,640]{2,1,0:T(8,128)(2,1)S(1)}) fusion(bf16[3,320,640]{2,1,0:T(8,128)(2,1)} %collective-permute-done.14, pred[]{:T(512)S(6)} %eq.8, bf16[1,320,640]{2,1,0:T(8,128)(2,1)} %bitcast.4, bf16[1,320,640]{2,1,0:T(8,128)(2,1)} %bitcast.3, bf16[1,320,640]{2,1,0:T(8,128)(2,1)} %bitcast.2), kind=kLoop, calls=%fused_computation.29 | loop fusion | flops 2457600 | bytes 4915201 | tf_op jit(solution)/shard_map/jit(_where)/select_n | solution.py:178
  83.0 6.1 %collective-permute-done.16 = bf16[256,320]{1,0:T(8,128)(2,1)S(1)} collective-permute-done((bf16[256,320]{1,0:T(8,128)(2,1)S(1)}, bf16[256,320]{1,0:T(8,128)(2,1)S(1)}, u32[]{:S(2)}, u32[]{:S(2)}) %collective-permute-start.16) | collective-permute-done | bytes 163872 | tf_op jit(solution)/shard_map/ppermute | solution.py:21
  90.1 2.9 %collective-permute-done.10 = bf16[256,320]{1,0:T(8,128)(2,1)S(1)} collective-permute-done((bf16[256,320]{1,0:T(8,128)(2,1)S(1)}, bf16[256,320]{1,0:T(8,128)(2,1)S(1)}, u32[]{:S(2)}, u32[]{:S(2)}) %collective-permute-start.10) | collective-permute-done | bytes 163872 | tf_op jit(solution)/shard_map/ppermute | solution.py:21
  94.1 1.1 copy-done.7
  95.5 7.7 %convolution_convert_fusion.1 = bf16[256,1280]{1,0:T(8,128)(2,1)} fusion(bf16[1280,1280]{1,0:T(8,128)(2,1)S(1)} %copy-done, bf16[1280,1280]{1,0:T(8,128)(2,1)} %param.17, f32[256,1280]{1,0:T(8,128)} %copy-done.7, f32[1280]{0:T(1024)S(1)} %copy-done.10, f32[256]{0:T(256)S(1)} %add_rsqrt_fusion, f32[256]{0:T(256)S(1)} %broadcast_multiply_fusion), kind=kOutput, calls=%fused_computation.5 | convolution fusion | flops 1700659200 | bytes 8526848 | tf_op jit(solution)/shard_map/dot_general | solution.py:191
  103.1 1.9 %dynamic-slice_bitcast_fusion.5 = (bf16[64,1280]{1,0:T(8,128)(2,1)}, bf16[64,1280]{1,0:T(8,128)(2,1)}, bf16[64,1280]{1,0:T(8,128)(2,1)}) fusion(bf16[4,64,1280]{2,1,0:T(8,128)(2,1)} %bitcast.106, s32[]{:T(128)S(6)} %select_n.71, s32[]{:T(128)S(6)} %select_n.73, s32[]{:T(128)S(6)} %select_n.72), kind=kLoop, calls=%fused_computation.142 | loop fusion | bytes 983052 | tf_op jit(solution)/shard_map/jit(dynamic_index_in_dim)/squeeze | solution.py:195
  105.0 1.6 collective-permute-start.19
  106.6 0.9 collective-permute-start.17
  107.5 4.7 %collective-permute-done.19 = bf16[64,1280]{1,0:T(8,128)(2,1)S(1)} collective-permute-done((bf16[64,1280]{1,0:T(8,128)(2,1)}, bf16[64,1280]{1,0:T(8,128)(2,1)S(1)}, u32[]{:S(2)}, u32[]{:S(2)}) %collective-permute-start.19) | collective-permute-done | bytes 163872 | tf_op jit(solution)/shard_map/ppermute | solution.py:21
  112.3 3.3 %collective-permute-done.18 = bf16[64,1280]{1,0:T(8,128)(2,1)} collective-permute-done((bf16[64,1280]{1,0:T(8,128)(2,1)}, bf16[64,1280]{1,0:T(8,128)(2,1)}, u32[]{:S(2)}, u32[]{:S(2)}) %collective-permute-start.18) | collective-permute-done | bytes 163872 | tf_op jit(solution)/shard_map/ppermute | solution.py:21
  115.5 2.1 %collective-permute-done.17 = bf16[64,1280]{1,0:T(8,128)(2,1)} collective-permute-done((bf16[64,1280]{1,0:T(8,128)(2,1)}, bf16[64,1280]{1,0:T(8,128)(2,1)}, u32[]{:S(2)}, u32[]{:S(2)}) %collective-permute-start.17) | collective-permute-done | bytes 163872 | tf_op jit(solution)/shard_map/ppermute | solution.py:21
  117.7 1.3 bitcast_dynamic-update-slice_fusion.6
  119.0 1.0 collective-permute-start.20
  120.0 0.7 fusion.136
  120.9 1.0 collective-permute-start.22
  121.9 4.3 %collective-permute-done.20 = bf16[64,1280]{1,0:T(8,128)(2,1)S(1)} collective-permute-done((bf16[64,1280]{1,0:T(8,128)(2,1)S(1)}, bf16[64,1280]{1,0:T(8,128)(2,1)S(1)}, u32[]{:S(2)}, u32[]{:S(2)}) %collective-permute-start.20) | collective-permute-done | bytes 163872 | tf_op jit(solution)/shard_map/ppermute | solution.py:21
  126.2 3.0 %collective-permute-done.21 = bf16[64,1280]{1,0:T(8,128)(2,1)S(1)} collective-permute-done((bf16[64,1280]{1,0:T(8,128)(2,1)S(1)}, bf16[64,1280]{1,0:T(8,128)(2,1)S(1)}, u32[]{:S(2)}, u32[]{:S(2)}) %collective-permute-start.21) | collective-permute-done | bytes 163872 | tf_op jit(solution)/shard_map/ppermute | solution.py:21
  129.2 1.4 collective-permute-done.22
  130.7 0.9 constant_dynamic-slice_fusion
  131.6 2.6 %reshape_reshape.3 = bf16[128,2,1280]{2,1,0:T(2,128)(2,1)} reshape(bf16[4,64,1280]{2,1,0:T(8,128)(2,1)} %constant_dynamic-slice_fusion) | data formatting | bytes 1310720 | tf_op jit(solution)/shard_map/reshape;reshape | solution.py:209
  134.3 2.6 %fusion.205 = (bf16[128,1,1280]{2,1,0:T(2,128)(2,1)S(1)}, bf16[128,1,1280]{2,1,0:T(2,128)(2,1)S(1)}) fusion(bf16[128,2,1280]{2,1,0:T(2,128)(2,1)} %reshape_reshape.3), kind=kLoop, calls=%fused_computation.262 | loop fusion | bytes 1310720 | tf_op jit(solution)/shard_map/slice | solution.py:211
  136.9 0.7 slice.98
  137.6 2.1 %collective-permute-start.23 = (bf16[1,1280]{1,0:T(2,128)(2,1)S(1)}, bf16[1,1280]{1,0:T(2,128)(2,1)S(1)}, u32[]{:S(2)}, u32[]{:S(2)}) collective-permute-start(bf16[1,1280]{1,0:T(2,128)(2,1)S(1)} %slice.98), channel_id=1, source_target_pairs={{0,4},{4,8},{8,12},{12,16},{16,20},{20,24},{24,28},{28,32},{32,36}... | collective-permute-start | bytes 7688 | tf_op jit(solution)/shard_map/ppermute | solution.py:26
  140.1 1.0 fusion.29
  141.2 0.7 slice.99
  141.9 0.8 copy.32
  142.7 4.6 %convolution_convert_fusion = bf16[128,4096]{1,0:T(8,128)(2,1)} fusion(bf16[320,4096]{1,0:T(8,128)(2,1)} %param.20, f32[128,320]{0,1:T(8,128)S(1)} %fusion.27, f32[128,320]{0,1:T(8,128)} %fusion.29, bf16[3,1280,320]{1,2,0:T(8,128)(2,1)} %param.19, bf16[127,1280]{1,0:T(8,128)(2,1)} %bitcast.108, bf16[1,1280]{1,0:T(2,128)(2,1)S(1)} %collective-permute-done.23, ...), kind=kOutput, calls=%fused_computation | convolution fusion | flops 444653568 | bytes 5147392 | tf_op jit(solution)/shard_map/dot_general | solution.py:220
  147.3 1.2 dynamic-slice_bitcast_fusion.2
  148.5 0.9 collective-permute-start.27
  150.0 0.9 collective-permute-start.25
  150.8 6.9 %collective-permute-done.27 = bf16[32,4096]{1,0:T(8,128)(2,1)S(1)} collective-permute-done((bf16[32,4096]{1,0:T(8,128)(2,1)S(1)}, bf16[32,4096]{1,0:T(8,128)(2,1)S(1)}, u32[]{:S(2)}, u32[]{:S(2)}) %collective-permute-start.27) | collective-permute-done | bytes 262176 | tf_op jit(solution)/shard_map/ppermute | solution.py:21
  157.7 2.3 %collective-permute-done.26 = bf16[32,4096]{1,0:T(8,128)(2,1)S(1)} collective-permute-done((bf16[32,4096]{1,0:T(8,128)(2,1)S(1)}, bf16[32,4096]{1,0:T(8,128)(2,1)S(1)}, u32[]{:S(2)}, u32[]{:S(2)}) %collective-permute-start.26) | collective-permute-done | bytes 262176 | tf_op jit(solution)/shard_map/ppermute | solution.py:21
  160.0 5.2 %collective-permute-done.25 = bf16[32,4096]{1,0:T(8,128)(2,1)S(1)} collective-permute-done((bf16[32,4096]{1,0:T(8,128)(2,1)S(1)}, bf16[32,4096]{1,0:T(8,128)(2,1)S(1)}, u32[]{:S(2)}, u32[]{:S(2)}) %collective-permute-start.25) | collective-permute-done | bytes 262176 | tf_op jit(solution)/shard_map/ppermute | solution.py:21
  165.3 1.8 %fusion.75 = bf16[32,4096]{1,0:T(8,128)(2,1)} fusion(bf16[32,4096]{1,0:T(8,128)(2,1)S(1)} %collective-permute-done.27, bf16[32,4096]{1,0:T(8,128)(2,1)S(1)} %collective-permute-done.26, bf16[32,4096]{1,0:T(8,128)(2,1)S(1)} %collective-permute-done.25, bf16[4,32,4096]{2,1,0:T(8,128)(2,1)} %bitcast.105, s32[]{:T(128)S(6)} %select_n.70), kind=kLoop, calls=%fused_computation.92 | loop fusion | flops 1048576 | bytes 1310724 | tf_op jit(solution)/shard_map/convert_element_type | solution.py:226
  (70 shorter events, 6.1 us)
Async XLA Ops:
  0.0 95.5 %copy-start = (bf16[1280,1280]{1,0:T(8,128)(2,1)S(1)}, bf16[1280,1280]{1,0:T(8,128)(2,1)}, u32[]{:S(2)}) copy-start(bf16[1280,1280]{1,0:T(8,128)(2,1)} %param.18) | copy-start | bytes 9830404
  0.9 5.4 %copy-start.4 = (s32[2]{0:T(128)S(1)}, s32[2]{0:T(128)}, u32[]{:S(2)}) copy-start(s32[2]{0:T(128)} %ids_ref.1) | copy-start | bytes 28
  6.3 1.8 %copy-start.1 = (bf16[3,1280,320]{2,1,0:T(8,128)(2,1)S(1)}, bf16[3,1280,320]{2,1,0:T(8,128)(2,1)}, u32[]{:S(2)}) copy-start(bf16[3,1280,320]{2,1,0:T(8,128)(2,1)} %copy.18.w_ref) | copy-start | bytes 7372804
  8.1 1.1 copy-start.2
  11.7 0.8 copy-start.5
  12.6 39.9 %collective-permute-start = (bf16[272,640]{1,0:T(8,128)(2,1)}, bf16[272,640]{1,0:T(8,128)(2,1)}, u32[]{:S(2)}, u32[]{:S(2)}) collective-permute-start(bf16[272,640]{1,0:T(8,128)(2,1)} %get-tuple-element.20.refs_2_), channel_id=1, source_target_pairs={{0,16},{4,20},{8,24},{12,28},{16,32},{20,36},{24,40},{28,44},{32,4... | collective-permute-start | bytes 1044488 | tf_op jit(solution)/shard_map/ppermute | solution.py:26
  16.9 36.0 %collective-permute-start.1 = (bf16[272,640]{1,0:T(8,128)(2,1)}, bf16[272,640]{1,0:T(8,128)(2,1)}, u32[]{:S(2)}, u32[]{:S(2)}) collective-permute-start(bf16[272,640]{1,0:T(8,128)(2,1)} %get-tuple-element.20.refs_2_), channel_id=1, source_target_pairs={{0,8},{4,12},{8,16},{12,20},{16,24},{20,28},{24,32},{28,36},{32,40... | collective-permute-start | bytes 1044488 | tf_op jit(solution)/shard_map/ppermute | solution.py:26
  22.8 20.3 %collective-permute-start.13 = (bf16[320,640]{1,0:T(8,128)(2,1)}, bf16[320,640]{1,0:T(8,128)(2,1)}, u32[]{:S(2)}, u32[]{:S(2)}) collective-permute-start(bf16[320,640]{1,0:T(8,128)(2,1)} %constant_dynamic-slice_fusion.1), channel_id=1, source_target_pairs={{0,3},{1,0},{2,1},{3,2},{4,7},{5,4},{6,5},{7,6},{8,11},{9,8},{10,9... | collective-permute-start | bytes 1228808 | tf_op jit(solution)/shard_map/ppermute | solution.py:21
  25.8 19.2 %collective-permute-start.12 = (bf16[320,640]{1,0:T(8,128)(2,1)}, bf16[320,640]{1,0:T(8,128)(2,1)}, u32[]{:S(2)}, u32[]{:S(2)}) collective-permute-start(bf16[320,640]{1,0:T(8,128)(2,1)} %constant_dynamic-slice_fusion.1), channel_id=1, source_target_pairs={{0,2},{1,3},{2,0},{3,1},{4,6},{5,7},{6,4},{7,5},{8,10},{9,11},{10,... | collective-permute-start | bytes 1228808 | tf_op jit(solution)/shard_map/ppermute | solution.py:21
  26.4 21.5 %collective-permute-start.11 = (bf16[320,640]{1,0:T(8,128)(2,1)}, bf16[320,640]{1,0:T(8,128)(2,1)}, u32[]{:S(2)}, u32[]{:S(2)}) collective-permute-start(bf16[320,640]{1,0:T(8,128)(2,1)} %constant_dynamic-slice_fusion.1), channel_id=1, source_target_pairs={{0,1},{1,2},{2,3},{3,0},{4,5},{5,6},{6,7},{7,4},{8,9},{9,10},{10,1... | collective-permute-start | bytes 1228808 | tf_op jit(solution)/shard_map/ppermute | solution.py:21
  43.0 15.3 %collective-permute-start.2 = (bf16[272,640]{1,0:T(8,128)(2,1)}, bf16[272,640]{1,0:T(8,128)(2,1)}, u32[]{:S(2)}, u32[]{:S(2)}) collective-permute-start(bf16[272,640]{1,0:T(8,128)(2,1)} %get-tuple-element.20.refs_2_), channel_id=1, source_target_pairs={{8,0},{12,4},{16,8},{20,12},{24,16},{28,20},{32,24},{36,28},{40,32... | collective-permute-start | bytes 1044488 | tf_op jit(solution)/shard_map/ppermute | solution.py:26
  45.0 15.5 %collective-permute-start.3 = (bf16[272,640]{1,0:T(8,128)(2,1)}, bf16[272,640]{1,0:T(8,128)(2,1)}, u32[]{:S(2)}, u32[]{:S(2)}) collective-permute-start(bf16[272,640]{1,0:T(8,128)(2,1)} %get-tuple-element.20.refs_2_), channel_id=1, source_target_pairs={{16,0},{20,4},{24,8},{28,12},{32,16},{36,20},{40,24},{44,28},{48,3... | collective-permute-start | bytes 1044488 | tf_op jit(solution)/shard_map/ppermute | solution.py:26
  50.3 30.5 %collective-permute-start.14 = (bf16[3,320,640]{2,1,0:T(8,128)(2,1)}, bf16[3,320,640]{2,1,0:T(8,128)(2,1)}, u32[]{:S(2)}, u32[]{:S(2)}) collective-permute-start(bf16[3,320,640]{2,1,0:T(8,128)(2,1)} %pad_maximum_fusion), channel_id=1, source_target_pairs={{0,4},{4,0},{8,12},{12,8},{16,20},{20,16},{24,28},{28,24},{32,36},... | collective-permute-start | bytes 3686408 | tf_op jit(solution)/shard_map/ppermute | solution.py:33
  52.4 8.1 %collective-permute-start.6 = (bf16[272,640]{1,0:T(8,128)(2,1)}, bf16[272,640]{1,0:T(8,128)(2,1)}, u32[]{:S(2)}, u32[]{:S(2)}) collective-permute-start(bf16[272,640]{1,0:T(8,128)(2,1)} %get-tuple-element.20.refs_2_), channel_id=1, source_target_pairs={{0,4},{4,0},{8,12},{12,8},{16,20},{20,16},{24,28},{28,24},{32,36},... | collective-permute-start | bytes 1044488 | tf_op jit(solution)/shard_map/ppermute | solution.py:33
  52.9 10.1 %collective-permute-start.9 = (bf16[272,640]{1,0:T(8,128)(2,1)}, bf16[272,640]{1,0:T(8,128)(2,1)}, u32[]{:S(2)}, u32[]{:S(2)}) collective-permute-start(bf16[272,640]{1,0:T(8,128)(2,1)} %get-tuple-element.20.refs_2_), channel_id=1, source_target_pairs={{4,24},{12,32},{20,40},{24,4},{28,48},{32,12},{36,56},{40,20},{44,... | collective-permute-start | bytes 1044488 | tf_op jit(solution)/shard_map/ppermute | solution.py:39
  58.4 8.5 %collective-permute-start.4 = (bf16[272,640]{1,0:T(8,128)(2,1)}, bf16[272,640]{1,0:T(8,128)(2,1)S(1)}, u32[]{:S(2)}, u32[]{:S(2)}) collective-permute-start(bf16[272,640]{1,0:T(8,128)(2,1)} %collective-permute-done.refs_0_), channel_id=1, source_target_pairs={{0,4},{4,0},{8,12},{12,8},{16,20},{20,16},{24,28},{28,24},{32,36},... | collective-permute-start | bytes 1044488 | tf_op jit(solution)/shard_map/ppermute | solution.py:33
  60.4 8.4 %collective-permute-start.5 = (bf16[272,640]{1,0:T(8,128)(2,1)}, bf16[272,640]{1,0:T(8,128)(2,1)S(1)}, u32[]{:S(2)}, u32[]{:S(2)}) collective-permute-start(bf16[272,640]{1,0:T(8,128)(2,1)} %collective-permute-done.1.refs_1_), channel_id=1, source_target_pairs={{0,4},{4,0},{8,12},{12,8},{16,20},{20,16},{24,28},{28,24},{32,36},... | collective-permute-start | bytes 1044488 | tf_op jit(solution)/shard_map/ppermute | solution.py:33
  60.5 8.3 %collective-permute-start.7 = (bf16[272,640]{1,0:T(8,128)(2,1)}, bf16[272,640]{1,0:T(8,128)(2,1)S(1)}, u32[]{:S(2)}, u32[]{:S(2)}) collective-permute-start(bf16[272,640]{1,0:T(8,128)(2,1)} %collective-permute-done.2.refs_3_), channel_id=1, source_target_pairs={{0,4},{4,0},{8,12},{12,8},{16,20},{20,16},{24,28},{28,24},{32,36},... | collective-permute-start | bytes 1044488 | tf_op jit(solution)/shard_map/ppermute | solution.py:33
  63.1 5.8 %collective-permute-start.8 = (bf16[272,640]{1,0:T(8,128)(2,1)}, bf16[272,640]{1,0:T(8,128)(2,1)S(1)}, u32[]{:S(2)}, u32[]{:S(2)}) collective-permute-start(bf16[272,640]{1,0:T(8,128)(2,1)} %collective-permute-done.3.refs_4_), channel_id=1, source_target_pairs={{0,4},{4,0},{8,12},{12,8},{16,20},{20,16},{24,28},{28,24},{32,36},... | collective-permute-start | bytes 1044488 | tf_op jit(solution)/shard_map/ppermute | solution.py:33
  66.9 53.0 %collective-permute-start.24 = (s32[1]{0:T(128)}, s32[1]{0:T(128)}, u32[]{:S(2)}, u32[]{:S(2)}) collective-permute-start(s32[1]{0:T(128)} %slice.81), channel_id=1, source_target_pairs={{0,4},{4,8},{8,12},{12,16},{16,20},{20,24},{24,28},{28,32},{32,36}... | collective-permute-start | bytes 20 | tf_op jit(solution)/shard_map/ppermute | solution.py:26
  76.1 13.0 %collective-permute-start.16 = (bf16[256,320]{1,0:T(8,128)(2,1)S(1)}, bf16[256,320]{1,0:T(8,128)(2,1)S(1)}, u32[]{:S(2)}, u32[]{:S(2)}) collective-permute-start(bf16[256,320]{1,0:T(8,128)(2,1)S(1)} %shard_map.101), channel_id=1, source_target_pairs={{0,3},{1,0},{2,1},{3,2},{4,7},{5,4},{6,5},{7,6},{8,11},{9,8},{10,9... | collective-permute-start | bytes 491528 | tf_op jit(solution)/shard_map/ppermute | solution.py:21
  79.9 9.7 %collective-permute-start.15 = (bf16[256,320]{1,0:T(8,128)(2,1)S(1)}, bf16[256,320]{1,0:T(8,128)(2,1)S(1)}, u32[]{:S(2)}, u32[]{:S(2)}) collective-permute-start(bf16[256,320]{1,0:T(8,128)(2,1)S(1)} %shard_map.101), channel_id=1, source_target_pairs={{0,2},{1,3},{2,0},{3,1},{4,6},{5,7},{6,4},{7,5},{8,10},{9,11},{10,... | collective-permute-start | bytes 491528 | tf_op jit(solution)/shard_map/ppermute | solution.py:21
  79.9 13.1 %collective-permute-start.10 = (bf16[256,320]{1,0:T(8,128)(2,1)S(1)}, bf16[256,320]{1,0:T(8,128)(2,1)S(1)}, u32[]{:S(2)}, u32[]{:S(2)}) collective-permute-start(bf16[256,320]{1,0:T(8,128)(2,1)S(1)} %shard_map.101), channel_id=1, source_target_pairs={{0,1},{1,2},{2,3},{3,0},{4,5},{5,6},{6,7},{7,4},{8,9},{9,10},{10,1... | collective-permute-start | bytes 491528 | tf_op jit(solution)/shard_map/ppermute | solution.py:21
  90.1 3.4 %copy-start.3 = (bf16[256,1280]{1,0:T(8,128)(2,1)S(1)}, bf16[256,1280]{1,0:T(8,128)(2,1)}, u32[]{:S(2)}) copy-start(bf16[256,1280]{1,0:T(8,128)(2,1)} %frames_ref.1) | copy-start | bytes 1966084
  90.1 3.4 %copy-start.8 = (bf16[320,1280]{1,0:T(8,128)(2,1)S(1)}, bf16[320,1280]{1,0:T(8,128)(2,1)}, u32[]{:S(2)}) copy-start(bf16[320,1280]{1,0:T(8,128)(2,1)} %param.15) | copy-start | bytes 2457604
  94.1 1.1 copy-start.7
  94.1 1.4 copy-start.10
  105.0 7.3 %collective-permute-start.19 = (bf16[64,1280]{1,0:T(8,128)(2,1)}, bf16[64,1280]{1,0:T(8,128)(2,1)S(1)}, u32[]{:S(2)}, u32[]{:S(2)}) collective-permute-start(bf16[64,1280]{1,0:T(8,128)(2,1)} %get-tuple-element.39), channel_id=1, source_target_pairs={{0,3},{1,0},{2,1},{3,2},{4,7},{5,4},{6,5},{7,6},{8,11},{9,8},{10,9... | collective-permute-start | bytes 491528 | tf_op jit(solution)/shard_map/ppermute | solution.py:21
  106.6 8.9 %collective-permute-start.18 = (bf16[64,1280]{1,0:T(8,128)(2,1)}, bf16[64,1280]{1,0:T(8,128)(2,1)}, u32[]{:S(2)}, u32[]{:S(2)}) collective-permute-start(bf16[64,1280]{1,0:T(8,128)(2,1)} %get-tuple-element.40), channel_id=1, source_target_pairs={{0,2},{1,3},{2,0},{3,1},{4,6},{5,7},{6,4},{7,5},{8,10},{9,11},{10,... | collective-permute-start | bytes 491528 | tf_op jit(solution)/shard_map/ppermute | solution.py:21
  106.6 11.0 %collective-permute-start.17 = (bf16[64,1280]{1,0:T(8,128)(2,1)}, bf16[64,1280]{1,0:T(8,128)(2,1)}, u32[]{:S(2)}, u32[]{:S(2)}) collective-permute-start(bf16[64,1280]{1,0:T(8,128)(2,1)} %get-tuple-element.38), channel_id=1, source_target_pairs={{0,1},{1,2},{2,3},{3,0},{4,5},{5,6},{6,7},{7,4},{8,9},{9,10},{10,1... | collective-permute-start | bytes 491528 | tf_op jit(solution)/shard_map/ppermute | solution.py:21
  119.0 7.2 %collective-permute-start.20 = (bf16[64,1280]{1,0:T(8,128)(2,1)S(1)}, bf16[64,1280]{1,0:T(8,128)(2,1)S(1)}, u32[]{:S(2)}, u32[]{:S(2)}) collective-permute-start(bf16[64,1280]{1,0:T(8,128)(2,1)S(1)} %get-tuple-element.24), channel_id=1, source_target_pairs={{0,3},{1,0},{2,1},{3,2},{4,7},{5,4},{6,5},{7,6},{8,11},{9,8},{10,9... | collective-permute-start | bytes 491528 | tf_op jit(solution)/shard_map/ppermute | solution.py:21
  120.7 8.5 %collective-permute-start.21 = (bf16[64,1280]{1,0:T(8,128)(2,1)S(1)}, bf16[64,1280]{1,0:T(8,128)(2,1)S(1)}, u32[]{:S(2)}, u32[]{:S(2)}) collective-permute-start(bf16[64,1280]{1,0:T(8,128)(2,1)S(1)} %get-tuple-element.24), channel_id=1, source_target_pairs={{0,2},{1,3},{2,0},{3,1},{4,6},{5,7},{6,4},{7,5},{8,10},{9,11},{10,... | collective-permute-start | bytes 491528 | tf_op jit(solution)/shard_map/ppermute | solution.py:21
  120.9 9.7 %collective-permute-start.22 = (bf16[64,1280]{1,0:T(8,128)(2,1)S(1)}, bf16[64,1280]{1,0:T(8,128)(2,1)S(1)}, u32[]{:S(2)}, u32[]{:S(2)}) collective-permute-start(bf16[64,1280]{1,0:T(8,128)(2,1)S(1)} %get-tuple-element.24), channel_id=1, source_target_pairs={{0,1},{1,2},{2,3},{3,0},{4,5},{5,6},{6,7},{7,4},{8,9},{9,10},{10,1... | collective-permute-start | bytes 491528 | tf_op jit(solution)/shard_map/ppermute | solution.py:21
  134.3 5.5 %copy-start.9 = (bf16[3,1280,320]{1,2,0:T(8,128)(2,1)S(1)}, bf16[3,1280,320]{1,2,0:T(8,128)(2,1)}, u32[]{:S(2)}) copy-start(bf16[3,1280,320]{1,2,0:T(8,128)(2,1)} %param.19) | copy-start | bytes 7372804
  137.6 5.1 %collective-permute-start.23 = (bf16[1,1280]{1,0:T(2,128)(2,1)S(1)}, bf16[1,1280]{1,0:T(2,128)(2,1)S(1)}, u32[]{:S(2)}, u32[]{:S(2)}) collective-permute-start(bf16[1,1280]{1,0:T(2,128)(2,1)S(1)} %slice.98), channel_id=1, source_target_pairs={{0,4},{4,8},{8,12},{12,16},{16,20},{20,24},{24,28},{28,32},{32,36}... | collective-permute-start | bytes 7688 | tf_op jit(solution)/shard_map/ppermute | solution.py:26
  139.8 1.4 copy-start.6
  148.5 9.2 %collective-permute-start.27 = (bf16[32,4096]{1,0:T(8,128)(2,1)S(1)}, bf16[32,4096]{1,0:T(8,128)(2,1)S(1)}, u32[]{:S(2)}, u32[]{:S(2)}) collective-permute-start(bf16[32,4096]{1,0:T(8,128)(2,1)S(1)} %get-tuple-element.34), channel_id=1, source_target_pairs={{0,3},{1,0},{2,1},{3,2},{4,7},{5,4},{6,5},{7,6},{8,11},{9,8},{10,9... | collective-permute-start | bytes 786440 | tf_op jit(solution)/shard_map/ppermute | solution.py:21
  149.4 10.6 %collective-permute-start.26 = (bf16[32,4096]{1,0:T(8,128)(2,1)S(1)}, bf16[32,4096]{1,0:T(8,128)(2,1)S(1)}, u32[]{:S(2)}, u32[]{:S(2)}) collective-permute-start(bf16[32,4096]{1,0:T(8,128)(2,1)S(1)} %get-tuple-element.35), channel_id=1, source_target_pairs={{0,2},{1,3},{2,0},{3,1},{4,6},{5,7},{6,4},{7,5},{8,10},{9,11},{10,... | collective-permute-start | bytes 786440 | tf_op jit(solution)/shard_map/ppermute | solution.py:21
  150.0 15.3 %collective-permute-start.25 = (bf16[32,4096]{1,0:T(8,128)(2,1)S(1)}, bf16[32,4096]{1,0:T(8,128)(2,1)S(1)}, u32[]{:S(2)}, u32[]{:S(2)}) collective-permute-start(bf16[32,4096]{1,0:T(8,128)(2,1)S(1)} %get-tuple-element.33), channel_id=1, source_target_pairs={{0,1},{1,2},{2,3},{3,0},{4,5},{5,6},{6,7},{7,4},{8,9},{9,10},{10,1... | collective-permute-start | bytes 786440 | tf_op jit(solution)/shard_map/ppermute | solution.py:21

commit v2 on v1

v2 whole, which is shorter than its diff:
```python
import jax
import jax.numpy as jnp
from jax import lax
from jax.experimental import pallas as pl
from jax.experimental.pallas import tpu as pltpu
from jax.sharding import PartitionSpec as P

HEAD_DIM = 64
BLK = 128
MOST = 11
IDROWS = 16
SEQ = "seq"
TP = "tp"
VMEM = pl.BlockSpec(memory_space=pltpu.VMEM)
SMEM = pl.BlockSpec(memory_space=pltpu.SMEM)
ANY = pl.BlockSpec(memory_space=pl.ANY)


def send_tp(value, steps):
    count = lax.axis_size(TP)
    return lax.ppermute(value, TP, [(t, (t + steps) % count) for t in range(count)])


def send_seq(value, steps):
    count = lax.axis_size(SEQ)
    return lax.ppermute(
        value, SEQ, [(s, s + steps) for s in range(count) if 0 <= s + steps < count]
    )


def send_partner(value):
    count = lax.axis_size(SEQ)
    return lax.ppermute(value, SEQ, [(s, s ^ 1) for s in range(count)])


def send_five(value):
    count = lax.axis_size(SEQ)
    pairs = [(s, s + 5 if s % 2 else s - 5) for s in range(count)]
    return lax.ppermute(value, SEQ, [(a, b) for a, b in pairs if 0 <= b < count])


def layer_norm(value, gain):
    mean = jnp.mean(value, axis=-1, keepdims=True)
    centred = value - mean
    spread = jnp.mean(centred * centred, axis=-1, keepdims=True)
    return centred * lax.rsqrt(spread + 1e-05) * gain


def dot_t(left, right):
    return lax.dot_general(left, right, (((1,), (1,)), ((), ())), preferred_element_type=jnp.float32)


def dot(left, right):
    return jnp.dot(left, right, preferred_element_type=jnp.float32)


def gelu(value):
    return 0.5 * value * (1.0 + lax.erf(value * (0.5 ** 0.5)))


def kv_kernel(ids_ref, frames_ref, gain_ref, w_ref, normed_ref, kv_ref):
    rows = frames_ref.shape[0]
    normed = layer_norm(frames_ref[...].astype(jnp.float32), gain_ref[...]).astype(jnp.bfloat16)
    normed_ref[...] = normed
    keys = dot_t(normed, w_ref[1]).astype(jnp.bfloat16)
    values = dot_t(normed, w_ref[2]).astype(jnp.bfloat16)
    kv_ref[:rows, :256] = keys[:, :256]
    kv_ref[:rows, 256:512] = values[:, :256]
    kv_ref[:rows, 512:576] = keys[:, 256:]
    kv_ref[:rows, 576:] = values[:, 256:]
    row = lax.broadcasted_iota(jnp.int32, (IDROWS, kv_ref.shape[1]), 0)
    marks = jnp.where(row == 0, ids_ref[0] + 1, jnp.where(row == 1, ids_ref[1] + 1, 0))
    kv_ref[rows:, :] = marks.astype(jnp.float32).astype(jnp.bfloat16)


def attend_kernel(info_ref, q_ref, *refs):
    pieces, (out_ref, joined_ref, buf, marks, sems, mark_sems) = refs[:11], refs[11:]
    parity = info_ref[2]
    rows = q_ref.shape[0]
    copies = []
    for n, piece in enumerate(pieces):
        if n < 5:
            slot = 1 + 2 * n + parity
        elif n < 10:
            slot = 2 * (n - 4) - parity
        else:
            slot = 11 * parity
        copies.append(pltpu.make_async_copy(
            piece.at[pl.ds(rows, IDROWS), pl.ds(0, 128)], marks.at[slot], mark_sems.at[n]))
        copies.append(pltpu.make_async_copy(
            piece.at[pl.ds(0, rows), :], buf.at[pl.ds(pl.multiple_of(slot * rows, rows), rows), :], sems.at[n]))
    for copy in copies:
        copy.start()
    unused = 11 - 11 * parity
    marks[unused] = jnp.zeros(marks.shape[1:], marks.dtype)
    for copy in copies:
        copy.wait()
    seen = marks[...].astype(jnp.float32)
    row = lax.broadcasted_iota(jnp.int32, seen.shape, 1)
    place = (2 * lax.broadcasted_iota(jnp.int32, seen.shape, 0) + row).astype(jnp.float32)
    lane = lax.broadcasted_iota(jnp.int32, (BLK, 128), 1)
    column = lax.broadcasted_iota(jnp.int32, (1, MOST * BLK), 1)
    low = lane < HEAD_DIM
    for i in range(2):
        mine = (info_ref[i] + 1).astype(jnp.float32)
        same = (seen == mine) & (row < 2)
        first = jnp.min(jnp.where(same, place, 99.0)).astype(jnp.int32)
        last = jnp.max(jnp.where(same, place, -1.0)).astype(jnp.int32)
        if i == 0:
            joined_ref[0] = (first < 10 + 2 * parity).astype(jnp.int32)
        start = jnp.clip(first, 2 * parity, MOST + 2 * parity)
        begin = pl.multiple_of(start * BLK, BLK)
        kept = (last + 1 - start) * BLK
        bias = jnp.where(column < kept, 0.0, -1e30)
        window = pl.ds(begin, MOST * BLK)
        for pair in range(3):
            if pair < 2:
                q_pair = q_ref[i * BLK:(i + 1) * BLK, pair * 128:(pair + 1) * 128]
                keys = buf[window, pair * 128:(pair + 1) * 128]
                values = buf[window, 256 + pair * 128:256 + (pair + 1) * 128]
            else:
                q_pair = q_ref[i * BLK:(i + 1) * BLK, 256:384]
                keys = buf[window, 512:640]
                values = keys
            q_pair = q_pair * jnp.asarray(HEAD_DIM ** -0.5, q_pair.dtype)
            halves = []
            for half in range(2 if pair < 2 else 1):
                q_head = jnp.where(low if half == 0 else ~low, q_pair, jnp.zeros_like(q_pair))
                scores = lax.dot_general(
                    q_head, keys, (((1,), (1,)), ((), ())), preferred_element_type=jnp.float32) + bias
                top = jnp.max(scores, axis=-1, keepdims=True)
                weights = jnp.exp(scores - top)
                total = jnp.sum(weights, axis=-1, keepdims=True)
                summed = jnp.dot(weights.astype(jnp.bfloat16), values, preferred_element_type=jnp.float32)
                halves.append(summed / total)
            if pair < 2:
                merged = jnp.where(low, halves[0], halves[1])
                out_ref[i * BLK:(i + 1) * BLK, pair * 128:(pair + 1) * 128] = merged.astype(jnp.bfloat16)
            else:
                out_ref[i * BLK:(i + 1) * BLK, 256:] = halves[0][:, HEAD_DIM:].astype(jnp.bfloat16)


def query_kernel(normed_ref, w_ref, q_ref):
    q_ref[...] = jnp.zeros_like(q_ref)
    q_ref[:, :w_ref.shape[1]] = dot_t(normed_ref[...], w_ref[0]).astype(jnp.bfloat16)


def mlp_kernel(tp_ref, att0, att1, att2, att3, w_out_ref, frames_ref, gain_ref, w_up_ref, w_down_ref,
               resid_ref, part0, part1, part2, part3, resid_all, part_all):
    tp = tp_ref[0]
    rows, heads = att0.shape
    share = rows // 4
    resid = frames_ref[...].astype(jnp.float32)
    for k, att in enumerate((att0, att1, att2, att3)):
        source = lax.rem(tp + 4 - k, 4)
        resid = resid + dot(att[...], w_out_ref[pl.ds(pl.multiple_of(source * heads, heads), heads), :])
    resid_all[...] = resid
    normed = layer_norm(resid, gain_ref[...]).astype(jnp.bfloat16)
    hidden = gelu(dot(normed, w_up_ref[...])).astype(jnp.bfloat16)
    part_all[...] = dot(hidden, w_down_ref[...]).astype(jnp.bfloat16)
    mine = pl.ds(pl.multiple_of(tp * share, share), share)
    resid_ref[:share, :] = resid_all[mine, :]
    resid_ref[share:, :] = resid_all[rows - IDROWS:, :]
    for k, part in enumerate((part0, part1, part2, part3)):
        target = lax.rem(tp + k, 4)
        part[:share, :] = part_all[pl.ds(pl.multiple_of(target * share, share), share), :]
        part[share:, :] = part_all[rows - IDROWS:, :]


def layer_sum_kernel(resid_ref, own, got1, got2, got3, out_ref, rim_ref):
    total = resid_ref[...] + own[...].astype(jnp.float32)
    for piece in (got1, got2, got3):
        total = total + piece[...].astype(jnp.float32)
    share = out_ref.shape[0]
    out_ref[...] = total[:share].astype(jnp.bfloat16)
    rim_ref[...] = total[share:].astype(jnp.bfloat16)


def adapter_kernel(info_ref, own, got1, got2, got3, rim_ref, w_conv_ref, w_proj_ref,
                   lm0, lm1, lm2, lm3, rows_ref, pooled_ref):
    tp = info_ref[0]
    share = own.shape[0]
    for k, piece in enumerate((own, got1, got2, got3)):
        source = lax.rem(tp + 4 - k, 4)
        rows_ref[pl.ds(pl.multiple_of(source * share, share), share), :] = piece[...]
    rows = rows_ref[...]
    count = rows.shape[0] // 2
    j = lax.broadcasted_iota(jnp.int32, (count, 2 * count), 0)
    r = lax.broadcasted_iota(jnp.int32, (count, 2 * count), 1)
    same_block = info_ref[1] == info_ref[2]
    cut = jnp.where(same_block, -1, count // 2)
    one = lambda flag: jnp.where(flag, 1.0, 0.0).astype(jnp.bfloat16)
    pick = lambda flag, source: dot(one(flag), source).astype(jnp.bfloat16)
    even = pick(r == 2 * j, rows)
    odd = pick(r == 2 * j + 1, rows)
    rim_first = jnp.where(info_ref[3] == 1, 0, -1)
    j_rim = lax.broadcasted_iota(jnp.int32, (count, IDROWS), 0)
    r_rim = lax.broadcasted_iota(jnp.int32, (count, IDROWS), 1)
    before = dot(one((r == 2 * j - 1) & (j != cut)), rows)
    before = before + dot(one((j_rim == rim_first) & (r_rim == IDROWS - 1)), rim_ref[...])
    conv = dot_t(before.astype(jnp.bfloat16), w_conv_ref[0])
    conv = conv + dot_t(even, w_conv_ref[1])
    conv = conv + dot_t(odd, w_conv_ref[2])
    pooled_ref[...] = gelu(conv).astype(jnp.bfloat16)
    piece = count // 4
    turned = [pooled_ref[pl.ds(pl.multiple_of(lax.rem(tp + k, 4) * piece, piece), piece), :] for k in range(4)]
    lm = dot(jnp.concatenate(turned, axis=0), w_proj_ref[...]).astype(jnp.bfloat16)
    for k, out in enumerate((lm0, lm1, lm2, lm3)):
        out[...] = lm[k * piece:(k + 1) * piece]


def lm_sum_kernel(own, got1, got2, got3, out_ref):
    total = own[...].astype(jnp.float32)
    for piece in (got1, got2, got3):
        total = total + piece[...].astype(jnp.float32)
    out_ref[...] = total.astype(jnp.bfloat16)


def params(mib):
    return pltpu.CompilerParams(vmem_limit_bytes=mib << 20)


def cost(flops, moved):
    return pl.CostEstimate(flops=int(flops), bytes_accessed=int(moved), transcendentals=0)


def bf16(*shape):
    return jax.ShapeDtypeStruct(shape, jnp.bfloat16)


def attend(ids, normed, w_qkv, kv):
    rows = normed.shape[0]
    width = w_qkv.shape[1]
    parity = lax.rem(lax.axis_index(SEQ), 2)
    far_back, far_on = send_seq(kv, 4), send_seq(kv, -4)
    back, on = send_seq(kv, 2), send_seq(kv, -2)
    five = send_five(kv)
    beside = send_partner(kv)
    queries = pl.pallas_call(
        query_kernel,
        out_shape=bf16(rows, 384),
        grid=(1,),
        in_specs=[
            pl.BlockSpec(normed.shape, lambda i: (0, 0)),
            pl.BlockSpec((1,) + w_qkv.shape[1:], lambda i: (0, 0, 0)),
        ],
        out_specs=pl.BlockSpec((rows, 384), lambda i: (0, 0)),
        compiler_params=params(16),
        cost_estimate=cost(2e8, 2e6),
    )(normed, w_qkv)
    chain = [far_back, back, kv, on, far_on]
    swapped = [send_partner(far_back), send_partner(back), beside, send_partner(on), send_partner(far_on)]
    info = jnp.concatenate([ids, parity[None].astype(jnp.int32)])
    return pl.pallas_call(
        attend_kernel,
        out_shape=(bf16(rows, width), jax.ShapeDtypeStruct((1,), jnp.int32)),
        in_specs=[SMEM, VMEM] + [ANY] * 11,
        out_specs=(VMEM, SMEM),
        scratch_shapes=[
            pltpu.VMEM((12 * rows, kv.shape[1]), jnp.bfloat16),
            pltpu.VMEM((12, IDROWS, 128), jnp.bfloat16),
            pltpu.SemaphoreType.DMA((11,)),
            pltpu.SemaphoreType.DMA((11,)),
        ],
        compiler_params=params(24),
        cost_estimate=cost(1e9, 4e6),
    )(info, queries, *chain, *swapped, five)


def exchange(parts):
    far = send_tp(parts[1], 2)
    return [send_tp(parts[0], 1), far, send_tp(parts[2], 3)]


def shards(frames, gain_attn, w_qkv, w_out, gain_ffn, w_up, w_down, w_conv, w_proj, block_utt):
    rows, width = frames.shape
    share = rows // 4
    lm_width = w_proj.shape[1]
    w_qkv = jnp.swapaxes(w_qkv, 1, 2)
    w_conv = jnp.swapaxes(w_conv, 1, 2)
    tp = lax.axis_index(TP).astype(jnp.int32)[None]
    w_out_all = lax.all_gather(w_out, TP, tiled=True)
    normed, kv = pl.pallas_call(
        kv_kernel,
        out_shape=(bf16(rows, width), bf16(rows + IDROWS, 2 * w_qkv.shape[1])),
        in_specs=[SMEM, VMEM, VMEM, VMEM],
        out_specs=(VMEM, VMEM),
        compiler_params=params(16),
        cost_estimate=cost(4e8, 4e6),
    )(block_utt, frames, gain_attn[None], w_qkv)
    attended, joined = attend(block_utt, normed, w_qkv, kv)
    heads = exchange([attended] * 3)

    resid, *parts = pl.pallas_call(
        mlp_kernel,
        out_shape=[jax.ShapeDtypeStruct((share + IDROWS, width), jnp.float32)] + [bf16(share + IDROWS, width)] * 4,
        in_specs=[SMEM] + [VMEM] * 9,
        out_specs=[VMEM] * 5,
        scratch_shapes=[pltpu.VMEM((rows, width), jnp.float32), pltpu.VMEM((rows, width), jnp.bfloat16)],
        compiler_params=params(32),
        cost_estimate=cost(2.5e9, 1e7),
    )(tp, attended, *heads, w_out_all, frames, gain_ffn[None], w_up, w_down)
    own, rim = pl.pallas_call(
        layer_sum_kernel,
        out_shape=[bf16(share, width), bf16(IDROWS, width)],
        in_specs=[VMEM] * 5,
        out_specs=[VMEM] * 2,
        compiler_params=params(8),
        cost_estimate=cost(1e6, 1e6),
    )(resid, parts[0], *exchange(parts[1:]))
    layer = exchange([own] * 3)
    rim = send_seq(rim, 1)
    info = jnp.concatenate([tp, block_utt, joined])
    pooled_count = rows // 2
    lm = pl.pallas_call(
        adapter_kernel,
        out_shape=[bf16(pooled_count // 4, lm_width)] * 4,
        in_specs=[SMEM] + [VMEM] * 7,
        out_specs=[VMEM] * 4,
        scratch_shapes=[pltpu.VMEM((rows, width), jnp.bfloat16), pltpu.VMEM((pooled_count, w_conv.shape[1]), jnp.bfloat16)],
        compiler_params=params(24),
        cost_estimate=cost(1e9, 6e6),
    )(info, own, *layer, rim, w_conv, w_proj)
    return pl.pallas_call(
        lm_sum_kernel,
        out_shape=bf16(pooled_count // 4, lm_width),
        in_specs=[VMEM] * 4,
        out_specs=VMEM,
        compiler_params=params(8),
        cost_estimate=cost(1e6, 1e6),
    )(lm[0], *exchange(lm[1:]))


def solution(mesh):
    placed = (
        P("seq", None),
        P(),
        P(None, None, "tp"),
        P("tp", None),
        P(),
        P(None, "tp"),
        P("tp", None),
        P(None, None, "tp"),
        P("tp", None),
        P("seq"),
    )
    return jax.shard_map(
        shards, mesh=mesh, in_specs=placed, out_specs=P(("seq", "tp"), None), check_vma=False
    )
```

time: 169 us -> 134 us (0.79)
  local copies, waits for them, and re-layouts: 28.8 us -> 9.83 us
  matrix products: 17.7 us -> 0 us
  between operations: 0.39 us -> 13.6 us
  Pallas kernels: 9.75 us -> 20.1 us
  other arithmetic: 10.5 us -> 0.8 us
  waiting for transfers between devices: 57.7 us -> 49.5 us
  starting transfers between devices: 42.2 us -> 39.3 us
    ppermute x15 -> x12, waiting for transfers between devices: 54.4 us -> 26.6 us  [send_tp(): lax.ppermute(value, TP, [(t, (t + steps) % count) for t in range(count)])]
    ppermute x6 -> x5, waiting for transfers between devices: 1.15 us -> 20.8 us  [send_seq(): lax.ppermute(value, SEQ, [(s, s + steps) for s in range(count) if 0 <= s...]
    dot_general x9 -> x0, matrix products: 17.7 us -> none  [the longest x1 7.66 us: shards(): jnp.dot(hidden, w_down, preferred_element_type=jnp.float32)]
    pallas_call x2 -> x7, Pallas kernels: 9.75 us -> 20.1 us  [the longest x1 7.41 us: attend(): pl.pallas_call(attend_kernel, out_shape=(bf16(rows, width), jax.ShapeDtyp...]
    squeeze x4 -> x0, local copies, waits for them, and re-layouts: 5.32 us -> none  [the longest x2 3.01 us: shards(): lax.dynamic_index_in_dim(array, lax.rem(tp + k, 4), 0, False)]
    slice x5 -> x0, local copies, waits for them, and re-layouts: 4.68 us -> none  [the longest x1 2.59 us: shards(): even_rows = pairs[:, 0]]
    ppermute x15 -> x12, starting transfers between devices: 16.4 us -> 20.9 us  [send_tp(): lax.ppermute(value, TP, [(t, (t + steps) % count) for t in range(count)])]
    ppermute x6 -> x5, starting transfers between devices: 4.98 us -> 0.6 us  [send_partner(): return lax.ppermute(value, SEQ, [(s, s ^ 1) for s in range(count)])]
  transfers between devices with their start and end apart: 28 -> 24, of which waited for: 14 -> 14; matrix products, arithmetic and copies ran while one was open for 19% -> 1% of each run, Pallas kernels for 4% -> 8%
where the time goes in v2:
time: 134 us; the launch traced here: 133 us
  waiting for transfers between devices  49.5 us (37%)
  starting transfers between devices  39.3 us (29%)
  Pallas kernels  20.1 us (15%)
  between operations  13.6 us (10%)
  local copies, waits for them, and re-layouts  9.83 us (7%)
    ppermute x12, waiting for transfers between devices, send_tp(): lax.ppermute(value, TP, [(t, (t + steps) % count) for t in range(count)])  26.6 us
    ppermute x12, starting transfers between devices, send_tp(): lax.ppermute(value, TP, [(t, (t + steps) % count) for t in range(count)])  20.9 us
    ppermute x5, waiting for transfers between devices, send_seq(): lax.ppermute(value, SEQ, [(s, s + steps) for s in range(count) if 0 <= s...  20.8 us
    ppermute x5, starting transfers between devices, send_seq(): lax.ppermute(value, SEQ, [(s, s + steps) for s in range(count) if 0 <= s...  15.1 us
    unnamed x28, local copies, waits for them, and re-layouts  9.12 us
    pallas_call x1, Pallas kernels, attend(): pl.pallas_call(attend_kernel, out_shape=(bf16(rows, width), jax.ShapeDtyp...  7.41 us
    pallas_call x1, Pallas kernels, shards(): pl.pallas_call(mlp_kernel, out_shape=[jax.ShapeDtypeStruct((share + IDROW...  5.63 us
    pallas_call x1, Pallas kernels, shards(): pl.pallas_call(adapter_kernel, out_shape=[bf16(pooled_count // 4, lm_widt...  3.03 us
  transfers between devices with their start and end apart: 24, of which 14 were waited for; matrix products, arithmetic and copies ran while one was open for 1% of the time, Pallas kernels for 8%

profile of v2, /device:TPU:70, one launch (start us, length us, event | category | flops | bytes accessed | tf_op | source)
XLA Modules:
  0.0 133.1 jit_solution(16334077697144470094)
XLA Ops:
  6.5 0.7 all-gather.2.cloned.1.call-update
  7.3 0.0 copy-start.12
  7.3 0.7 broadcast_in_dim.14.gain_ref
  8.0 1.7 %copy-done = bf16[3,1280,320]{1,2,0:T(8,128)(2,1)S(1)} copy-done((bf16[3,1280,320]{1,2,0:T(8,128)(2,1)S(1)}, bf16[3,1280,320]{1,2,0:T(8,128)(2,1)}, u32[]{:S(2)}) %copy-start) | copy-done | bytes 2457624
  9.7 1.1 copy-done.5
  10.8 0.7 copy-done.11
  11.4 2.5 %shard_map.100 = (bf16[256,1280]{1,0:T(8,128)(2,1)S(1)}, bf16[272,640]{1,0:T(8,128)(2,1)}) custom-call(s32[2]{0:T(128)S(1)} %copy-done.11, bf16[256,1280]{1,0:T(8,128)(2,1)S(1)} %copy-done.5, f32[1,1280]{1,0:T(1,128)S(1)} %broadcast_in_dim.14.gain_ref, bf16[3,320,1280]{2,1,0:T(8,128)(2,1)S(1)} %bitcast.4), custom_call_target="tpu_custom_call" | custom-call | flops 400000000 | bytes 4000000 | tf_op jit(solution)/shard_map/pallas_call | solution.py:283
  13.9 4.4 %collective-permute-start = (bf16[272,640]{1,0:T(8,128)(2,1)}, bf16[272,640]{1,0:T(8,128)(2,1)}, u32[]{:S(2)}, u32[]{:S(2)}) collective-permute-start(bf16[272,640]{1,0:T(8,128)(2,1)} %get-tuple-element.21.refs_2_), channel_id=1, source_target_pairs={{0,16},{4,20},{8,24},{12,28},{16,32},{20,36},{24,40},{28,44},{32,4... | collective-permute-start | bytes 1044488 | tf_op jit(solution)/shard_map/ppermute | solution.py:26
  18.3 4.0 %collective-permute-start.1 = (bf16[272,640]{1,0:T(8,128)(2,1)}, bf16[272,640]{1,0:T(8,128)(2,1)}, u32[]{:S(2)}, u32[]{:S(2)}) collective-permute-start(bf16[272,640]{1,0:T(8,128)(2,1)} %get-tuple-element.21.refs_2_), channel_id=1, source_target_pairs={{0,8},{4,12},{8,16},{12,20},{16,24},{20,28},{24,32},{28,36},{32,40... | collective-permute-start | bytes 1044488 | tf_op jit(solution)/shard_map/ppermute | solution.py:26
  22.3 1.9 %collective-permute-start.2 = (bf16[272,640]{1,0:T(8,128)(2,1)}, bf16[272,640]{1,0:T(8,128)(2,1)}, u32[]{:S(2)}, u32[]{:S(2)}) collective-permute-start(bf16[272,640]{1,0:T(8,128)(2,1)} %get-tuple-element.21.refs_2_), channel_id=1, source_target_pairs={{8,0},{12,4},{16,8},{20,12},{24,16},{28,20},{32,24},{36,28},{40,32... | collective-permute-start | bytes 1044488 | tf_op jit(solution)/shard_map/ppermute | solution.py:26
  24.3 2.9 %collective-permute-start.3 = (bf16[272,640]{1,0:T(8,128)(2,1)}, bf16[272,640]{1,0:T(8,128)(2,1)}, u32[]{:S(2)}, u32[]{:S(2)}) collective-permute-start(bf16[272,640]{1,0:T(8,128)(2,1)} %get-tuple-element.21.refs_2_), channel_id=1, source_target_pairs={{16,0},{20,4},{24,8},{28,12},{32,16},{36,20},{40,24},{44,28},{48,3... | collective-permute-start | bytes 1044488 | tf_op jit(solution)/shard_map/ppermute | solution.py:26
  27.2 0.1 collective-permute-start.6
  27.3 1.4 %collective-permute-done.refs_0_ = bf16[272,640]{1,0:T(8,128)(2,1)} collective-permute-done((bf16[272,640]{1,0:T(8,128)(2,1)}, bf16[272,640]{1,0:T(8,128)(2,1)}, u32[]{:S(2)}, u32[]{:S(2)}) %collective-permute-start) | collective-permute-done | bytes 348192 | tf_op jit(solution)/shard_map/ppermute | solution.py:26
  28.7 2.7 %collective-permute-start.9 = (bf16[272,640]{1,0:T(8,128)(2,1)}, bf16[272,640]{1,0:T(8,128)(2,1)}, u32[]{:S(2)}, u32[]{:S(2)}) collective-permute-start(bf16[272,640]{1,0:T(8,128)(2,1)} %get-tuple-element.21.refs_2_), channel_id=1, source_target_pairs={{4,24},{12,32},{20,40},{24,4},{28,48},{32,12},{36,56},{40,20},{44,... | collective-permute-start | bytes 1044488 | tf_op jit(solution)/shard_map/ppermute | solution.py:39
  31.4 3.7 %collective-permute-done.1.refs_1_ = bf16[272,640]{1,0:T(8,128)(2,1)} collective-permute-done((bf16[272,640]{1,0:T(8,128)(2,1)}, bf16[272,640]{1,0:T(8,128)(2,1)}, u32[]{:S(2)}, u32[]{:S(2)}) %collective-permute-start.1) | collective-permute-done | bytes 348192 | tf_op jit(solution)/shard_map/ppermute | solution.py:26
  35.1 0.0 collective-permute-start.4
  35.1 13.0 %collective-permute-done.2.refs_3_ = bf16[272,640]{1,0:T(8,128)(2,1)} collective-permute-done((bf16[272,640]{1,0:T(8,128)(2,1)}, bf16[272,640]{1,0:T(8,128)(2,1)}, u32[]{:S(2)}, u32[]{:S(2)}) %collective-permute-start.2) | collective-permute-done | bytes 348192 | tf_op jit(solution)/shard_map/ppermute | solution.py:26
  48.1 0.0 collective-permute-start.5
  48.1 0.0 collective-permute-done.3.refs_4_
  48.1 0.5 collective-permute-start.7
  48.6 0.0 collective-permute-done.6.refs_7_
  48.6 0.7 copy-done.9
  49.3 0.0 collective-permute-start.8
  49.3 0.5 shard_map.101.q_ref
  49.9 0.0 copy-start.2
  49.9 0.1 pad_add_fusion.info_ref
  50.0 0.0 collective-permute-done.9.refs_10_
  50.0 0.0 collective-permute-done.4.refs_5_
  50.0 0.1 collective-permute-done.5.refs_6_
  50.1 0.5 collective-permute-done.7.refs_8_
  50.6 0.7 collective-permute-done.8.refs_9_
  51.3 7.4 %shard_map.102 = (bf16[256,320]{1,0:T(8,128)(2,1)S(1)}, s32[1]{0:T(128)}) custom-call(s32[3]{0:T(128)S(1)} %pad_add_fusion.info_ref, bf16[256,384]{1,0:T(8,128)(2,1)S(1)} %shard_map.101.q_ref, bf16[272,640]{1,0:T(8,128)(2,1)} %collective-permute-done.refs_0_, bf16[272,640]{1,0:T(8,128)(2,1)} %collective-permute-done.1.refs_1_, ...), custom_call_target="tpu_custom_call" | custom-call | flops 1000000000 | bytes 4000000 | tf_op jit(solution)/shard_map/pallas_call | solution.py:254
  58.7 1.6 %collective-permute-start.10 = (bf16[256,320]{1,0:T(8,128)(2,1)S(1)}, bf16[256,320]{1,0:T(8,128)(2,1)}, u32[]{:S(2)}, u32[]{:S(2)}) collective-permute-start(bf16[256,320]{1,0:T(8,128)(2,1)S(1)} %get-tuple-element.23.att0), channel_id=1, source_target_pairs={{0,1},{1,2},{2,3},{3,0},{4,5},{5,6},{6,7},{7,4},{8,9},{9,10},{10,1... | collective-permute-start | bytes 491528 | tf_op jit(solution)/shard_map/ppermute | solution.py:21
  60.4 2.9 %collective-permute-start.11 = (bf16[256,320]{1,0:T(8,128)(2,1)S(1)}, bf16[256,320]{1,0:T(8,128)(2,1)}, u32[]{:S(2)}, u32[]{:S(2)}) collective-permute-start(bf16[256,320]{1,0:T(8,128)(2,1)S(1)} %get-tuple-element.23.att0), channel_id=1, source_target_pairs={{0,2},{1,3},{2,0},{3,1},{4,6},{5,7},{6,4},{7,5},{8,10},{9,11},{10,... | collective-permute-start | bytes 491528 | tf_op jit(solution)/shard_map/ppermute | solution.py:21
  63.3 1.3 %collective-permute-start.12 = (bf16[256,320]{1,0:T(8,128)(2,1)S(1)}, bf16[256,320]{1,0:T(8,128)(2,1)}, u32[]{:S(2)}, u32[]{:S(2)}) collective-permute-start(bf16[256,320]{1,0:T(8,128)(2,1)S(1)} %get-tuple-element.23.att0), channel_id=1, source_target_pairs={{0,3},{1,0},{2,1},{3,2},{4,7},{5,4},{6,5},{7,6},{8,11},{9,8},{10,9... | collective-permute-start | bytes 491528 | tf_op jit(solution)/shard_map/ppermute | solution.py:21
  64.6 2.5 %collective-permute-done.10.att1 = bf16[256,320]{1,0:T(8,128)(2,1)} collective-permute-done((bf16[256,320]{1,0:T(8,128)(2,1)S(1)}, bf16[256,320]{1,0:T(8,128)(2,1)}, u32[]{:S(2)}, u32[]{:S(2)}) %collective-permute-start.10) | collective-permute-done | bytes 163872 | tf_op jit(solution)/shard_map/ppermute | solution.py:21
  67.1 5.4 %collective-permute-done.11.att2 = bf16[256,320]{1,0:T(8,128)(2,1)} collective-permute-done((bf16[256,320]{1,0:T(8,128)(2,1)S(1)}, bf16[256,320]{1,0:T(8,128)(2,1)}, u32[]{:S(2)}, u32[]{:S(2)}) %collective-permute-start.11) | collective-permute-done | bytes 163872 | tf_op jit(solution)/shard_map/ppermute | solution.py:21
  72.5 0.0 copy-start.3
  72.5 1.9 %copy-done.3 = bf16[1280,1280]{1,0:T(8,128)(2,1)S(1)} copy-done((bf16[1280,1280]{1,0:T(8,128)(2,1)S(1)}, bf16[1280,1280]{1,0:T(8,128)(2,1)}, u32[]{:S(2)}) %copy-start.3) | copy-done | bytes 3276824
  74.5 1.9 %copy-done.4 = bf16[1280,1280]{1,0:T(8,128)(2,1)S(1)} copy-done((bf16[1280,1280]{1,0:T(8,128)(2,1)S(1)}, bf16[1280,1280]{1,0:T(8,128)(2,1)}, u32[]{:S(2)}) %copy-start.4) | copy-done | bytes 3276824
  76.4 1.1 copy-done.6
  77.5 5.6 %shard_map.103 = (f32[80,1280]{1,0:T(8,128)S(1)}, bf16[80,1280]{1,0:T(8,128)(2,1)S(1)}, bf16[80,1280]{1,0:T(8,128)(2,1)S(1)}, bf16[80,1280]{1,0:T(8,128)(2,1)S(1)}, bf16[80,1280]{1,0:T(8,128)(2,1)S(1)}) custom-call(s32[1]{0:T(128)} %bitcast.tp_ref, bf16[256,320]{1,0:T(8,128)(2,1)S(1)} %get-tuple-element.23.att0, ...), custom_call_target="tpu_custom_call" | custom-call | flops 2500000000 | bytes 10000000 | tf_op jit(solution)/shard_map/pallas_call | solution.py:294
  83.1 1.5 %collective-permute-start.13 = (bf16[80,1280]{1,0:T(8,128)(2,1)S(1)}, bf16[80,1280]{1,0:T(8,128)(2,1)S(1)}, u32[]{:S(2)}, u32[]{:S(2)}) collective-permute-start(bf16[80,1280]{1,0:T(8,128)(2,1)S(1)} %get-tuple-element.26), channel_id=1, source_target_pairs={{0,1},{1,2},{2,3},{3,0},{4,5},{5,6},{6,7},{7,4},{8,9},{9,10},{10,1... | collective-permute-start | bytes 614408 | tf_op jit(solution)/shard_map/ppermute | solution.py:21
  84.6 2.4 %collective-permute-start.14 = (bf16[80,1280]{1,0:T(8,128)(2,1)S(1)}, bf16[80,1280]{1,0:T(8,128)(2,1)S(1)}, u32[]{:S(2)}, u32[]{:S(2)}) collective-permute-start(bf16[80,1280]{1,0:T(8,128)(2,1)S(1)} %get-tuple-element.27), channel_id=1, source_target_pairs={{0,2},{1,3},{2,0},{3,1},{4,6},{5,7},{6,4},{7,5},{8,10},{9,11},{10,... | collective-permute-start | bytes 614408 | tf_op jit(solution)/shard_map/ppermute | solution.py:21
  87.0 1.6 %collective-permute-start.15 = (bf16[80,1280]{1,0:T(8,128)(2,1)S(1)}, bf16[80,1280]{1,0:T(8,128)(2,1)S(1)}, u32[]{:S(2)}, u32[]{:S(2)}) collective-permute-start(bf16[80,1280]{1,0:T(8,128)(2,1)S(1)} %get-tuple-element.28), channel_id=1, source_target_pairs={{0,3},{1,0},{2,1},{3,2},{4,7},{5,4},{6,5},{7,6},{8,11},{9,8},{10,9... | collective-permute-start | bytes 614408 | tf_op jit(solution)/shard_map/ppermute | solution.py:21
  88.6 2.3 %collective-permute-done.13.got1 = bf16[80,1280]{1,0:T(8,128)(2,1)S(1)} collective-permute-done((bf16[80,1280]{1,0:T(8,128)(2,1)S(1)}, bf16[80,1280]{1,0:T(8,128)(2,1)S(1)}, u32[]{:S(2)}, u32[]{:S(2)}) %collective-permute-start.13) | collective-permute-done | bytes 204832 | tf_op jit(solution)/shard_map/ppermute | solution.py:21
  90.8 5.5 %collective-permute-done.14.got2 = bf16[80,1280]{1,0:T(8,128)(2,1)S(1)} collective-permute-done((bf16[80,1280]{1,0:T(8,128)(2,1)S(1)}, bf16[80,1280]{1,0:T(8,128)(2,1)S(1)}, u32[]{:S(2)}, u32[]{:S(2)}) %collective-permute-start.14) | collective-permute-done | bytes 204832 | tf_op jit(solution)/shard_map/ppermute | solution.py:21
  96.3 0.0 collective-permute-done.15.got3
  96.3 0.1 shard_map.104
  96.5 1.2 collective-permute-start.16
  97.7 2.5 %collective-permute-start.17 = (bf16[64,1280]{1,0:T(8,128)(2,1)S(1)}, bf16[64,1280]{1,0:T(8,128)(2,1)S(1)}, u32[]{:S(2)}, u32[]{:S(2)}) collective-permute-start(bf16[64,1280]{1,0:T(8,128)(2,1)S(1)} %get-tuple-element.29.own), channel_id=1, source_target_pairs={{0,2},{1,3},{2,0},{3,1},{4,6},{5,7},{6,4},{7,5},{8,10},{9,11},{10,... | collective-permute-start | bytes 491528 | tf_op jit(solution)/shard_map/ppermute | solution.py:21
  100.2 0.8 collective-permute-start.18
  101.0 1.9 %collective-permute-start.19 = (bf16[16,1280]{1,0:T(8,128)(2,1)S(1)}, bf16[16,1280]{1,0:T(8,128)(2,1)S(1)}, u32[]{:S(2)}, u32[]{:S(2)}) collective-permute-start(bf16[16,1280]{1,0:T(8,128)(2,1)S(1)} %get-tuple-element.30), channel_id=1, source_target_pairs={{0,4},{4,8},{8,12},{12,16},{16,20},{20,24},{24,28},{28,32},{32,36}... | collective-permute-start | bytes 122888 | tf_op jit(solution)/shard_map/ppermute | solution.py:26
  102.9 0.7 pad_add_fusion.1.info_ref
  103.6 2.7 %collective-permute-done.19.rim_ref = bf16[16,1280]{1,0:T(8,128)(2,1)S(1)} collective-permute-done((bf16[16,1280]{1,0:T(8,128)(2,1)S(1)}, bf16[16,1280]{1,0:T(8,128)(2,1)S(1)}, u32[]{:S(2)}, u32[]{:S(2)}) %collective-permute-start.19) | collective-permute-done | bytes 40992 | tf_op jit(solution)/shard_map/ppermute | solution.py:26
  106.3 0.0 collective-permute-done.16.got1
  106.3 0.9 collective-permute-done.17.got2
  107.2 3.0 %shard_map.105 = (bf16[32,4096]{1,0:T(8,128)(2,1)S(1)}, bf16[32,4096]{1,0:T(8,128)(2,1)S(1)}, bf16[32,4096]{1,0:T(8,128)(2,1)S(1)}, bf16[32,4096]{1,0:T(8,128)(2,1)S(1)}) custom-call(s32[4]{0:T(128)S(1)} %pad_add_fusion.1.info_ref, bf16[64,1280]{1,0:T(8,128)(2,1)S(1)} %get-tuple-element.29.own, bf16[64,1280]{1,0:T(8,128)(2,1)S(1)} %collective-permute-done.16.got1, ...), custom_call_target="tpu_custom_call" | custom-call | flops 1000000000 | bytes 6000000 | tf_op jit(solution)/shard_map/pallas_call | solution.py:315
  110.2 1.7 %collective-permute-start.20 = (bf16[32,4096]{1,0:T(8,128)(2,1)S(1)}, bf16[32,4096]{1,0:T(8,128)(2,1)S(1)}, u32[]{:S(2)}, u32[]{:S(2)}) collective-permute-start(bf16[32,4096]{1,0:T(8,128)(2,1)S(1)} %get-tuple-element.32), channel_id=1, source_target_pairs={{0,1},{1,2},{2,3},{3,0},{4,5},{5,6},{6,7},{7,4},{8,9},{9,10},{10,1... | collective-permute-start | bytes 786440 | tf_op jit(solution)/shard_map/ppermute | solution.py:21
  112.0 2.4 %collective-permute-start.21 = (bf16[32,4096]{1,0:T(8,128)(2,1)S(1)}, bf16[32,4096]{1,0:T(8,128)(2,1)S(1)}, u32[]{:S(2)}, u32[]{:S(2)}) collective-permute-start(bf16[32,4096]{1,0:T(8,128)(2,1)S(1)} %get-tuple-element.33), channel_id=1, source_target_pairs={{0,2},{1,3},{2,0},{3,1},{4,6},{5,7},{6,4},{7,5},{8,10},{9,11},{10,... | collective-permute-start | bytes 786440 | tf_op jit(solution)/shard_map/ppermute | solution.py:21
  114.4 1.0 collective-permute-start.22
  115.3 3.9 %collective-permute-done.20.got1 = bf16[32,4096]{1,0:T(8,128)(2,1)S(1)} collective-permute-done((bf16[32,4096]{1,0:T(8,128)(2,1)S(1)}, bf16[32,4096]{1,0:T(8,128)(2,1)S(1)}, u32[]{:S(2)}, u32[]{:S(2)}) %collective-permute-start.20) | collective-permute-done | bytes 262176 | tf_op jit(solution)/shard_map/ppermute | solution.py:21
  119.2 6.2 %collective-permute-done.21.got2 = bf16[32,4096]{1,0:T(8,128)(2,1)S(1)} collective-permute-done((bf16[32,4096]{1,0:T(8,128)(2,1)S(1)}, bf16[32,4096]{1,0:T(8,128)(2,1)S(1)}, u32[]{:S(2)}, u32[]{:S(2)}) %collective-permute-start.21) | collective-permute-done | bytes 262176 | tf_op jit(solution)/shard_map/ppermute | solution.py:21
  125.4 0.8 shard_map.106
  (24 shorter events, 0.0 us)
Async XLA Ops:
  6.5 66.0 %all-gather.2.cloned.1.call-start = ((), (), s32[]{:S(2)}) async-start(), calls=%async_computation | async-start | bytes 4096000 | tf_op jit(solution)/shard_map/all_gather | solution.py:282
  7.3 42.6 %copy-start.12 = (s32[2]{0:T(128)S(1)}, s32[2]{0:T(128)}, u32[]{:S(2)}) copy-start(s32[2]{0:T(128)} %ids_ref.1) | copy-start | bytes 28
  8.0 1.7 %copy-start = (bf16[3,1280,320]{1,2,0:T(8,128)(2,1)S(1)}, bf16[3,1280,320]{1,2,0:T(8,128)(2,1)}, u32[]{:S(2)}) copy-start(bf16[3,1280,320]{1,2,0:T(8,128)(2,1)} %param.12) | copy-start | bytes 7372804
  9.7 1.1 copy-start.5
  10.8 0.7 copy-start.11
  11.4 37.9 %copy-start.1 = (bf16[3,1280,320]{1,2,0:T(8,128)(2,1)S(1)}, bf16[3,1280,320]{1,2,0:T(8,128)(2,1)}, u32[]{:S(2)}) copy-start(bf16[3,1280,320]{1,2,0:T(8,128)(2,1)} %param.12) | copy-start | bytes 7372804
  13.9 14.7 %collective-permute-start = (bf16[272,640]{1,0:T(8,128)(2,1)}, bf16[272,640]{1,0:T(8,128)(2,1)}, u32[]{:S(2)}, u32[]{:S(2)}) collective-permute-start(bf16[272,640]{1,0:T(8,128)(2,1)} %get-tuple-element.21.refs_2_), channel_id=1, source_target_pairs={{0,16},{4,20},{8,24},{12,28},{16,32},{20,36},{24,40},{28,44},{32,4... | collective-permute-start | bytes 1044488 | tf_op jit(solution)/shard_map/ppermute | solution.py:26
  18.3 16.7 %collective-permute-start.1 = (bf16[272,640]{1,0:T(8,128)(2,1)}, bf16[272,640]{1,0:T(8,128)(2,1)}, u32[]{:S(2)}, u32[]{:S(2)}) collective-permute-start(bf16[272,640]{1,0:T(8,128)(2,1)} %get-tuple-element.21.refs_2_), channel_id=1, source_target_pairs={{0,8},{4,12},{8,16},{12,20},{16,24},{20,28},{24,32},{28,36},{32,40... | collective-permute-start | bytes 1044488 | tf_op jit(solution)/shard_map/ppermute | solution.py:26
  22.3 25.7 %collective-permute-start.2 = (bf16[272,640]{1,0:T(8,128)(2,1)}, bf16[272,640]{1,0:T(8,128)(2,1)}, u32[]{:S(2)}, u32[]{:S(2)}) collective-permute-start(bf16[272,640]{1,0:T(8,128)(2,1)} %get-tuple-element.21.refs_2_), channel_id=1, source_target_pairs={{8,0},{12,4},{16,8},{20,12},{24,16},{28,20},{32,24},{36,28},{40,32... | collective-permute-start | bytes 1044488 | tf_op jit(solution)/shard_map/ppermute | solution.py:26
  24.3 23.8 %collective-permute-start.3 = (bf16[272,640]{1,0:T(8,128)(2,1)}, bf16[272,640]{1,0:T(8,128)(2,1)}, u32[]{:S(2)}, u32[]{:S(2)}) collective-permute-start(bf16[272,640]{1,0:T(8,128)(2,1)} %get-tuple-element.21.refs_2_), channel_id=1, source_target_pairs={{16,0},{20,4},{24,8},{28,12},{32,16},{36,20},{40,24},{44,28},{48,3... | collective-permute-start | bytes 1044488 | tf_op jit(solution)/shard_map/ppermute | solution.py:26
  27.2 21.4 %collective-permute-start.6 = (bf16[272,640]{1,0:T(8,128)(2,1)}, bf16[272,640]{1,0:T(8,128)(2,1)S(1)}, u32[]{:S(2)}, u32[]{:S(2)}) collective-permute-start(bf16[272,640]{1,0:T(8,128)(2,1)} %get-tuple-element.21.refs_2_), channel_id=1, source_target_pairs={{0,4},{4,0},{8,12},{12,8},{16,20},{20,16},{24,28},{28,24},{32,36},... | collective-permute-start | bytes 1044488 | tf_op jit(solution)/shard_map/ppermute | solution.py:33
  28.7 21.3 %collective-permute-start.9 = (bf16[272,640]{1,0:T(8,128)(2,1)}, bf16[272,640]{1,0:T(8,128)(2,1)}, u32[]{:S(2)}, u32[]{:S(2)}) collective-permute-start(bf16[272,640]{1,0:T(8,128)(2,1)} %get-tuple-element.21.refs_2_), channel_id=1, source_target_pairs={{4,24},{12,32},{20,40},{24,4},{28,48},{32,12},{36,56},{40,20},{44,... | collective-permute-start | bytes 1044488 | tf_op jit(solution)/shard_map/ppermute | solution.py:39
  35.1 14.9 %collective-permute-start.4 = (bf16[272,640]{1,0:T(8,128)(2,1)}, bf16[272,640]{1,0:T(8,128)(2,1)}, u32[]{:S(2)}, u32[]{:S(2)}) collective-permute-start(bf16[272,640]{1,0:T(8,128)(2,1)} %collective-permute-done.refs_0_), channel_id=1, source_target_pairs={{0,4},{4,0},{8,12},{12,8},{16,20},{20,16},{24,28},{28,24},{32,36},... | collective-permute-start | bytes 1044488 | tf_op jit(solution)/shard_map/ppermute | solution.py:33
  48.1 2.0 %collective-permute-start.5 = (bf16[272,640]{1,0:T(8,128)(2,1)}, bf16[272,640]{1,0:T(8,128)(2,1)}, u32[]{:S(2)}, u32[]{:S(2)}) collective-permute-start(bf16[272,640]{1,0:T(8,128)(2,1)} %collective-permute-done.1.refs_1_), channel_id=1, source_target_pairs={{0,4},{4,0},{8,12},{12,8},{16,20},{20,16},{24,28},{28,24},{32,36},... | collective-permute-start | bytes 1044488 | tf_op jit(solution)/shard_map/ppermute | solution.py:33
  48.1 2.5 %collective-permute-start.7 = (bf16[272,640]{1,0:T(8,128)(2,1)}, bf16[272,640]{1,0:T(8,128)(2,1)}, u32[]{:S(2)}, u32[]{:S(2)}) collective-permute-start(bf16[272,640]{1,0:T(8,128)(2,1)} %collective-permute-done.2.refs_3_), channel_id=1, source_target_pairs={{0,4},{4,0},{8,12},{12,8},{16,20},{20,16},{24,28},{28,24},{32,36},... | collective-permute-start | bytes 1044488 | tf_op jit(solution)/shard_map/ppermute | solution.py:33
  48.6 0.7 copy-start.9
  49.3 2.0 %collective-permute-start.8 = (bf16[272,640]{1,0:T(8,128)(2,1)}, bf16[272,640]{1,0:T(8,128)(2,1)}, u32[]{:S(2)}, u32[]{:S(2)}) collective-permute-start(bf16[272,640]{1,0:T(8,128)(2,1)} %collective-permute-done.3.refs_4_), channel_id=1, source_target_pairs={{0,4},{4,0},{8,12},{12,8},{16,20},{20,16},{24,28},{28,24},{32,36},... | collective-permute-start | bytes 1044488 | tf_op jit(solution)/shard_map/ppermute | solution.py:33
  49.3 2.0 %copy-start.10 = (bf16[272,640]{1,0:T(8,128)(2,1)S(1)}, bf16[272,640]{1,0:T(8,128)(2,1)}, u32[]{:S(2)}) copy-start(bf16[272,640]{1,0:T(8,128)(2,1)} %copy-done.9) | copy-start | bytes 1044484
  49.3 15.3 %copy-start.13 = (f32[1280]{0:T(1024)S(1)}, f32[1280]{0:T(1024)}, u32[]{:S(2)}) copy-start(f32[1280]{0:T(1024)} %param.14) | copy-start | bytes 15364
  49.9 22.7 %copy-start.2 = (bf16[1280,1280]{1,0:T(8,128)(2,1)S(1)}, bf16[1280,1280]{1,0:T(8,128)(2,1)}, u32[]{:S(2)}) copy-start(bf16[1280,1280]{1,0:T(8,128)(2,1)} %w_up_ref.1) | copy-start | bytes 9830404
  58.7 8.4 %collective-permute-start.10 = (bf16[256,320]{1,0:T(8,128)(2,1)S(1)}, bf16[256,320]{1,0:T(8,128)(2,1)}, u32[]{:S(2)}, u32[]{:S(2)}) collective-permute-start(bf16[256,320]{1,0:T(8,128)(2,1)S(1)} %get-tuple-element.23.att0), channel_id=1, source_target_pairs={{0,1},{1,2},{2,3},{3,0},{4,5},{5,6},{6,7},{7,4},{8,9},{9,10},{10,1... | collective-permute-start | bytes 491528 | tf_op jit(solution)/shard_map/ppermute | solution.py:21
  60.4 12.1 %collective-permute-start.11 = (bf16[256,320]{1,0:T(8,128)(2,1)S(1)}, bf16[256,320]{1,0:T(8,128)(2,1)}, u32[]{:S(2)}, u32[]{:S(2)}) collective-permute-start(bf16[256,320]{1,0:T(8,128)(2,1)S(1)} %get-tuple-element.23.att0), channel_id=1, source_target_pairs={{0,2},{1,3},{2,0},{3,1},{4,6},{5,7},{6,4},{7,5},{8,10},{9,11},{10,... | collective-permute-start | bytes 491528 | tf_op jit(solution)/shard_map/ppermute | solution.py:21
  63.3 9.2 %collective-permute-start.12 = (bf16[256,320]{1,0:T(8,128)(2,1)S(1)}, bf16[256,320]{1,0:T(8,128)(2,1)}, u32[]{:S(2)}, u32[]{:S(2)}) collective-permute-start(bf16[256,320]{1,0:T(8,128)(2,1)S(1)} %get-tuple-element.23.att0), channel_id=1, source_target_pairs={{0,3},{1,0},{2,1},{3,2},{4,7},{5,4},{6,5},{7,6},{8,11},{9,8},{10,9... | collective-permute-start | bytes 491528 | tf_op jit(solution)/shard_map/ppermute | solution.py:21
  72.5 1.9 %copy-start.3 = (bf16[1280,1280]{1,0:T(8,128)(2,1)S(1)}, bf16[1280,1280]{1,0:T(8,128)(2,1)}, u32[]{:S(2)}) copy-start(bf16[1280,1280]{1,0:T(8,128)(2,1)} %w_down_ref.1) | copy-start | bytes 9830404
  74.5 1.9 %copy-start.4 = (bf16[1280,1280]{1,0:T(8,128)(2,1)S(1)}, bf16[1280,1280]{1,0:T(8,128)(2,1)}, u32[]{:S(2)}) copy-start(bf16[1280,1280]{1,0:T(8,128)(2,1)} %all-gather.2.cloned.1.call-done.w_out_ref) | copy-start | bytes 9830404
  76.4 1.1 copy-start.6
  77.5 29.7 %copy-start.7 = (bf16[320,4096]{1,0:T(8,128)(2,1)S(1)}, bf16[320,4096]{1,0:T(8,128)(2,1)}, u32[]{:S(2)}) copy-start(bf16[320,4096]{1,0:T(8,128)(2,1)} %w_proj_ref.1) | copy-start | bytes 7864324
  77.5 29.7 %copy-start.8 = (bf16[3,1280,320]{1,2,0:T(8,128)(2,1)S(1)}, bf16[3,1280,320]{1,2,0:T(8,128)(2,1)}, u32[]{:S(2)}) copy-start(bf16[3,1280,320]{1,2,0:T(8,128)(2,1)} %param.17) | copy-start | bytes 7372804
  83.1 7.7 %collective-permute-start.13 = (bf16[80,1280]{1,0:T(8,128)(2,1)S(1)}, bf16[80,1280]{1,0:T(8,128)(2,1)S(1)}, u32[]{:S(2)}, u32[]{:S(2)}) collective-permute-start(bf16[80,1280]{1,0:T(8,128)(2,1)S(1)} %get-tuple-element.26), channel_id=1, source_target_pairs={{0,1},{1,2},{2,3},{3,0},{4,5},{5,6},{6,7},{7,4},{8,9},{9,10},{10,1... | collective-permute-start | bytes 614408 | tf_op jit(solution)/shard_map/ppermute | solution.py:21
  84.6 11.8 %collective-permute-start.14 = (bf16[80,1280]{1,0:T(8,128)(2,1)S(1)}, bf16[80,1280]{1,0:T(8,128)(2,1)S(1)}, u32[]{:S(2)}, u32[]{:S(2)}) collective-permute-start(bf16[80,1280]{1,0:T(8,128)(2,1)S(1)} %get-tuple-element.27), channel_id=1, source_target_pairs={{0,2},{1,3},{2,0},{3,1},{4,6},{5,7},{6,4},{7,5},{8,10},{9,11},{10,... | collective-permute-start | bytes 614408 | tf_op jit(solution)/shard_map/ppermute | solution.py:21
  87.0 9.4 %collective-permute-start.15 = (bf16[80,1280]{1,0:T(8,128)(2,1)S(1)}, bf16[80,1280]{1,0:T(8,128)(2,1)S(1)}, u32[]{:S(2)}, u32[]{:S(2)}) collective-permute-start(bf16[80,1280]{1,0:T(8,128)(2,1)S(1)} %get-tuple-element.28), channel_id=1, source_target_pairs={{0,3},{1,0},{2,1},{3,2},{4,7},{5,4},{6,5},{7,6},{8,11},{9,8},{10,9... | collective-permute-start | bytes 614408 | tf_op jit(solution)/shard_map/ppermute | solution.py:21
  96.5 9.8 %collective-permute-start.16 = (bf16[64,1280]{1,0:T(8,128)(2,1)S(1)}, bf16[64,1280]{1,0:T(8,128)(2,1)S(1)}, u32[]{:S(2)}, u32[]{:S(2)}) collective-permute-start(bf16[64,1280]{1,0:T(8,128)(2,1)S(1)} %get-tuple-element.29.own), channel_id=1, source_target_pairs={{0,1},{1,2},{2,3},{3,0},{4,5},{5,6},{6,7},{7,4},{8,9},{9,10},{10,1... | collective-permute-start | bytes 491528 | tf_op jit(solution)/shard_map/ppermute | solution.py:21
  97.7 9.5 %collective-permute-start.17 = (bf16[64,1280]{1,0:T(8,128)(2,1)S(1)}, bf16[64,1280]{1,0:T(8,128)(2,1)S(1)}, u32[]{:S(2)}, u32[]{:S(2)}) collective-permute-start(bf16[64,1280]{1,0:T(8,128)(2,1)S(1)} %get-tuple-element.29.own), channel_id=1, source_target_pairs={{0,2},{1,3},{2,0},{3,1},{4,6},{5,7},{6,4},{7,5},{8,10},{9,11},{10,... | collective-permute-start | bytes 491528 | tf_op jit(solution)/shard_map/ppermute | solution.py:21
  100.2 7.0 %collective-permute-start.18 = (bf16[64,1280]{1,0:T(8,128)(2,1)S(1)}, bf16[64,1280]{1,0:T(8,128)(2,1)S(1)}, u32[]{:S(2)}, u32[]{:S(2)}) collective-permute-start(bf16[64,1280]{1,0:T(8,128)(2,1)S(1)} %get-tuple-element.29.own), channel_id=1, source_target_pairs={{0,3},{1,0},{2,1},{3,2},{4,7},{5,4},{6,5},{7,6},{8,11},{9,8},{10,9... | collective-permute-start | bytes 491528 | tf_op jit(solution)/shard_map/ppermute | solution.py:21
  101.0 5.3 %collective-permute-start.19 = (bf16[16,1280]{1,0:T(8,128)(2,1)S(1)}, bf16[16,1280]{1,0:T(8,128)(2,1)S(1)}, u32[]{:S(2)}, u32[]{:S(2)}) collective-permute-start(bf16[16,1280]{1,0:T(8,128)(2,1)S(1)} %get-tuple-element.30), channel_id=1, source_target_pairs={{0,4},{4,8},{8,12},{12,16},{16,20},{20,24},{24,28},{28,32},{32,36}... | collective-permute-start | bytes 122888 | tf_op jit(solution)/shard_map/ppermute | solution.py:26
  110.2 9.0 %collective-permute-start.20 = (bf16[32,4096]{1,0:T(8,128)(2,1)S(1)}, bf16[32,4096]{1,0:T(8,128)(2,1)S(1)}, u32[]{:S(2)}, u32[]{:S(2)}) collective-permute-start(bf16[32,4096]{1,0:T(8,128)(2,1)S(1)} %get-tuple-element.32), channel_id=1, source_target_pairs={{0,1},{1,2},{2,3},{3,0},{4,5},{5,6},{6,7},{7,4},{8,9},{9,10},{10,1... | collective-permute-start | bytes 786440 | tf_op jit(solution)/shard_map/ppermute | solution.py:21
  112.0 13.4 %collective-permute-start.21 = (bf16[32,4096]{1,0:T(8,128)(2,1)S(1)}, bf16[32,4096]{1,0:T(8,128)(2,1)S(1)}, u32[]{:S(2)}, u32[]{:S(2)}) collective-permute-start(bf16[32,4096]{1,0:T(8,128)(2,1)S(1)} %get-tuple-element.33), channel_id=1, source_target_pairs={{0,2},{1,3},{2,0},{3,1},{4,6},{5,7},{6,4},{7,5},{8,10},{9,11},{10,... | collective-permute-start | bytes 786440 | tf_op jit(solution)/shard_map/ppermute | solution.py:21
  114.4 11.0 %collective-permute-start.22 = (bf16[32,4096]{1,0:T(8,128)(2,1)S(1)}, bf16[32,4096]{1,0:T(8,128)(2,1)S(1)}, u32[]{:S(2)}, u32[]{:S(2)}) collective-permute-start(bf16[32,4096]{1,0:T(8,128)(2,1)S(1)} %get-tuple-element.34), channel_id=1, source_target_pairs={{0,3},{1,0},{2,1},{3,2},{4,7},{5,4},{6,5},{7,6},{8,11},{9,8},{10,9... | collective-permute-start | bytes 786440 | tf_op jit(solution)/shard_map/ppermute | solution.py:21
Sparse Core Ops, SparseCore 0:
  9.0 42.2 all-gather.1

commit v3 on v2

--- a/solution.py
+++ b/solution.py
@@ -14,6 +14,7 @@
 VMEM = pl.BlockSpec(memory_space=pltpu.VMEM)
 SMEM = pl.BlockSpec(memory_space=pltpu.SMEM)
 ANY = pl.BlockSpec(memory_space=pl.ANY)
+HBM = pl.BlockSpec(memory_space=pltpu.HBM)
 
 
 def send_tp(value, steps):
@@ -58,12 +59,26 @@
     return 0.5 * value * (1.0 + lax.erf(value * (0.5 ** 0.5)))
 
 
-def kv_kernel(ids_ref, frames_ref, gain_ref, w_ref, normed_ref, kv_ref):
+def kv_kernel(ids_ref, core_ref, tp_ref, frames_hbm, gain_ref, w_hbm, w_out_hbm,
+              core_out, tp_out, normed_ref, kv_ref, w_mine_ref,
+              frames_ref, w_ref, sems):
     rows = frames_ref.shape[0]
-    normed = layer_norm(frames_ref[...].astype(jnp.float32), gain_ref[...]).astype(jnp.bfloat16)
+    core_out[0] = core_ref[0]
+    tp_out[0] = tp_ref[0]
+    copies = [pltpu.make_async_copy(frames_hbm, frames_ref, sems.at[0])]
+    copies += [pltpu.make_async_copy(w_hbm.at[k], w_ref.at[k - 1], sems.at[k]) for k in (1, 2)]
+    half = w_mine_ref.shape[1]
+    copies.append(pltpu.make_async_copy(
+        w_out_hbm.at[:, pl.ds(pl.multiple_of(core_ref[0] * half, half), half)], w_mine_ref, sems.at[3]))
+    for copy in copies:
+        copy.start()
+    copies[0].wait()
+    normed = layer_norm(frames_ref[...].astype(jnp.float32), gain_ref[...][None]).astype(jnp.bfloat16)
     normed_ref[...] = normed
-    keys = dot_t(normed, w_ref[1]).astype(jnp.bfloat16)
-    values = dot_t(normed, w_ref[2]).astype(jnp.bfloat16)
+    copies[1].wait()
+    keys = dot_t(normed, w_ref[0]).astype(jnp.bfloat16)
+    copies[2].wait()
+    values = dot_t(normed, w_ref[1]).astype(jnp.bfloat16)
     kv_ref[:rows, :256] = keys[:, :256]
     kv_ref[:rows, 256:512] = values[:, :256]
     kv_ref[:rows, 512:576] = keys[:, 256:]
@@ -71,11 +86,12 @@
     row = lax.broadcasted_iota(jnp.int32, (IDROWS, kv_ref.shape[1]), 0)
     marks = jnp.where(row == 0, ids_ref[0] + 1, jnp.where(row == 1, ids_ref[1] + 1, 0))
     kv_ref[rows:, :] = marks.astype(jnp.float32).astype(jnp.bfloat16)
-
-
-def attend_kernel(info_ref, q_ref, *refs):
+    copies[3].wait()
+
+
+def attend_kernel(ids_ref, core_ref, q_ref, *refs):
     pieces, (out_ref, joined_ref, buf, marks, sems, mark_sems) = refs[:11], refs[11:]
-    parity = info_ref[2]
+    parity = core_ref[0]
     rows = q_ref.shape[0]
     copies = []
     for n, piece in enumerate(pieces):
@@ -102,7 +118,7 @@
     column = lax.broadcasted_iota(jnp.int32, (1, MOST * BLK), 1)
     low = lane < HEAD_DIM
     for i in range(2):
-        mine = (info_ref[i] + 1).astype(jnp.float32)
+        mine = (ids_ref[i] + 1).astype(jnp.float32)
         same = (seen == mine) & (row < 2)
         first = jnp.min(jnp.where(same, place, 99.0)).astype(jnp.int32)
         last = jnp.max(jnp.where(same, place, -1.0)).astype(jnp.int32)
@@ -145,17 +161,23 @@
     q_ref[:, :w_ref.shape[1]] = dot_t(normed_ref[...], w_ref[0]).astype(jnp.bfloat16)
 
 
-def mlp_kernel(tp_ref, att0, att1, att2, att3, w_out_ref, frames_ref, gain_ref, w_up_ref, w_down_ref,
-               resid_ref, part0, part1, part2, part3, resid_all, part_all):
+def mlp_kernel(tp_ref, core_ref, att0, att1, att2, att3, w_out_ref, *refs):
+    pieces, frames_ref, gain_ref, w_up_ref, w_down_ref = refs[:6], *refs[6:10]
+    resid_ref, part0, part1, part2, part3 = refs[10:15]
+    resid_all, part_all = refs[15:]
     tp = tp_ref[0]
-    rows, heads = att0.shape
+    rows = att0.shape[0]
     share = rows // 4
-    resid = frames_ref[...].astype(jnp.float32)
-    for k, att in enumerate((att0, att1, att2, att3)):
-        source = lax.rem(tp + 4 - k, 4)
-        resid = resid + dot(att[...], w_out_ref[pl.ds(pl.multiple_of(source * heads, heads), heads), :])
-    resid_all[...] = resid
-    normed = layer_norm(resid, gain_ref[...]).astype(jnp.bfloat16)
+    half = pieces[0].shape[1]
+    resid_all[...] = frames_ref[...].astype(jnp.float32) + dot(att0[...], w_out_ref[...])
+    for n, side in enumerate((core_ref[0], 1 - core_ref[0])):
+        columns = pl.ds(pl.multiple_of(side * half, half), half)
+        term = resid_all[:, columns]
+        for k, att in enumerate((att1, att2, att3)):
+            term = term + dot(att[...], pieces[3 * n + k][...])
+        resid_all[:, columns] = term
+    resid = resid_all[...]
+    normed = layer_norm(resid, gain_ref[...][None]).astype(jnp.bfloat16)
     hidden = gelu(dot(normed, w_up_ref[...])).astype(jnp.bfloat16)
     part_all[...] = dot(hidden, w_down_ref[...]).astype(jnp.bfloat16)
     mine = pl.ds(pl.multiple_of(tp * share, share), share)
@@ -176,9 +198,9 @@
     rim_ref[...] = total[share:].astype(jnp.bfloat16)
 
 
-def adapter_kernel(info_ref, own, got1, got2, got3, rim_ref, w_conv_ref, w_proj_ref,
+def adapter_kernel(tp_ref, ids_ref, joined_ref, own, got1, got2, got3, rim_ref, w_conv_ref, w_proj_ref,
                    lm0, lm1, lm2, lm3, rows_ref, pooled_ref):
-    tp = info_ref[0]
+    tp = tp_ref[0]
     share = own.shape[0]
     for k, piece in enumerate((own, got1, got2, got3)):
         source = lax.rem(tp + 4 - k, 4)
@@ -187,13 +209,13 @@
     count = rows.shape[0] // 2
     j = lax.broadcasted_iota(jnp.int32, (count, 2 * count), 0)
     r = lax.broadcasted_iota(jnp.int32, (count, 2 * count), 1)
-    same_block = info_ref[1] == info_ref[2]
+    same_block = ids_ref[0] == ids_ref[1]
     cut = jnp.where(same_block, -1, count // 2)
     one = lambda flag: jnp.where(flag, 1.0, 0.0).astype(jnp.bfloat16)
     pick = lambda flag, source: dot(one(flag), source).astype(jnp.bfloat16)
     even = pick(r == 2 * j, rows)
     odd = pick(r == 2 * j + 1, rows)
-    rim_first = jnp.where(info_ref[3] == 1, 0, -1)
+    rim_first = jnp.where(joined_ref[0] == 1, 0, -1)
     j_rim = lax.broadcasted_iota(jnp.int32, (count, IDROWS), 0)
     r_rim = lax.broadcasted_iota(jnp.int32, (count, IDROWS), 1)
     before = dot(one((r == 2 * j - 1) & (j != cut)), rows)
@@ -228,33 +250,33 @@
     return jax.ShapeDtypeStruct(shape, jnp.bfloat16)
 
 
-def attend(ids, normed, w_qkv, kv):
+def attend(ids, core, normed, w_qkv, kv, w_mine):
     rows = normed.shape[0]
     width = w_qkv.shape[1]
-    parity = lax.rem(lax.axis_index(SEQ), 2)
-    far_back, far_on = send_seq(kv, 4), send_seq(kv, -4)
     back, on = send_seq(kv, 2), send_seq(kv, -2)
     five = send_five(kv)
+    w_two = send_tp(w_mine, 2)
     beside = send_partner(kv)
+    whole = lambda array: pl.BlockSpec(array.shape, lambda i: (0,) * array.ndim)
     queries = pl.pallas_call(
         query_kernel,
+        grid=(1,),
         out_shape=bf16(rows, 384),
-        grid=(1,),
-        in_specs=[
-            pl.BlockSpec(normed.shape, lambda i: (0, 0)),
-            pl.BlockSpec((1,) + w_qkv.shape[1:], lambda i: (0, 0, 0)),
-        ],
+        in_specs=[whole(normed), pl.BlockSpec((1,) + w_qkv.shape[1:], lambda i: (0, 0, 0))],
         out_specs=pl.BlockSpec((rows, 384), lambda i: (0, 0)),
-        compiler_params=params(16),
+        compiler_params=params(4),
         cost_estimate=cost(2e8, 2e6),
     )(normed, w_qkv)
+    back, on, five, queries = lax.optimization_barrier((back, on, five, queries))
+    far_back, far_on = send_seq(back, 2), send_seq(on, -2)
+    w_one, w_three = send_tp(w_mine, 1), send_tp(w_mine, 3)
+    far_back, far_on, w_two = lax.optimization_barrier((far_back, far_on, w_two))
     chain = [far_back, back, kv, on, far_on]
     swapped = [send_partner(far_back), send_partner(back), beside, send_partner(on), send_partner(far_on)]
-    info = jnp.concatenate([ids, parity[None].astype(jnp.int32)])
     return pl.pallas_call(
         attend_kernel,
         out_shape=(bf16(rows, width), jax.ShapeDtypeStruct((1,), jnp.int32)),
-        in_specs=[SMEM, VMEM] + [ANY] * 11,
+        in_specs=[SMEM, SMEM, VMEM] + [ANY] * 11,
         out_specs=(VMEM, SMEM),
         scratch_shapes=[
             pltpu.VMEM((12 * rows, kv.shape[1]), jnp.bfloat16),
@@ -262,9 +284,9 @@
             pltpu.SemaphoreType.DMA((11,)),
             pltpu.SemaphoreType.DMA((11,)),
         ],
-        compiler_params=params(24),
+        compiler_params=params(14),
         cost_estimate=cost(1e9, 4e6),
-    )(info, queries, *chain, *swapped, five)
+    )(ids, core, queries, *chain, *swapped, five), [w_one, w_two, w_three]
 
 
 def exchange(parts):
@@ -279,54 +301,61 @@
     w_qkv = jnp.swapaxes(w_qkv, 1, 2)
     w_conv = jnp.swapaxes(w_conv, 1, 2)
     tp = lax.axis_index(TP).astype(jnp.int32)[None]
-    w_out_all = lax.all_gather(w_out, TP, tiled=True)
-    normed, kv = pl.pallas_call(
+    core = lax.rem(lax.axis_index(SEQ), 2).astype(jnp.int32)[None]
+    scalar = jax.ShapeDtypeStruct((1,), jnp.int32)
+    core, tp, normed, kv, w_mine = pl.pallas_call(
         kv_kernel,
-        out_shape=(bf16(rows, width), bf16(rows + IDROWS, 2 * w_qkv.shape[1])),
-        in_specs=[SMEM, VMEM, VMEM, VMEM],
-        out_specs=(VMEM, VMEM),
-        compiler_params=params(16),
+        out_shape=(scalar, scalar, bf16(rows, width), bf16(rows + IDROWS, 2 * w_qkv.shape[1]), bf16(w_out.shape[0], width // 2)),
+        in_specs=[SMEM, SMEM, SMEM, HBM, VMEM, HBM, HBM],
+        out_specs=(SMEM, SMEM, VMEM, VMEM, VMEM),
+        scratch_shapes=[
+            pltpu.VMEM((rows, width), jnp.bfloat16),
+            pltpu.VMEM((2,) + w_qkv.shape[1:], jnp.bfloat16),
+            pltpu.SemaphoreType.DMA((4,)),
+        ],
+        compiler_params=params(60),
         cost_estimate=cost(4e8, 4e6),
-    )(block_utt, frames, gain_attn[None], w_qkv)
-    attended, joined = attend(block_utt, normed, w_qkv, kv)
+    )(block_utt, core, tp, frames, gain_attn, w_qkv, w_out)
+    (attended, joined), w_mine = attend(block_utt, core, normed, w_qkv, kv, w_mine)
+    attended, *w_mine = lax.optimization_barrier((attended, *w_mine))
+    w_other = [send_partner(piece) for piece in w_mine]
     heads = exchange([attended] * 3)
 
     resid, *parts = pl.pallas_call(
         mlp_kernel,
         out_shape=[jax.ShapeDtypeStruct((share + IDROWS, width), jnp.float32)] + [bf16(share + IDROWS, width)] * 4,
-        in_specs=[SMEM] + [VMEM] * 9,
+        in_specs=[SMEM] * 2 + [VMEM] * 15,
         out_specs=[VMEM] * 5,
         scratch_shapes=[pltpu.VMEM((rows, width), jnp.float32), pltpu.VMEM((rows, width), jnp.bfloat16)],
-        compiler_params=params(32),
+        compiler_params=params(14),
         cost_estimate=cost(2.5e9, 1e7),
-    )(tp, attended, *heads, w_out_all, frames, gain_ffn[None], w_up, w_down)
+    )(tp, core, attended, *heads, w_out, *w_mine, *w_other, frames, gain_ffn, w_up, w_down)
     own, rim = pl.pallas_call(
         layer_sum_kernel,
         out_shape=[bf16(share, width), bf16(IDROWS, width)],
         in_specs=[VMEM] * 5,
         out_specs=[VMEM] * 2,
-        compiler_params=params(8),
+        compiler_params=params(4),
         cost_estimate=cost(1e6, 1e6),
     )(resid, parts[0], *exchange(parts[1:]))
     layer = exchange([own] * 3)
     rim = send_seq(rim, 1)
-    info = jnp.concatenate([tp, block_utt, joined])
     pooled_count = rows // 2
     lm = pl.pallas_call(
         adapter_kernel,
         out_shape=[bf16(pooled_count // 4, lm_width)] * 4,
-        in_specs=[SMEM] + [VMEM] * 7,
+        in_specs=[SMEM] * 3 + [VMEM] * 7,
         out_specs=[VMEM] * 4,
         scratch_shapes=[pltpu.VMEM((rows, width), jnp.bfloat16), pltpu.VMEM((pooled_count, w_conv.shape[1]), jnp.bfloat16)],
-        compiler_params=params(24),
+        compiler_params=params(10),
         cost_estimate=cost(1e9, 6e6),
-    )(info, own, *layer, rim, w_conv, w_proj)
+    )(tp, block_utt, joined, own, *layer, rim, w_conv, w_proj)
     return pl.pallas_call(
         lm_sum_kernel,
         out_shape=bf16(pooled_count // 4, lm_width),
         in_specs=[VMEM] * 4,
         out_specs=VMEM,
-        compiler_params=params(8),
+        compiler_params=params(4),
         cost_estimate=cost(1e6, 1e6),
     )(lm[0], *exchange(lm[1:]))
 

time: 134 us -> 123 us (0.918)
  between operations: 13.6 us -> 0.22 us
  local copies, waits for them, and re-layouts: 9.83 us -> 4.02 us
  starting transfers between devices: 39.3 us -> 44.1 us
  Pallas kernels: 20.1 us -> 23.4 us
    unnamed x28 -> x22, local copies, waits for them, and re-layouts: 9.12 us -> 4.02 us
    ppermute x12 -> x15, starting transfers between devices: 20.9 us -> 25.4 us  [send_tp(): lax.ppermute(value, TP, [(t, (t + steps) % count) for t in range(count)])]
    ppermute x12 -> x15, waiting for transfers between devices: 26.6 us -> 30.7 us  [send_tp(): lax.ppermute(value, TP, [(t, (t + steps) % count) for t in range(count)])]
    pallas_call x2, Pallas kernels: 3.05 us -> 5.16 us  [the longest x1 4.64 us: shards(): pl.pallas_call(kv_kernel, out_shape=(scalar, scalar, bf16(rows, width), b...]
    ppermute x5, starting transfers between devices: 15.1 us -> 13.6 us  [send_seq(): lax.ppermute(value, SEQ, [(s, s + steps) for s in range(count) if 0 <= s...]
  transfers between devices with their start and end apart: 24 -> 29, of which waited for: 14 -> 13; matrix products, arithmetic and copies ran while one was open for 1% -> 0% of each run, Pallas kernels for 8% -> 6%
where the time goes in v3:
time: 123 us; the launch traced here: 122 us
  waiting for transfers between devices  50.4 us (41%)
  starting transfers between devices  44.1 us (36%)
  Pallas kernels  23.4 us (19%)
  local copies, waits for them, and re-layouts  4.02 us (3%)
    ppermute x15, waiting for transfers between devices, send_tp(): lax.ppermute(value, TP, [(t, (t + steps) % count) for t in range(count)])  30.7 us
    ppermute x15, starting transfers between devices, send_tp(): lax.ppermute(value, TP, [(t, (t + steps) % count) for t in range(count)])  25.4 us
    ppermute x5, waiting for transfers between devices, send_seq(): lax.ppermute(value, SEQ, [(s, s + steps) for s in range(count) if 0 <= s...  19.7 us
    ppermute x5, starting transfers between devices, send_seq(): lax.ppermute(value, SEQ, [(s, s + steps) for s in range(count) if 0 <= s...  13.6 us
    pallas_call x1, Pallas kernels, attend(): pl.pallas_call(attend_kernel, out_shape=(bf16(rows, width), jax.ShapeDtyp...  7.35 us
    pallas_call x1, Pallas kernels, shards(): pl.pallas_call(mlp_kernel, out_shape=[jax.ShapeDtypeStruct((share + IDROW...  5.66 us
    pallas_call x1, Pallas kernels, shards(): pl.pallas_call(kv_kernel, out_shape=(scalar, scalar, bf16(rows, width), b...  4.64 us
    pallas_call x1, Pallas kernels, shards(): pl.pallas_call(adapter_kernel, out_shape=[bf16(pooled_count // 4, lm_widt...  4.24 us
  transfers between devices with their start and end apart: 29, of which 13 were waited for; matrix products, arithmetic and copies ran while one was open for 0% of the time, Pallas kernels for 6%

profile of v3, /device:TPU:70, one launch (start us, length us, event | category | flops | bytes accessed | tf_op | source)
XLA Modules:
  0.0 122.1 jit_solution(6475951264900515091)
XLA Ops:
  0.0 4.6 %shard_map.100 = (s32[1]{0:T(128)}, s32[1]{0:T(128)}, bf16[256,1280]{1,0:T(8,128)(2,1)}, bf16[272,640]{1,0:T(8,128)(2,1)}, bf16[320,640]{1,0:T(8,128)(2,1)}) custom-call(s32[2]{0:T(128)} %ids_ref.5, s32[1]{0:T(128)} %bitcast.core_ref, s32[1]{0:T(128)} %bitcast.1.tp_ref, bf16[256,1280]{1,0:T(8,128)(2,1)} %refs_6_.1, f32[1280]{0:T(1024)} %gain_ref.1, ...), custom_call_target="tpu_custom_call" | custom-call | flops 400000000 | bytes 4000000 | tf_op jit(solution)/shard_map/pallas_call | solution.py:306
  4.7 0.0 copy-start.10
  4.7 3.4 %collective-permute-start = (bf16[272,640]{1,0:T(8,128)(2,1)}, bf16[272,640]{1,0:T(8,128)(2,1)S(1)}, u32[]{:S(2)}, u32[]{:S(2)}) collective-permute-start(bf16[272,640]{1,0:T(8,128)(2,1)} %get-tuple-element.36.refs_2_), channel_id=1, source_target_pairs={{0,8},{4,12},{8,16},{12,20},{16,24},{20,28},{24,32},{28,36},{32,40... | collective-permute-start | bytes 1044488 | tf_op jit(solution)/shard_map/ppermute | solution.py:27
  8.1 2.4 %collective-permute-start.1 = (bf16[272,640]{1,0:T(8,128)(2,1)}, bf16[272,640]{1,0:T(8,128)(2,1)S(1)}, u32[]{:S(2)}, u32[]{:S(2)}) collective-permute-start(bf16[272,640]{1,0:T(8,128)(2,1)} %get-tuple-element.36.refs_2_), channel_id=1, source_target_pairs={{8,0},{12,4},{16,8},{20,12},{24,16},{28,20},{32,24},{36,28},{40,32... | collective-permute-start | bytes 1044488 | tf_op jit(solution)/shard_map/ppermute | solution.py:27
  10.5 3.4 %collective-permute-start.2 = (bf16[272,640]{1,0:T(8,128)(2,1)}, bf16[272,640]{1,0:T(8,128)(2,1)S(1)}, u32[]{:S(2)}, u32[]{:S(2)}) collective-permute-start(bf16[272,640]{1,0:T(8,128)(2,1)} %get-tuple-element.36.refs_2_), channel_id=1, source_target_pairs={{4,24},{12,32},{20,40},{24,4},{28,48},{32,12},{36,56},{40,20},{44,... | collective-permute-start | bytes 1044488 | tf_op jit(solution)/shard_map/ppermute | solution.py:40
  13.9 3.3 %collective-permute-start.5 = (bf16[320,640]{1,0:T(8,128)(2,1)}, bf16[320,640]{1,0:T(8,128)(2,1)S(1)}, u32[]{:S(2)}, u32[]{:S(2)}) collective-permute-start(bf16[320,640]{1,0:T(8,128)(2,1)} %get-tuple-element.41), channel_id=1, source_target_pairs={{0,2},{1,3},{2,0},{3,1},{4,6},{5,7},{6,4},{7,5},{8,10},{9,11},{10,... | collective-permute-start | bytes 1228808 | tf_op jit(solution)/shard_map/ppermute | solution.py:22
  17.2 1.1 copy-done.7
  18.3 0.5 shard_map.101.q_ref
  18.8 0.0 copy-start.1
  18.8 0.0 copy-start.4
  18.8 0.0 collective-permute-done.refs_1_
  18.8 6.3 %collective-permute-done.1.refs_3_ = bf16[272,640]{1,0:T(8,128)(2,1)S(1)} collective-permute-done((bf16[272,640]{1,0:T(8,128)(2,1)}, bf16[272,640]{1,0:T(8,128)(2,1)S(1)}, u32[]{:S(2)}, u32[]{:S(2)}) %collective-permute-start.1) | collective-permute-done | bytes 348192 | tf_op jit(solution)/shard_map/ppermute | solution.py:27
  25.2 0.0 collective-permute-done.2.refs_10_
  25.2 1.9 %collective-permute-start.3 = (bf16[272,640]{1,0:T(8,128)(2,1)S(1)}, bf16[272,640]{1,0:T(8,128)(2,1)S(1)}, u32[]{:S(2)}, u32[]{:S(2)}) collective-permute-start(bf16[272,640]{1,0:T(8,128)(2,1)S(1)} %collective-permute-done.refs_1_), channel_id=1, source_target_pairs={{0,8},{4,12},{8,16},{12,20},{16,24},{20,28},{24,32},{28,36},{32,40... | collective-permute-start | bytes 1044488 | tf_op jit(solution)/shard_map/ppermute | solution.py:27
  27.1 3.9 %collective-permute-start.4 = (bf16[272,640]{1,0:T(8,128)(2,1)S(1)}, bf16[272,640]{1,0:T(8,128)(2,1)S(1)}, u32[]{:S(2)}, u32[]{:S(2)}) collective-permute-start(bf16[272,640]{1,0:T(8,128)(2,1)S(1)} %collective-permute-done.1.refs_3_), channel_id=1, source_target_pairs={{8,0},{12,4},{16,8},{20,12},{24,16},{28,20},{32,24},{36,28},{40,32... | collective-permute-start | bytes 1044488 | tf_op jit(solution)/shard_map/ppermute | solution.py:27
  31.0 0.1 collective-permute-start.8
  31.1 0.5 collective-permute-start.7
  31.6 0.1 collective-permute-start.9
  31.7 5.7 %collective-permute-done.3.refs_0_ = bf16[272,640]{1,0:T(8,128)(2,1)S(1)} collective-permute-done((bf16[272,640]{1,0:T(8,128)(2,1)S(1)}, bf16[272,640]{1,0:T(8,128)(2,1)S(1)}, u32[]{:S(2)}, u32[]{:S(2)}) %collective-permute-start.3) | collective-permute-done | bytes 348192 | tf_op jit(solution)/shard_map/ppermute | solution.py:27
  37.4 4.2 %collective-permute-done.4.refs_4_ = bf16[272,640]{1,0:T(8,128)(2,1)S(1)} collective-permute-done((bf16[272,640]{1,0:T(8,128)(2,1)S(1)}, bf16[272,640]{1,0:T(8,128)(2,1)S(1)}, u32[]{:S(2)}, u32[]{:S(2)}) %collective-permute-start.4) | collective-permute-done | bytes 348192 | tf_op jit(solution)/shard_map/ppermute | solution.py:27
  41.7 0.5 collective-permute-start.10
  42.2 0.0 collective-permute-done.8.refs_7_
  42.2 1.6 %collective-permute-start.11 = (bf16[320,640]{1,0:T(8,128)(2,1)}, bf16[320,640]{1,0:T(8,128)(2,1)S(1)}, u32[]{:S(2)}, u32[]{:S(2)}) collective-permute-start(bf16[320,640]{1,0:T(8,128)(2,1)} %get-tuple-element.41), channel_id=1, source_target_pairs={{0,1},{1,2},{2,3},{3,0},{4,5},{5,6},{6,7},{7,4},{8,9},{9,10},{10,1... | collective-permute-start | bytes 1228808 | tf_op jit(solution)/shard_map/ppermute | solution.py:22
  43.7 0.0 collective-permute-done.7.refs_6_
  43.7 1.7 %collective-permute-start.12 = (bf16[320,640]{1,0:T(8,128)(2,1)}, bf16[320,640]{1,0:T(8,128)(2,1)S(1)}, u32[]{:S(2)}, u32[]{:S(2)}) collective-permute-start(bf16[320,640]{1,0:T(8,128)(2,1)} %get-tuple-element.41), channel_id=1, source_target_pairs={{0,3},{1,0},{2,1},{3,2},{4,7},{5,4},{6,5},{7,6},{8,11},{9,8},{10,9... | collective-permute-start | bytes 1228808 | tf_op jit(solution)/shard_map/ppermute | solution.py:22
  45.4 0.0 collective-permute-done.9.refs_8_
  45.4 1.0 copy-done.8
  46.4 7.3 %shard_map.102 = (bf16[256,320]{1,0:T(8,128)(2,1)S(1)}, s32[1]{0:T(128)}) custom-call(s32[2]{0:T(128)S(1)} %copy-done.10, s32[1]{0:T(128)} %get-tuple-element.35.core_ref, bf16[256,384]{1,0:T(8,128)(2,1)S(1)} %shard_map.101.q_ref, bf16[272,640]{1,0:T(8,128)(2,1)S(1)} %collective-permute-done.3.refs_0_, bf16[272,640]{1,0:T(8,128)(2,1)S(1)} %collective-permute-done.refs_1_, ...), custom_call_target="tpu_custom_call" | custom-call | flops 1000000000 | bytes 4000000 | tf_op jit(solution)/shard_map/pallas_call | solution.py:276
  53.8 1.3 %collective-permute-done.11.refs_0_ = bf16[320,640]{1,0:T(8,128)(2,1)S(1)} collective-permute-done((bf16[320,640]{1,0:T(8,128)(2,1)}, bf16[320,640]{1,0:T(8,128)(2,1)S(1)}, u32[]{:S(2)}, u32[]{:S(2)}) %collective-permute-start.11) | collective-permute-done | bytes 409632 | tf_op jit(solution)/shard_map/ppermute | solution.py:22
  55.0 0.0 collective-permute-done.12.refs_2_
  55.0 0.0 collective-permute-start.16
  55.1 0.5 collective-permute-start.17
  55.6 0.0 collective-permute-start.18
  55.6 1.6 %collective-permute-start.13 = (bf16[256,320]{1,0:T(8,128)(2,1)S(1)}, bf16[256,320]{1,0:T(8,128)(2,1)S(1)}, u32[]{:S(2)}, u32[]{:S(2)}) collective-permute-start(bf16[256,320]{1,0:T(8,128)(2,1)S(1)} %get-tuple-element.48.att0), channel_id=1, source_target_pairs={{0,1},{1,2},{2,3},{3,0},{4,5},{5,6},{6,7},{7,4},{8,9},{9,10},{10,1... | collective-permute-start | bytes 491528 | tf_op jit(solution)/shard_map/ppermute | solution.py:22
  57.1 2.9 %collective-permute-start.14 = (bf16[256,320]{1,0:T(8,128)(2,1)S(1)}, bf16[256,320]{1,0:T(8,128)(2,1)S(1)}, u32[]{:S(2)}, u32[]{:S(2)}) collective-permute-start(bf16[256,320]{1,0:T(8,128)(2,1)S(1)} %get-tuple-element.48.att0), channel_id=1, source_target_pairs={{0,2},{1,3},{2,0},{3,1},{4,6},{5,7},{6,4},{7,5},{8,10},{9,11},{10,... | collective-permute-start | bytes 491528 | tf_op jit(solution)/shard_map/ppermute | solution.py:22
  60.0 4.1 %collective-permute-done.13.att1 = bf16[256,320]{1,0:T(8,128)(2,1)S(1)} collective-permute-done((bf16[256,320]{1,0:T(8,128)(2,1)S(1)}, bf16[256,320]{1,0:T(8,128)(2,1)S(1)}, u32[]{:S(2)}, u32[]{:S(2)}) %collective-permute-start.13) | collective-permute-done | bytes 163872 | tf_op jit(solution)/shard_map/ppermute | solution.py:22
  64.1 2.1 %collective-permute-start.15 = (bf16[256,320]{1,0:T(8,128)(2,1)S(1)}, bf16[256,320]{1,0:T(8,128)(2,1)S(1)}, u32[]{:S(2)}, u32[]{:S(2)}) collective-permute-start(bf16[256,320]{1,0:T(8,128)(2,1)S(1)} %get-tuple-element.48.att0), channel_id=1, source_target_pairs={{0,3},{1,0},{2,1},{3,2},{4,7},{5,4},{6,5},{7,6},{8,11},{9,8},{10,9... | collective-permute-start | bytes 491528 | tf_op jit(solution)/shard_map/ppermute | solution.py:22
  66.3 3.3 %collective-permute-done.14.att2 = bf16[256,320]{1,0:T(8,128)(2,1)S(1)} collective-permute-done((bf16[256,320]{1,0:T(8,128)(2,1)S(1)}, bf16[256,320]{1,0:T(8,128)(2,1)S(1)}, u32[]{:S(2)}, u32[]{:S(2)}) %collective-permute-start.14) | collective-permute-done | bytes 163872 | tf_op jit(solution)/shard_map/ppermute | solution.py:22
  69.5 1.2 collective-permute-done.15.att3
  70.8 0.0 collective-permute-done.16.refs_3_
  70.8 0.0 collective-permute-done.17.refs_4_
  70.8 0.0 copy-start.3
  70.8 1.9 %copy-done.3 = bf16[1280,1280]{1,0:T(8,128)(2,1)S(1)} copy-done((bf16[1280,1280]{1,0:T(8,128)(2,1)S(1)}, bf16[1280,1280]{1,0:T(8,128)(2,1)}, u32[]{:S(2)}) %copy-start.3) | copy-done | bytes 3276824
  72.7 5.7 %shard_map.103 = (f32[80,1280]{1,0:T(8,128)S(1)}, bf16[80,1280]{1,0:T(8,128)(2,1)S(1)}, bf16[80,1280]{1,0:T(8,128)(2,1)S(1)}, bf16[80,1280]{1,0:T(8,128)(2,1)S(1)}, bf16[80,1280]{1,0:T(8,128)(2,1)S(1)}) custom-call(s32[1]{0:T(128)} %get-tuple-element.34.tp_ref, s32[1]{0:T(128)} %get-tuple-element.35.core_ref, bf16[256,320]{1,0:T(8,128)(2,1)S(1)} %get-tuple-element.48.att0, ...), custom_call_target="tpu_custom_call" | custom-call | flops 2500000000 | bytes 10000000 | tf_op jit(solution)/shard_map/pallas_call | solution.py:324
  78.4 0.5 collective-permute-start.19
  78.9 3.9 %collective-permute-start.20 = (bf16[80,1280]{1,0:T(8,128)(2,1)S(1)}, bf16[80,1280]{1,0:T(8,128)(2,1)S(1)}, u32[]{:S(2)}, u32[]{:S(2)}) collective-permute-start(bf16[80,1280]{1,0:T(8,128)(2,1)S(1)} %get-tuple-element.55), channel_id=1, source_target_pairs={{0,2},{1,3},{2,0},{3,1},{4,6},{5,7},{6,4},{7,5},{8,10},{9,11},{10,... | collective-permute-start | bytes 614408 | tf_op jit(solution)/shard_map/ppermute | solution.py:22
  82.8 0.0 collective-permute-start.21
  82.8 4.7 %collective-permute-done.19.got1 = bf16[80,1280]{1,0:T(8,128)(2,1)S(1)} collective-permute-done((bf16[80,1280]{1,0:T(8,128)(2,1)S(1)}, bf16[80,1280]{1,0:T(8,128)(2,1)S(1)}, u32[]{:S(2)}, u32[]{:S(2)}) %collective-permute-start.19) | collective-permute-done | bytes 204832 | tf_op jit(solution)/shard_map/ppermute | solution.py:22
  87.6 3.0 %collective-permute-done.20.got2 = bf16[80,1280]{1,0:T(8,128)(2,1)S(1)} collective-permute-done((bf16[80,1280]{1,0:T(8,128)(2,1)S(1)}, bf16[80,1280]{1,0:T(8,128)(2,1)S(1)}, u32[]{:S(2)}, u32[]{:S(2)}) %collective-permute-start.20) | collective-permute-done | bytes 204832 | tf_op jit(solution)/shard_map/ppermute | solution.py:22
  90.6 0.0 collective-permute-done.21.got3
  90.6 0.1 shard_map.104
  90.7 0.7 collective-permute-start.22
  91.4 3.5 %collective-permute-start.23 = (bf16[64,1280]{1,0:T(8,128)(2,1)S(1)}, bf16[64,1280]{1,0:T(8,128)(2,1)S(1)}, u32[]{:S(2)}, u32[]{:S(2)}) collective-permute-start(bf16[64,1280]{1,0:T(8,128)(2,1)S(1)} %get-tuple-element.57.own), channel_id=1, source_target_pairs={{0,2},{1,3},{2,0},{3,1},{4,6},{5,7},{6,4},{7,5},{8,10},{9,11},{10,... | collective-permute-start | bytes 491528 | tf_op jit(solution)/shard_map/ppermute | solution.py:22
  94.9 0.0 collective-permute-start.24
  94.9 1.9 %collective-permute-start.25 = (bf16[16,1280]{1,0:T(8,128)(2,1)S(1)}, bf16[16,1280]{1,0:T(8,128)(2,1)S(1)}, u32[]{:S(2)}, u32[]{:S(2)}) collective-permute-start(bf16[16,1280]{1,0:T(8,128)(2,1)S(1)} %get-tuple-element.58), channel_id=1, source_target_pairs={{0,4},{4,8},{8,12},{12,16},{16,20},{20,24},{24,28},{28,32},{32,36}... | collective-permute-start | bytes 122888 | tf_op jit(solution)/shard_map/ppermute | solution.py:27
  96.8 3.4 %collective-permute-done.25.rim_ref = bf16[16,1280]{1,0:T(8,128)(2,1)S(1)} collective-permute-done((bf16[16,1280]{1,0:T(8,128)(2,1)S(1)}, bf16[16,1280]{1,0:T(8,128)(2,1)S(1)}, u32[]{:S(2)}, u32[]{:S(2)}) %collective-permute-start.25) | collective-permute-done | bytes 40992 | tf_op jit(solution)/shard_map/ppermute | solution.py:27
  100.2 0.0 collective-permute-done.22.got1
  100.2 1.7 %collective-permute-done.23.got2 = bf16[64,1280]{1,0:T(8,128)(2,1)S(1)} collective-permute-done((bf16[64,1280]{1,0:T(8,128)(2,1)S(1)}, bf16[64,1280]{1,0:T(8,128)(2,1)S(1)}, u32[]{:S(2)}, u32[]{:S(2)}) %collective-permute-start.23) | collective-permute-done | bytes 163872 | tf_op jit(solution)/shard_map/ppermute | solution.py:22
  102.0 4.2 %shard_map.105 = (bf16[32,4096]{1,0:T(8,128)(2,1)S(1)}, bf16[32,4096]{1,0:T(8,128)(2,1)S(1)}, bf16[32,4096]{1,0:T(8,128)(2,1)S(1)}, bf16[32,4096]{1,0:T(8,128)(2,1)S(1)}) custom-call(s32[1]{0:T(128)} %get-tuple-element.34.tp_ref, s32[2]{0:T(128)S(1)} %copy-done.10, s32[1]{0:T(128)} %get-tuple-element.45.joined_ref, ...), custom_call_target="tpu_custom_call" | custom-call | flops 1000000000 | bytes 6000000 | tf_op jit(solution)/shard_map/pallas_call | solution.py:344
  106.2 0.4 collective-permute-start.26
  106.6 3.3 %collective-permute-start.27 = (bf16[32,4096]{1,0:T(8,128)(2,1)S(1)}, bf16[32,4096]{1,0:T(8,128)(2,1)S(1)}, u32[]{:S(2)}, u32[]{:S(2)}) collective-permute-start(bf16[32,4096]{1,0:T(8,128)(2,1)S(1)} %get-tuple-element.61), channel_id=1, source_target_pairs={{0,2},{1,3},{2,0},{3,1},{4,6},{5,7},{6,4},{7,5},{8,10},{9,11},{10,... | collective-permute-start | bytes 786440 | tf_op jit(solution)/shard_map/ppermute | solution.py:22
  109.9 4.8 %collective-permute-done.26.got1 = bf16[32,4096]{1,0:T(8,128)(2,1)S(1)} collective-permute-done((bf16[32,4096]{1,0:T(8,128)(2,1)S(1)}, bf16[32,4096]{1,0:T(8,128)(2,1)S(1)}, u32[]{:S(2)}, u32[]{:S(2)}) %collective-permute-start.26) | collective-permute-done | bytes 262176 | tf_op jit(solution)/shard_map/ppermute | solution.py:22
  114.8 6.5 %collective-permute-done.27.got2 = bf16[32,4096]{1,0:T(8,128)(2,1)S(1)} collective-permute-done((bf16[32,4096]{1,0:T(8,128)(2,1)S(1)}, bf16[32,4096]{1,0:T(8,128)(2,1)S(1)}, u32[]{:S(2)}, u32[]{:S(2)}) %collective-permute-start.27) | collective-permute-done | bytes 262176 | tf_op jit(solution)/shard_map/ppermute | solution.py:22
  121.2 0.8 shard_map.106
  (23 shorter events, 0.0 us)
Async XLA Ops:
  0.0 17.2 %copy-start = (bf16[3,1280,320]{1,2,0:T(8,128)(2,1)S(1)}, bf16[3,1280,320]{1,2,0:T(8,128)(2,1)}, u32[]{:S(2)}) copy-start(bf16[3,1280,320]{1,2,0:T(8,128)(2,1)} %param.12) | copy-start | bytes 7372804
  4.7 40.8 %copy-start.10 = (s32[2]{0:T(128)S(1)}, s32[2]{0:T(128)}, u32[]{:S(2)}) copy-start(s32[2]{0:T(128)} %ids_ref.5) | copy-start | bytes 28
  4.7 14.2 %collective-permute-start = (bf16[272,640]{1,0:T(8,128)(2,1)}, bf16[272,640]{1,0:T(8,128)(2,1)S(1)}, u32[]{:S(2)}, u32[]{:S(2)}) collective-permute-start(bf16[272,640]{1,0:T(8,128)(2,1)} %get-tuple-element.36.refs_2_), channel_id=1, source_target_pairs={{0,8},{4,12},{8,16},{12,20},{16,24},{20,28},{24,32},{28,36},{32,40... | collective-permute-start | bytes 1044488 | tf_op jit(solution)/shard_map/ppermute | solution.py:27
  8.1 17.1 %collective-permute-start.1 = (bf16[272,640]{1,0:T(8,128)(2,1)}, bf16[272,640]{1,0:T(8,128)(2,1)S(1)}, u32[]{:S(2)}, u32[]{:S(2)}) collective-permute-start(bf16[272,640]{1,0:T(8,128)(2,1)} %get-tuple-element.36.refs_2_), channel_id=1, source_target_pairs={{8,0},{12,4},{16,8},{20,12},{24,16},{28,20},{32,24},{36,28},{40,32... | collective-permute-start | bytes 1044488 | tf_op jit(solution)/shard_map/ppermute | solution.py:27
  10.5 14.7 %collective-permute-start.2 = (bf16[272,640]{1,0:T(8,128)(2,1)}, bf16[272,640]{1,0:T(8,128)(2,1)S(1)}, u32[]{:S(2)}, u32[]{:S(2)}) collective-permute-start(bf16[272,640]{1,0:T(8,128)(2,1)} %get-tuple-element.36.refs_2_), channel_id=1, source_target_pairs={{4,24},{12,32},{20,40},{24,4},{28,48},{32,12},{36,56},{40,20},{44,... | collective-permute-start | bytes 1044488 | tf_op jit(solution)/shard_map/ppermute | solution.py:40
  13.9 17.7 %collective-permute-start.5 = (bf16[320,640]{1,0:T(8,128)(2,1)}, bf16[320,640]{1,0:T(8,128)(2,1)S(1)}, u32[]{:S(2)}, u32[]{:S(2)}) collective-permute-start(bf16[320,640]{1,0:T(8,128)(2,1)} %get-tuple-element.41), channel_id=1, source_target_pairs={{0,2},{1,3},{2,0},{3,1},{4,6},{5,7},{6,4},{7,5},{8,10},{9,11},{10,... | collective-permute-start | bytes 1228808 | tf_op jit(solution)/shard_map/ppermute | solution.py:22
  17.2 1.1 copy-start.7
  18.3 52.5 %copy-start.2 = (bf16[1280,1280]{1,0:T(8,128)(2,1)S(1)}, bf16[1280,1280]{1,0:T(8,128)(2,1)}, u32[]{:S(2)}) copy-start(bf16[1280,1280]{1,0:T(8,128)(2,1)} %refs_8_.1) | copy-start | bytes 9830404
  18.3 52.5 %copy-start.9 = (f32[1280]{0:T(1024)S(1)}, f32[1280]{0:T(1024)}, u32[]{:S(2)}) copy-start(f32[1280]{0:T(1024)} %refs_7_.1) | copy-start | bytes 15364
  18.8 52.0 %copy-start.1 = (bf16[320,1280]{1,0:T(8,128)(2,1)S(1)}, bf16[320,1280]{1,0:T(8,128)(2,1)}, u32[]{:S(2)}) copy-start(bf16[320,1280]{1,0:T(8,128)(2,1)} %w_out_ref.1) | copy-start | bytes 2457604
  18.8 52.0 %copy-start.4 = (bf16[256,1280]{1,0:T(8,128)(2,1)S(1)}, bf16[256,1280]{1,0:T(8,128)(2,1)}, u32[]{:S(2)}) copy-start(bf16[256,1280]{1,0:T(8,128)(2,1)} %refs_6_.1) | copy-start | bytes 1966084
  25.2 12.3 %collective-permute-start.3 = (bf16[272,640]{1,0:T(8,128)(2,1)S(1)}, bf16[272,640]{1,0:T(8,128)(2,1)S(1)}, u32[]{:S(2)}, u32[]{:S(2)}) collective-permute-start(bf16[272,640]{1,0:T(8,128)(2,1)S(1)} %collective-permute-done.refs_1_), channel_id=1, source_target_pairs={{0,8},{4,12},{8,16},{12,20},{16,24},{20,28},{24,32},{28,36},{32,40... | collective-permute-start | bytes 1044488 | tf_op jit(solution)/shard_map/ppermute | solution.py:27
  27.1 14.6 %collective-permute-start.4 = (bf16[272,640]{1,0:T(8,128)(2,1)S(1)}, bf16[272,640]{1,0:T(8,128)(2,1)S(1)}, u32[]{:S(2)}, u32[]{:S(2)}) collective-permute-start(bf16[272,640]{1,0:T(8,128)(2,1)S(1)} %collective-permute-done.1.refs_3_), channel_id=1, source_target_pairs={{8,0},{12,4},{16,8},{20,12},{24,16},{28,20},{32,24},{36,28},{40,32... | collective-permute-start | bytes 1044488 | tf_op jit(solution)/shard_map/ppermute | solution.py:27
  31.0 11.1 %collective-permute-start.8 = (bf16[272,640]{1,0:T(8,128)(2,1)}, bf16[272,640]{1,0:T(8,128)(2,1)S(1)}, u32[]{:S(2)}, u32[]{:S(2)}) collective-permute-start(bf16[272,640]{1,0:T(8,128)(2,1)} %get-tuple-element.36.refs_2_), channel_id=1, source_target_pairs={{0,4},{4,0},{8,12},{12,8},{16,20},{20,16},{24,28},{28,24},{32,36},... | collective-permute-start | bytes 1044488 | tf_op jit(solution)/shard_map/ppermute | solution.py:34
  31.1 12.6 %collective-permute-start.7 = (bf16[272,640]{1,0:T(8,128)(2,1)S(1)}, bf16[272,640]{1,0:T(8,128)(2,1)S(1)}, u32[]{:S(2)}, u32[]{:S(2)}) collective-permute-start(bf16[272,640]{1,0:T(8,128)(2,1)S(1)} %collective-permute-done.refs_1_), channel_id=1, source_target_pairs={{0,4},{4,0},{8,12},{12,8},{16,20},{20,16},{24,28},{28,24},{32,36},... | collective-permute-start | bytes 1044488 | tf_op jit(solution)/shard_map/ppermute | solution.py:34
  31.6 13.8 %collective-permute-start.9 = (bf16[272,640]{1,0:T(8,128)(2,1)S(1)}, bf16[272,640]{1,0:T(8,128)(2,1)S(1)}, u32[]{:S(2)}, u32[]{:S(2)}) collective-permute-start(bf16[272,640]{1,0:T(8,128)(2,1)S(1)} %collective-permute-done.1.refs_3_), channel_id=1, source_target_pairs={{0,4},{4,0},{8,12},{12,8},{16,20},{20,16},{24,28},{28,24},{32,36},... | collective-permute-start | bytes 1044488 | tf_op jit(solution)/shard_map/ppermute | solution.py:34
  41.6 3.8 %collective-permute-start.6 = (bf16[272,640]{1,0:T(8,128)(2,1)S(1)}, bf16[272,640]{1,0:T(8,128)(2,1)S(1)}, u32[]{:S(2)}, u32[]{:S(2)}) collective-permute-start(bf16[272,640]{1,0:T(8,128)(2,1)S(1)} %collective-permute-done.3.refs_0_), channel_id=1, source_target_pairs={{0,4},{4,0},{8,12},{12,8},{16,20},{20,16},{24,28},{28,24},{32,36},... | collective-permute-start | bytes 1044488 | tf_op jit(solution)/shard_map/ppermute | solution.py:34
  41.7 3.8 %collective-permute-start.10 = (bf16[272,640]{1,0:T(8,128)(2,1)S(1)}, bf16[272,640]{1,0:T(8,128)(2,1)S(1)}, u32[]{:S(2)}, u32[]{:S(2)}) collective-permute-start(bf16[272,640]{1,0:T(8,128)(2,1)S(1)} %collective-permute-done.4.refs_4_), channel_id=1, source_target_pairs={{0,4},{4,0},{8,12},{12,8},{16,20},{20,16},{24,28},{28,24},{32,36},... | collective-permute-start | bytes 1044488 | tf_op jit(solution)/shard_map/ppermute | solution.py:34
  42.2 12.9 %collective-permute-start.11 = (bf16[320,640]{1,0:T(8,128)(2,1)}, bf16[320,640]{1,0:T(8,128)(2,1)S(1)}, u32[]{:S(2)}, u32[]{:S(2)}) collective-permute-start(bf16[320,640]{1,0:T(8,128)(2,1)} %get-tuple-element.41), channel_id=1, source_target_pairs={{0,1},{1,2},{2,3},{3,0},{4,5},{5,6},{6,7},{7,4},{8,9},{9,10},{10,1... | collective-permute-start | bytes 1228808 | tf_op jit(solution)/shard_map/ppermute | solution.py:22
  43.7 11.3 %collective-permute-start.12 = (bf16[320,640]{1,0:T(8,128)(2,1)}, bf16[320,640]{1,0:T(8,128)(2,1)S(1)}, u32[]{:S(2)}, u32[]{:S(2)}) collective-permute-start(bf16[320,640]{1,0:T(8,128)(2,1)} %get-tuple-element.41), channel_id=1, source_target_pairs={{0,3},{1,0},{2,1},{3,2},{4,7},{5,4},{6,5},{7,6},{8,11},{9,8},{10,9... | collective-permute-start | bytes 1228808 | tf_op jit(solution)/shard_map/ppermute | solution.py:22
  45.4 1.0 copy-start.8
  55.0 15.7 %collective-permute-start.16 = (bf16[320,640]{1,0:T(8,128)(2,1)S(1)}, bf16[320,640]{1,0:T(8,128)(2,1)S(1)}, u32[]{:S(2)}, u32[]{:S(2)}) collective-permute-start(bf16[320,640]{1,0:T(8,128)(2,1)S(1)} %collective-permute-done.11.refs_0_), channel_id=1, source_target_pairs={{0,4},{4,0},{8,12},{12,8},{16,20},{20,16},{24,28},{28,24},{32,36},... | collective-permute-start | bytes 1228808 | tf_op jit(solution)/shard_map/ppermute | solution.py:34
  55.1 15.7 %collective-permute-start.17 = (bf16[320,640]{1,0:T(8,128)(2,1)S(1)}, bf16[320,640]{1,0:T(8,128)(2,1)S(1)}, u32[]{:S(2)}, u32[]{:S(2)}) collective-permute-start(bf16[320,640]{1,0:T(8,128)(2,1)S(1)} %collective-permute-done.5.refs_1_), channel_id=1, source_target_pairs={{0,4},{4,0},{8,12},{12,8},{16,20},{20,16},{24,28},{28,24},{32,36},... | collective-permute-start | bytes 1228808 | tf_op jit(solution)/shard_map/ppermute | solution.py:34
  55.6 15.2 %collective-permute-start.18 = (bf16[320,640]{1,0:T(8,128)(2,1)S(1)}, bf16[320,640]{1,0:T(8,128)(2,1)S(1)}, u32[]{:S(2)}, u32[]{:S(2)}) collective-permute-start(bf16[320,640]{1,0:T(8,128)(2,1)S(1)} %collective-permute-done.12.refs_2_), channel_id=1, source_target_pairs={{0,4},{4,0},{8,12},{12,8},{16,20},{20,16},{24,28},{28,24},{32,36},... | collective-permute-start | bytes 1228808 | tf_op jit(solution)/shard_map/ppermute | solution.py:34
  55.6 8.6 %collective-permute-start.13 = (bf16[256,320]{1,0:T(8,128)(2,1)S(1)}, bf16[256,320]{1,0:T(8,128)(2,1)S(1)}, u32[]{:S(2)}, u32[]{:S(2)}) collective-permute-start(bf16[256,320]{1,0:T(8,128)(2,1)S(1)} %get-tuple-element.48.att0), channel_id=1, source_target_pairs={{0,1},{1,2},{2,3},{3,0},{4,5},{5,6},{6,7},{7,4},{8,9},{9,10},{10,1... | collective-permute-start | bytes 491528 | tf_op jit(solution)/shard_map/ppermute | solution.py:22
  57.1 12.4 %collective-permute-start.14 = (bf16[256,320]{1,0:T(8,128)(2,1)S(1)}, bf16[256,320]{1,0:T(8,128)(2,1)S(1)}, u32[]{:S(2)}, u32[]{:S(2)}) collective-permute-start(bf16[256,320]{1,0:T(8,128)(2,1)S(1)} %get-tuple-element.48.att0), channel_id=1, source_target_pairs={{0,2},{1,3},{2,0},{3,1},{4,6},{5,7},{6,4},{7,5},{8,10},{9,11},{10,... | collective-permute-start | bytes 491528 | tf_op jit(solution)/shard_map/ppermute | solution.py:22
  64.1 6.6 %collective-permute-start.15 = (bf16[256,320]{1,0:T(8,128)(2,1)S(1)}, bf16[256,320]{1,0:T(8,128)(2,1)S(1)}, u32[]{:S(2)}, u32[]{:S(2)}) collective-permute-start(bf16[256,320]{1,0:T(8,128)(2,1)S(1)} %get-tuple-element.48.att0), channel_id=1, source_target_pairs={{0,3},{1,0},{2,1},{3,2},{4,7},{5,4},{6,5},{7,6},{8,11},{9,8},{10,9... | collective-permute-start | bytes 491528 | tf_op jit(solution)/shard_map/ppermute | solution.py:22
  70.8 1.9 %copy-start.3 = (bf16[1280,1280]{1,0:T(8,128)(2,1)S(1)}, bf16[1280,1280]{1,0:T(8,128)(2,1)}, u32[]{:S(2)}) copy-start(bf16[1280,1280]{1,0:T(8,128)(2,1)} %refs_9_.1) | copy-start | bytes 9830404
  72.7 29.2 %copy-start.5 = (bf16[320,4096]{1,0:T(8,128)(2,1)S(1)}, bf16[320,4096]{1,0:T(8,128)(2,1)}, u32[]{:S(2)}) copy-start(bf16[320,4096]{1,0:T(8,128)(2,1)} %w_proj_ref.1) | copy-start | bytes 7864324
  72.7 29.2 %copy-start.6 = (bf16[3,1280,320]{1,2,0:T(8,128)(2,1)S(1)}, bf16[3,1280,320]{1,2,0:T(8,128)(2,1)}, u32[]{:S(2)}) copy-start(bf16[3,1280,320]{1,2,0:T(8,128)(2,1)} %param.17) | copy-start | bytes 7372804
  78.4 9.2 %collective-permute-start.19 = (bf16[80,1280]{1,0:T(8,128)(2,1)S(1)}, bf16[80,1280]{1,0:T(8,128)(2,1)S(1)}, u32[]{:S(2)}, u32[]{:S(2)}) collective-permute-start(bf16[80,1280]{1,0:T(8,128)(2,1)S(1)} %get-tuple-element.54), channel_id=1, source_target_pairs={{0,1},{1,2},{2,3},{3,0},{4,5},{5,6},{6,7},{7,4},{8,9},{9,10},{10,1... | collective-permute-start | bytes 614408 | tf_op jit(solution)/shard_map/ppermute | solution.py:22
  78.9 11.7 %collective-permute-start.20 = (bf16[80,1280]{1,0:T(8,128)(2,1)S(1)}, bf16[80,1280]{1,0:T(8,128)(2,1)S(1)}, u32[]{:S(2)}, u32[]{:S(2)}) collective-permute-start(bf16[80,1280]{1,0:T(8,128)(2,1)S(1)} %get-tuple-element.55), channel_id=1, source_target_pairs={{0,2},{1,3},{2,0},{3,1},{4,6},{5,7},{6,4},{7,5},{8,10},{9,11},{10,... | collective-permute-start | bytes 614408 | tf_op jit(solution)/shard_map/ppermute | solution.py:22
  82.8 7.8 %collective-permute-start.21 = (bf16[80,1280]{1,0:T(8,128)(2,1)S(1)}, bf16[80,1280]{1,0:T(8,128)(2,1)S(1)}, u32[]{:S(2)}, u32[]{:S(2)}) collective-permute-start(bf16[80,1280]{1,0:T(8,128)(2,1)S(1)} %get-tuple-element.56), channel_id=1, source_target_pairs={{0,3},{1,0},{2,1},{3,2},{4,7},{5,4},{6,5},{7,6},{8,11},{9,8},{10,9... | collective-permute-start | bytes 614408 | tf_op jit(solution)/shard_map/ppermute | solution.py:22
  90.7 9.5 %collective-permute-start.22 = (bf16[64,1280]{1,0:T(8,128)(2,1)S(1)}, bf16[64,1280]{1,0:T(8,128)(2,1)S(1)}, u32[]{:S(2)}, u32[]{:S(2)}) collective-permute-start(bf16[64,1280]{1,0:T(8,128)(2,1)S(1)} %get-tuple-element.57.own), channel_id=1, source_target_pairs={{0,1},{1,2},{2,3},{3,0},{4,5},{5,6},{6,7},{7,4},{8,9},{9,10},{10,1... | collective-permute-start | bytes 491528 | tf_op jit(solution)/shard_map/ppermute | solution.py:22
  91.4 10.6 %collective-permute-start.23 = (bf16[64,1280]{1,0:T(8,128)(2,1)S(1)}, bf16[64,1280]{1,0:T(8,128)(2,1)S(1)}, u32[]{:S(2)}, u32[]{:S(2)}) collective-permute-start(bf16[64,1280]{1,0:T(8,128)(2,1)S(1)} %get-tuple-element.57.own), channel_id=1, source_target_pairs={{0,2},{1,3},{2,0},{3,1},{4,6},{5,7},{6,4},{7,5},{8,10},{9,11},{10,... | collective-permute-start | bytes 491528 | tf_op jit(solution)/shard_map/ppermute | solution.py:22
  94.9 7.1 %collective-permute-start.24 = (bf16[64,1280]{1,0:T(8,128)(2,1)S(1)}, bf16[64,1280]{1,0:T(8,128)(2,1)S(1)}, u32[]{:S(2)}, u32[]{:S(2)}) collective-permute-start(bf16[64,1280]{1,0:T(8,128)(2,1)S(1)} %get-tuple-element.57.own), channel_id=1, source_target_pairs={{0,3},{1,0},{2,1},{3,2},{4,7},{5,4},{6,5},{7,6},{8,11},{9,8},{10,9... | collective-permute-start | bytes 491528 | tf_op jit(solution)/shard_map/ppermute | solution.py:22
  94.9 5.3 %collective-permute-start.25 = (bf16[16,1280]{1,0:T(8,128)(2,1)S(1)}, bf16[16,1280]{1,0:T(8,128)(2,1)S(1)}, u32[]{:S(2)}, u32[]{:S(2)}) collective-permute-start(bf16[16,1280]{1,0:T(8,128)(2,1)S(1)} %get-tuple-element.58), channel_id=1, source_target_pairs={{0,4},{4,8},{8,12},{12,16},{16,20},{20,24},{24,28},{28,32},{32,36}... | collective-permute-start | bytes 122888 | tf_op jit(solution)/shard_map/ppermute | solution.py:27
  106.2 8.5 %collective-permute-start.26 = (bf16[32,4096]{1,0:T(8,128)(2,1)S(1)}, bf16[32,4096]{1,0:T(8,128)(2,1)S(1)}, u32[]{:S(2)}, u32[]{:S(2)}) collective-permute-start(bf16[32,4096]{1,0:T(8,128)(2,1)S(1)} %get-tuple-element.60), channel_id=1, source_target_pairs={{0,1},{1,2},{2,3},{3,0},{4,5},{5,6},{6,7},{7,4},{8,9},{9,10},{10,1... | collective-permute-start | bytes 786440 | tf_op jit(solution)/shard_map/ppermute | solution.py:22
  106.6 14.6 %collective-permute-start.27 = (bf16[32,4096]{1,0:T(8,128)(2,1)S(1)}, bf16[32,4096]{1,0:T(8,128)(2,1)S(1)}, u32[]{:S(2)}, u32[]{:S(2)}) collective-permute-start(bf16[32,4096]{1,0:T(8,128)(2,1)S(1)} %get-tuple-element.61), channel_id=1, source_target_pairs={{0,2},{1,3},{2,0},{3,1},{4,6},{5,7},{6,4},{7,5},{8,10},{9,11},{10,... | collective-permute-start | bytes 786440 | tf_op jit(solution)/shard_map/ppermute | solution.py:22
  109.9 11.3 %collective-permute-start.28 = (bf16[32,4096]{1,0:T(8,128)(2,1)S(1)}, bf16[32,4096]{1,0:T(8,128)(2,1)S(1)}, u32[]{:S(2)}, u32[]{:S(2)}) collective-permute-start(bf16[32,4096]{1,0:T(8,128)(2,1)S(1)} %get-tuple-element.62), channel_id=1, source_target_pairs={{0,3},{1,0},{2,1},{3,2},{4,7},{5,4},{6,5},{7,6},{8,11},{9,8},{10,9... | collective-permute-start | bytes 786440 | tf_op jit(solution)/shard_map/ppermute | solution.py:22

commit v4 on v3

--- a/solution.py
+++ b/solution.py
@@ -130,35 +130,30 @@
         bias = jnp.where(column < kept, 0.0, -1e30)
         window = pl.ds(begin, MOST * BLK)
         for pair in range(3):
+            q_pair = q_ref[i * BLK:(i + 1) * BLK, pair * 128:(pair + 1) * 128]
+            q_pair = q_pair * jnp.asarray(HEAD_DIM ** -0.5, q_pair.dtype)
+            none = jnp.zeros_like(q_pair)
+            key_at, value_at = ((0, 256), (128, 384), (512, 512))[pair]
+            q_both = jnp.where(low, q_pair, none)
             if pair < 2:
-                q_pair = q_ref[i * BLK:(i + 1) * BLK, pair * 128:(pair + 1) * 128]
-                keys = buf[window, pair * 128:(pair + 1) * 128]
-                values = buf[window, 256 + pair * 128:256 + (pair + 1) * 128]
-            else:
-                q_pair = q_ref[i * BLK:(i + 1) * BLK, 256:384]
-                keys = buf[window, 512:640]
-                values = keys
-            q_pair = q_pair * jnp.asarray(HEAD_DIM ** -0.5, q_pair.dtype)
-            halves = []
-            for half in range(2 if pair < 2 else 1):
-                q_head = jnp.where(low if half == 0 else ~low, q_pair, jnp.zeros_like(q_pair))
-                scores = lax.dot_general(
-                    q_head, keys, (((1,), (1,)), ((), ())), preferred_element_type=jnp.float32) + bias
-                top = jnp.max(scores, axis=-1, keepdims=True)
-                weights = jnp.exp(scores - top)
-                total = jnp.sum(weights, axis=-1, keepdims=True)
-                summed = jnp.dot(weights.astype(jnp.bfloat16), values, preferred_element_type=jnp.float32)
-                halves.append(summed / total)
+                q_both = jnp.concatenate([q_both, jnp.where(low, none, q_pair)], axis=0)
+            scores = dot_t(q_both, buf[window, key_at:key_at + 128]) + bias
+            top = jnp.max(scores, axis=-1, keepdims=True)
+            weights = jnp.exp(scores - top)
+            total = jnp.sum(weights, axis=-1, keepdims=True)
+            summed = dot(weights.astype(jnp.bfloat16), buf[window, value_at:value_at + 128]) / total
             if pair < 2:
-                merged = jnp.where(low, halves[0], halves[1])
+                merged = jnp.where(low, summed[:BLK], summed[BLK:])
                 out_ref[i * BLK:(i + 1) * BLK, pair * 128:(pair + 1) * 128] = merged.astype(jnp.bfloat16)
             else:
-                out_ref[i * BLK:(i + 1) * BLK, 256:] = halves[0][:, HEAD_DIM:].astype(jnp.bfloat16)
-
-
-def query_kernel(normed_ref, w_ref, q_ref):
+                out_ref[i * BLK:(i + 1) * BLK, 256:] = summed[:, HEAD_DIM:].astype(jnp.bfloat16)
+
+
+def query_kernel(normed_ref, w_ref, kv_in, w_down_in, q_ref, kv_ref, w_down_ref):
     q_ref[...] = jnp.zeros_like(q_ref)
     q_ref[:, :w_ref.shape[1]] = dot_t(normed_ref[...], w_ref[0]).astype(jnp.bfloat16)
+    kv_ref[...] = kv_in[...]
+    w_down_ref[...] = w_down_in[...]
 
 
 def mlp_kernel(tp_ref, core_ref, att0, att1, att2, att3, w_out_ref, *refs):
@@ -250,28 +245,28 @@
     return jax.ShapeDtypeStruct(shape, jnp.bfloat16)
 
 
-def attend(ids, core, normed, w_qkv, kv, w_mine):
+def attend(ids, core, normed, w_qkv, kv, w_mine, w_down):
     rows = normed.shape[0]
     width = w_qkv.shape[1]
     back, on = send_seq(kv, 2), send_seq(kv, -2)
-    five = send_five(kv)
     w_two = send_tp(w_mine, 2)
     beside = send_partner(kv)
     whole = lambda array: pl.BlockSpec(array.shape, lambda i: (0,) * array.ndim)
-    queries = pl.pallas_call(
+    queries, kv_held, w_down = pl.pallas_call(
         query_kernel,
         grid=(1,),
-        out_shape=bf16(rows, 384),
-        in_specs=[whole(normed), pl.BlockSpec((1,) + w_qkv.shape[1:], lambda i: (0, 0, 0))],
-        out_specs=pl.BlockSpec((rows, 384), lambda i: (0, 0)),
+        out_shape=[bf16(rows, 384), bf16(*kv.shape), bf16(*w_down.shape)],
+        in_specs=[whole(normed), pl.BlockSpec((1,) + w_qkv.shape[1:], lambda i: (0, 0, 0)), VMEM, VMEM],
+        out_specs=[pl.BlockSpec((rows, 384), lambda i: (0, 0)), VMEM, VMEM],
         compiler_params=params(4),
         cost_estimate=cost(2e8, 2e6),
-    )(normed, w_qkv)
-    back, on, five, queries = lax.optimization_barrier((back, on, five, queries))
+    )(normed, w_qkv, kv, w_down)
+    back, on, queries, kv_late = lax.optimization_barrier((back, on, queries, kv))
+    five = send_five(kv_late)
     far_back, far_on = send_seq(back, 2), send_seq(on, -2)
     w_one, w_three = send_tp(w_mine, 1), send_tp(w_mine, 3)
-    far_back, far_on, w_two = lax.optimization_barrier((far_back, far_on, w_two))
-    chain = [far_back, back, kv, on, far_on]
+    far_back, far_on, w_two, w_one, five = lax.optimization_barrier((far_back, far_on, w_two, w_one, five))
+    chain = [far_back, back, kv_held, on, far_on]
     swapped = [send_partner(far_back), send_partner(back), beside, send_partner(on), send_partner(far_on)]
     return pl.pallas_call(
         attend_kernel,
@@ -286,7 +281,7 @@
         ],
         compiler_params=params(14),
         cost_estimate=cost(1e9, 4e6),
-    )(ids, core, queries, *chain, *swapped, five), [w_one, w_two, w_three]
+    )(ids, core, queries, *chain, *swapped, five), [w_one, w_two, w_three], w_down
 
 
 def exchange(parts):
@@ -316,9 +311,9 @@
         compiler_params=params(60),
         cost_estimate=cost(4e8, 4e6),
     )(block_utt, core, tp, frames, gain_attn, w_qkv, w_out)
-    (attended, joined), w_mine = attend(block_utt, core, normed, w_qkv, kv, w_mine)
-    attended, *w_mine = lax.optimization_barrier((attended, *w_mine))
+    (attended, joined), w_mine, w_down = attend(block_utt, core, normed, w_qkv, kv, w_mine, w_down)
     w_other = [send_partner(piece) for piece in w_mine]
+    attended, *w_other = lax.optimization_barrier((attended, *w_other))
     heads = exchange([attended] * 3)
 
     resid, *parts = pl.pallas_call(

time: 123 us -> 115 us (0.935)
  waiting for transfers between devices: 50.4 us -> 43.3 us
    ppermute x5, waiting for transfers between devices: 19.7 us -> 13.5 us  [send_seq(): lax.ppermute(value, SEQ, [(s, s + steps) for s in range(count) if 0 <= s...]
    ppermute x15, waiting for transfers between devices: 30.7 us -> 28.4 us  [send_tp(): lax.ppermute(value, TP, [(t, (t + steps) % count) for t in range(count)])]
    ppermute x1, starting transfers between devices: 3.37 us -> 1.91 us  [send_five(): lax.ppermute(value, SEQ, [(a, b) for a, b in pairs if 0 <= b < count])]
    ppermute x8, waiting for transfers between devices: 0.02 us -> 1.41 us  [send_partner(): return lax.ppermute(value, SEQ, [(s, s ^ 1) for s in range(count)])]
    unnamed x22 -> x26, local copies, waits for them, and re-layouts: 4.02 us -> 4.04 us
where the time goes in v4:
time: 115 us; the launch traced here: 114 us
  starting transfers between devices  43.3 us (38%)
  waiting for transfers between devices  43.3 us (38%)
  Pallas kernels  22.9 us (20%)
  local copies, waits for them, and re-layouts  4.04 us (4%)
    ppermute x15, waiting for transfers between devices, send_tp(): lax.ppermute(value, TP, [(t, (t + steps) % count) for t in range(count)])  28.4 us
    ppermute x15, starting transfers between devices, send_tp(): lax.ppermute(value, TP, [(t, (t + steps) % count) for t in range(count)])  26 us
    ppermute x5, starting transfers between devices, send_seq(): lax.ppermute(value, SEQ, [(s, s + steps) for s in range(count) if 0 <= s...  13.6 us
    ppermute x5, waiting for transfers between devices, send_seq(): lax.ppermute(value, SEQ, [(s, s + steps) for s in range(count) if 0 <= s...  13.5 us
    pallas_call x1, Pallas kernels, attend(): pl.pallas_call(attend_kernel, out_shape=(bf16(rows, width), jax.ShapeDtyp...  6.49 us
    pallas_call x1, Pallas kernels, shards(): pl.pallas_call(mlp_kernel, out_shape=[jax.ShapeDtypeStruct((share + IDROW...  5.84 us
    pallas_call x1, Pallas kernels, shards(): pl.pallas_call(kv_kernel, out_shape=(scalar, scalar, bf16(rows, width), b...  4.65 us
    pallas_call x1, Pallas kernels, shards(): pl.pallas_call(adapter_kernel, out_shape=[bf16(pooled_count // 4, lm_widt...  4.3 us
  transfers between devices with their start and end apart: 29, of which 13 were waited for; matrix products, arithmetic and copies ran while one was open for 0% of the time, Pallas kernels for 6%

profile of v4, /device:TPU:70, one launch (start us, length us, event | category | flops | bytes accessed | tf_op | source)
XLA Modules:
  0.0 113.9 jit_solution(11904718663477843361)
XLA Ops:
  0.0 4.7 %shard_map.100 = (s32[1]{0:T(128)}, s32[1]{0:T(128)}, bf16[256,1280]{1,0:T(8,128)(2,1)}, bf16[272,640]{1,0:T(8,128)(2,1)}, bf16[320,640]{1,0:T(8,128)(2,1)}) custom-call(s32[2]{0:T(128)} %ids_ref.5, s32[1]{0:T(128)} %bitcast.core_ref, s32[1]{0:T(128)} %bitcast.1.tp_ref, bf16[256,1280]{1,0:T(8,128)(2,1)} %refs_6_.1, f32[1280]{0:T(1024)} %gain_ref.1, ...), custom_call_target="tpu_custom_call" | custom-call | flops 400000000 | bytes 4000000 | tf_op jit(solution)/shard_map/pallas_call | solution.py:301
  4.7 3.4 %collective-permute-start = (bf16[272,640]{1,0:T(8,128)(2,1)}, bf16[272,640]{1,0:T(8,128)(2,1)S(1)}, u32[]{:S(2)}, u32[]{:S(2)}) collective-permute-start(bf16[272,640]{1,0:T(8,128)(2,1)} %get-tuple-element.48.kv_in), channel_id=1, source_target_pairs={{0,8},{4,12},{8,16},{12,20},{16,24},{20,28},{24,32},{28,36},{32,40... | collective-permute-start | bytes 1044488 | tf_op jit(solution)/shard_map/ppermute | solution.py:27
  8.1 2.4 %collective-permute-start.1 = (bf16[272,640]{1,0:T(8,128)(2,1)}, bf16[272,640]{1,0:T(8,128)(2,1)S(1)}, u32[]{:S(2)}, u32[]{:S(2)}) collective-permute-start(bf16[272,640]{1,0:T(8,128)(2,1)} %get-tuple-element.48.kv_in), channel_id=1, source_target_pairs={{8,0},{12,4},{16,8},{20,12},{24,16},{28,20},{32,24},{36,28},{40,32... | collective-permute-start | bytes 1044488 | tf_op jit(solution)/shard_map/ppermute | solution.py:27
  10.5 3.3 %collective-permute-start.4 = (bf16[320,640]{1,0:T(8,128)(2,1)}, bf16[320,640]{1,0:T(8,128)(2,1)S(1)}, u32[]{:S(2)}, u32[]{:S(2)}) collective-permute-start(bf16[320,640]{1,0:T(8,128)(2,1)} %get-tuple-element.47), channel_id=1, source_target_pairs={{0,2},{1,3},{2,0},{3,1},{4,6},{5,7},{6,4},{7,5},{8,10},{9,11},{10,... | collective-permute-start | bytes 1228808 | tf_op jit(solution)/shard_map/ppermute | solution.py:22
  13.8 0.7 collective-permute-start.5
  14.5 1.9 %copy-done.2 = bf16[1280,1280]{1,0:T(8,128)(2,1)S(1)} copy-done((bf16[1280,1280]{1,0:T(8,128)(2,1)S(1)}, bf16[1280,1280]{1,0:T(8,128)(2,1)}, u32[]{:S(2)}) %copy-start.2) | copy-done | bytes 3276824
  16.4 1.1 copy-done.7
  17.5 1.0 copy-done.8
  18.5 0.7 shard_map.101
  19.2 0.0 copy-start.1
  19.2 0.0 copy-start.4
  19.2 0.0 copy-start.10
  19.2 0.0 collective-permute-done.refs_1_
  19.2 2.7 %collective-permute-done.1.refs_3_ = bf16[272,640]{1,0:T(8,128)(2,1)S(1)} collective-permute-done((bf16[272,640]{1,0:T(8,128)(2,1)}, bf16[272,640]{1,0:T(8,128)(2,1)S(1)}, u32[]{:S(2)}, u32[]{:S(2)}) %collective-permute-start.1) | collective-permute-done | bytes 348192 | tf_op jit(solution)/shard_map/ppermute | solution.py:27
  21.9 3.1 %collective-permute-start.2 = (bf16[272,640]{1,0:T(8,128)(2,1)S(1)}, bf16[272,640]{1,0:T(8,128)(2,1)S(1)}, u32[]{:S(2)}, u32[]{:S(2)}) collective-permute-start(bf16[272,640]{1,0:T(8,128)(2,1)S(1)} %collective-permute-done.refs_1_), channel_id=1, source_target_pairs={{0,8},{4,12},{8,16},{12,20},{16,24},{20,28},{24,32},{28,36},{32,40... | collective-permute-start | bytes 1044488 | tf_op jit(solution)/shard_map/ppermute | solution.py:27
  25.0 2.7 %collective-permute-start.3 = (bf16[272,640]{1,0:T(8,128)(2,1)S(1)}, bf16[272,640]{1,0:T(8,128)(2,1)S(1)}, u32[]{:S(2)}, u32[]{:S(2)}) collective-permute-start(bf16[272,640]{1,0:T(8,128)(2,1)S(1)} %collective-permute-done.1.refs_3_), channel_id=1, source_target_pairs={{8,0},{12,4},{16,8},{20,12},{24,16},{28,20},{32,24},{36,28},{40,32... | collective-permute-start | bytes 1044488 | tf_op jit(solution)/shard_map/ppermute | solution.py:27
  27.8 3.1 %collective-permute-start.14 = (bf16[320,640]{1,0:T(8,128)(2,1)S(1)}, bf16[320,640]{1,0:T(8,128)(2,1)S(1)}, u32[]{:S(2)}, u32[]{:S(2)}) collective-permute-start(bf16[320,640]{1,0:T(8,128)(2,1)S(1)} %copy-done.12), channel_id=1, source_target_pairs={{0,3},{1,0},{2,1},{3,2},{4,7},{5,4},{6,5},{7,6},{8,11},{9,8},{10,9... | collective-permute-start | bytes 1228808 | tf_op jit(solution)/shard_map/ppermute | solution.py:22
  30.9 0.0 collective-permute-done.4.refs_1_
  30.9 1.9 %collective-permute-start.6 = (bf16[272,640]{1,0:T(8,128)(2,1)S(1)}, bf16[272,640]{1,0:T(8,128)(2,1)S(1)}, u32[]{:S(2)}, u32[]{:S(2)}) collective-permute-start(bf16[272,640]{1,0:T(8,128)(2,1)S(1)} %copy-done.9), channel_id=1, source_target_pairs={{4,24},{12,32},{20,40},{24,4},{28,48},{32,12},{36,56},{40,20},{44,... | collective-permute-start | bytes 1044488 | tf_op jit(solution)/shard_map/ppermute | solution.py:40
  32.8 0.0 collective-permute-done.5.refs_0_
  32.8 0.1 collective-permute-start.9
  32.9 0.0 collective-permute-done.2.refs_0_
  32.9 0.5 collective-permute-start.8
  33.4 7.4 %collective-permute-done.3.refs_4_ = bf16[272,640]{1,0:T(8,128)(2,1)S(1)} collective-permute-done((bf16[272,640]{1,0:T(8,128)(2,1)S(1)}, bf16[272,640]{1,0:T(8,128)(2,1)S(1)}, u32[]{:S(2)}, u32[]{:S(2)}) %collective-permute-start.3) | collective-permute-done | bytes 348192 | tf_op jit(solution)/shard_map/ppermute | solution.py:27
  40.8 0.5 collective-permute-start.7
  41.3 0.1 collective-permute-start.11
  41.4 0.4 collective-permute-start.15
  41.8 0.1 collective-permute-start.12
  41.9 0.5 collective-permute-done.10.refs_8_
  42.5 0.1 collective-permute-start.13
  42.6 0.4 collective-permute-done.7.refs_5_
  43.0 0.5 collective-permute-done.11.refs_9_
  43.5 6.5 %shard_map.102 = (bf16[256,320]{1,0:T(8,128)(2,1)S(1)}, s32[1]{0:T(128)}) custom-call(s32[2]{0:T(128)S(1)} %copy-done.11, s32[1]{0:T(128)} %get-tuple-element.40.core_ref, bf16[256,384]{1,0:T(8,128)(2,1)S(1)} %get-tuple-element.44.q_ref, bf16[272,640]{1,0:T(8,128)(2,1)S(1)} %collective-permute-done.2.refs_0_, ...), custom_call_target="tpu_custom_call" | custom-call | flops 1000000000 | bytes 4000000 | tf_op jit(solution)/shard_map/pallas_call | solution.py:271
  50.0 0.0 collective-permute-done.12.refs_3_
  50.0 0.9 collective-permute-start.16
  50.9 3.6 %collective-permute-start.17 = (bf16[256,320]{1,0:T(8,128)(2,1)S(1)}, bf16[256,320]{1,0:T(8,128)(2,1)S(1)}, u32[]{:S(2)}, u32[]{:S(2)}) collective-permute-start(bf16[256,320]{1,0:T(8,128)(2,1)S(1)} %get-tuple-element.57.att0), channel_id=1, source_target_pairs={{0,2},{1,3},{2,0},{3,1},{4,6},{5,7},{6,4},{7,5},{8,10},{9,11},{10,... | collective-permute-start | bytes 491528 | tf_op jit(solution)/shard_map/ppermute | solution.py:22
  54.6 0.6 collective-permute-start.18
  55.2 3.1 %collective-permute-done.16.att1 = bf16[256,320]{1,0:T(8,128)(2,1)S(1)} collective-permute-done((bf16[256,320]{1,0:T(8,128)(2,1)S(1)}, bf16[256,320]{1,0:T(8,128)(2,1)S(1)}, u32[]{:S(2)}, u32[]{:S(2)}) %collective-permute-start.16) | collective-permute-done | bytes 163872 | tf_op jit(solution)/shard_map/ppermute | solution.py:22
  58.3 5.4 %collective-permute-done.17.att2 = bf16[256,320]{1,0:T(8,128)(2,1)S(1)} collective-permute-done((bf16[256,320]{1,0:T(8,128)(2,1)S(1)}, bf16[256,320]{1,0:T(8,128)(2,1)S(1)}, u32[]{:S(2)}, u32[]{:S(2)}) %collective-permute-start.17) | collective-permute-done | bytes 163872 | tf_op jit(solution)/shard_map/ppermute | solution.py:22
  63.7 0.0 collective-permute-done.18.att3
  63.7 0.0 copy-start.5
  63.7 0.0 copy-start.6
  63.7 5.8 %shard_map.103 = (f32[80,1280]{1,0:T(8,128)S(1)}, bf16[80,1280]{1,0:T(8,128)(2,1)S(1)}, bf16[80,1280]{1,0:T(8,128)(2,1)S(1)}, bf16[80,1280]{1,0:T(8,128)(2,1)S(1)}, bf16[80,1280]{1,0:T(8,128)(2,1)S(1)}) custom-call(s32[1]{0:T(128)} %get-tuple-element.39.tp_ref, s32[1]{0:T(128)} %get-tuple-element.40.core_ref, bf16[256,320]{1,0:T(8,128)(2,1)S(1)} %get-tuple-element.57.att0, ...), custom_call_target="tpu_custom_call" | custom-call | flops 2500000000 | bytes 10000000 | tf_op jit(solution)/shard_map/pallas_call | solution.py:319
  69.6 1.3 %collective-permute-start.19 = (bf16[80,1280]{1,0:T(8,128)(2,1)S(1)}, bf16[80,1280]{1,0:T(8,128)(2,1)S(1)}, u32[]{:S(2)}, u32[]{:S(2)}) collective-permute-start(bf16[80,1280]{1,0:T(8,128)(2,1)S(1)} %get-tuple-element.64), channel_id=1, source_target_pairs={{0,1},{1,2},{2,3},{3,0},{4,5},{5,6},{6,7},{7,4},{8,9},{9,10},{10,1... | collective-permute-start | bytes 614408 | tf_op jit(solution)/shard_map/ppermute | solution.py:22
  70.9 2.4 %collective-permute-start.20 = (bf16[80,1280]{1,0:T(8,128)(2,1)S(1)}, bf16[80,1280]{1,0:T(8,128)(2,1)S(1)}, u32[]{:S(2)}, u32[]{:S(2)}) collective-permute-start(bf16[80,1280]{1,0:T(8,128)(2,1)S(1)} %get-tuple-element.65), channel_id=1, source_target_pairs={{0,2},{1,3},{2,0},{3,1},{4,6},{5,7},{6,4},{7,5},{8,10},{9,11},{10,... | collective-permute-start | bytes 614408 | tf_op jit(solution)/shard_map/ppermute | solution.py:22
  73.3 0.9 collective-permute-start.21
  74.1 3.0 %collective-permute-done.19.got1 = bf16[80,1280]{1,0:T(8,128)(2,1)S(1)} collective-permute-done((bf16[80,1280]{1,0:T(8,128)(2,1)S(1)}, bf16[80,1280]{1,0:T(8,128)(2,1)S(1)}, u32[]{:S(2)}, u32[]{:S(2)}) %collective-permute-start.19) | collective-permute-done | bytes 204832 | tf_op jit(solution)/shard_map/ppermute | solution.py:22
  77.2 5.5 %collective-permute-done.20.got2 = bf16[80,1280]{1,0:T(8,128)(2,1)S(1)} collective-permute-done((bf16[80,1280]{1,0:T(8,128)(2,1)S(1)}, bf16[80,1280]{1,0:T(8,128)(2,1)S(1)}, u32[]{:S(2)}, u32[]{:S(2)}) %collective-permute-start.20) | collective-permute-done | bytes 204832 | tf_op jit(solution)/shard_map/ppermute | solution.py:22
  82.7 0.1 shard_map.104
  82.8 1.3 %collective-permute-start.22 = (bf16[64,1280]{1,0:T(8,128)(2,1)S(1)}, bf16[64,1280]{1,0:T(8,128)(2,1)S(1)}, u32[]{:S(2)}, u32[]{:S(2)}) collective-permute-start(bf16[64,1280]{1,0:T(8,128)(2,1)S(1)} %get-tuple-element.67.own), channel_id=1, source_target_pairs={{0,1},{1,2},{2,3},{3,0},{4,5},{5,6},{6,7},{7,4},{8,9},{9,10},{10,1... | collective-permute-start | bytes 491528 | tf_op jit(solution)/shard_map/ppermute | solution.py:22
  84.0 2.4 %collective-permute-start.23 = (bf16[64,1280]{1,0:T(8,128)(2,1)S(1)}, bf16[64,1280]{1,0:T(8,128)(2,1)S(1)}, u32[]{:S(2)}, u32[]{:S(2)}) collective-permute-start(bf16[64,1280]{1,0:T(8,128)(2,1)S(1)} %get-tuple-element.67.own), channel_id=1, source_target_pairs={{0,2},{1,3},{2,0},{3,1},{4,6},{5,7},{6,4},{7,5},{8,10},{9,11},{10,... | collective-permute-start | bytes 491528 | tf_op jit(solution)/shard_map/ppermute | solution.py:22
  86.5 0.9 collective-permute-start.24
  87.3 1.9 %collective-permute-start.25 = (bf16[16,1280]{1,0:T(8,128)(2,1)S(1)}, bf16[16,1280]{1,0:T(8,128)(2,1)S(1)}, u32[]{:S(2)}, u32[]{:S(2)}) collective-permute-start(bf16[16,1280]{1,0:T(8,128)(2,1)S(1)} %get-tuple-element.68), channel_id=1, source_target_pairs={{0,4},{4,8},{8,12},{12,16},{16,20},{20,24},{24,28},{28,32},{32,36}... | collective-permute-start | bytes 122888 | tf_op jit(solution)/shard_map/ppermute | solution.py:27
  89.2 3.4 %collective-permute-done.25.rim_ref = bf16[16,1280]{1,0:T(8,128)(2,1)S(1)} collective-permute-done((bf16[16,1280]{1,0:T(8,128)(2,1)S(1)}, bf16[16,1280]{1,0:T(8,128)(2,1)S(1)}, u32[]{:S(2)}, u32[]{:S(2)}) %collective-permute-start.25) | collective-permute-done | bytes 40992 | tf_op jit(solution)/shard_map/ppermute | solution.py:27
  92.6 0.0 collective-permute-done.22.got1
  92.6 1.3 %collective-permute-done.23.got2 = bf16[64,1280]{1,0:T(8,128)(2,1)S(1)} collective-permute-done((bf16[64,1280]{1,0:T(8,128)(2,1)S(1)}, bf16[64,1280]{1,0:T(8,128)(2,1)S(1)}, u32[]{:S(2)}, u32[]{:S(2)}) %collective-permute-start.23) | collective-permute-done | bytes 163872 | tf_op jit(solution)/shard_map/ppermute | solution.py:22
  93.9 0.0 collective-permute-done.24.got3
  94.0 4.3 %shard_map.105 = (bf16[32,4096]{1,0:T(8,128)(2,1)S(1)}, bf16[32,4096]{1,0:T(8,128)(2,1)S(1)}, bf16[32,4096]{1,0:T(8,128)(2,1)S(1)}, bf16[32,4096]{1,0:T(8,128)(2,1)S(1)}) custom-call(s32[1]{0:T(128)} %get-tuple-element.39.tp_ref, s32[2]{0:T(128)S(1)} %copy-done.11, s32[1]{0:T(128)} %get-tuple-element.53.joined_ref, ...), custom_call_target="tpu_custom_call" | custom-call | flops 1000000000 | bytes 6000000 | tf_op jit(solution)/shard_map/pallas_call | solution.py:339
  98.3 1.3 %collective-permute-start.26 = (bf16[32,4096]{1,0:T(8,128)(2,1)S(1)}, bf16[32,4096]{1,0:T(8,128)(2,1)S(1)}, u32[]{:S(2)}, u32[]{:S(2)}) collective-permute-start(bf16[32,4096]{1,0:T(8,128)(2,1)S(1)} %get-tuple-element.70), channel_id=1, source_target_pairs={{0,1},{1,2},{2,3},{3,0},{4,5},{5,6},{6,7},{7,4},{8,9},{9,10},{10,1... | collective-permute-start | bytes 786440 | tf_op jit(solution)/shard_map/ppermute | solution.py:22
  99.6 2.4 %collective-permute-start.27 = (bf16[32,4096]{1,0:T(8,128)(2,1)S(1)}, bf16[32,4096]{1,0:T(8,128)(2,1)S(1)}, u32[]{:S(2)}, u32[]{:S(2)}) collective-permute-start(bf16[32,4096]{1,0:T(8,128)(2,1)S(1)} %get-tuple-element.71), channel_id=1, source_target_pairs={{0,2},{1,3},{2,0},{3,1},{4,6},{5,7},{6,4},{7,5},{8,10},{9,11},{10,... | collective-permute-start | bytes 786440 | tf_op jit(solution)/shard_map/ppermute | solution.py:22
  102.0 1.0 collective-permute-start.28
  103.0 4.9 %collective-permute-done.26.got1 = bf16[32,4096]{1,0:T(8,128)(2,1)S(1)} collective-permute-done((bf16[32,4096]{1,0:T(8,128)(2,1)S(1)}, bf16[32,4096]{1,0:T(8,128)(2,1)S(1)}, u32[]{:S(2)}, u32[]{:S(2)}) %collective-permute-start.26) | collective-permute-done | bytes 262176 | tf_op jit(solution)/shard_map/ppermute | solution.py:22
  107.9 5.1 %collective-permute-done.27.got2 = bf16[32,4096]{1,0:T(8,128)(2,1)S(1)} collective-permute-done((bf16[32,4096]{1,0:T(8,128)(2,1)S(1)}, bf16[32,4096]{1,0:T(8,128)(2,1)S(1)}, u32[]{:S(2)}, u32[]{:S(2)}) %collective-permute-start.27) | collective-permute-done | bytes 262176 | tf_op jit(solution)/shard_map/ppermute | solution.py:22
  113.0 0.8 shard_map.106
  (27 shorter events, 0.1 us)
Async XLA Ops:
  0.0 14.5 %copy-start = (bf16[3,1280,320]{1,2,0:T(8,128)(2,1)S(1)}, bf16[3,1280,320]{1,2,0:T(8,128)(2,1)}, u32[]{:S(2)}) copy-start(bf16[3,1280,320]{1,2,0:T(8,128)(2,1)} %param.12) | copy-start | bytes 7372804
  4.7 14.5 %collective-permute-start = (bf16[272,640]{1,0:T(8,128)(2,1)}, bf16[272,640]{1,0:T(8,128)(2,1)S(1)}, u32[]{:S(2)}, u32[]{:S(2)}) collective-permute-start(bf16[272,640]{1,0:T(8,128)(2,1)} %get-tuple-element.48.kv_in), channel_id=1, source_target_pairs={{0,8},{4,12},{8,16},{12,20},{16,24},{20,28},{24,32},{28,36},{32,40... | collective-permute-start | bytes 1044488 | tf_op jit(solution)/shard_map/ppermute | solution.py:27
  8.1 13.8 %collective-permute-start.1 = (bf16[272,640]{1,0:T(8,128)(2,1)}, bf16[272,640]{1,0:T(8,128)(2,1)S(1)}, u32[]{:S(2)}, u32[]{:S(2)}) collective-permute-start(bf16[272,640]{1,0:T(8,128)(2,1)} %get-tuple-element.48.kv_in), channel_id=1, source_target_pairs={{8,0},{12,4},{16,8},{20,12},{24,16},{28,20},{32,24},{36,28},{40,32... | collective-permute-start | bytes 1044488 | tf_op jit(solution)/shard_map/ppermute | solution.py:27
  10.5 20.4 %collective-permute-start.4 = (bf16[320,640]{1,0:T(8,128)(2,1)}, bf16[320,640]{1,0:T(8,128)(2,1)S(1)}, u32[]{:S(2)}, u32[]{:S(2)}) collective-permute-start(bf16[320,640]{1,0:T(8,128)(2,1)} %get-tuple-element.47), channel_id=1, source_target_pairs={{0,2},{1,3},{2,0},{3,1},{4,6},{5,7},{6,4},{7,5},{8,10},{9,11},{10,... | collective-permute-start | bytes 1228808 | tf_op jit(solution)/shard_map/ppermute | solution.py:22
  13.8 19.0 %collective-permute-start.5 = (bf16[320,640]{1,0:T(8,128)(2,1)}, bf16[320,640]{1,0:T(8,128)(2,1)S(1)}, u32[]{:S(2)}, u32[]{:S(2)}) collective-permute-start(bf16[320,640]{1,0:T(8,128)(2,1)} %get-tuple-element.47), channel_id=1, source_target_pairs={{0,1},{1,2},{2,3},{3,0},{4,5},{5,6},{6,7},{7,4},{8,9},{9,10},{10,1... | collective-permute-start | bytes 1228808 | tf_op jit(solution)/shard_map/ppermute | solution.py:22
  14.5 1.9 %copy-start.2 = (bf16[1280,1280]{1,0:T(8,128)(2,1)S(1)}, bf16[1280,1280]{1,0:T(8,128)(2,1)}, u32[]{:S(2)}) copy-start(bf16[1280,1280]{1,0:T(8,128)(2,1)} %w_down_in.1) | copy-start | bytes 9830404
  16.4 1.1 copy-start.7
  17.5 1.0 copy-start.8
  18.5 9.3 %copy-start.12 = (bf16[320,640]{1,0:T(8,128)(2,1)S(1)}, bf16[320,640]{1,0:T(8,128)(2,1)}, u32[]{:S(2)}) copy-start(bf16[320,640]{1,0:T(8,128)(2,1)} %get-tuple-element.47) | copy-start | bytes 1228804
  18.5 12.4 %copy-start.9 = (bf16[272,640]{1,0:T(8,128)(2,1)S(1)}, bf16[272,640]{1,0:T(8,128)(2,1)}, u32[]{:S(2)}) copy-start(bf16[272,640]{1,0:T(8,128)(2,1)} %get-tuple-element.48.kv_in) | copy-start | bytes 1044484
  18.5 25.0 %copy-start.11 = (s32[2]{0:T(128)S(1)}, s32[2]{0:T(128)}, u32[]{:S(2)}) copy-start(s32[2]{0:T(128)} %ids_ref.5) | copy-start | bytes 28
  18.5 45.2 %copy-start.3 = (bf16[1280,1280]{1,0:T(8,128)(2,1)S(1)}, bf16[1280,1280]{1,0:T(8,128)(2,1)}, u32[]{:S(2)}) copy-start(bf16[1280,1280]{1,0:T(8,128)(2,1)} %refs_8_.1) | copy-start | bytes 9830404
  19.2 44.5 %copy-start.1 = (bf16[320,1280]{1,0:T(8,128)(2,1)S(1)}, bf16[320,1280]{1,0:T(8,128)(2,1)}, u32[]{:S(2)}) copy-start(bf16[320,1280]{1,0:T(8,128)(2,1)} %w_out_ref.1) | copy-start | bytes 2457604
  19.2 44.5 %copy-start.4 = (bf16[256,1280]{1,0:T(8,128)(2,1)S(1)}, bf16[256,1280]{1,0:T(8,128)(2,1)}, u32[]{:S(2)}) copy-start(bf16[256,1280]{1,0:T(8,128)(2,1)} %refs_6_.1) | copy-start | bytes 1966084
  19.2 44.5 %copy-start.10 = (f32[1280]{0:T(1024)S(1)}, f32[1280]{0:T(1024)}, u32[]{:S(2)}) copy-start(f32[1280]{0:T(1024)} %refs_7_.1) | copy-start | bytes 15364
  21.9 11.0 %collective-permute-start.2 = (bf16[272,640]{1,0:T(8,128)(2,1)S(1)}, bf16[272,640]{1,0:T(8,128)(2,1)S(1)}, u32[]{:S(2)}, u32[]{:S(2)}) collective-permute-start(bf16[272,640]{1,0:T(8,128)(2,1)S(1)} %collective-permute-done.refs_1_), channel_id=1, source_target_pairs={{0,8},{4,12},{8,16},{12,20},{16,24},{20,28},{24,32},{28,36},{32,40... | collective-permute-start | bytes 1044488 | tf_op jit(solution)/shard_map/ppermute | solution.py:27
  25.0 15.8 %collective-permute-start.3 = (bf16[272,640]{1,0:T(8,128)(2,1)S(1)}, bf16[272,640]{1,0:T(8,128)(2,1)S(1)}, u32[]{:S(2)}, u32[]{:S(2)}) collective-permute-start(bf16[272,640]{1,0:T(8,128)(2,1)S(1)} %collective-permute-done.1.refs_3_), channel_id=1, source_target_pairs={{8,0},{12,4},{16,8},{20,12},{24,16},{28,20},{32,24},{36,28},{40,32... | collective-permute-start | bytes 1044488 | tf_op jit(solution)/shard_map/ppermute | solution.py:27
  27.8 13.6 %collective-permute-start.14 = (bf16[320,640]{1,0:T(8,128)(2,1)S(1)}, bf16[320,640]{1,0:T(8,128)(2,1)S(1)}, u32[]{:S(2)}, u32[]{:S(2)}) collective-permute-start(bf16[320,640]{1,0:T(8,128)(2,1)S(1)} %copy-done.12), channel_id=1, source_target_pairs={{0,3},{1,0},{2,1},{3,2},{4,7},{5,4},{6,5},{7,6},{8,11},{9,8},{10,9... | collective-permute-start | bytes 1228808 | tf_op jit(solution)/shard_map/ppermute | solution.py:22
  30.9 9.9 %collective-permute-start.6 = (bf16[272,640]{1,0:T(8,128)(2,1)S(1)}, bf16[272,640]{1,0:T(8,128)(2,1)S(1)}, u32[]{:S(2)}, u32[]{:S(2)}) collective-permute-start(bf16[272,640]{1,0:T(8,128)(2,1)S(1)} %copy-done.9), channel_id=1, source_target_pairs={{4,24},{12,32},{20,40},{24,4},{28,48},{32,12},{36,56},{40,20},{44,... | collective-permute-start | bytes 1044488 | tf_op jit(solution)/shard_map/ppermute | solution.py:40
  32.8 8.5 %collective-permute-start.9 = (bf16[272,640]{1,0:T(8,128)(2,1)S(1)}, bf16[272,640]{1,0:T(8,128)(2,1)S(1)}, u32[]{:S(2)}, u32[]{:S(2)}) collective-permute-start(bf16[272,640]{1,0:T(8,128)(2,1)S(1)} %copy-done.9), channel_id=1, source_target_pairs={{0,4},{4,0},{8,12},{12,8},{16,20},{20,16},{24,28},{28,24},{32,36},... | collective-permute-start | bytes 1044488 | tf_op jit(solution)/shard_map/ppermute | solution.py:34
  32.9 8.9 %collective-permute-start.8 = (bf16[272,640]{1,0:T(8,128)(2,1)S(1)}, bf16[272,640]{1,0:T(8,128)(2,1)S(1)}, u32[]{:S(2)}, u32[]{:S(2)}) collective-permute-start(bf16[272,640]{1,0:T(8,128)(2,1)S(1)} %collective-permute-done.refs_1_), channel_id=1, source_target_pairs={{0,4},{4,0},{8,12},{12,8},{16,20},{20,16},{24,28},{28,24},{32,36},... | collective-permute-start | bytes 1044488 | tf_op jit(solution)/shard_map/ppermute | solution.py:34
  40.8 1.7 %collective-permute-start.10 = (bf16[272,640]{1,0:T(8,128)(2,1)S(1)}, bf16[272,640]{1,0:T(8,128)(2,1)S(1)}, u32[]{:S(2)}, u32[]{:S(2)}) collective-permute-start(bf16[272,640]{1,0:T(8,128)(2,1)S(1)} %collective-permute-done.1.refs_3_), channel_id=1, source_target_pairs={{0,4},{4,0},{8,12},{12,8},{16,20},{20,16},{24,28},{28,24},{32,36},... | collective-permute-start | bytes 1044488 | tf_op jit(solution)/shard_map/ppermute | solution.py:34
  40.8 2.2 %collective-permute-start.7 = (bf16[272,640]{1,0:T(8,128)(2,1)S(1)}, bf16[272,640]{1,0:T(8,128)(2,1)S(1)}, u32[]{:S(2)}, u32[]{:S(2)}) collective-permute-start(bf16[272,640]{1,0:T(8,128)(2,1)S(1)} %collective-permute-done.2.refs_0_), channel_id=1, source_target_pairs={{0,4},{4,0},{8,12},{12,8},{16,20},{20,16},{24,28},{28,24},{32,36},... | collective-permute-start | bytes 1044488 | tf_op jit(solution)/shard_map/ppermute | solution.py:34
  41.3 2.1 %collective-permute-start.11 = (bf16[272,640]{1,0:T(8,128)(2,1)S(1)}, bf16[272,640]{1,0:T(8,128)(2,1)S(1)}, u32[]{:S(2)}, u32[]{:S(2)}) collective-permute-start(bf16[272,640]{1,0:T(8,128)(2,1)S(1)} %collective-permute-done.3.refs_4_), channel_id=1, source_target_pairs={{0,4},{4,0},{8,12},{12,8},{16,20},{20,16},{24,28},{28,24},{32,36},... | collective-permute-start | bytes 1044488 | tf_op jit(solution)/shard_map/ppermute | solution.py:34
  41.4 8.6 %collective-permute-start.15 = (bf16[320,640]{1,0:T(8,128)(2,1)S(1)}, bf16[320,640]{1,0:T(8,128)(2,1)S(1)}, u32[]{:S(2)}, u32[]{:S(2)}) collective-permute-start(bf16[320,640]{1,0:T(8,128)(2,1)S(1)} %collective-permute-done.14.refs_2_), channel_id=1, source_target_pairs={{0,4},{4,0},{8,12},{12,8},{16,20},{20,16},{24,28},{28,24},{32,36},... | collective-permute-start | bytes 1228808 | tf_op jit(solution)/shard_map/ppermute | solution.py:34
  41.8 8.1 %collective-permute-start.12 = (bf16[320,640]{1,0:T(8,128)(2,1)S(1)}, bf16[320,640]{1,0:T(8,128)(2,1)S(1)}, u32[]{:S(2)}, u32[]{:S(2)}) collective-permute-start(bf16[320,640]{1,0:T(8,128)(2,1)S(1)} %collective-permute-done.5.refs_0_), channel_id=1, source_target_pairs={{0,4},{4,0},{8,12},{12,8},{16,20},{20,16},{24,28},{28,24},{32,36},... | collective-permute-start | bytes 1228808 | tf_op jit(solution)/shard_map/ppermute | solution.py:34
  42.5 7.5 %collective-permute-start.13 = (bf16[320,640]{1,0:T(8,128)(2,1)S(1)}, bf16[320,640]{1,0:T(8,128)(2,1)S(1)}, u32[]{:S(2)}, u32[]{:S(2)}) collective-permute-start(bf16[320,640]{1,0:T(8,128)(2,1)S(1)} %collective-permute-done.4.refs_1_), channel_id=1, source_target_pairs={{0,4},{4,0},{8,12},{12,8},{16,20},{20,16},{24,28},{28,24},{32,36},... | collective-permute-start | bytes 1228808 | tf_op jit(solution)/shard_map/ppermute | solution.py:34
  50.0 8.3 %collective-permute-start.16 = (bf16[256,320]{1,0:T(8,128)(2,1)S(1)}, bf16[256,320]{1,0:T(8,128)(2,1)S(1)}, u32[]{:S(2)}, u32[]{:S(2)}) collective-permute-start(bf16[256,320]{1,0:T(8,128)(2,1)S(1)} %get-tuple-element.57.att0), channel_id=1, source_target_pairs={{0,1},{1,2},{2,3},{3,0},{4,5},{5,6},{6,7},{7,4},{8,9},{9,10},{10,1... | collective-permute-start | bytes 491528 | tf_op jit(solution)/shard_map/ppermute | solution.py:22
  50.9 12.8 %collective-permute-start.17 = (bf16[256,320]{1,0:T(8,128)(2,1)S(1)}, bf16[256,320]{1,0:T(8,128)(2,1)S(1)}, u32[]{:S(2)}, u32[]{:S(2)}) collective-permute-start(bf16[256,320]{1,0:T(8,128)(2,1)S(1)} %get-tuple-element.57.att0), channel_id=1, source_target_pairs={{0,2},{1,3},{2,0},{3,1},{4,6},{5,7},{6,4},{7,5},{8,10},{9,11},{10,... | collective-permute-start | bytes 491528 | tf_op jit(solution)/shard_map/ppermute | solution.py:22
  54.6 9.1 %collective-permute-start.18 = (bf16[256,320]{1,0:T(8,128)(2,1)S(1)}, bf16[256,320]{1,0:T(8,128)(2,1)S(1)}, u32[]{:S(2)}, u32[]{:S(2)}) collective-permute-start(bf16[256,320]{1,0:T(8,128)(2,1)S(1)} %get-tuple-element.57.att0), channel_id=1, source_target_pairs={{0,3},{1,0},{2,1},{3,2},{4,7},{5,4},{6,5},{7,6},{8,11},{9,8},{10,9... | collective-permute-start | bytes 491528 | tf_op jit(solution)/shard_map/ppermute | solution.py:22
  63.7 30.2 %copy-start.5 = (bf16[320,4096]{1,0:T(8,128)(2,1)S(1)}, bf16[320,4096]{1,0:T(8,128)(2,1)}, u32[]{:S(2)}) copy-start(bf16[320,4096]{1,0:T(8,128)(2,1)} %w_proj_ref.1) | copy-start | bytes 7864324
  63.7 30.2 %copy-start.6 = (bf16[3,1280,320]{1,2,0:T(8,128)(2,1)S(1)}, bf16[3,1280,320]{1,2,0:T(8,128)(2,1)}, u32[]{:S(2)}) copy-start(bf16[3,1280,320]{1,2,0:T(8,128)(2,1)} %param.17) | copy-start | bytes 7372804
  69.6 7.6 %collective-permute-start.19 = (bf16[80,1280]{1,0:T(8,128)(2,1)S(1)}, bf16[80,1280]{1,0:T(8,128)(2,1)S(1)}, u32[]{:S(2)}, u32[]{:S(2)}) collective-permute-start(bf16[80,1280]{1,0:T(8,128)(2,1)S(1)} %get-tuple-element.64), channel_id=1, source_target_pairs={{0,1},{1,2},{2,3},{3,0},{4,5},{5,6},{6,7},{7,4},{8,9},{9,10},{10,1... | collective-permute-start | bytes 614408 | tf_op jit(solution)/shard_map/ppermute | solution.py:22
  70.9 11.8 %collective-permute-start.20 = (bf16[80,1280]{1,0:T(8,128)(2,1)S(1)}, bf16[80,1280]{1,0:T(8,128)(2,1)S(1)}, u32[]{:S(2)}, u32[]{:S(2)}) collective-permute-start(bf16[80,1280]{1,0:T(8,128)(2,1)S(1)} %get-tuple-element.65), channel_id=1, source_target_pairs={{0,2},{1,3},{2,0},{3,1},{4,6},{5,7},{6,4},{7,5},{8,10},{9,11},{10,... | collective-permute-start | bytes 614408 | tf_op jit(solution)/shard_map/ppermute | solution.py:22
  73.3 9.4 %collective-permute-start.21 = (bf16[80,1280]{1,0:T(8,128)(2,1)S(1)}, bf16[80,1280]{1,0:T(8,128)(2,1)S(1)}, u32[]{:S(2)}, u32[]{:S(2)}) collective-permute-start(bf16[80,1280]{1,0:T(8,128)(2,1)S(1)} %get-tuple-element.66), channel_id=1, source_target_pairs={{0,3},{1,0},{2,1},{3,2},{4,7},{5,4},{6,5},{7,6},{8,11},{9,8},{10,9... | collective-permute-start | bytes 614408 | tf_op jit(solution)/shard_map/ppermute | solution.py:22
  82.8 9.9 %collective-permute-start.22 = (bf16[64,1280]{1,0:T(8,128)(2,1)S(1)}, bf16[64,1280]{1,0:T(8,128)(2,1)S(1)}, u32[]{:S(2)}, u32[]{:S(2)}) collective-permute-start(bf16[64,1280]{1,0:T(8,128)(2,1)S(1)} %get-tuple-element.67.own), channel_id=1, source_target_pairs={{0,1},{1,2},{2,3},{3,0},{4,5},{5,6},{6,7},{7,4},{8,9},{9,10},{10,1... | collective-permute-start | bytes 491528 | tf_op jit(solution)/shard_map/ppermute | solution.py:22
  84.0 9.9 %collective-permute-start.23 = (bf16[64,1280]{1,0:T(8,128)(2,1)S(1)}, bf16[64,1280]{1,0:T(8,128)(2,1)S(1)}, u32[]{:S(2)}, u32[]{:S(2)}) collective-permute-start(bf16[64,1280]{1,0:T(8,128)(2,1)S(1)} %get-tuple-element.67.own), channel_id=1, source_target_pairs={{0,2},{1,3},{2,0},{3,1},{4,6},{5,7},{6,4},{7,5},{8,10},{9,11},{10,... | collective-permute-start | bytes 491528 | tf_op jit(solution)/shard_map/ppermute | solution.py:22
  86.5 7.5 %collective-permute-start.24 = (bf16[64,1280]{1,0:T(8,128)(2,1)S(1)}, bf16[64,1280]{1,0:T(8,128)(2,1)S(1)}, u32[]{:S(2)}, u32[]{:S(2)}) collective-permute-start(bf16[64,1280]{1,0:T(8,128)(2,1)S(1)} %get-tuple-element.67.own), channel_id=1, source_target_pairs={{0,3},{1,0},{2,1},{3,2},{4,7},{5,4},{6,5},{7,6},{8,11},{9,8},{10,9... | collective-permute-start | bytes 491528 | tf_op jit(solution)/shard_map/ppermute | solution.py:22
  87.3 5.3 %collective-permute-start.25 = (bf16[16,1280]{1,0:T(8,128)(2,1)S(1)}, bf16[16,1280]{1,0:T(8,128)(2,1)S(1)}, u32[]{:S(2)}, u32[]{:S(2)}) collective-permute-start(bf16[16,1280]{1,0:T(8,128)(2,1)S(1)} %get-tuple-element.68), channel_id=1, source_target_pairs={{0,4},{4,8},{8,12},{12,16},{16,20},{20,24},{24,28},{28,32},{32,36}... | collective-permute-start | bytes 122888 | tf_op jit(solution)/shard_map/ppermute | solution.py:27
  98.3 9.6 %collective-permute-start.26 = (bf16[32,4096]{1,0:T(8,128)(2,1)S(1)}, bf16[32,4096]{1,0:T(8,128)(2,1)S(1)}, u32[]{:S(2)}, u32[]{:S(2)}) collective-permute-start(bf16[32,4096]{1,0:T(8,128)(2,1)S(1)} %get-tuple-element.70), channel_id=1, source_target_pairs={{0,1},{1,2},{2,3},{3,0},{4,5},{5,6},{6,7},{7,4},{8,9},{9,10},{10,1... | collective-permute-start | bytes 786440 | tf_op jit(solution)/shard_map/ppermute | solution.py:22
  99.6 13.5 %collective-permute-start.27 = (bf16[32,4096]{1,0:T(8,128)(2,1)S(1)}, bf16[32,4096]{1,0:T(8,128)(2,1)S(1)}, u32[]{:S(2)}, u32[]{:S(2)}) collective-permute-start(bf16[32,4096]{1,0:T(8,128)(2,1)S(1)} %get-tuple-element.71), channel_id=1, source_target_pairs={{0,2},{1,3},{2,0},{3,1},{4,6},{5,7},{6,4},{7,5},{8,10},{9,11},{10,... | collective-permute-start | bytes 786440 | tf_op jit(solution)/shard_map/ppermute | solution.py:22
  102.0 11.1 %collective-permute-start.28 = (bf16[32,4096]{1,0:T(8,128)(2,1)S(1)}, bf16[32,4096]{1,0:T(8,128)(2,1)S(1)}, u32[]{:S(2)}, u32[]{:S(2)}) collective-permute-start(bf16[32,4096]{1,0:T(8,128)(2,1)S(1)} %get-tuple-element.72), channel_id=1, source_target_pairs={{0,3},{1,0},{2,1},{3,2},{4,7},{5,4},{6,5},{7,6},{8,11},{9,8},{10,9... | collective-permute-start | bytes 786440 | tf_op jit(solution)/shard_map/ppermute | solution.py:22

commit v5 on v4

--- a/solution.py
+++ b/solution.py
@@ -27,6 +27,12 @@
     return lax.ppermute(
         value, SEQ, [(s, s + steps) for s in range(count) if 0 <= s + steps < count]
     )
+
+
+def send_chip(value, turn):
+    count = lax.axis_size(SEQ)
+    pairs = [(s, s + 2 * turn * (1 if s % 2 else -1)) for s in range(count)]
+    return lax.ppermute(value, SEQ, [(a, b) for a, b in pairs if 0 <= b < count])
 
 
 def send_partner(value):
@@ -95,12 +101,8 @@
     rows = q_ref.shape[0]
     copies = []
     for n, piece in enumerate(pieces):
-        if n < 5:
-            slot = 1 + 2 * n + parity
-        elif n < 10:
-            slot = 2 * (n - 4) - parity
-        else:
-            slot = 11 * parity
+        slot = (9 - 7 * parity, 7 - 3 * parity, 5 + parity, 3 + 5 * parity, 1 + 9 * parity,
+                2 + 7 * parity, 4 + 3 * parity, 6 - parity, 8 - 5 * parity, 10 - 9 * parity, 11 * parity)[n]
         copies.append(pltpu.make_async_copy(
             piece.at[pl.ds(rows, IDROWS), pl.ds(0, 128)], marks.at[slot], mark_sems.at[n]))
         copies.append(pltpu.make_async_copy(
@@ -156,6 +158,14 @@
     w_down_ref[...] = w_down_in[...]
 
 
+def last_row(ref):
+    rows, width = ref.shape
+    row = ref[rows - 8:, :][7:8]
+    pieces = [row[:, g * 128:(g + 1) * 128] for g in range(width // 128)]
+    pieces.append(jnp.zeros((IDROWS - len(pieces), 128), row.dtype))
+    return jnp.concatenate(pieces, axis=0)
+
+
 def mlp_kernel(tp_ref, core_ref, att0, att1, att2, att3, w_out_ref, *refs):
     pieces, frames_ref, gain_ref, w_up_ref, w_down_ref = refs[:6], *refs[6:10]
     resid_ref, part0, part1, part2, part3 = refs[10:15]
@@ -174,23 +184,29 @@
     resid = resid_all[...]
     normed = layer_norm(resid, gain_ref[...][None]).astype(jnp.bfloat16)
     hidden = gelu(dot(normed, w_up_ref[...])).astype(jnp.bfloat16)
-    part_all[...] = dot(hidden, w_down_ref[...]).astype(jnp.bfloat16)
+    part_all[...] = dot(hidden, w_down_ref[...])
     mine = pl.ds(pl.multiple_of(tp * share, share), share)
-    resid_ref[:share, :] = resid_all[mine, :]
-    resid_ref[share:, :] = resid_all[rows - IDROWS:, :]
+    groups = resid_all.shape[1] // 128
+    resid_ref[groups * share:, :] = last_row(resid_all)
+    last = last_row(part_all).astype(jnp.bfloat16)
+    for g in range(groups):
+        resid_ref[g * share:(g + 1) * share, :] = resid_all[mine, g * 128:(g + 1) * 128]
     for k, part in enumerate((part0, part1, part2, part3)):
-        target = lax.rem(tp + k, 4)
-        part[:share, :] = part_all[pl.ds(pl.multiple_of(target * share, share), share), :]
-        part[share:, :] = part_all[rows - IDROWS:, :]
+        target = pl.ds(pl.multiple_of(lax.rem(tp + k, 4) * share, share), share)
+        for g in range(groups):
+            part[g * share:(g + 1) * share, :] = part_all[target, g * 128:(g + 1) * 128].astype(jnp.bfloat16)
+        part[groups * share:, :] = last
 
 
 def layer_sum_kernel(resid_ref, own, got1, got2, got3, out_ref, rim_ref):
     total = resid_ref[...] + own[...].astype(jnp.float32)
     for piece in (got1, got2, got3):
         total = total + piece[...].astype(jnp.float32)
-    share = out_ref.shape[0]
-    out_ref[...] = total[:share].astype(jnp.bfloat16)
-    rim_ref[...] = total[share:].astype(jnp.bfloat16)
+    share, width = out_ref.shape
+    groups = width // 128
+    for g in range(groups):
+        out_ref[:, g * 128:(g + 1) * 128] = total[g * share:(g + 1) * share].astype(jnp.bfloat16)
+    rim_ref[...] = total[groups * share:].astype(jnp.bfloat16)
 
 
 def adapter_kernel(tp_ref, ids_ref, joined_ref, own, got1, got2, got3, rim_ref, w_conv_ref, w_proj_ref,
@@ -210,11 +226,12 @@
     pick = lambda flag, source: dot(one(flag), source).astype(jnp.bfloat16)
     even = pick(r == 2 * j, rows)
     odd = pick(r == 2 * j + 1, rows)
+    before = dot(one((r == 2 * j - 1) & (j != cut)), rows)
+    rim = rim_ref[...].astype(jnp.float32)
+    rim = jnp.concatenate([rim[g:g + 1] for g in range(before.shape[1] // 128)], axis=1)
     rim_first = jnp.where(joined_ref[0] == 1, 0, -1)
-    j_rim = lax.broadcasted_iota(jnp.int32, (count, IDROWS), 0)
-    r_rim = lax.broadcasted_iota(jnp.int32, (count, IDROWS), 1)
-    before = dot(one((r == 2 * j - 1) & (j != cut)), rows)
-    before = before + dot(one((j_rim == rim_first) & (r_rim == IDROWS - 1)), rim_ref[...])
+    top_row = lax.broadcasted_iota(jnp.int32, before.shape, 0) == rim_first
+    before = before + jnp.where(top_row, rim, 0.0)
     conv = dot_t(before.astype(jnp.bfloat16), w_conv_ref[0])
     conv = conv + dot_t(even, w_conv_ref[1])
     conv = conv + dot_t(odd, w_conv_ref[2])
@@ -248,9 +265,8 @@
 def attend(ids, core, normed, w_qkv, kv, w_mine, w_down):
     rows = normed.shape[0]
     width = w_qkv.shape[1]
-    back, on = send_seq(kv, 2), send_seq(kv, -2)
+    back, on = send_chip(kv, 1), send_chip(kv, -1)
     w_two = send_tp(w_mine, 2)
-    beside = send_partner(kv)
     whole = lambda array: pl.BlockSpec(array.shape, lambda i: (0,) * array.ndim)
     queries, kv_held, w_down = pl.pallas_call(
         query_kernel,
@@ -261,13 +277,15 @@
         compiler_params=params(4),
         cost_estimate=cost(2e8, 2e6),
     )(normed, w_qkv, kv, w_down)
-    back, on, queries, kv_late = lax.optimization_barrier((back, on, queries, kv))
+    back, kv_late = lax.optimization_barrier((back, kv))
     five = send_five(kv_late)
-    far_back, far_on = send_seq(back, 2), send_seq(on, -2)
+    far_back, far_on = send_chip(back, 1), send_chip(on, -1)
     w_one, w_three = send_tp(w_mine, 1), send_tp(w_mine, 3)
     far_back, far_on, w_two, w_one, five = lax.optimization_barrier((far_back, far_on, w_two, w_one, five))
+    back_again, on_again, kv_again, queries = lax.optimization_barrier((back, on, kv_held, queries))
+    beside = send_partner(kv_again)
     chain = [far_back, back, kv_held, on, far_on]
-    swapped = [send_partner(far_back), send_partner(back), beside, send_partner(on), send_partner(far_on)]
+    swapped = [send_partner(far_back), send_partner(back_again), beside, send_partner(on_again), send_partner(far_on)]
     return pl.pallas_call(
         attend_kernel,
         out_shape=(bf16(rows, width), jax.ShapeDtypeStruct((1,), jnp.int32)),
@@ -308,7 +326,7 @@
             pltpu.VMEM((2,) + w_qkv.shape[1:], jnp.bfloat16),
             pltpu.SemaphoreType.DMA((4,)),
         ],
-        compiler_params=params(60),
+        compiler_params=params(56),
         cost_estimate=cost(4e8, 4e6),
     )(block_utt, core, tp, frames, gain_attn, w_qkv, w_out)
     (attended, joined), w_mine, w_down = attend(block_utt, core, normed, w_qkv, kv, w_mine, w_down)
@@ -316,18 +334,19 @@
     attended, *w_other = lax.optimization_barrier((attended, *w_other))
     heads = exchange([attended] * 3)
 
+    tall = share * (width // 128) + IDROWS
     resid, *parts = pl.pallas_call(
         mlp_kernel,
-        out_shape=[jax.ShapeDtypeStruct((share + IDROWS, width), jnp.float32)] + [bf16(share + IDROWS, width)] * 4,
+        out_shape=[jax.ShapeDtypeStruct((tall, 128), jnp.float32)] + [bf16(tall, 128)] * 4,
         in_specs=[SMEM] * 2 + [VMEM] * 15,
         out_specs=[VMEM] * 5,
-        scratch_shapes=[pltpu.VMEM((rows, width), jnp.float32), pltpu.VMEM((rows, width), jnp.bfloat16)],
+        scratch_shapes=[pltpu.VMEM((rows, width), jnp.float32)] * 2,
         compiler_params=params(14),
         cost_estimate=cost(2.5e9, 1e7),
     )(tp, core, attended, *heads, w_out, *w_mine, *w_other, frames, gain_ffn, w_up, w_down)
     own, rim = pl.pallas_call(
         layer_sum_kernel,
-        out_shape=[bf16(share, width), bf16(IDROWS, width)],
+        out_shape=[bf16(share, width), bf16(IDROWS, 128)],
         in_specs=[VMEM] * 5,
         out_specs=[VMEM] * 2,
         compiler_params=params(4),

time: 115 us -> 112 us (0.974)
  waiting for transfers between devices: 43.3 us -> 39.3 us
    ppermute x0 -> x4, starting transfers between devices: none -> 15.9 us  [send_chip(): lax.ppermute(value, SEQ, [(a, b) for a, b in pairs if 0 <= b < count])]
    ppermute x5 -> x1, starting transfers between devices: 13.6 us -> 1.91 us  [send_seq(): lax.ppermute(value, SEQ, [(s, s + steps) for s in range(count) if 0 <= s...]
    ppermute x5 -> x1, waiting for transfers between devices: 13.5 us -> 3 us  [send_seq(): lax.ppermute(value, SEQ, [(s, s + steps) for s in range(count) if 0 <= s...]
    ppermute x15, starting transfers between devices: 26 us -> 22.4 us  [send_tp(): lax.ppermute(value, TP, [(t, (t + steps) % count) for t in range(count)])]
    ppermute x15, waiting for transfers between devices: 28.4 us -> 31.3 us  [send_tp(): lax.ppermute(value, TP, [(t, (t + steps) % count) for t in range(count)])]
    ppermute x1, waiting for transfers between devices: 0.01 us -> 2.67 us  [send_five(): lax.ppermute(value, SEQ, [(a, b) for a, b in pairs if 0 <= b < count])]
    ppermute x0 -> x4, waiting for transfers between devices: none -> 1.22 us  [send_chip(): lax.ppermute(value, SEQ, [(a, b) for a, b in pairs if 0 <= b < count])]
    unnamed x26 -> x22, local copies, waits for them, and re-layouts: 4.04 us -> 4.03 us
  transfers between devices with their start and end apart: 29 -> 29, of which waited for: 13 -> 12; matrix products, arithmetic and copies ran while one was open for 0% -> 0% of each run, Pallas kernels for 6% -> 6%
where the time goes in v5:
time: 112 us; the launch traced here: 111 us
  starting transfers between devices  43.9 us (39%)
  waiting for transfers between devices  39.3 us (35%)
  Pallas kernels  23 us (21%)
  local copies, waits for them, and re-layouts  4.03 us (4%)
    ppermute x15, waiting for transfers between devices, send_tp(): lax.ppermute(value, TP, [(t, (t + steps) % count) for t in range(count)])  31.3 us
    ppermute x15, starting transfers between devices, send_tp(): lax.ppermute(value, TP, [(t, (t + steps) % count) for t in range(count)])  22.4 us
    ppermute x4, starting transfers between devices, send_chip(): lax.ppermute(value, SEQ, [(a, b) for a, b in pairs if 0 <= b < count])  15.9 us
    pallas_call x1, Pallas kernels, attend(): pl.pallas_call(attend_kernel, out_shape=(bf16(rows, width), jax.ShapeDtyp...  6.43 us
    pallas_call x1, Pallas kernels, shards(): pl.pallas_call(mlp_kernel, out_shape=[jax.ShapeDtypeStruct((tall, 128), j...  5.9 us
    pallas_call x1, Pallas kernels, shards(): pl.pallas_call(kv_kernel, out_shape=(scalar, scalar, bf16(rows, width), b...  4.66 us
    pallas_call x1, Pallas kernels, shards(): pl.pallas_call(adapter_kernel, out_shape=[bf16(pooled_count // 4, lm_widt...  4.42 us
    unnamed x22, local copies, waits for them, and re-layouts  4.03 us
  transfers between devices with their start and end apart: 29, of which 12 were waited for; matrix products, arithmetic and copies ran while one was open for 0% of the time, Pallas kernels for 6%

profile of v5, /device:TPU:70, one launch (start us, length us, event | category | flops | bytes accessed | tf_op | source)
XLA Modules:
  0.0 110.5 jit_solution(12116917650163403670)
XLA Ops:
  0.0 4.7 %shard_map.100 = (s32[1]{0:T(128)}, s32[1]{0:T(128)}, bf16[256,1280]{1,0:T(8,128)(2,1)}, bf16[272,640]{1,0:T(8,128)(2,1)}, bf16[320,640]{1,0:T(8,128)(2,1)}) custom-call(s32[2]{0:T(128)} %ids_ref.5, s32[1]{0:T(128)} %bitcast.core_ref, s32[1]{0:T(128)} %bitcast.1.tp_ref, bf16[256,1280]{1,0:T(8,128)(2,1)} %refs_6_.1, f32[1280]{0:T(1024)} %gain_ref.1, ...), custom_call_target="tpu_custom_call" | custom-call | flops 400000000 | bytes 4000000 | tf_op jit(solution)/shard_map/pallas_call | solution.py:319
  4.7 2.7 %collective-permute-start = (bf16[272,640]{1,0:T(8,128)(2,1)}, bf16[272,640]{1,0:T(8,128)(2,1)S(1)}, u32[]{:S(2)}, u32[]{:S(2)}) collective-permute-start(bf16[272,640]{1,0:T(8,128)(2,1)} %get-tuple-element.50.kv_in), channel_id=1, source_target_pairs={{4,12},{8,0},{12,20},{16,8},{20,28},{24,16},{28,36},{32,24},{36,44... | collective-permute-start | bytes 1044488 | tf_op jit(solution)/shard_map/ppermute | solution.py:35
  7.4 5.2 %collective-permute-start.1 = (bf16[272,640]{1,0:T(8,128)(2,1)}, bf16[272,640]{1,0:T(8,128)(2,1)S(1)}, u32[]{:S(2)}, u32[]{:S(2)}) collective-permute-start(bf16[272,640]{1,0:T(8,128)(2,1)} %get-tuple-element.50.kv_in), channel_id=1, source_target_pairs={{0,8},{8,16},{12,4},{16,24},{20,12},{24,32},{28,20},{32,40},{36,28... | collective-permute-start | bytes 1044488 | tf_op jit(solution)/shard_map/ppermute | solution.py:35
  12.6 3.3 %collective-permute-start.4 = (bf16[320,640]{1,0:T(8,128)(2,1)}, bf16[320,640]{1,0:T(8,128)(2,1)S(1)}, u32[]{:S(2)}, u32[]{:S(2)}) collective-permute-start(bf16[320,640]{1,0:T(8,128)(2,1)} %get-tuple-element.49), channel_id=1, source_target_pairs={{0,2},{1,3},{2,0},{3,1},{4,6},{5,7},{6,4},{7,5},{8,10},{9,11},{10,... | collective-permute-start | bytes 1228808 | tf_op jit(solution)/shard_map/ppermute | solution.py:22
  15.9 0.7 collective-permute-start.5
  16.6 1.2 %collective-permute-done.refs_1_ = bf16[272,640]{1,0:T(8,128)(2,1)S(1)} collective-permute-done((bf16[272,640]{1,0:T(8,128)(2,1)}, bf16[272,640]{1,0:T(8,128)(2,1)S(1)}, u32[]{:S(2)}, u32[]{:S(2)}) %collective-permute-start) | collective-permute-done | bytes 348192 | tf_op jit(solution)/shard_map/ppermute | solution.py:35
  17.8 1.9 %collective-permute-start.2 = (bf16[272,640]{1,0:T(8,128)(2,1)S(1)}, bf16[272,640]{1,0:T(8,128)(2,1)S(1)}, u32[]{:S(2)}, u32[]{:S(2)}) collective-permute-start(bf16[272,640]{1,0:T(8,128)(2,1)S(1)} %collective-permute-done.refs_1_), channel_id=1, source_target_pairs={{4,12},{8,0},{12,20},{16,8},{20,28},{24,16},{28,36},{32,24},{36,44... | collective-permute-start | bytes 1044488 | tf_op jit(solution)/shard_map/ppermute | solution.py:35
  19.7 0.0 collective-permute-done.1.refs_3_
  19.7 6.0 %collective-permute-start.3 = (bf16[272,640]{1,0:T(8,128)(2,1)S(1)}, bf16[272,640]{1,0:T(8,128)(2,1)S(1)}, u32[]{:S(2)}, u32[]{:S(2)}) collective-permute-start(bf16[272,640]{1,0:T(8,128)(2,1)S(1)} %collective-permute-done.1.refs_3_), channel_id=1, source_target_pairs={{0,8},{8,16},{12,4},{16,24},{20,12},{24,32},{28,20},{32,40},{36,28... | collective-permute-start | bytes 1044488 | tf_op jit(solution)/shard_map/ppermute | solution.py:35
  25.8 3.1 %collective-permute-start.14 = (bf16[320,640]{1,0:T(8,128)(2,1)}, bf16[320,640]{1,0:T(8,128)(2,1)S(1)}, u32[]{:S(2)}, u32[]{:S(2)}) collective-permute-start(bf16[320,640]{1,0:T(8,128)(2,1)} %get-tuple-element.49), channel_id=1, source_target_pairs={{0,3},{1,0},{2,1},{3,2},{4,7},{5,4},{6,5},{7,6},{8,11},{9,8},{10,9... | collective-permute-start | bytes 1228808 | tf_op jit(solution)/shard_map/ppermute | solution.py:22
  28.8 0.0 collective-permute-done.4.refs_1_
  28.9 1.9 %collective-permute-start.6 = (bf16[272,640]{1,0:T(8,128)(2,1)}, bf16[272,640]{1,0:T(8,128)(2,1)S(1)}, u32[]{:S(2)}, u32[]{:S(2)}) collective-permute-start(bf16[272,640]{1,0:T(8,128)(2,1)} %get-tuple-element.50.kv_in), channel_id=1, source_target_pairs={{4,24},{12,32},{20,40},{24,4},{28,48},{32,12},{36,56},{40,20},{44,... | collective-permute-start | bytes 1044488 | tf_op jit(solution)/shard_map/ppermute | solution.py:46
  30.8 0.0 copy-start.2
  30.8 1.9 %copy-done.2 = bf16[1280,1280]{1,0:T(8,128)(2,1)S(1)} copy-done((bf16[1280,1280]{1,0:T(8,128)(2,1)S(1)}, bf16[1280,1280]{1,0:T(8,128)(2,1)}, u32[]{:S(2)}) %copy-start.2) | copy-done | bytes 3276824
  32.7 1.1 copy-done.7
  33.8 1.0 copy-done.8
  34.8 0.7 shard_map.101
  35.5 0.0 copy-start.1
  35.5 0.0 copy-start.4
  35.5 0.0 copy-start.9
  35.5 0.0 collective-permute-done.5.refs_0_
  35.5 0.1 collective-permute-start.8
  35.6 0.0 collective-permute-done.2.refs_0_
  35.6 0.5 collective-permute-start.9
  36.1 0.1 collective-permute-start.10
  36.2 2.7 %collective-permute-done.6.refs_10_ = bf16[272,640]{1,0:T(8,128)(2,1)S(1)} collective-permute-done((bf16[272,640]{1,0:T(8,128)(2,1)}, bf16[272,640]{1,0:T(8,128)(2,1)S(1)}, u32[]{:S(2)}, u32[]{:S(2)}) %collective-permute-start.6) | collective-permute-done | bytes 348192 | tf_op jit(solution)/shard_map/ppermute | solution.py:46
  38.9 0.5 collective-permute-start.11
  39.4 0.0 collective-permute-done.8.refs_6_
  39.4 0.1 collective-permute-start.15
  39.5 0.4 collective-permute-start.12
  39.9 0.1 collective-permute-start.13
  40.0 0.5 collective-permute-done.7.refs_5_
  40.5 0.5 collective-permute-done.11.refs_9_
  41.0 6.4 %shard_map.102 = (bf16[256,320]{1,0:T(8,128)(2,1)S(1)}, s32[1]{0:T(128)}) custom-call(s32[2]{0:T(128)S(1)} %copy-done.10, s32[1]{0:T(128)} %get-tuple-element.42.core_ref, bf16[256,384]{1,0:T(8,128)(2,1)S(1)} %get-tuple-element.48.q_ref, bf16[272,640]{1,0:T(8,128)(2,1)S(1)} %collective-permute-done.2.refs_0_, ...), custom_call_target="tpu_custom_call" | custom-call | flops 1000000000 | bytes 4000000 | tf_op jit(solution)/shard_map/pallas_call | solution.py:289
  47.5 0.0 collective-permute-done.13.refs_4_
  47.5 0.1 collective-permute-start.16
  47.6 2.2 %collective-permute-start.17 = (bf16[256,320]{1,0:T(8,128)(2,1)S(1)}, bf16[256,320]{1,0:T(8,128)(2,1)S(1)}, u32[]{:S(2)}, u32[]{:S(2)}) collective-permute-start(bf16[256,320]{1,0:T(8,128)(2,1)S(1)} %get-tuple-element.61.att0), channel_id=1, source_target_pairs={{0,2},{1,3},{2,0},{3,1},{4,6},{5,7},{6,4},{7,5},{8,10},{9,11},{10,... | collective-permute-start | bytes 491528 | tf_op jit(solution)/shard_map/ppermute | solution.py:22
  49.8 1.6 %collective-permute-start.18 = (bf16[256,320]{1,0:T(8,128)(2,1)S(1)}, bf16[256,320]{1,0:T(8,128)(2,1)S(1)}, u32[]{:S(2)}, u32[]{:S(2)}) collective-permute-start(bf16[256,320]{1,0:T(8,128)(2,1)S(1)} %get-tuple-element.61.att0), channel_id=1, source_target_pairs={{0,3},{1,0},{2,1},{3,2},{4,7},{5,4},{6,5},{7,6},{8,11},{9,8},{10,9... | collective-permute-start | bytes 491528 | tf_op jit(solution)/shard_map/ppermute | solution.py:22
  51.4 8.6 %collective-permute-done.16.att1 = bf16[256,320]{1,0:T(8,128)(2,1)S(1)} collective-permute-done((bf16[256,320]{1,0:T(8,128)(2,1)S(1)}, bf16[256,320]{1,0:T(8,128)(2,1)S(1)}, u32[]{:S(2)}, u32[]{:S(2)}) %collective-permute-start.16) | collective-permute-done | bytes 163872 | tf_op jit(solution)/shard_map/ppermute | solution.py:22
  59.9 0.0 collective-permute-done.17.att2
  59.9 0.6 collective-permute-done.18.att3
  60.6 0.0 copy-start.5
  60.6 0.0 copy-start.6
  60.6 5.9 %shard_map.103 = (f32[656,128]{1,0:T(8,128)S(1)}, bf16[656,128]{1,0:T(8,128)(2,1)S(1)}, bf16[656,128]{1,0:T(8,128)(2,1)S(1)}, bf16[656,128]{1,0:T(8,128)(2,1)S(1)}, bf16[656,128]{1,0:T(8,128)(2,1)S(1)}) custom-call(s32[1]{0:T(128)} %get-tuple-element.41.tp_ref, s32[1]{0:T(128)} %get-tuple-element.42.core_ref, bf16[256,320]{1,0:T(8,128)(2,1)S(1)} %get-tuple-element.61.att0, ...), custom_call_target="tpu_custom_call" | custom-call | flops 2500000000 | bytes 10000000 | tf_op jit(solution)/shard_map/pallas_call | solution.py:338
  66.5 0.6 collective-permute-start.19
  67.1 3.6 %collective-permute-start.20 = (bf16[656,128]{1,0:T(8,128)(2,1)S(1)}, bf16[656,128]{1,0:T(8,128)(2,1)S(1)}, u32[]{:S(2)}, u32[]{:S(2)}) collective-permute-start(bf16[656,128]{1,0:T(8,128)(2,1)S(1)} %get-tuple-element.69), channel_id=1, source_target_pairs={{0,2},{1,3},{2,0},{3,1},{4,6},{5,7},{6,4},{7,5},{8,10},{9,11},{10,... | collective-permute-start | bytes 503816 | tf_op jit(solution)/shard_map/ppermute | solution.py:22
  70.7 0.0 collective-permute-start.21
  70.7 3.0 %collective-permute-done.19.got1 = bf16[656,128]{1,0:T(8,128)(2,1)S(1)} collective-permute-done((bf16[656,128]{1,0:T(8,128)(2,1)S(1)}, bf16[656,128]{1,0:T(8,128)(2,1)S(1)}, u32[]{:S(2)}, u32[]{:S(2)}) %collective-permute-start.19) | collective-permute-done | bytes 167968 | tf_op jit(solution)/shard_map/ppermute | solution.py:22
  73.7 4.8 %collective-permute-done.20.got2 = bf16[656,128]{1,0:T(8,128)(2,1)S(1)} collective-permute-done((bf16[656,128]{1,0:T(8,128)(2,1)S(1)}, bf16[656,128]{1,0:T(8,128)(2,1)S(1)}, u32[]{:S(2)}, u32[]{:S(2)}) %collective-permute-start.20) | collective-permute-done | bytes 167968 | tf_op jit(solution)/shard_map/ppermute | solution.py:22
  78.5 0.1 shard_map.104
  78.6 0.1 collective-permute-start.22
  78.7 3.6 %collective-permute-start.23 = (bf16[64,1280]{1,0:T(8,128)(2,1)S(1)}, bf16[64,1280]{1,0:T(8,128)(2,1)S(1)}, u32[]{:S(2)}, u32[]{:S(2)}) collective-permute-start(bf16[64,1280]{1,0:T(8,128)(2,1)S(1)} %get-tuple-element.71.own), channel_id=1, source_target_pairs={{0,2},{1,3},{2,0},{3,1},{4,6},{5,7},{6,4},{7,5},{8,10},{9,11},{10,... | collective-permute-start | bytes 491528 | tf_op jit(solution)/shard_map/ppermute | solution.py:22
  82.3 0.0 collective-permute-start.24
  82.3 1.9 %collective-permute-start.25 = (bf16[16,128]{1,0:T(8,128)(2,1)S(1)}, bf16[16,128]{1,0:T(8,128)(2,1)S(1)}, u32[]{:S(2)}, u32[]{:S(2)}) collective-permute-start(bf16[16,128]{1,0:T(8,128)(2,1)S(1)} %get-tuple-element.72), channel_id=1, source_target_pairs={{0,4},{4,8},{8,12},{12,16},{16,20},{20,24},{24,28},{28,32},{32,36}... | collective-permute-start | bytes 12296 | tf_op jit(solution)/shard_map/ppermute | solution.py:27
  84.2 3.0 %collective-permute-done.25.rim_ref = bf16[16,128]{1,0:T(8,128)(2,1)S(1)} collective-permute-done((bf16[16,128]{1,0:T(8,128)(2,1)S(1)}, bf16[16,128]{1,0:T(8,128)(2,1)S(1)}, u32[]{:S(2)}, u32[]{:S(2)}) %collective-permute-start.25) | collective-permute-done | bytes 4128 | tf_op jit(solution)/shard_map/ppermute | solution.py:27
  87.2 0.0 collective-permute-done.22.got1
  87.2 2.7 %collective-permute-done.23.got2 = bf16[64,1280]{1,0:T(8,128)(2,1)S(1)} collective-permute-done((bf16[64,1280]{1,0:T(8,128)(2,1)S(1)}, bf16[64,1280]{1,0:T(8,128)(2,1)S(1)}, u32[]{:S(2)}, u32[]{:S(2)}) %collective-permute-start.23) | collective-permute-done | bytes 163872 | tf_op jit(solution)/shard_map/ppermute | solution.py:22
  89.9 4.4 %shard_map.105 = (bf16[32,4096]{1,0:T(8,128)(2,1)S(1)}, bf16[32,4096]{1,0:T(8,128)(2,1)S(1)}, bf16[32,4096]{1,0:T(8,128)(2,1)S(1)}, bf16[32,4096]{1,0:T(8,128)(2,1)S(1)}) custom-call(s32[1]{0:T(128)} %get-tuple-element.41.tp_ref, s32[2]{0:T(128)S(1)} %copy-done.10, s32[1]{0:T(128)} %get-tuple-element.57.joined_ref, ...), custom_call_target="tpu_custom_call" | custom-call | flops 1000000000 | bytes 6000000 | tf_op jit(solution)/shard_map/pallas_call | solution.py:358
  94.3 0.1 collective-permute-start.26
  94.4 3.6 %collective-permute-start.27 = (bf16[32,4096]{1,0:T(8,128)(2,1)S(1)}, bf16[32,4096]{1,0:T(8,128)(2,1)S(1)}, u32[]{:S(2)}, u32[]{:S(2)}) collective-permute-start(bf16[32,4096]{1,0:T(8,128)(2,1)S(1)} %get-tuple-element.75), channel_id=1, source_target_pairs={{0,2},{1,3},{2,0},{3,1},{4,6},{5,7},{6,4},{7,5},{8,10},{9,11},{10,... | collective-permute-start | bytes 786440 | tf_op jit(solution)/shard_map/ppermute | solution.py:22
  98.0 5.0 %collective-permute-done.26.got1 = bf16[32,4096]{1,0:T(8,128)(2,1)S(1)} collective-permute-done((bf16[32,4096]{1,0:T(8,128)(2,1)S(1)}, bf16[32,4096]{1,0:T(8,128)(2,1)S(1)}, u32[]{:S(2)}, u32[]{:S(2)}) %collective-permute-start.26) | collective-permute-done | bytes 262176 | tf_op jit(solution)/shard_map/ppermute | solution.py:22
  103.0 6.7 %collective-permute-done.27.got2 = bf16[32,4096]{1,0:T(8,128)(2,1)S(1)} collective-permute-done((bf16[32,4096]{1,0:T(8,128)(2,1)S(1)}, bf16[32,4096]{1,0:T(8,128)(2,1)S(1)}, u32[]{:S(2)}, u32[]{:S(2)}) %collective-permute-start.27) | collective-permute-done | bytes 262176 | tf_op jit(solution)/shard_map/ppermute | solution.py:22
  109.7 0.0 collective-permute-done.28.got3
  109.7 0.8 shard_map.106
  (23 shorter events, 0.1 us)
Async XLA Ops:
  0.0 30.8 %copy-start = (bf16[3,1280,320]{1,2,0:T(8,128)(2,1)S(1)}, bf16[3,1280,320]{1,2,0:T(8,128)(2,1)}, u32[]{:S(2)}) copy-start(bf16[3,1280,320]{1,2,0:T(8,128)(2,1)} %param.12) | copy-start | bytes 7372804
  4.7 13.1 %collective-permute-start = (bf16[272,640]{1,0:T(8,128)(2,1)}, bf16[272,640]{1,0:T(8,128)(2,1)S(1)}, u32[]{:S(2)}, u32[]{:S(2)}) collective-permute-start(bf16[272,640]{1,0:T(8,128)(2,1)} %get-tuple-element.50.kv_in), channel_id=1, source_target_pairs={{4,12},{8,0},{12,20},{16,8},{20,28},{24,16},{28,36},{32,24},{36,44... | collective-permute-start | bytes 1044488 | tf_op jit(solution)/shard_map/ppermute | solution.py:35
  7.4 12.3 %collective-permute-start.1 = (bf16[272,640]{1,0:T(8,128)(2,1)}, bf16[272,640]{1,0:T(8,128)(2,1)S(1)}, u32[]{:S(2)}, u32[]{:S(2)}) collective-permute-start(bf16[272,640]{1,0:T(8,128)(2,1)} %get-tuple-element.50.kv_in), channel_id=1, source_target_pairs={{0,8},{8,16},{12,4},{16,24},{20,12},{24,32},{28,20},{32,40},{36,28... | collective-permute-start | bytes 1044488 | tf_op jit(solution)/shard_map/ppermute | solution.py:35
  12.6 16.2 %collective-permute-start.4 = (bf16[320,640]{1,0:T(8,128)(2,1)}, bf16[320,640]{1,0:T(8,128)(2,1)S(1)}, u32[]{:S(2)}, u32[]{:S(2)}) collective-permute-start(bf16[320,640]{1,0:T(8,128)(2,1)} %get-tuple-element.49), channel_id=1, source_target_pairs={{0,2},{1,3},{2,0},{3,1},{4,6},{5,7},{6,4},{7,5},{8,10},{9,11},{10,... | collective-permute-start | bytes 1228808 | tf_op jit(solution)/shard_map/ppermute | solution.py:22
  15.9 19.6 %collective-permute-start.5 = (bf16[320,640]{1,0:T(8,128)(2,1)}, bf16[320,640]{1,0:T(8,128)(2,1)S(1)}, u32[]{:S(2)}, u32[]{:S(2)}) collective-permute-start(bf16[320,640]{1,0:T(8,128)(2,1)} %get-tuple-element.49), channel_id=1, source_target_pairs={{0,1},{1,2},{2,3},{3,0},{4,5},{5,6},{6,7},{7,4},{8,9},{9,10},{10,1... | collective-permute-start | bytes 1228808 | tf_op jit(solution)/shard_map/ppermute | solution.py:22
  17.8 17.8 %collective-permute-start.2 = (bf16[272,640]{1,0:T(8,128)(2,1)S(1)}, bf16[272,640]{1,0:T(8,128)(2,1)S(1)}, u32[]{:S(2)}, u32[]{:S(2)}) collective-permute-start(bf16[272,640]{1,0:T(8,128)(2,1)S(1)} %collective-permute-done.refs_1_), channel_id=1, source_target_pairs={{4,12},{8,0},{12,20},{16,8},{20,28},{24,16},{28,36},{32,24},{36,44... | collective-permute-start | bytes 1044488 | tf_op jit(solution)/shard_map/ppermute | solution.py:35
  19.7 16.4 %collective-permute-start.3 = (bf16[272,640]{1,0:T(8,128)(2,1)S(1)}, bf16[272,640]{1,0:T(8,128)(2,1)S(1)}, u32[]{:S(2)}, u32[]{:S(2)}) collective-permute-start(bf16[272,640]{1,0:T(8,128)(2,1)S(1)} %collective-permute-done.1.refs_3_), channel_id=1, source_target_pairs={{0,8},{8,16},{12,4},{16,24},{20,12},{24,32},{28,20},{32,40},{36,28... | collective-permute-start | bytes 1044488 | tf_op jit(solution)/shard_map/ppermute | solution.py:35
  25.8 13.1 %collective-permute-start.14 = (bf16[320,640]{1,0:T(8,128)(2,1)}, bf16[320,640]{1,0:T(8,128)(2,1)S(1)}, u32[]{:S(2)}, u32[]{:S(2)}) collective-permute-start(bf16[320,640]{1,0:T(8,128)(2,1)} %get-tuple-element.49), channel_id=1, source_target_pairs={{0,3},{1,0},{2,1},{3,2},{4,7},{5,4},{6,5},{7,6},{8,11},{9,8},{10,9... | collective-permute-start | bytes 1228808 | tf_op jit(solution)/shard_map/ppermute | solution.py:22
  28.9 10.0 %collective-permute-start.6 = (bf16[272,640]{1,0:T(8,128)(2,1)}, bf16[272,640]{1,0:T(8,128)(2,1)S(1)}, u32[]{:S(2)}, u32[]{:S(2)}) collective-permute-start(bf16[272,640]{1,0:T(8,128)(2,1)} %get-tuple-element.50.kv_in), channel_id=1, source_target_pairs={{4,24},{12,32},{20,40},{24,4},{28,48},{32,12},{36,56},{40,20},{44,... | collective-permute-start | bytes 1044488 | tf_op jit(solution)/shard_map/ppermute | solution.py:46
  30.8 1.9 %copy-start.2 = (bf16[1280,1280]{1,0:T(8,128)(2,1)S(1)}, bf16[1280,1280]{1,0:T(8,128)(2,1)}, u32[]{:S(2)}) copy-start(bf16[1280,1280]{1,0:T(8,128)(2,1)} %w_down_in.1) | copy-start | bytes 9830404
  32.7 1.1 copy-start.7
  33.8 1.0 copy-start.8
  34.8 6.3 %copy-start.10 = (s32[2]{0:T(128)S(1)}, s32[2]{0:T(128)}, u32[]{:S(2)}) copy-start(s32[2]{0:T(128)} %ids_ref.5) | copy-start | bytes 28
  34.8 25.8 %copy-start.3 = (bf16[1280,1280]{1,0:T(8,128)(2,1)S(1)}, bf16[1280,1280]{1,0:T(8,128)(2,1)}, u32[]{:S(2)}) copy-start(bf16[1280,1280]{1,0:T(8,128)(2,1)} %refs_8_.1) | copy-start | bytes 9830404
  35.5 25.1 %copy-start.1 = (bf16[320,1280]{1,0:T(8,128)(2,1)S(1)}, bf16[320,1280]{1,0:T(8,128)(2,1)}, u32[]{:S(2)}) copy-start(bf16[320,1280]{1,0:T(8,128)(2,1)} %w_out_ref.1) | copy-start | bytes 2457604
  35.5 25.1 %copy-start.4 = (bf16[256,1280]{1,0:T(8,128)(2,1)S(1)}, bf16[256,1280]{1,0:T(8,128)(2,1)}, u32[]{:S(2)}) copy-start(bf16[256,1280]{1,0:T(8,128)(2,1)} %refs_6_.1) | copy-start | bytes 1966084
  35.5 25.1 %copy-start.9 = (f32[1280]{0:T(1024)S(1)}, f32[1280]{0:T(1024)}, u32[]{:S(2)}) copy-start(f32[1280]{0:T(1024)} %refs_7_.1) | copy-start | bytes 15364
  35.5 3.9 %collective-permute-start.8 = (bf16[272,640]{1,0:T(8,128)(2,1)S(1)}, bf16[272,640]{1,0:T(8,128)(2,1)S(1)}, u32[]{:S(2)}, u32[]{:S(2)}) collective-permute-start(bf16[272,640]{1,0:T(8,128)(2,1)S(1)} %collective-permute-done.refs_1_), channel_id=1, source_target_pairs={{0,4},{4,0},{8,12},{12,8},{16,20},{20,16},{24,28},{28,24},{32,36},... | collective-permute-start | bytes 1044488 | tf_op jit(solution)/shard_map/ppermute | solution.py:40
  35.6 3.9 %collective-permute-start.9 = (bf16[272,640]{1,0:T(8,128)(2,1)S(1)}, bf16[272,640]{1,0:T(8,128)(2,1)S(1)}, u32[]{:S(2)}, u32[]{:S(2)}) collective-permute-start(bf16[272,640]{1,0:T(8,128)(2,1)S(1)} %get-tuple-element.54.refs_2_), channel_id=1, source_target_pairs={{0,4},{4,0},{8,12},{12,8},{16,20},{20,16},{24,28},{28,24},{32,36},... | collective-permute-start | bytes 1044488 | tf_op jit(solution)/shard_map/ppermute | solution.py:40
  36.1 3.8 %collective-permute-start.10 = (bf16[272,640]{1,0:T(8,128)(2,1)S(1)}, bf16[272,640]{1,0:T(8,128)(2,1)S(1)}, u32[]{:S(2)}, u32[]{:S(2)}) collective-permute-start(bf16[272,640]{1,0:T(8,128)(2,1)S(1)} %collective-permute-done.1.refs_3_), channel_id=1, source_target_pairs={{0,4},{4,0},{8,12},{12,8},{16,20},{20,16},{24,28},{28,24},{32,36},... | collective-permute-start | bytes 1044488 | tf_op jit(solution)/shard_map/ppermute | solution.py:40
  38.9 1.7 %collective-permute-start.7 = (bf16[272,640]{1,0:T(8,128)(2,1)S(1)}, bf16[272,640]{1,0:T(8,128)(2,1)S(1)}, u32[]{:S(2)}, u32[]{:S(2)}) collective-permute-start(bf16[272,640]{1,0:T(8,128)(2,1)S(1)} %collective-permute-done.2.refs_0_), channel_id=1, source_target_pairs={{0,4},{4,0},{8,12},{12,8},{16,20},{20,16},{24,28},{28,24},{32,36},... | collective-permute-start | bytes 1044488 | tf_op jit(solution)/shard_map/ppermute | solution.py:40
  38.9 2.2 %collective-permute-start.11 = (bf16[272,640]{1,0:T(8,128)(2,1)S(1)}, bf16[272,640]{1,0:T(8,128)(2,1)S(1)}, u32[]{:S(2)}, u32[]{:S(2)}) collective-permute-start(bf16[272,640]{1,0:T(8,128)(2,1)S(1)} %collective-permute-done.3.refs_4_), channel_id=1, source_target_pairs={{0,4},{4,0},{8,12},{12,8},{16,20},{20,16},{24,28},{28,24},{32,36},... | collective-permute-start | bytes 1044488 | tf_op jit(solution)/shard_map/ppermute | solution.py:40
  39.4 8.1 %collective-permute-start.15 = (bf16[320,640]{1,0:T(8,128)(2,1)S(1)}, bf16[320,640]{1,0:T(8,128)(2,1)S(1)}, u32[]{:S(2)}, u32[]{:S(2)}) collective-permute-start(bf16[320,640]{1,0:T(8,128)(2,1)S(1)} %collective-permute-done.14.refs_2_), channel_id=1, source_target_pairs={{0,4},{4,0},{8,12},{12,8},{16,20},{20,16},{24,28},{28,24},{32,36},... | collective-permute-start | bytes 1228808 | tf_op jit(solution)/shard_map/ppermute | solution.py:40
  39.5 8.0 %collective-permute-start.12 = (bf16[320,640]{1,0:T(8,128)(2,1)S(1)}, bf16[320,640]{1,0:T(8,128)(2,1)S(1)}, u32[]{:S(2)}, u32[]{:S(2)}) collective-permute-start(bf16[320,640]{1,0:T(8,128)(2,1)S(1)} %collective-permute-done.5.refs_0_), channel_id=1, source_target_pairs={{0,4},{4,0},{8,12},{12,8},{16,20},{20,16},{24,28},{28,24},{32,36},... | collective-permute-start | bytes 1228808 | tf_op jit(solution)/shard_map/ppermute | solution.py:40
  39.9 7.6 %collective-permute-start.13 = (bf16[320,640]{1,0:T(8,128)(2,1)S(1)}, bf16[320,640]{1,0:T(8,128)(2,1)S(1)}, u32[]{:S(2)}, u32[]{:S(2)}) collective-permute-start(bf16[320,640]{1,0:T(8,128)(2,1)S(1)} %collective-permute-done.4.refs_1_), channel_id=1, source_target_pairs={{0,4},{4,0},{8,12},{12,8},{16,20},{20,16},{24,28},{28,24},{32,36},... | collective-permute-start | bytes 1228808 | tf_op jit(solution)/shard_map/ppermute | solution.py:40
  47.5 12.4 %collective-permute-start.16 = (bf16[256,320]{1,0:T(8,128)(2,1)S(1)}, bf16[256,320]{1,0:T(8,128)(2,1)S(1)}, u32[]{:S(2)}, u32[]{:S(2)}) collective-permute-start(bf16[256,320]{1,0:T(8,128)(2,1)S(1)} %get-tuple-element.61.att0), channel_id=1, source_target_pairs={{0,1},{1,2},{2,3},{3,0},{4,5},{5,6},{6,7},{7,4},{8,9},{9,10},{10,1... | collective-permute-start | bytes 491528 | tf_op jit(solution)/shard_map/ppermute | solution.py:22
  47.6 12.4 %collective-permute-start.17 = (bf16[256,320]{1,0:T(8,128)(2,1)S(1)}, bf16[256,320]{1,0:T(8,128)(2,1)S(1)}, u32[]{:S(2)}, u32[]{:S(2)}) collective-permute-start(bf16[256,320]{1,0:T(8,128)(2,1)S(1)} %get-tuple-element.61.att0), channel_id=1, source_target_pairs={{0,2},{1,3},{2,0},{3,1},{4,6},{5,7},{6,4},{7,5},{8,10},{9,11},{10,... | collective-permute-start | bytes 491528 | tf_op jit(solution)/shard_map/ppermute | solution.py:22
  49.8 10.8 %collective-permute-start.18 = (bf16[256,320]{1,0:T(8,128)(2,1)S(1)}, bf16[256,320]{1,0:T(8,128)(2,1)S(1)}, u32[]{:S(2)}, u32[]{:S(2)}) collective-permute-start(bf16[256,320]{1,0:T(8,128)(2,1)S(1)} %get-tuple-element.61.att0), channel_id=1, source_target_pairs={{0,3},{1,0},{2,1},{3,2},{4,7},{5,4},{6,5},{7,6},{8,11},{9,8},{10,9... | collective-permute-start | bytes 491528 | tf_op jit(solution)/shard_map/ppermute | solution.py:22
  60.6 29.3 %copy-start.5 = (bf16[320,4096]{1,0:T(8,128)(2,1)S(1)}, bf16[320,4096]{1,0:T(8,128)(2,1)}, u32[]{:S(2)}) copy-start(bf16[320,4096]{1,0:T(8,128)(2,1)} %w_proj_ref.1) | copy-start | bytes 7864324
  60.6 29.3 %copy-start.6 = (bf16[3,1280,320]{1,2,0:T(8,128)(2,1)S(1)}, bf16[3,1280,320]{1,2,0:T(8,128)(2,1)}, u32[]{:S(2)}) copy-start(bf16[3,1280,320]{1,2,0:T(8,128)(2,1)} %param.17) | copy-start | bytes 7372804
  66.5 7.2 %collective-permute-start.19 = (bf16[656,128]{1,0:T(8,128)(2,1)S(1)}, bf16[656,128]{1,0:T(8,128)(2,1)S(1)}, u32[]{:S(2)}, u32[]{:S(2)}) collective-permute-start(bf16[656,128]{1,0:T(8,128)(2,1)S(1)} %get-tuple-element.68), channel_id=1, source_target_pairs={{0,1},{1,2},{2,3},{3,0},{4,5},{5,6},{6,7},{7,4},{8,9},{9,10},{10,1... | collective-permute-start | bytes 503816 | tf_op jit(solution)/shard_map/ppermute | solution.py:22
  67.1 11.3 %collective-permute-start.20 = (bf16[656,128]{1,0:T(8,128)(2,1)S(1)}, bf16[656,128]{1,0:T(8,128)(2,1)S(1)}, u32[]{:S(2)}, u32[]{:S(2)}) collective-permute-start(bf16[656,128]{1,0:T(8,128)(2,1)S(1)} %get-tuple-element.69), channel_id=1, source_target_pairs={{0,2},{1,3},{2,0},{3,1},{4,6},{5,7},{6,4},{7,5},{8,10},{9,11},{10,... | collective-permute-start | bytes 503816 | tf_op jit(solution)/shard_map/ppermute | solution.py:22
  70.7 7.8 %collective-permute-start.21 = (bf16[656,128]{1,0:T(8,128)(2,1)S(1)}, bf16[656,128]{1,0:T(8,128)(2,1)S(1)}, u32[]{:S(2)}, u32[]{:S(2)}) collective-permute-start(bf16[656,128]{1,0:T(8,128)(2,1)S(1)} %get-tuple-element.70), channel_id=1, source_target_pairs={{0,3},{1,0},{2,1},{3,2},{4,7},{5,4},{6,5},{7,6},{8,11},{9,8},{10,9... | collective-permute-start | bytes 503816 | tf_op jit(solution)/shard_map/ppermute | solution.py:22
  78.6 8.6 %collective-permute-start.22 = (bf16[64,1280]{1,0:T(8,128)(2,1)S(1)}, bf16[64,1280]{1,0:T(8,128)(2,1)S(1)}, u32[]{:S(2)}, u32[]{:S(2)}) collective-permute-start(bf16[64,1280]{1,0:T(8,128)(2,1)S(1)} %get-tuple-element.71.own), channel_id=1, source_target_pairs={{0,1},{1,2},{2,3},{3,0},{4,5},{5,6},{6,7},{7,4},{8,9},{9,10},{10,1... | collective-permute-start | bytes 491528 | tf_op jit(solution)/shard_map/ppermute | solution.py:22
  78.7 11.2 %collective-permute-start.23 = (bf16[64,1280]{1,0:T(8,128)(2,1)S(1)}, bf16[64,1280]{1,0:T(8,128)(2,1)S(1)}, u32[]{:S(2)}, u32[]{:S(2)}) collective-permute-start(bf16[64,1280]{1,0:T(8,128)(2,1)S(1)} %get-tuple-element.71.own), channel_id=1, source_target_pairs={{0,2},{1,3},{2,0},{3,1},{4,6},{5,7},{6,4},{7,5},{8,10},{9,11},{10,... | collective-permute-start | bytes 491528 | tf_op jit(solution)/shard_map/ppermute | solution.py:22
  82.3 7.6 %collective-permute-start.24 = (bf16[64,1280]{1,0:T(8,128)(2,1)S(1)}, bf16[64,1280]{1,0:T(8,128)(2,1)S(1)}, u32[]{:S(2)}, u32[]{:S(2)}) collective-permute-start(bf16[64,1280]{1,0:T(8,128)(2,1)S(1)} %get-tuple-element.71.own), channel_id=1, source_target_pairs={{0,3},{1,0},{2,1},{3,2},{4,7},{5,4},{6,5},{7,6},{8,11},{9,8},{10,9... | collective-permute-start | bytes 491528 | tf_op jit(solution)/shard_map/ppermute | solution.py:22
  82.3 4.9 %collective-permute-start.25 = (bf16[16,128]{1,0:T(8,128)(2,1)S(1)}, bf16[16,128]{1,0:T(8,128)(2,1)S(1)}, u32[]{:S(2)}, u32[]{:S(2)}) collective-permute-start(bf16[16,128]{1,0:T(8,128)(2,1)S(1)} %get-tuple-element.72), channel_id=1, source_target_pairs={{0,4},{4,8},{8,12},{12,16},{16,20},{20,24},{24,28},{28,32},{32,36}... | collective-permute-start | bytes 12296 | tf_op jit(solution)/shard_map/ppermute | solution.py:27
  94.3 8.7 %collective-permute-start.26 = (bf16[32,4096]{1,0:T(8,128)(2,1)S(1)}, bf16[32,4096]{1,0:T(8,128)(2,1)S(1)}, u32[]{:S(2)}, u32[]{:S(2)}) collective-permute-start(bf16[32,4096]{1,0:T(8,128)(2,1)S(1)} %get-tuple-element.74), channel_id=1, source_target_pairs={{0,1},{1,2},{2,3},{3,0},{4,5},{5,6},{6,7},{7,4},{8,9},{9,10},{10,1... | collective-permute-start | bytes 786440 | tf_op jit(solution)/shard_map/ppermute | solution.py:22
  94.4 15.3 %collective-permute-start.27 = (bf16[32,4096]{1,0:T(8,128)(2,1)S(1)}, bf16[32,4096]{1,0:T(8,128)(2,1)S(1)}, u32[]{:S(2)}, u32[]{:S(2)}) collective-permute-start(bf16[32,4096]{1,0:T(8,128)(2,1)S(1)} %get-tuple-element.75), channel_id=1, source_target_pairs={{0,2},{1,3},{2,0},{3,1},{4,6},{5,7},{6,4},{7,5},{8,10},{9,11},{10,... | collective-permute-start | bytes 786440 | tf_op jit(solution)/shard_map/ppermute | solution.py:22
  98.0 11.7 %collective-permute-start.28 = (bf16[32,4096]{1,0:T(8,128)(2,1)S(1)}, bf16[32,4096]{1,0:T(8,128)(2,1)S(1)}, u32[]{:S(2)}, u32[]{:S(2)}) collective-permute-start(bf16[32,4096]{1,0:T(8,128)(2,1)S(1)} %get-tuple-element.76), channel_id=1, source_target_pairs={{0,3},{1,0},{2,1},{3,2},{4,7},{5,4},{6,5},{7,6},{8,11},{9,8},{10,9... | collective-permute-start | bytes 786440 | tf_op jit(solution)/shard_map/ppermute | solution.py:22

commit v6 on v5

--- a/solution.py
+++ b/solution.py
@@ -20,6 +20,12 @@
 def send_tp(value, steps):
     count = lax.axis_size(TP)
     return lax.ppermute(value, TP, [(t, (t + steps) % count) for t in range(count)])
+
+
+def send_pair(value, turn):
+    seq, count = lax.axis_size(SEQ), lax.axis_size(TP)
+    pairs = [(s * count + t, s * count + (t + turn * (-1 if s % 2 else 1)) % count) for s in range(seq) for t in range(count)]
+    return lax.ppermute(value, (SEQ, TP), pairs)
 
 
 def send_seq(value, steps):
@@ -280,7 +286,7 @@
     back, kv_late = lax.optimization_barrier((back, kv))
     five = send_five(kv_late)
     far_back, far_on = send_chip(back, 1), send_chip(on, -1)
-    w_one, w_three = send_tp(w_mine, 1), send_tp(w_mine, 3)
+    w_one, w_three = send_pair(w_mine, 1), send_pair(w_mine, -1)
     far_back, far_on, w_two, w_one, five = lax.optimization_barrier((far_back, far_on, w_two, w_one, five))
     back_again, on_again, kv_again, queries = lax.optimization_barrier((back, on, kv_held, queries))
     beside = send_partner(kv_again)
@@ -330,9 +336,9 @@
         cost_estimate=cost(4e8, 4e6),
     )(block_utt, core, tp, frames, gain_attn, w_qkv, w_out)
     (attended, joined), w_mine, w_down = attend(block_utt, core, normed, w_qkv, kv, w_mine, w_down)
-    w_other = [send_partner(piece) for piece in w_mine]
+    w_other = [send_partner(piece) for piece in reversed(w_mine)]
     attended, *w_other = lax.optimization_barrier((attended, *w_other))
-    heads = exchange([attended] * 3)
+    heads = [send_pair(attended, 1), send_tp(attended, 2), send_pair(attended, -1)]
 
     tall = share * (width // 128) + IDROWS
     resid, *parts = pl.pallas_call(

time: 112 us -> 111 us (level)
  starting transfers between devices: 43.9 us -> 42.7 us
    ppermute x0 -> x4, waiting for transfers between devices: none -> 9.68 us  [send_pair(): return lax.ppermute(value, (SEQ, TP), pairs)]
    ppermute x15 -> x11, waiting for transfers between devices: 31.3 us -> 22.3 us  [send_tp(): lax.ppermute(value, TP, [(t, (t + steps) % count) for t in range(count)])]
    ppermute x15 -> x11, starting transfers between devices: 22.4 us -> 16.6 us  [send_tp(): lax.ppermute(value, TP, [(t, (t + steps) % count) for t in range(count)])]
    ppermute x0 -> x4, starting transfers between devices: none -> 4.64 us  [send_pair(): return lax.ppermute(value, (SEQ, TP), pairs)]
  transfers between devices with their start and end apart: 29 -> 29, of which waited for: 12 -> 11; matrix products, arithmetic and copies ran while one was open for 0% -> 0% of each run, Pallas kernels for 6% -> 6%
where the time goes in v6:
time: 111 us; the launch traced here: 110 us
  starting transfers between devices  42.7 us (38%)
  waiting for transfers between devices  39.9 us (36%)
  Pallas kernels  23 us (21%)
  local copies, waits for them, and re-layouts  4.03 us (4%)
    ppermute x11, waiting for transfers between devices, send_tp(): lax.ppermute(value, TP, [(t, (t + steps) % count) for t in range(count)])  22.3 us
    ppermute x11, starting transfers between devices, send_tp(): lax.ppermute(value, TP, [(t, (t + steps) % count) for t in range(count)])  16.6 us
    ppermute x4, starting transfers between devices, send_chip(): lax.ppermute(value, SEQ, [(a, b) for a, b in pairs if 0 <= b < count])  15.9 us
    ppermute x4, waiting for transfers between devices, send_pair(): return lax.ppermute(value, (SEQ, TP), pairs)  9.68 us
    pallas_call x1, Pallas kernels, attend(): pl.pallas_call(attend_kernel, out_shape=(bf16(rows, width), jax.ShapeDtyp...  6.43 us
    pallas_call x1, Pallas kernels, shards(): pl.pallas_call(mlp_kernel, out_shape=[jax.ShapeDtypeStruct((tall, 128), j...  5.9 us
    pallas_call x1, Pallas kernels, shards(): pl.pallas_call(kv_kernel, out_shape=(scalar, scalar, bf16(rows, width), b...  4.66 us
    ppermute x4, starting transfers between devices, send_pair(): return lax.ppermute(value, (SEQ, TP), pairs)  4.64 us
  transfers between devices with their start and end apart: 29, of which 11 were waited for; matrix products, arithmetic and copies ran while one was open for 0% of the time, Pallas kernels for 6%

profile of v6, /device:TPU:70, one launch (start us, length us, event | category | flops | bytes accessed | tf_op | source)
XLA Modules:
  0.0 109.9 jit_solution(15467299980686677495)
XLA Ops:
  0.0 4.7 %shard_map.100 = (s32[1]{0:T(128)}, s32[1]{0:T(128)}, bf16[256,1280]{1,0:T(8,128)(2,1)}, bf16[272,640]{1,0:T(8,128)(2,1)}, bf16[320,640]{1,0:T(8,128)(2,1)}) custom-call(s32[2]{0:T(128)} %ids_ref.5, s32[1]{0:T(128)} %bitcast.core_ref, s32[1]{0:T(128)} %bitcast.1.tp_ref, bf16[256,1280]{1,0:T(8,128)(2,1)} %refs_6_.1, f32[1280]{0:T(1024)} %gain_ref.1, ...), custom_call_target="tpu_custom_call" | custom-call | flops 400000000 | bytes 4000000 | tf_op jit(solution)/shard_map/pallas_call | solution.py:325
  4.7 2.7 %collective-permute-start = (bf16[272,640]{1,0:T(8,128)(2,1)}, bf16[272,640]{1,0:T(8,128)(2,1)S(1)}, u32[]{:S(2)}, u32[]{:S(2)}) collective-permute-start(bf16[272,640]{1,0:T(8,128)(2,1)} %get-tuple-element.50.kv_in), channel_id=1, source_target_pairs={{4,12},{8,0},{12,20},{16,8},{20,28},{24,16},{28,36},{32,24},{36,44... | collective-permute-start | bytes 1044488 | tf_op jit(solution)/shard_map/ppermute | solution.py:41
  7.4 5.2 %collective-permute-start.1 = (bf16[272,640]{1,0:T(8,128)(2,1)}, bf16[272,640]{1,0:T(8,128)(2,1)S(1)}, u32[]{:S(2)}, u32[]{:S(2)}) collective-permute-start(bf16[272,640]{1,0:T(8,128)(2,1)} %get-tuple-element.50.kv_in), channel_id=1, source_target_pairs={{0,8},{8,16},{12,4},{16,24},{20,12},{24,32},{28,20},{32,40},{36,28... | collective-permute-start | bytes 1044488 | tf_op jit(solution)/shard_map/ppermute | solution.py:41
  12.6 3.3 %collective-permute-start.4 = (bf16[320,640]{1,0:T(8,128)(2,1)}, bf16[320,640]{1,0:T(8,128)(2,1)S(1)}, u32[]{:S(2)}, u32[]{:S(2)}) collective-permute-start(bf16[320,640]{1,0:T(8,128)(2,1)} %get-tuple-element.49), channel_id=1, source_target_pairs={{0,2},{1,3},{2,0},{3,1},{4,6},{5,7},{6,4},{7,5},{8,10},{9,11},{10,... | collective-permute-start | bytes 1228808 | tf_op jit(solution)/shard_map/ppermute | solution.py:22
  15.9 0.7 collective-permute-start.5
  16.6 1.2 %collective-permute-done.refs_1_ = bf16[272,640]{1,0:T(8,128)(2,1)S(1)} collective-permute-done((bf16[272,640]{1,0:T(8,128)(2,1)}, bf16[272,640]{1,0:T(8,128)(2,1)S(1)}, u32[]{:S(2)}, u32[]{:S(2)}) %collective-permute-start) | collective-permute-done | bytes 348192 | tf_op jit(solution)/shard_map/ppermute | solution.py:41
  17.8 1.9 %collective-permute-start.2 = (bf16[272,640]{1,0:T(8,128)(2,1)S(1)}, bf16[272,640]{1,0:T(8,128)(2,1)S(1)}, u32[]{:S(2)}, u32[]{:S(2)}) collective-permute-start(bf16[272,640]{1,0:T(8,128)(2,1)S(1)} %collective-permute-done.refs_1_), channel_id=1, source_target_pairs={{4,12},{8,0},{12,20},{16,8},{20,28},{24,16},{28,36},{32,24},{36,44... | collective-permute-start | bytes 1044488 | tf_op jit(solution)/shard_map/ppermute | solution.py:41
  19.7 0.0 collective-permute-done.1.refs_3_
  19.7 6.0 %collective-permute-start.3 = (bf16[272,640]{1,0:T(8,128)(2,1)S(1)}, bf16[272,640]{1,0:T(8,128)(2,1)S(1)}, u32[]{:S(2)}, u32[]{:S(2)}) collective-permute-start(bf16[272,640]{1,0:T(8,128)(2,1)S(1)} %collective-permute-done.1.refs_3_), channel_id=1, source_target_pairs={{0,8},{8,16},{12,4},{16,24},{20,12},{24,32},{28,20},{32,40},{36,28... | collective-permute-start | bytes 1044488 | tf_op jit(solution)/shard_map/ppermute | solution.py:41
  25.8 3.1 %collective-permute-start.12 = (bf16[320,640]{1,0:T(8,128)(2,1)}, bf16[320,640]{1,0:T(8,128)(2,1)S(1)}, u32[]{:S(2)}, u32[]{:S(2)}) collective-permute-start(bf16[320,640]{1,0:T(8,128)(2,1)} %get-tuple-element.49), channel_id=1, source_target_pairs={{0,3},{1,0},{2,1},{3,2},{4,5},{5,6},{6,7},{7,4},{8,11},{9,8},{10,9... | collective-permute-start | bytes 1228808 | tf_op jit(solution)/shard_map/ppermute | solution.py:28
  28.8 0.0 collective-permute-done.4.refs_1_
  28.9 1.9 %collective-permute-start.6 = (bf16[272,640]{1,0:T(8,128)(2,1)}, bf16[272,640]{1,0:T(8,128)(2,1)S(1)}, u32[]{:S(2)}, u32[]{:S(2)}) collective-permute-start(bf16[272,640]{1,0:T(8,128)(2,1)} %get-tuple-element.50.kv_in), channel_id=1, source_target_pairs={{4,24},{12,32},{20,40},{24,4},{28,48},{32,12},{36,56},{40,20},{44,... | collective-permute-start | bytes 1044488 | tf_op jit(solution)/shard_map/ppermute | solution.py:52
  30.8 0.0 copy-start.2
  30.8 1.9 %copy-done.2 = bf16[1280,1280]{1,0:T(8,128)(2,1)S(1)} copy-done((bf16[1280,1280]{1,0:T(8,128)(2,1)S(1)}, bf16[1280,1280]{1,0:T(8,128)(2,1)}, u32[]{:S(2)}) %copy-start.2) | copy-done | bytes 3276824
  32.7 1.1 copy-done.7
  33.8 1.0 copy-done.8
  34.8 0.7 shard_map.101
  35.5 0.0 copy-start.1
  35.5 0.0 copy-start.4
  35.5 0.0 copy-start.9
  35.5 0.0 collective-permute-done.5.refs_0_
  35.5 0.1 collective-permute-start.8
  35.6 0.0 collective-permute-done.2.refs_0_
  35.6 0.5 collective-permute-start.9
  36.1 0.0 collective-permute-done.3.refs_4_
  36.1 0.1 collective-permute-start.10
  36.2 2.7 %collective-permute-done.6.refs_10_ = bf16[272,640]{1,0:T(8,128)(2,1)S(1)} collective-permute-done((bf16[272,640]{1,0:T(8,128)(2,1)}, bf16[272,640]{1,0:T(8,128)(2,1)S(1)}, u32[]{:S(2)}, u32[]{:S(2)}) %collective-permute-start.6) | collective-permute-done | bytes 348192 | tf_op jit(solution)/shard_map/ppermute | solution.py:52
  38.9 0.0 collective-permute-start.7
  38.9 0.0 collective-permute-done.12.refs_2_
  38.9 0.5 collective-permute-start.11
  39.4 0.0 collective-permute-done.8.refs_6_
  39.4 0.1 collective-permute-start.13
  39.5 0.0 collective-permute-done.9.refs_7_
  39.5 0.4 collective-permute-start.14
  39.9 0.1 collective-permute-start.15
  40.0 0.5 collective-permute-done.7.refs_5_
  40.5 0.5 collective-permute-done.11.refs_9_
  41.0 6.4 %shard_map.102 = (bf16[256,320]{1,0:T(8,128)(2,1)S(1)}, s32[1]{0:T(128)}) custom-call(s32[2]{0:T(128)S(1)} %copy-done.10, s32[1]{0:T(128)} %get-tuple-element.42.core_ref, bf16[256,384]{1,0:T(8,128)(2,1)S(1)} %get-tuple-element.48.q_ref, bf16[272,640]{1,0:T(8,128)(2,1)S(1)} %collective-permute-done.2.refs_0_, ...), custom_call_target="tpu_custom_call" | custom-call | flops 1000000000 | bytes 4000000 | tf_op jit(solution)/shard_map/pallas_call | solution.py:295
  47.5 0.0 collective-permute-done.15.refs_5_
  47.5 0.1 collective-permute-start.16
  47.6 2.4 %collective-permute-start.17 = (bf16[256,320]{1,0:T(8,128)(2,1)S(1)}, bf16[256,320]{1,0:T(8,128)(2,1)S(1)}, u32[]{:S(2)}, u32[]{:S(2)}) collective-permute-start(bf16[256,320]{1,0:T(8,128)(2,1)S(1)} %get-tuple-element.61.att0), channel_id=1, source_target_pairs={{0,2},{1,3},{2,0},{3,1},{4,6},{5,7},{6,4},{7,5},{8,10},{9,11},{10,... | collective-permute-start | bytes 491528 | tf_op jit(solution)/shard_map/ppermute | solution.py:22
  50.0 0.8 collective-permute-start.18
  50.8 9.7 %collective-permute-done.16.att1 = bf16[256,320]{1,0:T(8,128)(2,1)S(1)} collective-permute-done((bf16[256,320]{1,0:T(8,128)(2,1)S(1)}, bf16[256,320]{1,0:T(8,128)(2,1)S(1)}, u32[]{:S(2)}, u32[]{:S(2)}) %collective-permute-start.16) | collective-permute-done | bytes 163872 | tf_op jit(solution)/shard_map/ppermute | solution.py:28
  60.5 0.0 copy-start.5
  60.5 0.0 copy-start.6
  60.6 5.9 %shard_map.103 = (f32[656,128]{1,0:T(8,128)S(1)}, bf16[656,128]{1,0:T(8,128)(2,1)S(1)}, bf16[656,128]{1,0:T(8,128)(2,1)S(1)}, bf16[656,128]{1,0:T(8,128)(2,1)S(1)}, bf16[656,128]{1,0:T(8,128)(2,1)S(1)}) custom-call(s32[1]{0:T(128)} %get-tuple-element.41.tp_ref, s32[1]{0:T(128)} %get-tuple-element.42.core_ref, bf16[256,320]{1,0:T(8,128)(2,1)S(1)} %get-tuple-element.61.att0, ...), custom_call_target="tpu_custom_call" | custom-call | flops 2500000000 | bytes 10000000 | tf_op jit(solution)/shard_map/pallas_call | solution.py:344
  66.5 0.1 collective-permute-start.19
  66.5 2.4 %collective-permute-start.20 = (bf16[656,128]{1,0:T(8,128)(2,1)S(1)}, bf16[656,128]{1,0:T(8,128)(2,1)S(1)}, u32[]{:S(2)}, u32[]{:S(2)}) collective-permute-start(bf16[656,128]{1,0:T(8,128)(2,1)S(1)} %get-tuple-element.69), channel_id=1, source_target_pairs={{0,2},{1,3},{2,0},{3,1},{4,6},{5,7},{6,4},{7,5},{8,10},{9,11},{10,... | collective-permute-start | bytes 503816 | tf_op jit(solution)/shard_map/ppermute | solution.py:22
  68.9 0.9 collective-permute-start.21
  69.8 7.9 %collective-permute-done.19.got1 = bf16[656,128]{1,0:T(8,128)(2,1)S(1)} collective-permute-done((bf16[656,128]{1,0:T(8,128)(2,1)S(1)}, bf16[656,128]{1,0:T(8,128)(2,1)S(1)}, u32[]{:S(2)}, u32[]{:S(2)}) %collective-permute-start.19) | collective-permute-done | bytes 167968 | tf_op jit(solution)/shard_map/ppermute | solution.py:22
  77.6 0.6 collective-permute-done.21.got3
  78.3 0.1 shard_map.104
  78.4 0.3 collective-permute-start.22
  78.7 3.6 %collective-permute-start.23 = (bf16[64,1280]{1,0:T(8,128)(2,1)S(1)}, bf16[64,1280]{1,0:T(8,128)(2,1)S(1)}, u32[]{:S(2)}, u32[]{:S(2)}) collective-permute-start(bf16[64,1280]{1,0:T(8,128)(2,1)S(1)} %get-tuple-element.71.own), channel_id=1, source_target_pairs={{0,2},{1,3},{2,0},{3,1},{4,6},{5,7},{6,4},{7,5},{8,10},{9,11},{10,... | collective-permute-start | bytes 491528 | tf_op jit(solution)/shard_map/ppermute | solution.py:22
  82.3 0.0 collective-permute-start.24
  82.3 1.9 %collective-permute-start.25 = (bf16[16,128]{1,0:T(8,128)(2,1)S(1)}, bf16[16,128]{1,0:T(8,128)(2,1)S(1)}, u32[]{:S(2)}, u32[]{:S(2)}) collective-permute-start(bf16[16,128]{1,0:T(8,128)(2,1)S(1)} %get-tuple-element.72), channel_id=1, source_target_pairs={{0,4},{4,8},{8,12},{12,16},{16,20},{20,24},{24,28},{28,32},{32,36}... | collective-permute-start | bytes 12296 | tf_op jit(solution)/shard_map/ppermute | solution.py:33
  84.2 3.0 %collective-permute-done.25.rim_ref = bf16[16,128]{1,0:T(8,128)(2,1)S(1)} collective-permute-done((bf16[16,128]{1,0:T(8,128)(2,1)S(1)}, bf16[16,128]{1,0:T(8,128)(2,1)S(1)}, u32[]{:S(2)}, u32[]{:S(2)}) %collective-permute-start.25) | collective-permute-done | bytes 4128 | tf_op jit(solution)/shard_map/ppermute | solution.py:33
  87.2 2.4 %collective-permute-done.23.got2 = bf16[64,1280]{1,0:T(8,128)(2,1)S(1)} collective-permute-done((bf16[64,1280]{1,0:T(8,128)(2,1)S(1)}, bf16[64,1280]{1,0:T(8,128)(2,1)S(1)}, u32[]{:S(2)}, u32[]{:S(2)}) %collective-permute-start.23) | collective-permute-done | bytes 163872 | tf_op jit(solution)/shard_map/ppermute | solution.py:22
  89.6 4.4 %shard_map.105 = (bf16[32,4096]{1,0:T(8,128)(2,1)S(1)}, bf16[32,4096]{1,0:T(8,128)(2,1)S(1)}, bf16[32,4096]{1,0:T(8,128)(2,1)S(1)}, bf16[32,4096]{1,0:T(8,128)(2,1)S(1)}) custom-call(s32[1]{0:T(128)} %get-tuple-element.41.tp_ref, s32[2]{0:T(128)S(1)} %copy-done.10, s32[1]{0:T(128)} %get-tuple-element.57.joined_ref, ...), custom_call_target="tpu_custom_call" | custom-call | flops 1000000000 | bytes 6000000 | tf_op jit(solution)/shard_map/pallas_call | solution.py:364
  94.0 0.4 collective-permute-start.26
  94.4 3.3 %collective-permute-start.27 = (bf16[32,4096]{1,0:T(8,128)(2,1)S(1)}, bf16[32,4096]{1,0:T(8,128)(2,1)S(1)}, u32[]{:S(2)}, u32[]{:S(2)}) collective-permute-start(bf16[32,4096]{1,0:T(8,128)(2,1)S(1)} %get-tuple-element.75), channel_id=1, source_target_pairs={{0,2},{1,3},{2,0},{3,1},{4,6},{5,7},{6,4},{7,5},{8,10},{9,11},{10,... | collective-permute-start | bytes 786440 | tf_op jit(solution)/shard_map/ppermute | solution.py:22
  97.7 4.9 %collective-permute-done.26.got1 = bf16[32,4096]{1,0:T(8,128)(2,1)S(1)} collective-permute-done((bf16[32,4096]{1,0:T(8,128)(2,1)S(1)}, bf16[32,4096]{1,0:T(8,128)(2,1)S(1)}, u32[]{:S(2)}, u32[]{:S(2)}) %collective-permute-start.26) | collective-permute-done | bytes 262176 | tf_op jit(solution)/shard_map/ppermute | solution.py:22
  102.6 6.5 %collective-permute-done.27.got2 = bf16[32,4096]{1,0:T(8,128)(2,1)S(1)} collective-permute-done((bf16[32,4096]{1,0:T(8,128)(2,1)S(1)}, bf16[32,4096]{1,0:T(8,128)(2,1)S(1)}, u32[]{:S(2)}, u32[]{:S(2)}) %collective-permute-start.27) | collective-permute-done | bytes 262176 | tf_op jit(solution)/shard_map/ppermute | solution.py:22
  109.1 0.8 shard_map.106
  (23 shorter events, 0.1 us)
Async XLA Ops:
  0.0 30.8 %copy-start = (bf16[3,1280,320]{1,2,0:T(8,128)(2,1)S(1)}, bf16[3,1280,320]{1,2,0:T(8,128)(2,1)}, u32[]{:S(2)}) copy-start(bf16[3,1280,320]{1,2,0:T(8,128)(2,1)} %param.12) | copy-start | bytes 7372804
  4.7 13.1 %collective-permute-start = (bf16[272,640]{1,0:T(8,128)(2,1)}, bf16[272,640]{1,0:T(8,128)(2,1)S(1)}, u32[]{:S(2)}, u32[]{:S(2)}) collective-permute-start(bf16[272,640]{1,0:T(8,128)(2,1)} %get-tuple-element.50.kv_in), channel_id=1, source_target_pairs={{4,12},{8,0},{12,20},{16,8},{20,28},{24,16},{28,36},{32,24},{36,44... | collective-permute-start | bytes 1044488 | tf_op jit(solution)/shard_map/ppermute | solution.py:41
  7.4 12.3 %collective-permute-start.1 = (bf16[272,640]{1,0:T(8,128)(2,1)}, bf16[272,640]{1,0:T(8,128)(2,1)S(1)}, u32[]{:S(2)}, u32[]{:S(2)}) collective-permute-start(bf16[272,640]{1,0:T(8,128)(2,1)} %get-tuple-element.50.kv_in), channel_id=1, source_target_pairs={{0,8},{8,16},{12,4},{16,24},{20,12},{24,32},{28,20},{32,40},{36,28... | collective-permute-start | bytes 1044488 | tf_op jit(solution)/shard_map/ppermute | solution.py:41
  12.6 16.2 %collective-permute-start.4 = (bf16[320,640]{1,0:T(8,128)(2,1)}, bf16[320,640]{1,0:T(8,128)(2,1)S(1)}, u32[]{:S(2)}, u32[]{:S(2)}) collective-permute-start(bf16[320,640]{1,0:T(8,128)(2,1)} %get-tuple-element.49), channel_id=1, source_target_pairs={{0,2},{1,3},{2,0},{3,1},{4,6},{5,7},{6,4},{7,5},{8,10},{9,11},{10,... | collective-permute-start | bytes 1228808 | tf_op jit(solution)/shard_map/ppermute | solution.py:22
  15.9 19.6 %collective-permute-start.5 = (bf16[320,640]{1,0:T(8,128)(2,1)}, bf16[320,640]{1,0:T(8,128)(2,1)S(1)}, u32[]{:S(2)}, u32[]{:S(2)}) collective-permute-start(bf16[320,640]{1,0:T(8,128)(2,1)} %get-tuple-element.49), channel_id=1, source_target_pairs={{0,1},{1,2},{2,3},{3,0},{4,7},{5,4},{6,5},{7,6},{8,9},{9,10},{10,1... | collective-permute-start | bytes 1228808 | tf_op jit(solution)/shard_map/ppermute | solution.py:28
  17.8 17.8 %collective-permute-start.2 = (bf16[272,640]{1,0:T(8,128)(2,1)S(1)}, bf16[272,640]{1,0:T(8,128)(2,1)S(1)}, u32[]{:S(2)}, u32[]{:S(2)}) collective-permute-start(bf16[272,640]{1,0:T(8,128)(2,1)S(1)} %collective-permute-done.refs_1_), channel_id=1, source_target_pairs={{4,12},{8,0},{12,20},{16,8},{20,28},{24,16},{28,36},{32,24},{36,44... | collective-permute-start | bytes 1044488 | tf_op jit(solution)/shard_map/ppermute | solution.py:41
  19.7 16.4 %collective-permute-start.3 = (bf16[272,640]{1,0:T(8,128)(2,1)S(1)}, bf16[272,640]{1,0:T(8,128)(2,1)S(1)}, u32[]{:S(2)}, u32[]{:S(2)}) collective-permute-start(bf16[272,640]{1,0:T(8,128)(2,1)S(1)} %collective-permute-done.1.refs_3_), channel_id=1, source_target_pairs={{0,8},{8,16},{12,4},{16,24},{20,12},{24,32},{28,20},{32,40},{36,28... | collective-permute-start | bytes 1044488 | tf_op jit(solution)/shard_map/ppermute | solution.py:41
  25.8 13.1 %collective-permute-start.12 = (bf16[320,640]{1,0:T(8,128)(2,1)}, bf16[320,640]{1,0:T(8,128)(2,1)S(1)}, u32[]{:S(2)}, u32[]{:S(2)}) collective-permute-start(bf16[320,640]{1,0:T(8,128)(2,1)} %get-tuple-element.49), channel_id=1, source_target_pairs={{0,3},{1,0},{2,1},{3,2},{4,5},{5,6},{6,7},{7,4},{8,11},{9,8},{10,9... | collective-permute-start | bytes 1228808 | tf_op jit(solution)/shard_map/ppermute | solution.py:28
  28.9 10.0 %collective-permute-start.6 = (bf16[272,640]{1,0:T(8,128)(2,1)}, bf16[272,640]{1,0:T(8,128)(2,1)S(1)}, u32[]{:S(2)}, u32[]{:S(2)}) collective-permute-start(bf16[272,640]{1,0:T(8,128)(2,1)} %get-tuple-element.50.kv_in), channel_id=1, source_target_pairs={{4,24},{12,32},{20,40},{24,4},{28,48},{32,12},{36,56},{40,20},{44,... | collective-permute-start | bytes 1044488 | tf_op jit(solution)/shard_map/ppermute | solution.py:52
  30.8 1.9 %copy-start.2 = (bf16[1280,1280]{1,0:T(8,128)(2,1)S(1)}, bf16[1280,1280]{1,0:T(8,128)(2,1)}, u32[]{:S(2)}) copy-start(bf16[1280,1280]{1,0:T(8,128)(2,1)} %w_down_in.1) | copy-start | bytes 9830404
  32.7 1.1 copy-start.7
  33.8 1.0 copy-start.8
  34.8 6.3 %copy-start.10 = (s32[2]{0:T(128)S(1)}, s32[2]{0:T(128)}, u32[]{:S(2)}) copy-start(s32[2]{0:T(128)} %ids_ref.5) | copy-start | bytes 28
  34.8 25.7 %copy-start.3 = (bf16[1280,1280]{1,0:T(8,128)(2,1)S(1)}, bf16[1280,1280]{1,0:T(8,128)(2,1)}, u32[]{:S(2)}) copy-start(bf16[1280,1280]{1,0:T(8,128)(2,1)} %refs_8_.1) | copy-start | bytes 9830404
  35.5 25.0 %copy-start.1 = (bf16[320,1280]{1,0:T(8,128)(2,1)S(1)}, bf16[320,1280]{1,0:T(8,128)(2,1)}, u32[]{:S(2)}) copy-start(bf16[320,1280]{1,0:T(8,128)(2,1)} %w_out_ref.1) | copy-start | bytes 2457604
  35.5 25.0 %copy-start.4 = (bf16[256,1280]{1,0:T(8,128)(2,1)S(1)}, bf16[256,1280]{1,0:T(8,128)(2,1)}, u32[]{:S(2)}) copy-start(bf16[256,1280]{1,0:T(8,128)(2,1)} %refs_6_.1) | copy-start | bytes 1966084
  35.5 25.0 %copy-start.9 = (f32[1280]{0:T(1024)S(1)}, f32[1280]{0:T(1024)}, u32[]{:S(2)}) copy-start(f32[1280]{0:T(1024)} %refs_7_.1) | copy-start | bytes 15364
  35.5 3.9 %collective-permute-start.8 = (bf16[272,640]{1,0:T(8,128)(2,1)S(1)}, bf16[272,640]{1,0:T(8,128)(2,1)S(1)}, u32[]{:S(2)}, u32[]{:S(2)}) collective-permute-start(bf16[272,640]{1,0:T(8,128)(2,1)S(1)} %collective-permute-done.refs_1_), channel_id=1, source_target_pairs={{0,4},{4,0},{8,12},{12,8},{16,20},{20,16},{24,28},{28,24},{32,36},... | collective-permute-start | bytes 1044488 | tf_op jit(solution)/shard_map/ppermute | solution.py:46
  35.6 3.9 %collective-permute-start.9 = (bf16[272,640]{1,0:T(8,128)(2,1)S(1)}, bf16[272,640]{1,0:T(8,128)(2,1)S(1)}, u32[]{:S(2)}, u32[]{:S(2)}) collective-permute-start(bf16[272,640]{1,0:T(8,128)(2,1)S(1)} %get-tuple-element.54.refs_2_), channel_id=1, source_target_pairs={{0,4},{4,0},{8,12},{12,8},{16,20},{20,16},{24,28},{28,24},{32,36},... | collective-permute-start | bytes 1044488 | tf_op jit(solution)/shard_map/ppermute | solution.py:46
  36.1 3.8 %collective-permute-start.10 = (bf16[272,640]{1,0:T(8,128)(2,1)S(1)}, bf16[272,640]{1,0:T(8,128)(2,1)S(1)}, u32[]{:S(2)}, u32[]{:S(2)}) collective-permute-start(bf16[272,640]{1,0:T(8,128)(2,1)S(1)} %collective-permute-done.1.refs_3_), channel_id=1, source_target_pairs={{0,4},{4,0},{8,12},{12,8},{16,20},{20,16},{24,28},{28,24},{32,36},... | collective-permute-start | bytes 1044488 | tf_op jit(solution)/shard_map/ppermute | solution.py:46
  38.9 1.7 %collective-permute-start.7 = (bf16[272,640]{1,0:T(8,128)(2,1)S(1)}, bf16[272,640]{1,0:T(8,128)(2,1)S(1)}, u32[]{:S(2)}, u32[]{:S(2)}) collective-permute-start(bf16[272,640]{1,0:T(8,128)(2,1)S(1)} %collective-permute-done.2.refs_0_), channel_id=1, source_target_pairs={{0,4},{4,0},{8,12},{12,8},{16,20},{20,16},{24,28},{28,24},{32,36},... | collective-permute-start | bytes 1044488 | tf_op jit(solution)/shard_map/ppermute | solution.py:46
  38.9 2.2 %collective-permute-start.11 = (bf16[272,640]{1,0:T(8,128)(2,1)S(1)}, bf16[272,640]{1,0:T(8,128)(2,1)S(1)}, u32[]{:S(2)}, u32[]{:S(2)}) collective-permute-start(bf16[272,640]{1,0:T(8,128)(2,1)S(1)} %collective-permute-done.3.refs_4_), channel_id=1, source_target_pairs={{0,4},{4,0},{8,12},{12,8},{16,20},{20,16},{24,28},{28,24},{32,36},... | collective-permute-start | bytes 1044488 | tf_op jit(solution)/shard_map/ppermute | solution.py:46
  39.4 8.1 %collective-permute-start.13 = (bf16[320,640]{1,0:T(8,128)(2,1)S(1)}, bf16[320,640]{1,0:T(8,128)(2,1)S(1)}, u32[]{:S(2)}, u32[]{:S(2)}) collective-permute-start(bf16[320,640]{1,0:T(8,128)(2,1)S(1)} %collective-permute-done.12.refs_2_), channel_id=1, source_target_pairs={{0,4},{4,0},{8,12},{12,8},{16,20},{20,16},{24,28},{28,24},{32,36},... | collective-permute-start | bytes 1228808 | tf_op jit(solution)/shard_map/ppermute | solution.py:46
  39.5 8.0 %collective-permute-start.14 = (bf16[320,640]{1,0:T(8,128)(2,1)S(1)}, bf16[320,640]{1,0:T(8,128)(2,1)S(1)}, u32[]{:S(2)}, u32[]{:S(2)}) collective-permute-start(bf16[320,640]{1,0:T(8,128)(2,1)S(1)} %collective-permute-done.4.refs_1_), channel_id=1, source_target_pairs={{0,4},{4,0},{8,12},{12,8},{16,20},{20,16},{24,28},{28,24},{32,36},... | collective-permute-start | bytes 1228808 | tf_op jit(solution)/shard_map/ppermute | solution.py:46
  39.9 7.6 %collective-permute-start.15 = (bf16[320,640]{1,0:T(8,128)(2,1)S(1)}, bf16[320,640]{1,0:T(8,128)(2,1)S(1)}, u32[]{:S(2)}, u32[]{:S(2)}) collective-permute-start(bf16[320,640]{1,0:T(8,128)(2,1)S(1)} %collective-permute-done.5.refs_0_), channel_id=1, source_target_pairs={{0,4},{4,0},{8,12},{12,8},{16,20},{20,16},{24,28},{28,24},{32,36},... | collective-permute-start | bytes 1228808 | tf_op jit(solution)/shard_map/ppermute | solution.py:46
  47.5 13.0 %collective-permute-start.16 = (bf16[256,320]{1,0:T(8,128)(2,1)S(1)}, bf16[256,320]{1,0:T(8,128)(2,1)S(1)}, u32[]{:S(2)}, u32[]{:S(2)}) collective-permute-start(bf16[256,320]{1,0:T(8,128)(2,1)S(1)} %get-tuple-element.61.att0), channel_id=1, source_target_pairs={{0,1},{1,2},{2,3},{3,0},{4,7},{5,4},{6,5},{7,6},{8,9},{9,10},{10,1... | collective-permute-start | bytes 491528 | tf_op jit(solution)/shard_map/ppermute | solution.py:28
  47.6 12.9 %collective-permute-start.17 = (bf16[256,320]{1,0:T(8,128)(2,1)S(1)}, bf16[256,320]{1,0:T(8,128)(2,1)S(1)}, u32[]{:S(2)}, u32[]{:S(2)}) collective-permute-start(bf16[256,320]{1,0:T(8,128)(2,1)S(1)} %get-tuple-element.61.att0), channel_id=1, source_target_pairs={{0,2},{1,3},{2,0},{3,1},{4,6},{5,7},{6,4},{7,5},{8,10},{9,11},{10,... | collective-permute-start | bytes 491528 | tf_op jit(solution)/shard_map/ppermute | solution.py:22
  50.0 10.5 %collective-permute-start.18 = (bf16[256,320]{1,0:T(8,128)(2,1)S(1)}, bf16[256,320]{1,0:T(8,128)(2,1)S(1)}, u32[]{:S(2)}, u32[]{:S(2)}) collective-permute-start(bf16[256,320]{1,0:T(8,128)(2,1)S(1)} %get-tuple-element.61.att0), channel_id=1, source_target_pairs={{0,3},{1,0},{2,1},{3,2},{4,5},{5,6},{6,7},{7,4},{8,11},{9,8},{10,9... | collective-permute-start | bytes 491528 | tf_op jit(solution)/shard_map/ppermute | solution.py:28
  60.5 29.0 %copy-start.5 = (bf16[320,4096]{1,0:T(8,128)(2,1)S(1)}, bf16[320,4096]{1,0:T(8,128)(2,1)}, u32[]{:S(2)}) copy-start(bf16[320,4096]{1,0:T(8,128)(2,1)} %w_proj_ref.1) | copy-start | bytes 7864324
  60.5 29.0 %copy-start.6 = (bf16[3,1280,320]{1,2,0:T(8,128)(2,1)S(1)}, bf16[3,1280,320]{1,2,0:T(8,128)(2,1)}, u32[]{:S(2)}) copy-start(bf16[3,1280,320]{1,2,0:T(8,128)(2,1)} %param.17) | copy-start | bytes 7372804
  66.5 11.2 %collective-permute-start.19 = (bf16[656,128]{1,0:T(8,128)(2,1)S(1)}, bf16[656,128]{1,0:T(8,128)(2,1)S(1)}, u32[]{:S(2)}, u32[]{:S(2)}) collective-permute-start(bf16[656,128]{1,0:T(8,128)(2,1)S(1)} %get-tuple-element.68), channel_id=1, source_target_pairs={{0,1},{1,2},{2,3},{3,0},{4,5},{5,6},{6,7},{7,4},{8,9},{9,10},{10,1... | collective-permute-start | bytes 503816 | tf_op jit(solution)/shard_map/ppermute | solution.py:22
  66.5 11.1 %collective-permute-start.20 = (bf16[656,128]{1,0:T(8,128)(2,1)S(1)}, bf16[656,128]{1,0:T(8,128)(2,1)S(1)}, u32[]{:S(2)}, u32[]{:S(2)}) collective-permute-start(bf16[656,128]{1,0:T(8,128)(2,1)S(1)} %get-tuple-element.69), channel_id=1, source_target_pairs={{0,2},{1,3},{2,0},{3,1},{4,6},{5,7},{6,4},{7,5},{8,10},{9,11},{10,... | collective-permute-start | bytes 503816 | tf_op jit(solution)/shard_map/ppermute | solution.py:22
  68.9 9.4 %collective-permute-start.21 = (bf16[656,128]{1,0:T(8,128)(2,1)S(1)}, bf16[656,128]{1,0:T(8,128)(2,1)S(1)}, u32[]{:S(2)}, u32[]{:S(2)}) collective-permute-start(bf16[656,128]{1,0:T(8,128)(2,1)S(1)} %get-tuple-element.70), channel_id=1, source_target_pairs={{0,3},{1,0},{2,1},{3,2},{4,7},{5,4},{6,5},{7,6},{8,11},{9,8},{10,9... | collective-permute-start | bytes 503816 | tf_op jit(solution)/shard_map/ppermute | solution.py:22
  78.4 8.8 %collective-permute-start.22 = (bf16[64,1280]{1,0:T(8,128)(2,1)S(1)}, bf16[64,1280]{1,0:T(8,128)(2,1)S(1)}, u32[]{:S(2)}, u32[]{:S(2)}) collective-permute-start(bf16[64,1280]{1,0:T(8,128)(2,1)S(1)} %get-tuple-element.71.own), channel_id=1, source_target_pairs={{0,1},{1,2},{2,3},{3,0},{4,5},{5,6},{6,7},{7,4},{8,9},{9,10},{10,1... | collective-permute-start | bytes 491528 | tf_op jit(solution)/shard_map/ppermute | solution.py:22
  78.7 10.9 %collective-permute-start.23 = (bf16[64,1280]{1,0:T(8,128)(2,1)S(1)}, bf16[64,1280]{1,0:T(8,128)(2,1)S(1)}, u32[]{:S(2)}, u32[]{:S(2)}) collective-permute-start(bf16[64,1280]{1,0:T(8,128)(2,1)S(1)} %get-tuple-element.71.own), channel_id=1, source_target_pairs={{0,2},{1,3},{2,0},{3,1},{4,6},{5,7},{6,4},{7,5},{8,10},{9,11},{10,... | collective-permute-start | bytes 491528 | tf_op jit(solution)/shard_map/ppermute | solution.py:22
  82.3 7.3 %collective-permute-start.24 = (bf16[64,1280]{1,0:T(8,128)(2,1)S(1)}, bf16[64,1280]{1,0:T(8,128)(2,1)S(1)}, u32[]{:S(2)}, u32[]{:S(2)}) collective-permute-start(bf16[64,1280]{1,0:T(8,128)(2,1)S(1)} %get-tuple-element.71.own), channel_id=1, source_target_pairs={{0,3},{1,0},{2,1},{3,2},{4,7},{5,4},{6,5},{7,6},{8,11},{9,8},{10,9... | collective-permute-start | bytes 491528 | tf_op jit(solution)/shard_map/ppermute | solution.py:22
  82.3 4.9 %collective-permute-start.25 = (bf16[16,128]{1,0:T(8,128)(2,1)S(1)}, bf16[16,128]{1,0:T(8,128)(2,1)S(1)}, u32[]{:S(2)}, u32[]{:S(2)}) collective-permute-start(bf16[16,128]{1,0:T(8,128)(2,1)S(1)} %get-tuple-element.72), channel_id=1, source_target_pairs={{0,4},{4,8},{8,12},{12,16},{16,20},{20,24},{24,28},{28,32},{32,36}... | collective-permute-start | bytes 12296 | tf_op jit(solution)/shard_map/ppermute | solution.py:33
  94.0 8.6 %collective-permute-start.26 = (bf16[32,4096]{1,0:T(8,128)(2,1)S(1)}, bf16[32,4096]{1,0:T(8,128)(2,1)S(1)}, u32[]{:S(2)}, u32[]{:S(2)}) collective-permute-start(bf16[32,4096]{1,0:T(8,128)(2,1)S(1)} %get-tuple-element.74), channel_id=1, source_target_pairs={{0,1},{1,2},{2,3},{3,0},{4,5},{5,6},{6,7},{7,4},{8,9},{9,10},{10,1... | collective-permute-start | bytes 786440 | tf_op jit(solution)/shard_map/ppermute | solution.py:22
  94.4 14.7 %collective-permute-start.27 = (bf16[32,4096]{1,0:T(8,128)(2,1)S(1)}, bf16[32,4096]{1,0:T(8,128)(2,1)S(1)}, u32[]{:S(2)}, u32[]{:S(2)}) collective-permute-start(bf16[32,4096]{1,0:T(8,128)(2,1)S(1)} %get-tuple-element.75), channel_id=1, source_target_pairs={{0,2},{1,3},{2,0},{3,1},{4,6},{5,7},{6,4},{7,5},{8,10},{9,11},{10,... | collective-permute-start | bytes 786440 | tf_op jit(solution)/shard_map/ppermute | solution.py:22
  97.7 11.4 %collective-permute-start.28 = (bf16[32,4096]{1,0:T(8,128)(2,1)S(1)}, bf16[32,4096]{1,0:T(8,128)(2,1)S(1)}, u32[]{:S(2)}, u32[]{:S(2)}) collective-permute-start(bf16[32,4096]{1,0:T(8,128)(2,1)S(1)} %get-tuple-element.76), channel_id=1, source_target_pairs={{0,3},{1,0},{2,1},{3,2},{4,7},{5,4},{6,5},{7,6},{8,11},{9,8},{10,9... | collective-permute-start | bytes 786440 | tf_op jit(solution)/shard_map/ppermute | solution.py:22

commit v7 on v6

--- a/solution.py
+++ b/solution.py
@@ -72,8 +72,8 @@
 
 
 def kv_kernel(ids_ref, core_ref, tp_ref, frames_hbm, gain_ref, w_hbm, w_out_hbm,
-              core_out, tp_out, normed_ref, kv_ref, w_mine_ref,
-              frames_ref, w_ref, sems):
+              core_out, tp_out, normed_out, kv_ref, w_mine_ref,
+              frames_ref, w_ref, normed_ref, sems):
     rows = frames_ref.shape[0]
     core_out[0] = core_ref[0]
     tp_out[0] = tp_ref[0]
@@ -87,6 +87,8 @@
     copies[0].wait()
     normed = layer_norm(frames_ref[...].astype(jnp.float32), gain_ref[...][None]).astype(jnp.bfloat16)
     normed_ref[...] = normed
+    copies.append(pltpu.make_async_copy(normed_ref, normed_out, sems.at[4]))
+    copies[4].start()
     copies[1].wait()
     keys = dot_t(normed, w_ref[0]).astype(jnp.bfloat16)
     copies[2].wait()
@@ -99,6 +101,7 @@
     marks = jnp.where(row == 0, ids_ref[0] + 1, jnp.where(row == 1, ids_ref[1] + 1, 0))
     kv_ref[rows:, :] = marks.astype(jnp.float32).astype(jnp.bfloat16)
     copies[3].wait()
+    copies[4].wait()
 
 
 def attend_kernel(ids_ref, core_ref, q_ref, *refs):
@@ -229,10 +232,11 @@
     same_block = ids_ref[0] == ids_ref[1]
     cut = jnp.where(same_block, -1, count // 2)
     one = lambda flag: jnp.where(flag, 1.0, 0.0).astype(jnp.bfloat16)
-    pick = lambda flag, source: dot(one(flag), source).astype(jnp.bfloat16)
-    even = pick(r == 2 * j, rows)
-    odd = pick(r == 2 * j + 1, rows)
-    before = dot(one((r == 2 * j - 1) & (j != cut)), rows)
+    picks = [one(r == 2 * j), one(r == 2 * j + 1), one((r == 2 * j - 1) & (j != cut))]
+    picked = dot(jnp.concatenate(picks, axis=0), rows)
+    even = picked[:count].astype(jnp.bfloat16)
+    odd = picked[count:2 * count].astype(jnp.bfloat16)
+    before = picked[2 * count:]
     rim = rim_ref[...].astype(jnp.float32)
     rim = jnp.concatenate([rim[g:g + 1] for g in range(before.shape[1] // 128)], axis=1)
     rim_first = jnp.where(joined_ref[0] == 1, 0, -1)
@@ -326,11 +330,12 @@
         kv_kernel,
         out_shape=(scalar, scalar, bf16(rows, width), bf16(rows + IDROWS, 2 * w_qkv.shape[1]), bf16(w_out.shape[0], width // 2)),
         in_specs=[SMEM, SMEM, SMEM, HBM, VMEM, HBM, HBM],
-        out_specs=(SMEM, SMEM, VMEM, VMEM, VMEM),
+        out_specs=(SMEM, SMEM, ANY, VMEM, VMEM),
         scratch_shapes=[
             pltpu.VMEM((rows, width), jnp.bfloat16),
             pltpu.VMEM((2,) + w_qkv.shape[1:], jnp.bfloat16),
-            pltpu.SemaphoreType.DMA((4,)),
+            pltpu.VMEM((rows, width), jnp.bfloat16),
+            pltpu.SemaphoreType.DMA((5,)),
         ],
         compiler_params=params(56),
         cost_estimate=cost(4e8, 4e6),

time: 111 us -> 111 us (level)
  no operation moved by 1% of the time
where the time goes in v7:
time: 111 us; the launch traced here: 110 us
  starting transfers between devices  42.7 us (38%)
  waiting for transfers between devices  39.9 us (36%)
  Pallas kernels  22.6 us (20%)
  local copies, waits for them, and re-layouts  4.03 us (4%)
    ppermute x11, waiting for transfers between devices, send_tp(): lax.ppermute(value, TP, [(t, (t + steps) % count) for t in range(count)])  22.3 us
    ppermute x11, starting transfers between devices, send_tp(): lax.ppermute(value, TP, [(t, (t + steps) % count) for t in range(count)])  16.6 us
    ppermute x4, starting transfers between devices, send_chip(): lax.ppermute(value, SEQ, [(a, b) for a, b in pairs if 0 <= b < count])  15.9 us
    ppermute x4, waiting for transfers between devices, send_pair(): return lax.ppermute(value, (SEQ, TP), pairs)  9.67 us
    pallas_call x1, Pallas kernels, attend(): pl.pallas_call(attend_kernel, out_shape=(bf16(rows, width), jax.ShapeDtyp...  6.43 us
    pallas_call x1, Pallas kernels, shards(): pl.pallas_call(mlp_kernel, out_shape=[jax.ShapeDtypeStruct((tall, 128), j...  5.9 us
    ppermute x4, starting transfers between devices, send_pair(): return lax.ppermute(value, (SEQ, TP), pairs)  4.64 us
    pallas_call x1, Pallas kernels, shards(): pl.pallas_call(kv_kernel, out_shape=(scalar, scalar, bf16(rows, width), b...  4.47 us
  transfers between devices with their start and end apart: 29, of which 11 were waited for; matrix products, arithmetic and copies ran while one was open for 0% of the time, Pallas kernels for 6%

profile of v7, /device:TPU:70, one launch (start us, length us, event | category | flops | bytes accessed | tf_op | source)
XLA Modules:
  0.0 109.5 jit_solution(13758329610742141752)
XLA Ops:
  0.0 4.5 %shard_map.100 = (s32[1]{0:T(128)}, s32[1]{0:T(128)}, bf16[256,1280]{1,0:T(8,128)(2,1)}, bf16[272,640]{1,0:T(8,128)(2,1)}, bf16[320,640]{1,0:T(8,128)(2,1)}) custom-call(s32[2]{0:T(128)} %ids_ref.5, s32[1]{0:T(128)} %bitcast.core_ref, s32[1]{0:T(128)} %bitcast.1.tp_ref, bf16[256,1280]{1,0:T(8,128)(2,1)} %refs_6_.1, f32[1280]{0:T(1024)} %gain_ref.1, ...), custom_call_target="tpu_custom_call" | custom-call | flops 400000000 | bytes 4000000 | tf_op jit(solution)/shard_map/pallas_call | solution.py:329
  4.5 2.7 %collective-permute-start = (bf16[272,640]{1,0:T(8,128)(2,1)}, bf16[272,640]{1,0:T(8,128)(2,1)S(1)}, u32[]{:S(2)}, u32[]{:S(2)}) collective-permute-start(bf16[272,640]{1,0:T(8,128)(2,1)} %get-tuple-element.50.kv_in), channel_id=1, source_target_pairs={{4,12},{8,0},{12,20},{16,8},{20,28},{24,16},{28,36},{32,24},{36,44... | collective-permute-start | bytes 1044488 | tf_op jit(solution)/shard_map/ppermute | solution.py:41
  7.2 5.2 %collective-permute-start.1 = (bf16[272,640]{1,0:T(8,128)(2,1)}, bf16[272,640]{1,0:T(8,128)(2,1)S(1)}, u32[]{:S(2)}, u32[]{:S(2)}) collective-permute-start(bf16[272,640]{1,0:T(8,128)(2,1)} %get-tuple-element.50.kv_in), channel_id=1, source_target_pairs={{0,8},{8,16},{12,4},{16,24},{20,12},{24,32},{28,20},{32,40},{36,28... | collective-permute-start | bytes 1044488 | tf_op jit(solution)/shard_map/ppermute | solution.py:41
  12.4 3.3 %collective-permute-start.4 = (bf16[320,640]{1,0:T(8,128)(2,1)}, bf16[320,640]{1,0:T(8,128)(2,1)S(1)}, u32[]{:S(2)}, u32[]{:S(2)}) collective-permute-start(bf16[320,640]{1,0:T(8,128)(2,1)} %get-tuple-element.49), channel_id=1, source_target_pairs={{0,2},{1,3},{2,0},{3,1},{4,6},{5,7},{6,4},{7,5},{8,10},{9,11},{10,... | collective-permute-start | bytes 1228808 | tf_op jit(solution)/shard_map/ppermute | solution.py:22
  15.7 0.7 collective-permute-start.5
  16.4 1.2 %collective-permute-done.refs_1_ = bf16[272,640]{1,0:T(8,128)(2,1)S(1)} collective-permute-done((bf16[272,640]{1,0:T(8,128)(2,1)}, bf16[272,640]{1,0:T(8,128)(2,1)S(1)}, u32[]{:S(2)}, u32[]{:S(2)}) %collective-permute-start) | collective-permute-done | bytes 348192 | tf_op jit(solution)/shard_map/ppermute | solution.py:41
  17.6 1.9 %collective-permute-start.2 = (bf16[272,640]{1,0:T(8,128)(2,1)S(1)}, bf16[272,640]{1,0:T(8,128)(2,1)S(1)}, u32[]{:S(2)}, u32[]{:S(2)}) collective-permute-start(bf16[272,640]{1,0:T(8,128)(2,1)S(1)} %collective-permute-done.refs_1_), channel_id=1, source_target_pairs={{4,12},{8,0},{12,20},{16,8},{20,28},{24,16},{28,36},{32,24},{36,44... | collective-permute-start | bytes 1044488 | tf_op jit(solution)/shard_map/ppermute | solution.py:41
  19.5 0.0 collective-permute-done.1.refs_3_
  19.5 6.0 %collective-permute-start.3 = (bf16[272,640]{1,0:T(8,128)(2,1)S(1)}, bf16[272,640]{1,0:T(8,128)(2,1)S(1)}, u32[]{:S(2)}, u32[]{:S(2)}) collective-permute-start(bf16[272,640]{1,0:T(8,128)(2,1)S(1)} %collective-permute-done.1.refs_3_), channel_id=1, source_target_pairs={{0,8},{8,16},{12,4},{16,24},{20,12},{24,32},{28,20},{32,40},{36,28... | collective-permute-start | bytes 1044488 | tf_op jit(solution)/shard_map/ppermute | solution.py:41
  25.6 3.1 %collective-permute-start.12 = (bf16[320,640]{1,0:T(8,128)(2,1)}, bf16[320,640]{1,0:T(8,128)(2,1)S(1)}, u32[]{:S(2)}, u32[]{:S(2)}) collective-permute-start(bf16[320,640]{1,0:T(8,128)(2,1)} %get-tuple-element.49), channel_id=1, source_target_pairs={{0,3},{1,0},{2,1},{3,2},{4,5},{5,6},{6,7},{7,4},{8,11},{9,8},{10,9... | collective-permute-start | bytes 1228808 | tf_op jit(solution)/shard_map/ppermute | solution.py:28
  28.7 0.0 collective-permute-done.4.refs_1_
  28.7 1.9 %collective-permute-start.6 = (bf16[272,640]{1,0:T(8,128)(2,1)}, bf16[272,640]{1,0:T(8,128)(2,1)S(1)}, u32[]{:S(2)}, u32[]{:S(2)}) collective-permute-start(bf16[272,640]{1,0:T(8,128)(2,1)} %get-tuple-element.50.kv_in), channel_id=1, source_target_pairs={{4,24},{12,32},{20,40},{24,4},{28,48},{32,12},{36,56},{40,20},{44,... | collective-permute-start | bytes 1044488 | tf_op jit(solution)/shard_map/ppermute | solution.py:52
  30.6 0.0 copy-start.2
  30.6 1.9 %copy-done.2 = bf16[1280,1280]{1,0:T(8,128)(2,1)S(1)} copy-done((bf16[1280,1280]{1,0:T(8,128)(2,1)S(1)}, bf16[1280,1280]{1,0:T(8,128)(2,1)}, u32[]{:S(2)}) %copy-start.2) | copy-done | bytes 3276824
  32.5 1.1 copy-done.7
  33.6 1.0 copy-done.8
  34.6 0.7 shard_map.101
  35.3 0.0 copy-start.1
  35.3 0.0 copy-start.4
  35.3 0.0 copy-start.9
  35.3 0.0 collective-permute-done.5.refs_0_
  35.3 0.1 collective-permute-start.8
  35.4 0.0 collective-permute-done.2.refs_0_
  35.4 0.5 collective-permute-start.9
  35.9 0.1 collective-permute-start.10
  36.0 2.7 %collective-permute-done.6.refs_10_ = bf16[272,640]{1,0:T(8,128)(2,1)S(1)} collective-permute-done((bf16[272,640]{1,0:T(8,128)(2,1)}, bf16[272,640]{1,0:T(8,128)(2,1)S(1)}, u32[]{:S(2)}, u32[]{:S(2)}) %collective-permute-start.6) | collective-permute-done | bytes 348192 | tf_op jit(solution)/shard_map/ppermute | solution.py:52
  38.7 0.0 collective-permute-start.7
  38.7 0.5 collective-permute-start.11
  39.2 0.1 collective-permute-start.13
  39.3 0.4 collective-permute-start.14
  39.7 0.1 collective-permute-start.15
  39.8 0.5 collective-permute-done.7.refs_5_
  40.3 0.5 collective-permute-done.11.refs_9_
  40.8 6.4 %shard_map.102 = (bf16[256,320]{1,0:T(8,128)(2,1)S(1)}, s32[1]{0:T(128)}) custom-call(s32[2]{0:T(128)S(1)} %copy-done.10, s32[1]{0:T(128)} %get-tuple-element.42.core_ref, bf16[256,384]{1,0:T(8,128)(2,1)S(1)} %get-tuple-element.48.q_ref, bf16[272,640]{1,0:T(8,128)(2,1)S(1)} %collective-permute-done.2.refs_0_, ...), custom_call_target="tpu_custom_call" | custom-call | flops 1000000000 | bytes 4000000 | tf_op jit(solution)/shard_map/pallas_call | solution.py:299
  47.3 0.0 collective-permute-done.13.refs_3_
  47.3 0.0 collective-permute-done.15.refs_5_
  47.3 0.1 collective-permute-start.16
  47.4 2.4 %collective-permute-start.17 = (bf16[256,320]{1,0:T(8,128)(2,1)S(1)}, bf16[256,320]{1,0:T(8,128)(2,1)S(1)}, u32[]{:S(2)}, u32[]{:S(2)}) collective-permute-start(bf16[256,320]{1,0:T(8,128)(2,1)S(1)} %get-tuple-element.61.att0), channel_id=1, source_target_pairs={{0,2},{1,3},{2,0},{3,1},{4,6},{5,7},{6,4},{7,5},{8,10},{9,11},{10,... | collective-permute-start | bytes 491528 | tf_op jit(solution)/shard_map/ppermute | solution.py:22
  49.8 0.8 collective-permute-start.18
  50.6 9.7 %collective-permute-done.16.att1 = bf16[256,320]{1,0:T(8,128)(2,1)S(1)} collective-permute-done((bf16[256,320]{1,0:T(8,128)(2,1)S(1)}, bf16[256,320]{1,0:T(8,128)(2,1)S(1)}, u32[]{:S(2)}, u32[]{:S(2)}) %collective-permute-start.16) | collective-permute-done | bytes 163872 | tf_op jit(solution)/shard_map/ppermute | solution.py:28
  60.3 0.0 copy-start.5
  60.4 0.0 copy-start.6
  60.4 5.9 %shard_map.103 = (f32[656,128]{1,0:T(8,128)S(1)}, bf16[656,128]{1,0:T(8,128)(2,1)S(1)}, bf16[656,128]{1,0:T(8,128)(2,1)S(1)}, bf16[656,128]{1,0:T(8,128)(2,1)S(1)}, bf16[656,128]{1,0:T(8,128)(2,1)S(1)}) custom-call(s32[1]{0:T(128)} %get-tuple-element.41.tp_ref, s32[1]{0:T(128)} %get-tuple-element.42.core_ref, bf16[256,320]{1,0:T(8,128)(2,1)S(1)} %get-tuple-element.61.att0, ...), custom_call_target="tpu_custom_call" | custom-call | flops 2500000000 | bytes 10000000 | tf_op jit(solution)/shard_map/pallas_call | solution.py:349
  66.3 0.1 collective-permute-start.19
  66.4 2.3 %collective-permute-start.20 = (bf16[656,128]{1,0:T(8,128)(2,1)S(1)}, bf16[656,128]{1,0:T(8,128)(2,1)S(1)}, u32[]{:S(2)}, u32[]{:S(2)}) collective-permute-start(bf16[656,128]{1,0:T(8,128)(2,1)S(1)} %get-tuple-element.69), channel_id=1, source_target_pairs={{0,2},{1,3},{2,0},{3,1},{4,6},{5,7},{6,4},{7,5},{8,10},{9,11},{10,... | collective-permute-start | bytes 503816 | tf_op jit(solution)/shard_map/ppermute | solution.py:22
  68.7 0.9 collective-permute-start.21
  69.6 7.9 %collective-permute-done.19.got1 = bf16[656,128]{1,0:T(8,128)(2,1)S(1)} collective-permute-done((bf16[656,128]{1,0:T(8,128)(2,1)S(1)}, bf16[656,128]{1,0:T(8,128)(2,1)S(1)}, u32[]{:S(2)}, u32[]{:S(2)}) %collective-permute-start.19) | collective-permute-done | bytes 167968 | tf_op jit(solution)/shard_map/ppermute | solution.py:22
  77.5 0.0 collective-permute-done.20.got2
  77.5 0.6 collective-permute-done.21.got3
  78.1 0.1 shard_map.104
  78.2 0.3 collective-permute-start.22
  78.5 3.6 %collective-permute-start.23 = (bf16[64,1280]{1,0:T(8,128)(2,1)S(1)}, bf16[64,1280]{1,0:T(8,128)(2,1)S(1)}, u32[]{:S(2)}, u32[]{:S(2)}) collective-permute-start(bf16[64,1280]{1,0:T(8,128)(2,1)S(1)} %get-tuple-element.71.own), channel_id=1, source_target_pairs={{0,2},{1,3},{2,0},{3,1},{4,6},{5,7},{6,4},{7,5},{8,10},{9,11},{10,... | collective-permute-start | bytes 491528 | tf_op jit(solution)/shard_map/ppermute | solution.py:22
  82.1 0.0 collective-permute-start.24
  82.1 1.9 %collective-permute-start.25 = (bf16[16,128]{1,0:T(8,128)(2,1)S(1)}, bf16[16,128]{1,0:T(8,128)(2,1)S(1)}, u32[]{:S(2)}, u32[]{:S(2)}) collective-permute-start(bf16[16,128]{1,0:T(8,128)(2,1)S(1)} %get-tuple-element.72), channel_id=1, source_target_pairs={{0,4},{4,8},{8,12},{12,16},{16,20},{20,24},{24,28},{28,32},{32,36}... | collective-permute-start | bytes 12296 | tf_op jit(solution)/shard_map/ppermute | solution.py:33
  84.0 3.0 %collective-permute-done.25.rim_ref = bf16[16,128]{1,0:T(8,128)(2,1)S(1)} collective-permute-done((bf16[16,128]{1,0:T(8,128)(2,1)S(1)}, bf16[16,128]{1,0:T(8,128)(2,1)S(1)}, u32[]{:S(2)}, u32[]{:S(2)}) %collective-permute-start.25) | collective-permute-done | bytes 4128 | tf_op jit(solution)/shard_map/ppermute | solution.py:33
  87.0 0.0 collective-permute-done.22.got1
  87.0 2.4 %collective-permute-done.23.got2 = bf16[64,1280]{1,0:T(8,128)(2,1)S(1)} collective-permute-done((bf16[64,1280]{1,0:T(8,128)(2,1)S(1)}, bf16[64,1280]{1,0:T(8,128)(2,1)S(1)}, u32[]{:S(2)}, u32[]{:S(2)}) %collective-permute-start.23) | collective-permute-done | bytes 163872 | tf_op jit(solution)/shard_map/ppermute | solution.py:22
  89.4 4.2 %shard_map.105 = (bf16[32,4096]{1,0:T(8,128)(2,1)S(1)}, bf16[32,4096]{1,0:T(8,128)(2,1)S(1)}, bf16[32,4096]{1,0:T(8,128)(2,1)S(1)}, bf16[32,4096]{1,0:T(8,128)(2,1)S(1)}) custom-call(s32[1]{0:T(128)} %get-tuple-element.41.tp_ref, s32[2]{0:T(128)S(1)} %copy-done.10, s32[1]{0:T(128)} %get-tuple-element.57.joined_ref, ...), custom_call_target="tpu_custom_call" | custom-call | flops 1000000000 | bytes 6000000 | tf_op jit(solution)/shard_map/pallas_call | solution.py:369
  93.6 0.4 collective-permute-start.26
  94.0 3.3 %collective-permute-start.27 = (bf16[32,4096]{1,0:T(8,128)(2,1)S(1)}, bf16[32,4096]{1,0:T(8,128)(2,1)S(1)}, u32[]{:S(2)}, u32[]{:S(2)}) collective-permute-start(bf16[32,4096]{1,0:T(8,128)(2,1)S(1)} %get-tuple-element.75), channel_id=1, source_target_pairs={{0,2},{1,3},{2,0},{3,1},{4,6},{5,7},{6,4},{7,5},{8,10},{9,11},{10,... | collective-permute-start | bytes 786440 | tf_op jit(solution)/shard_map/ppermute | solution.py:22
  97.3 0.0 collective-permute-start.28
  97.3 4.9 %collective-permute-done.26.got1 = bf16[32,4096]{1,0:T(8,128)(2,1)S(1)} collective-permute-done((bf16[32,4096]{1,0:T(8,128)(2,1)S(1)}, bf16[32,4096]{1,0:T(8,128)(2,1)S(1)}, u32[]{:S(2)}, u32[]{:S(2)}) %collective-permute-start.26) | collective-permute-done | bytes 262176 | tf_op jit(solution)/shard_map/ppermute | solution.py:22
  102.2 6.5 %collective-permute-done.27.got2 = bf16[32,4096]{1,0:T(8,128)(2,1)S(1)} collective-permute-done((bf16[32,4096]{1,0:T(8,128)(2,1)S(1)}, bf16[32,4096]{1,0:T(8,128)(2,1)S(1)}, u32[]{:S(2)}, u32[]{:S(2)}) %collective-permute-start.27) | collective-permute-done | bytes 262176 | tf_op jit(solution)/shard_map/ppermute | solution.py:22
  108.7 0.8 shard_map.106
  (23 shorter events, 0.1 us)
Async XLA Ops:
  0.0 30.6 %copy-start = (bf16[3,1280,320]{1,2,0:T(8,128)(2,1)S(1)}, bf16[3,1280,320]{1,2,0:T(8,128)(2,1)}, u32[]{:S(2)}) copy-start(bf16[3,1280,320]{1,2,0:T(8,128)(2,1)} %param.12) | copy-start | bytes 7372804
  4.5 13.1 %collective-permute-start = (bf16[272,640]{1,0:T(8,128)(2,1)}, bf16[272,640]{1,0:T(8,128)(2,1)S(1)}, u32[]{:S(2)}, u32[]{:S(2)}) collective-permute-start(bf16[272,640]{1,0:T(8,128)(2,1)} %get-tuple-element.50.kv_in), channel_id=1, source_target_pairs={{4,12},{8,0},{12,20},{16,8},{20,28},{24,16},{28,36},{32,24},{36,44... | collective-permute-start | bytes 1044488 | tf_op jit(solution)/shard_map/ppermute | solution.py:41
  7.2 12.3 %collective-permute-start.1 = (bf16[272,640]{1,0:T(8,128)(2,1)}, bf16[272,640]{1,0:T(8,128)(2,1)S(1)}, u32[]{:S(2)}, u32[]{:S(2)}) collective-permute-start(bf16[272,640]{1,0:T(8,128)(2,1)} %get-tuple-element.50.kv_in), channel_id=1, source_target_pairs={{0,8},{8,16},{12,4},{16,24},{20,12},{24,32},{28,20},{32,40},{36,28... | collective-permute-start | bytes 1044488 | tf_op jit(solution)/shard_map/ppermute | solution.py:41
  12.4 16.2 %collective-permute-start.4 = (bf16[320,640]{1,0:T(8,128)(2,1)}, bf16[320,640]{1,0:T(8,128)(2,1)S(1)}, u32[]{:S(2)}, u32[]{:S(2)}) collective-permute-start(bf16[320,640]{1,0:T(8,128)(2,1)} %get-tuple-element.49), channel_id=1, source_target_pairs={{0,2},{1,3},{2,0},{3,1},{4,6},{5,7},{6,4},{7,5},{8,10},{9,11},{10,... | collective-permute-start | bytes 1228808 | tf_op jit(solution)/shard_map/ppermute | solution.py:22
  15.7 19.6 %collective-permute-start.5 = (bf16[320,640]{1,0:T(8,128)(2,1)}, bf16[320,640]{1,0:T(8,128)(2,1)S(1)}, u32[]{:S(2)}, u32[]{:S(2)}) collective-permute-start(bf16[320,640]{1,0:T(8,128)(2,1)} %get-tuple-element.49), channel_id=1, source_target_pairs={{0,1},{1,2},{2,3},{3,0},{4,7},{5,4},{6,5},{7,6},{8,9},{9,10},{10,1... | collective-permute-start | bytes 1228808 | tf_op jit(solution)/shard_map/ppermute | solution.py:28
  17.6 17.8 %collective-permute-start.2 = (bf16[272,640]{1,0:T(8,128)(2,1)S(1)}, bf16[272,640]{1,0:T(8,128)(2,1)S(1)}, u32[]{:S(2)}, u32[]{:S(2)}) collective-permute-start(bf16[272,640]{1,0:T(8,128)(2,1)S(1)} %collective-permute-done.refs_1_), channel_id=1, source_target_pairs={{4,12},{8,0},{12,20},{16,8},{20,28},{24,16},{28,36},{32,24},{36,44... | collective-permute-start | bytes 1044488 | tf_op jit(solution)/shard_map/ppermute | solution.py:41
  19.5 16.4 %collective-permute-start.3 = (bf16[272,640]{1,0:T(8,128)(2,1)S(1)}, bf16[272,640]{1,0:T(8,128)(2,1)S(1)}, u32[]{:S(2)}, u32[]{:S(2)}) collective-permute-start(bf16[272,640]{1,0:T(8,128)(2,1)S(1)} %collective-permute-done.1.refs_3_), channel_id=1, source_target_pairs={{0,8},{8,16},{12,4},{16,24},{20,12},{24,32},{28,20},{32,40},{36,28... | collective-permute-start | bytes 1044488 | tf_op jit(solution)/shard_map/ppermute | solution.py:41
  25.6 13.1 %collective-permute-start.12 = (bf16[320,640]{1,0:T(8,128)(2,1)}, bf16[320,640]{1,0:T(8,128)(2,1)S(1)}, u32[]{:S(2)}, u32[]{:S(2)}) collective-permute-start(bf16[320,640]{1,0:T(8,128)(2,1)} %get-tuple-element.49), channel_id=1, source_target_pairs={{0,3},{1,0},{2,1},{3,2},{4,5},{5,6},{6,7},{7,4},{8,11},{9,8},{10,9... | collective-permute-start | bytes 1228808 | tf_op jit(solution)/shard_map/ppermute | solution.py:28
  28.7 10.0 %collective-permute-start.6 = (bf16[272,640]{1,0:T(8,128)(2,1)}, bf16[272,640]{1,0:T(8,128)(2,1)S(1)}, u32[]{:S(2)}, u32[]{:S(2)}) collective-permute-start(bf16[272,640]{1,0:T(8,128)(2,1)} %get-tuple-element.50.kv_in), channel_id=1, source_target_pairs={{4,24},{12,32},{20,40},{24,4},{28,48},{32,12},{36,56},{40,20},{44,... | collective-permute-start | bytes 1044488 | tf_op jit(solution)/shard_map/ppermute | solution.py:52
  30.6 1.9 %copy-start.2 = (bf16[1280,1280]{1,0:T(8,128)(2,1)S(1)}, bf16[1280,1280]{1,0:T(8,128)(2,1)}, u32[]{:S(2)}) copy-start(bf16[1280,1280]{1,0:T(8,128)(2,1)} %w_down_in.1) | copy-start | bytes 9830404
  32.5 1.1 copy-start.7
  33.6 1.0 copy-start.8
  34.6 6.3 %copy-start.10 = (s32[2]{0:T(128)S(1)}, s32[2]{0:T(128)}, u32[]{:S(2)}) copy-start(s32[2]{0:T(128)} %ids_ref.5) | copy-start | bytes 28
  34.6 25.7 %copy-start.3 = (bf16[1280,1280]{1,0:T(8,128)(2,1)S(1)}, bf16[1280,1280]{1,0:T(8,128)(2,1)}, u32[]{:S(2)}) copy-start(bf16[1280,1280]{1,0:T(8,128)(2,1)} %refs_8_.1) | copy-start | bytes 9830404
  35.3 25.1 %copy-start.1 = (bf16[320,1280]{1,0:T(8,128)(2,1)S(1)}, bf16[320,1280]{1,0:T(8,128)(2,1)}, u32[]{:S(2)}) copy-start(bf16[320,1280]{1,0:T(8,128)(2,1)} %w_out_ref.1) | copy-start | bytes 2457604
  35.3 25.1 %copy-start.4 = (bf16[256,1280]{1,0:T(8,128)(2,1)S(1)}, bf16[256,1280]{1,0:T(8,128)(2,1)}, u32[]{:S(2)}) copy-start(bf16[256,1280]{1,0:T(8,128)(2,1)} %refs_6_.1) | copy-start | bytes 1966084
  35.3 25.0 %copy-start.9 = (f32[1280]{0:T(1024)S(1)}, f32[1280]{0:T(1024)}, u32[]{:S(2)}) copy-start(f32[1280]{0:T(1024)} %refs_7_.1) | copy-start | bytes 15364
  35.3 3.9 %collective-permute-start.8 = (bf16[272,640]{1,0:T(8,128)(2,1)S(1)}, bf16[272,640]{1,0:T(8,128)(2,1)S(1)}, u32[]{:S(2)}, u32[]{:S(2)}) collective-permute-start(bf16[272,640]{1,0:T(8,128)(2,1)S(1)} %collective-permute-done.refs_1_), channel_id=1, source_target_pairs={{0,4},{4,0},{8,12},{12,8},{16,20},{20,16},{24,28},{28,24},{32,36},... | collective-permute-start | bytes 1044488 | tf_op jit(solution)/shard_map/ppermute | solution.py:46
  35.4 3.9 %collective-permute-start.9 = (bf16[272,640]{1,0:T(8,128)(2,1)S(1)}, bf16[272,640]{1,0:T(8,128)(2,1)S(1)}, u32[]{:S(2)}, u32[]{:S(2)}) collective-permute-start(bf16[272,640]{1,0:T(8,128)(2,1)S(1)} %get-tuple-element.54.refs_2_), channel_id=1, source_target_pairs={{0,4},{4,0},{8,12},{12,8},{16,20},{20,16},{24,28},{28,24},{32,36},... | collective-permute-start | bytes 1044488 | tf_op jit(solution)/shard_map/ppermute | solution.py:46
  35.9 3.8 %collective-permute-start.10 = (bf16[272,640]{1,0:T(8,128)(2,1)S(1)}, bf16[272,640]{1,0:T(8,128)(2,1)S(1)}, u32[]{:S(2)}, u32[]{:S(2)}) collective-permute-start(bf16[272,640]{1,0:T(8,128)(2,1)S(1)} %collective-permute-done.1.refs_3_), channel_id=1, source_target_pairs={{0,4},{4,0},{8,12},{12,8},{16,20},{20,16},{24,28},{28,24},{32,36},... | collective-permute-start | bytes 1044488 | tf_op jit(solution)/shard_map/ppermute | solution.py:46
  38.7 1.7 %collective-permute-start.7 = (bf16[272,640]{1,0:T(8,128)(2,1)S(1)}, bf16[272,640]{1,0:T(8,128)(2,1)S(1)}, u32[]{:S(2)}, u32[]{:S(2)}) collective-permute-start(bf16[272,640]{1,0:T(8,128)(2,1)S(1)} %collective-permute-done.2.refs_0_), channel_id=1, source_target_pairs={{0,4},{4,0},{8,12},{12,8},{16,20},{20,16},{24,28},{28,24},{32,36},... | collective-permute-start | bytes 1044488 | tf_op jit(solution)/shard_map/ppermute | solution.py:46
  38.7 2.2 %collective-permute-start.11 = (bf16[272,640]{1,0:T(8,128)(2,1)S(1)}, bf16[272,640]{1,0:T(8,128)(2,1)S(1)}, u32[]{:S(2)}, u32[]{:S(2)}) collective-permute-start(bf16[272,640]{1,0:T(8,128)(2,1)S(1)} %collective-permute-done.3.refs_4_), channel_id=1, source_target_pairs={{0,4},{4,0},{8,12},{12,8},{16,20},{20,16},{24,28},{28,24},{32,36},... | collective-permute-start | bytes 1044488 | tf_op jit(solution)/shard_map/ppermute | solution.py:46
  39.2 8.1 %collective-permute-start.13 = (bf16[320,640]{1,0:T(8,128)(2,1)S(1)}, bf16[320,640]{1,0:T(8,128)(2,1)S(1)}, u32[]{:S(2)}, u32[]{:S(2)}) collective-permute-start(bf16[320,640]{1,0:T(8,128)(2,1)S(1)} %collective-permute-done.12.refs_2_), channel_id=1, source_target_pairs={{0,4},{4,0},{8,12},{12,8},{16,20},{20,16},{24,28},{28,24},{32,36},... | collective-permute-start | bytes 1228808 | tf_op jit(solution)/shard_map/ppermute | solution.py:46
  39.3 8.0 %collective-permute-start.14 = (bf16[320,640]{1,0:T(8,128)(2,1)S(1)}, bf16[320,640]{1,0:T(8,128)(2,1)S(1)}, u32[]{:S(2)}, u32[]{:S(2)}) collective-permute-start(bf16[320,640]{1,0:T(8,128)(2,1)S(1)} %collective-permute-done.4.refs_1_), channel_id=1, source_target_pairs={{0,4},{4,0},{8,12},{12,8},{16,20},{20,16},{24,28},{28,24},{32,36},... | collective-permute-start | bytes 1228808 | tf_op jit(solution)/shard_map/ppermute | solution.py:46
  39.7 7.6 %collective-permute-start.15 = (bf16[320,640]{1,0:T(8,128)(2,1)S(1)}, bf16[320,640]{1,0:T(8,128)(2,1)S(1)}, u32[]{:S(2)}, u32[]{:S(2)}) collective-permute-start(bf16[320,640]{1,0:T(8,128)(2,1)S(1)} %collective-permute-done.5.refs_0_), channel_id=1, source_target_pairs={{0,4},{4,0},{8,12},{12,8},{16,20},{20,16},{24,28},{28,24},{32,36},... | collective-permute-start | bytes 1228808 | tf_op jit(solution)/shard_map/ppermute | solution.py:46
  47.3 13.0 %collective-permute-start.16 = (bf16[256,320]{1,0:T(8,128)(2,1)S(1)}, bf16[256,320]{1,0:T(8,128)(2,1)S(1)}, u32[]{:S(2)}, u32[]{:S(2)}) collective-permute-start(bf16[256,320]{1,0:T(8,128)(2,1)S(1)} %get-tuple-element.61.att0), channel_id=1, source_target_pairs={{0,1},{1,2},{2,3},{3,0},{4,7},{5,4},{6,5},{7,6},{8,9},{9,10},{10,1... | collective-permute-start | bytes 491528 | tf_op jit(solution)/shard_map/ppermute | solution.py:28
  47.4 12.9 %collective-permute-start.17 = (bf16[256,320]{1,0:T(8,128)(2,1)S(1)}, bf16[256,320]{1,0:T(8,128)(2,1)S(1)}, u32[]{:S(2)}, u32[]{:S(2)}) collective-permute-start(bf16[256,320]{1,0:T(8,128)(2,1)S(1)} %get-tuple-element.61.att0), channel_id=1, source_target_pairs={{0,2},{1,3},{2,0},{3,1},{4,6},{5,7},{6,4},{7,5},{8,10},{9,11},{10,... | collective-permute-start | bytes 491528 | tf_op jit(solution)/shard_map/ppermute | solution.py:22
  49.8 10.5 %collective-permute-start.18 = (bf16[256,320]{1,0:T(8,128)(2,1)S(1)}, bf16[256,320]{1,0:T(8,128)(2,1)S(1)}, u32[]{:S(2)}, u32[]{:S(2)}) collective-permute-start(bf16[256,320]{1,0:T(8,128)(2,1)S(1)} %get-tuple-element.61.att0), channel_id=1, source_target_pairs={{0,3},{1,0},{2,1},{3,2},{4,5},{5,6},{6,7},{7,4},{8,11},{9,8},{10,9... | collective-permute-start | bytes 491528 | tf_op jit(solution)/shard_map/ppermute | solution.py:28
  60.3 29.0 %copy-start.5 = (bf16[320,4096]{1,0:T(8,128)(2,1)S(1)}, bf16[320,4096]{1,0:T(8,128)(2,1)}, u32[]{:S(2)}) copy-start(bf16[320,4096]{1,0:T(8,128)(2,1)} %w_proj_ref.1) | copy-start | bytes 7864324
  60.4 29.0 %copy-start.6 = (bf16[3,1280,320]{1,2,0:T(8,128)(2,1)S(1)}, bf16[3,1280,320]{1,2,0:T(8,128)(2,1)}, u32[]{:S(2)}) copy-start(bf16[3,1280,320]{1,2,0:T(8,128)(2,1)} %param.17) | copy-start | bytes 7372804
  66.3 11.2 %collective-permute-start.19 = (bf16[656,128]{1,0:T(8,128)(2,1)S(1)}, bf16[656,128]{1,0:T(8,128)(2,1)S(1)}, u32[]{:S(2)}, u32[]{:S(2)}) collective-permute-start(bf16[656,128]{1,0:T(8,128)(2,1)S(1)} %get-tuple-element.68), channel_id=1, source_target_pairs={{0,1},{1,2},{2,3},{3,0},{4,5},{5,6},{6,7},{7,4},{8,9},{9,10},{10,1... | collective-permute-start | bytes 503816 | tf_op jit(solution)/shard_map/ppermute | solution.py:22
  66.4 11.1 %collective-permute-start.20 = (bf16[656,128]{1,0:T(8,128)(2,1)S(1)}, bf16[656,128]{1,0:T(8,128)(2,1)S(1)}, u32[]{:S(2)}, u32[]{:S(2)}) collective-permute-start(bf16[656,128]{1,0:T(8,128)(2,1)S(1)} %get-tuple-element.69), channel_id=1, source_target_pairs={{0,2},{1,3},{2,0},{3,1},{4,6},{5,7},{6,4},{7,5},{8,10},{9,11},{10,... | collective-permute-start | bytes 503816 | tf_op jit(solution)/shard_map/ppermute | solution.py:22
  68.7 9.4 %collective-permute-start.21 = (bf16[656,128]{1,0:T(8,128)(2,1)S(1)}, bf16[656,128]{1,0:T(8,128)(2,1)S(1)}, u32[]{:S(2)}, u32[]{:S(2)}) collective-permute-start(bf16[656,128]{1,0:T(8,128)(2,1)S(1)} %get-tuple-element.70), channel_id=1, source_target_pairs={{0,3},{1,0},{2,1},{3,2},{4,7},{5,4},{6,5},{7,6},{8,11},{9,8},{10,9... | collective-permute-start | bytes 503816 | tf_op jit(solution)/shard_map/ppermute | solution.py:22
  78.2 8.8 %collective-permute-start.22 = (bf16[64,1280]{1,0:T(8,128)(2,1)S(1)}, bf16[64,1280]{1,0:T(8,128)(2,1)S(1)}, u32[]{:S(2)}, u32[]{:S(2)}) collective-permute-start(bf16[64,1280]{1,0:T(8,128)(2,1)S(1)} %get-tuple-element.71.own), channel_id=1, source_target_pairs={{0,1},{1,2},{2,3},{3,0},{4,5},{5,6},{6,7},{7,4},{8,9},{9,10},{10,1... | collective-permute-start | bytes 491528 | tf_op jit(solution)/shard_map/ppermute | solution.py:22
  78.5 10.9 %collective-permute-start.23 = (bf16[64,1280]{1,0:T(8,128)(2,1)S(1)}, bf16[64,1280]{1,0:T(8,128)(2,1)S(1)}, u32[]{:S(2)}, u32[]{:S(2)}) collective-permute-start(bf16[64,1280]{1,0:T(8,128)(2,1)S(1)} %get-tuple-element.71.own), channel_id=1, source_target_pairs={{0,2},{1,3},{2,0},{3,1},{4,6},{5,7},{6,4},{7,5},{8,10},{9,11},{10,... | collective-permute-start | bytes 491528 | tf_op jit(solution)/shard_map/ppermute | solution.py:22
  82.1 7.3 %collective-permute-start.24 = (bf16[64,1280]{1,0:T(8,128)(2,1)S(1)}, bf16[64,1280]{1,0:T(8,128)(2,1)S(1)}, u32[]{:S(2)}, u32[]{:S(2)}) collective-permute-start(bf16[64,1280]{1,0:T(8,128)(2,1)S(1)} %get-tuple-element.71.own), channel_id=1, source_target_pairs={{0,3},{1,0},{2,1},{3,2},{4,7},{5,4},{6,5},{7,6},{8,11},{9,8},{10,9... | collective-permute-start | bytes 491528 | tf_op jit(solution)/shard_map/ppermute | solution.py:22
  82.1 4.9 %collective-permute-start.25 = (bf16[16,128]{1,0:T(8,128)(2,1)S(1)}, bf16[16,128]{1,0:T(8,128)(2,1)S(1)}, u32[]{:S(2)}, u32[]{:S(2)}) collective-permute-start(bf16[16,128]{1,0:T(8,128)(2,1)S(1)} %get-tuple-element.72), channel_id=1, source_target_pairs={{0,4},{4,8},{8,12},{12,16},{16,20},{20,24},{24,28},{28,32},{32,36}... | collective-permute-start | bytes 12296 | tf_op jit(solution)/shard_map/ppermute | solution.py:33
  93.6 8.6 %collective-permute-start.26 = (bf16[32,4096]{1,0:T(8,128)(2,1)S(1)}, bf16[32,4096]{1,0:T(8,128)(2,1)S(1)}, u32[]{:S(2)}, u32[]{:S(2)}) collective-permute-start(bf16[32,4096]{1,0:T(8,128)(2,1)S(1)} %get-tuple-element.74), channel_id=1, source_target_pairs={{0,1},{1,2},{2,3},{3,0},{4,5},{5,6},{6,7},{7,4},{8,9},{9,10},{10,1... | collective-permute-start | bytes 786440 | tf_op jit(solution)/shard_map/ppermute | solution.py:22
  94.0 14.7 %collective-permute-start.27 = (bf16[32,4096]{1,0:T(8,128)(2,1)S(1)}, bf16[32,4096]{1,0:T(8,128)(2,1)S(1)}, u32[]{:S(2)}, u32[]{:S(2)}) collective-permute-start(bf16[32,4096]{1,0:T(8,128)(2,1)S(1)} %get-tuple-element.75), channel_id=1, source_target_pairs={{0,2},{1,3},{2,0},{3,1},{4,6},{5,7},{6,4},{7,5},{8,10},{9,11},{10,... | collective-permute-start | bytes 786440 | tf_op jit(solution)/shard_map/ppermute | solution.py:22
  97.3 11.4 %collective-permute-start.28 = (bf16[32,4096]{1,0:T(8,128)(2,1)S(1)}, bf16[32,4096]{1,0:T(8,128)(2,1)S(1)}, u32[]{:S(2)}, u32[]{:S(2)}) collective-permute-start(bf16[32,4096]{1,0:T(8,128)(2,1)S(1)} %get-tuple-element.76), channel_id=1, source_target_pairs={{0,3},{1,0},{2,1},{3,2},{4,7},{5,4},{6,5},{7,6},{8,11},{9,8},{10,9... | collective-permute-start | bytes 786440 | tf_op jit(solution)/shard_map/ppermute | solution.py:22

commit v8 on v7

--- a/solution.py
+++ b/solution.py
@@ -142,7 +142,6 @@
         window = pl.ds(begin, MOST * BLK)
         for pair in range(3):
             q_pair = q_ref[i * BLK:(i + 1) * BLK, pair * 128:(pair + 1) * 128]
-            q_pair = q_pair * jnp.asarray(HEAD_DIM ** -0.5, q_pair.dtype)
             none = jnp.zeros_like(q_pair)
             key_at, value_at = ((0, 256), (128, 384), (512, 512))[pair]
             q_both = jnp.where(low, q_pair, none)
@@ -162,7 +161,8 @@
 
 def query_kernel(normed_ref, w_ref, kv_in, w_down_in, q_ref, kv_ref, w_down_ref):
     q_ref[...] = jnp.zeros_like(q_ref)
-    q_ref[:, :w_ref.shape[1]] = dot_t(normed_ref[...], w_ref[0]).astype(jnp.bfloat16)
+    queries = dot_t(normed_ref[...], w_ref[0]).astype(jnp.bfloat16)
+    q_ref[:, :w_ref.shape[1]] = queries * jnp.asarray(HEAD_DIM ** -0.5, jnp.bfloat16)
     kv_ref[...] = kv_in[...]
     w_down_ref[...] = w_down_in[...]
 

time: 111 us -> 111 us (level)
  no operation moved by 1% of the time
where the time goes in v8:
time: 111 us; the launch traced here: 109 us
  starting transfers between devices  42.7 us (38%)
  waiting for transfers between devices  39.9 us (36%)
  Pallas kernels  22.6 us (20%)
  local copies, waits for them, and re-layouts  4.03 us (4%)
    ppermute x11, waiting for transfers between devices, send_tp(): lax.ppermute(value, TP, [(t, (t + steps) % count) for t in range(count)])  22.3 us
    ppermute x11, starting transfers between devices, send_tp(): lax.ppermute(value, TP, [(t, (t + steps) % count) for t in range(count)])  16.6 us
    ppermute x4, starting transfers between devices, send_chip(): lax.ppermute(value, SEQ, [(a, b) for a, b in pairs if 0 <= b < count])  15.9 us
    ppermute x4, waiting for transfers between devices, send_pair(): return lax.ppermute(value, (SEQ, TP), pairs)  9.65 us
    pallas_call x1, Pallas kernels, attend(): pl.pallas_call(attend_kernel, out_shape=(bf16(rows, width), jax.ShapeDtyp...  6.41 us
    pallas_call x1, Pallas kernels, shards(): pl.pallas_call(mlp_kernel, out_shape=[jax.ShapeDtypeStruct((tall, 128), j...  5.9 us
    ppermute x4, starting transfers between devices, send_pair(): return lax.ppermute(value, (SEQ, TP), pairs)  4.64 us
    pallas_call x1, Pallas kernels, shards(): pl.pallas_call(kv_kernel, out_shape=(scalar, scalar, bf16(rows, width), b...  4.47 us
  transfers between devices with their start and end apart: 29, of which 11 were waited for; matrix products, arithmetic and copies ran while one was open for 0% of the time, Pallas kernels for 6%

profile of v8, /device:TPU:70, one launch (start us, length us, event | category | flops | bytes accessed | tf_op | source)
XLA Modules:
  0.0 109.5 jit_solution(13942652636565686244)
XLA Ops:
  0.0 4.5 %shard_map.100 = (s32[1]{0:T(128)}, s32[1]{0:T(128)}, bf16[256,1280]{1,0:T(8,128)(2,1)}, bf16[272,640]{1,0:T(8,128)(2,1)}, bf16[320,640]{1,0:T(8,128)(2,1)}) custom-call(s32[2]{0:T(128)} %ids_ref.5, s32[1]{0:T(128)} %bitcast.core_ref, s32[1]{0:T(128)} %bitcast.1.tp_ref, bf16[256,1280]{1,0:T(8,128)(2,1)} %refs_6_.1, f32[1280]{0:T(1024)} %gain_ref.1, ...), custom_call_target="tpu_custom_call" | custom-call | flops 400000000 | bytes 4000000 | tf_op jit(solution)/shard_map/pallas_call | solution.py:329
  4.5 2.7 %collective-permute-start = (bf16[272,640]{1,0:T(8,128)(2,1)}, bf16[272,640]{1,0:T(8,128)(2,1)S(1)}, u32[]{:S(2)}, u32[]{:S(2)}) collective-permute-start(bf16[272,640]{1,0:T(8,128)(2,1)} %get-tuple-element.50.kv_in), channel_id=1, source_target_pairs={{4,12},{8,0},{12,20},{16,8},{20,28},{24,16},{28,36},{32,24},{36,44... | collective-permute-start | bytes 1044488 | tf_op jit(solution)/shard_map/ppermute | solution.py:41
  7.2 5.2 %collective-permute-start.1 = (bf16[272,640]{1,0:T(8,128)(2,1)}, bf16[272,640]{1,0:T(8,128)(2,1)S(1)}, u32[]{:S(2)}, u32[]{:S(2)}) collective-permute-start(bf16[272,640]{1,0:T(8,128)(2,1)} %get-tuple-element.50.kv_in), channel_id=1, source_target_pairs={{0,8},{8,16},{12,4},{16,24},{20,12},{24,32},{28,20},{32,40},{36,28... | collective-permute-start | bytes 1044488 | tf_op jit(solution)/shard_map/ppermute | solution.py:41
  12.4 3.3 %collective-permute-start.4 = (bf16[320,640]{1,0:T(8,128)(2,1)}, bf16[320,640]{1,0:T(8,128)(2,1)S(1)}, u32[]{:S(2)}, u32[]{:S(2)}) collective-permute-start(bf16[320,640]{1,0:T(8,128)(2,1)} %get-tuple-element.49), channel_id=1, source_target_pairs={{0,2},{1,3},{2,0},{3,1},{4,6},{5,7},{6,4},{7,5},{8,10},{9,11},{10,... | collective-permute-start | bytes 1228808 | tf_op jit(solution)/shard_map/ppermute | solution.py:22
  15.7 0.7 collective-permute-start.5
  16.4 1.2 %collective-permute-done.refs_1_ = bf16[272,640]{1,0:T(8,128)(2,1)S(1)} collective-permute-done((bf16[272,640]{1,0:T(8,128)(2,1)}, bf16[272,640]{1,0:T(8,128)(2,1)S(1)}, u32[]{:S(2)}, u32[]{:S(2)}) %collective-permute-start) | collective-permute-done | bytes 348192 | tf_op jit(solution)/shard_map/ppermute | solution.py:41
  17.6 1.9 %collective-permute-start.2 = (bf16[272,640]{1,0:T(8,128)(2,1)S(1)}, bf16[272,640]{1,0:T(8,128)(2,1)S(1)}, u32[]{:S(2)}, u32[]{:S(2)}) collective-permute-start(bf16[272,640]{1,0:T(8,128)(2,1)S(1)} %collective-permute-done.refs_1_), channel_id=1, source_target_pairs={{4,12},{8,0},{12,20},{16,8},{20,28},{24,16},{28,36},{32,24},{36,44... | collective-permute-start | bytes 1044488 | tf_op jit(solution)/shard_map/ppermute | solution.py:41
  19.5 0.0 collective-permute-done.1.refs_3_
  19.5 6.0 %collective-permute-start.3 = (bf16[272,640]{1,0:T(8,128)(2,1)S(1)}, bf16[272,640]{1,0:T(8,128)(2,1)S(1)}, u32[]{:S(2)}, u32[]{:S(2)}) collective-permute-start(bf16[272,640]{1,0:T(8,128)(2,1)S(1)} %collective-permute-done.1.refs_3_), channel_id=1, source_target_pairs={{0,8},{8,16},{12,4},{16,24},{20,12},{24,32},{28,20},{32,40},{36,28... | collective-permute-start | bytes 1044488 | tf_op jit(solution)/shard_map/ppermute | solution.py:41
  25.6 3.1 %collective-permute-start.12 = (bf16[320,640]{1,0:T(8,128)(2,1)}, bf16[320,640]{1,0:T(8,128)(2,1)S(1)}, u32[]{:S(2)}, u32[]{:S(2)}) collective-permute-start(bf16[320,640]{1,0:T(8,128)(2,1)} %get-tuple-element.49), channel_id=1, source_target_pairs={{0,3},{1,0},{2,1},{3,2},{4,5},{5,6},{6,7},{7,4},{8,11},{9,8},{10,9... | collective-permute-start | bytes 1228808 | tf_op jit(solution)/shard_map/ppermute | solution.py:28
  28.7 0.0 collective-permute-done.4.refs_1_
  28.7 1.9 %collective-permute-start.6 = (bf16[272,640]{1,0:T(8,128)(2,1)}, bf16[272,640]{1,0:T(8,128)(2,1)S(1)}, u32[]{:S(2)}, u32[]{:S(2)}) collective-permute-start(bf16[272,640]{1,0:T(8,128)(2,1)} %get-tuple-element.50.kv_in), channel_id=1, source_target_pairs={{4,24},{12,32},{20,40},{24,4},{28,48},{32,12},{36,56},{40,20},{44,... | collective-permute-start | bytes 1044488 | tf_op jit(solution)/shard_map/ppermute | solution.py:52
  30.6 0.0 copy-start.2
  30.6 1.9 %copy-done.2 = bf16[1280,1280]{1,0:T(8,128)(2,1)S(1)} copy-done((bf16[1280,1280]{1,0:T(8,128)(2,1)S(1)}, bf16[1280,1280]{1,0:T(8,128)(2,1)}, u32[]{:S(2)}) %copy-start.2) | copy-done | bytes 3276824
  32.5 1.1 copy-done.7
  33.6 1.0 copy-done.8
  34.6 0.7 shard_map.101
  35.3 0.0 copy-start.1
  35.3 0.0 copy-start.4
  35.3 0.0 copy-start.9
  35.3 0.0 collective-permute-done.5.refs_0_
  35.3 0.1 collective-permute-start.8
  35.4 0.5 collective-permute-start.9
  35.9 0.0 collective-permute-done.3.refs_4_
  35.9 0.1 collective-permute-start.10
  36.0 2.7 %collective-permute-done.6.refs_10_ = bf16[272,640]{1,0:T(8,128)(2,1)S(1)} collective-permute-done((bf16[272,640]{1,0:T(8,128)(2,1)}, bf16[272,640]{1,0:T(8,128)(2,1)S(1)}, u32[]{:S(2)}, u32[]{:S(2)}) %collective-permute-start.6) | collective-permute-done | bytes 348192 | tf_op jit(solution)/shard_map/ppermute | solution.py:52
  38.7 0.0 collective-permute-start.7
  38.7 0.5 collective-permute-start.11
  39.2 0.1 collective-permute-start.13
  39.3 0.4 collective-permute-start.14
  39.7 0.1 collective-permute-start.15
  39.8 0.5 collective-permute-done.7.refs_5_
  40.3 0.5 collective-permute-done.11.refs_9_
  40.8 6.4 %shard_map.102 = (bf16[256,320]{1,0:T(8,128)(2,1)S(1)}, s32[1]{0:T(128)}) custom-call(s32[2]{0:T(128)S(1)} %copy-done.10, s32[1]{0:T(128)} %get-tuple-element.42.core_ref, bf16[256,384]{1,0:T(8,128)(2,1)S(1)} %get-tuple-element.48.q_ref, bf16[272,640]{1,0:T(8,128)(2,1)S(1)} %collective-permute-done.2.refs_0_, ...), custom_call_target="tpu_custom_call" | custom-call | flops 1000000000 | bytes 4000000 | tf_op jit(solution)/shard_map/pallas_call | solution.py:299
  47.3 0.0 collective-permute-done.13.refs_3_
  47.3 0.0 collective-permute-done.14.refs_4_
  47.3 0.1 collective-permute-start.16
  47.4 2.4 %collective-permute-start.17 = (bf16[256,320]{1,0:T(8,128)(2,1)S(1)}, bf16[256,320]{1,0:T(8,128)(2,1)S(1)}, u32[]{:S(2)}, u32[]{:S(2)}) collective-permute-start(bf16[256,320]{1,0:T(8,128)(2,1)S(1)} %get-tuple-element.61.att0), channel_id=1, source_target_pairs={{0,2},{1,3},{2,0},{3,1},{4,6},{5,7},{6,4},{7,5},{8,10},{9,11},{10,... | collective-permute-start | bytes 491528 | tf_op jit(solution)/shard_map/ppermute | solution.py:22
  49.8 0.8 collective-permute-start.18
  50.6 9.6 %collective-permute-done.16.att1 = bf16[256,320]{1,0:T(8,128)(2,1)S(1)} collective-permute-done((bf16[256,320]{1,0:T(8,128)(2,1)S(1)}, bf16[256,320]{1,0:T(8,128)(2,1)S(1)}, u32[]{:S(2)}, u32[]{:S(2)}) %collective-permute-start.16) | collective-permute-done | bytes 163872 | tf_op jit(solution)/shard_map/ppermute | solution.py:28
  60.3 0.0 collective-permute-done.17.att2
  60.3 0.0 collective-permute-done.18.att3
  60.3 0.0 copy-start.5
  60.3 0.0 copy-start.6
  60.3 5.9 %shard_map.103 = (f32[656,128]{1,0:T(8,128)S(1)}, bf16[656,128]{1,0:T(8,128)(2,1)S(1)}, bf16[656,128]{1,0:T(8,128)(2,1)S(1)}, bf16[656,128]{1,0:T(8,128)(2,1)S(1)}, bf16[656,128]{1,0:T(8,128)(2,1)S(1)}) custom-call(s32[1]{0:T(128)} %get-tuple-element.41.tp_ref, s32[1]{0:T(128)} %get-tuple-element.42.core_ref, bf16[256,320]{1,0:T(8,128)(2,1)S(1)} %get-tuple-element.61.att0, ...), custom_call_target="tpu_custom_call" | custom-call | flops 2500000000 | bytes 10000000 | tf_op jit(solution)/shard_map/pallas_call | solution.py:349
  66.2 0.1 collective-permute-start.19
  66.3 2.4 %collective-permute-start.20 = (bf16[656,128]{1,0:T(8,128)(2,1)S(1)}, bf16[656,128]{1,0:T(8,128)(2,1)S(1)}, u32[]{:S(2)}, u32[]{:S(2)}) collective-permute-start(bf16[656,128]{1,0:T(8,128)(2,1)S(1)} %get-tuple-element.69), channel_id=1, source_target_pairs={{0,2},{1,3},{2,0},{3,1},{4,6},{5,7},{6,4},{7,5},{8,10},{9,11},{10,... | collective-permute-start | bytes 503816 | tf_op jit(solution)/shard_map/ppermute | solution.py:22
  68.7 0.9 collective-permute-start.21
  69.6 7.9 %collective-permute-done.19.got1 = bf16[656,128]{1,0:T(8,128)(2,1)S(1)} collective-permute-done((bf16[656,128]{1,0:T(8,128)(2,1)S(1)}, bf16[656,128]{1,0:T(8,128)(2,1)S(1)}, u32[]{:S(2)}, u32[]{:S(2)}) %collective-permute-start.19) | collective-permute-done | bytes 167968 | tf_op jit(solution)/shard_map/ppermute | solution.py:22
  77.4 0.0 collective-permute-done.20.got2
  77.4 0.6 collective-permute-done.21.got3
  78.0 0.1 shard_map.104
  78.2 0.3 collective-permute-start.22
  78.5 3.6 %collective-permute-start.23 = (bf16[64,1280]{1,0:T(8,128)(2,1)S(1)}, bf16[64,1280]{1,0:T(8,128)(2,1)S(1)}, u32[]{:S(2)}, u32[]{:S(2)}) collective-permute-start(bf16[64,1280]{1,0:T(8,128)(2,1)S(1)} %get-tuple-element.71.own), channel_id=1, source_target_pairs={{0,2},{1,3},{2,0},{3,1},{4,6},{5,7},{6,4},{7,5},{8,10},{9,11},{10,... | collective-permute-start | bytes 491528 | tf_op jit(solution)/shard_map/ppermute | solution.py:22
  82.0 0.0 collective-permute-start.24
  82.0 1.9 %collective-permute-start.25 = (bf16[16,128]{1,0:T(8,128)(2,1)S(1)}, bf16[16,128]{1,0:T(8,128)(2,1)S(1)}, u32[]{:S(2)}, u32[]{:S(2)}) collective-permute-start(bf16[16,128]{1,0:T(8,128)(2,1)S(1)} %get-tuple-element.72), channel_id=1, source_target_pairs={{0,4},{4,8},{8,12},{12,16},{16,20},{20,24},{24,28},{28,32},{32,36}... | collective-permute-start | bytes 12296 | tf_op jit(solution)/shard_map/ppermute | solution.py:33
  84.0 3.0 %collective-permute-done.25.rim_ref = bf16[16,128]{1,0:T(8,128)(2,1)S(1)} collective-permute-done((bf16[16,128]{1,0:T(8,128)(2,1)S(1)}, bf16[16,128]{1,0:T(8,128)(2,1)S(1)}, u32[]{:S(2)}, u32[]{:S(2)}) %collective-permute-start.25) | collective-permute-done | bytes 4128 | tf_op jit(solution)/shard_map/ppermute | solution.py:33
  87.0 2.4 %collective-permute-done.23.got2 = bf16[64,1280]{1,0:T(8,128)(2,1)S(1)} collective-permute-done((bf16[64,1280]{1,0:T(8,128)(2,1)S(1)}, bf16[64,1280]{1,0:T(8,128)(2,1)S(1)}, u32[]{:S(2)}, u32[]{:S(2)}) %collective-permute-start.23) | collective-permute-done | bytes 163872 | tf_op jit(solution)/shard_map/ppermute | solution.py:22
  89.4 4.2 %shard_map.105 = (bf16[32,4096]{1,0:T(8,128)(2,1)S(1)}, bf16[32,4096]{1,0:T(8,128)(2,1)S(1)}, bf16[32,4096]{1,0:T(8,128)(2,1)S(1)}, bf16[32,4096]{1,0:T(8,128)(2,1)S(1)}) custom-call(s32[1]{0:T(128)} %get-tuple-element.41.tp_ref, s32[2]{0:T(128)S(1)} %copy-done.10, s32[1]{0:T(128)} %get-tuple-element.57.joined_ref, ...), custom_call_target="tpu_custom_call" | custom-call | flops 1000000000 | bytes 6000000 | tf_op jit(solution)/shard_map/pallas_call | solution.py:369
  93.6 0.4 collective-permute-start.26
  94.0 3.3 %collective-permute-start.27 = (bf16[32,4096]{1,0:T(8,128)(2,1)S(1)}, bf16[32,4096]{1,0:T(8,128)(2,1)S(1)}, u32[]{:S(2)}, u32[]{:S(2)}) collective-permute-start(bf16[32,4096]{1,0:T(8,128)(2,1)S(1)} %get-tuple-element.75), channel_id=1, source_target_pairs={{0,2},{1,3},{2,0},{3,1},{4,6},{5,7},{6,4},{7,5},{8,10},{9,11},{10,... | collective-permute-start | bytes 786440 | tf_op jit(solution)/shard_map/ppermute | solution.py:22
  97.3 4.9 %collective-permute-done.26.got1 = bf16[32,4096]{1,0:T(8,128)(2,1)S(1)} collective-permute-done((bf16[32,4096]{1,0:T(8,128)(2,1)S(1)}, bf16[32,4096]{1,0:T(8,128)(2,1)S(1)}, u32[]{:S(2)}, u32[]{:S(2)}) %collective-permute-start.26) | collective-permute-done | bytes 262176 | tf_op jit(solution)/shard_map/ppermute | solution.py:22
  102.1 6.5 %collective-permute-done.27.got2 = bf16[32,4096]{1,0:T(8,128)(2,1)S(1)} collective-permute-done((bf16[32,4096]{1,0:T(8,128)(2,1)S(1)}, bf16[32,4096]{1,0:T(8,128)(2,1)S(1)}, u32[]{:S(2)}, u32[]{:S(2)}) %collective-permute-start.27) | collective-permute-done | bytes 262176 | tf_op jit(solution)/shard_map/ppermute | solution.py:22
  108.7 0.8 shard_map.106
  (23 shorter events, 0.1 us)
Async XLA Ops:
  0.0 30.6 %copy-start = (bf16[3,1280,320]{1,2,0:T(8,128)(2,1)S(1)}, bf16[3,1280,320]{1,2,0:T(8,128)(2,1)}, u32[]{:S(2)}) copy-start(bf16[3,1280,320]{1,2,0:T(8,128)(2,1)} %param.12) | copy-start | bytes 7372804
  4.5 13.1 %collective-permute-start = (bf16[272,640]{1,0:T(8,128)(2,1)}, bf16[272,640]{1,0:T(8,128)(2,1)S(1)}, u32[]{:S(2)}, u32[]{:S(2)}) collective-permute-start(bf16[272,640]{1,0:T(8,128)(2,1)} %get-tuple-element.50.kv_in), channel_id=1, source_target_pairs={{4,12},{8,0},{12,20},{16,8},{20,28},{24,16},{28,36},{32,24},{36,44... | collective-permute-start | bytes 1044488 | tf_op jit(solution)/shard_map/ppermute | solution.py:41
  7.2 12.3 %collective-permute-start.1 = (bf16[272,640]{1,0:T(8,128)(2,1)}, bf16[272,640]{1,0:T(8,128)(2,1)S(1)}, u32[]{:S(2)}, u32[]{:S(2)}) collective-permute-start(bf16[272,640]{1,0:T(8,128)(2,1)} %get-tuple-element.50.kv_in), channel_id=1, source_target_pairs={{0,8},{8,16},{12,4},{16,24},{20,12},{24,32},{28,20},{32,40},{36,28... | collective-permute-start | bytes 1044488 | tf_op jit(solution)/shard_map/ppermute | solution.py:41
  12.4 16.2 %collective-permute-start.4 = (bf16[320,640]{1,0:T(8,128)(2,1)}, bf16[320,640]{1,0:T(8,128)(2,1)S(1)}, u32[]{:S(2)}, u32[]{:S(2)}) collective-permute-start(bf16[320,640]{1,0:T(8,128)(2,1)} %get-tuple-element.49), channel_id=1, source_target_pairs={{0,2},{1,3},{2,0},{3,1},{4,6},{5,7},{6,4},{7,5},{8,10},{9,11},{10,... | collective-permute-start | bytes 1228808 | tf_op jit(solution)/shard_map/ppermute | solution.py:22
  15.7 19.6 %collective-permute-start.5 = (bf16[320,640]{1,0:T(8,128)(2,1)}, bf16[320,640]{1,0:T(8,128)(2,1)S(1)}, u32[]{:S(2)}, u32[]{:S(2)}) collective-permute-start(bf16[320,640]{1,0:T(8,128)(2,1)} %get-tuple-element.49), channel_id=1, source_target_pairs={{0,1},{1,2},{2,3},{3,0},{4,7},{5,4},{6,5},{7,6},{8,9},{9,10},{10,1... | collective-permute-start | bytes 1228808 | tf_op jit(solution)/shard_map/ppermute | solution.py:28
  17.6 17.8 %collective-permute-start.2 = (bf16[272,640]{1,0:T(8,128)(2,1)S(1)}, bf16[272,640]{1,0:T(8,128)(2,1)S(1)}, u32[]{:S(2)}, u32[]{:S(2)}) collective-permute-start(bf16[272,640]{1,0:T(8,128)(2,1)S(1)} %collective-permute-done.refs_1_), channel_id=1, source_target_pairs={{4,12},{8,0},{12,20},{16,8},{20,28},{24,16},{28,36},{32,24},{36,44... | collective-permute-start | bytes 1044488 | tf_op jit(solution)/shard_map/ppermute | solution.py:41
  19.5 16.4 %collective-permute-start.3 = (bf16[272,640]{1,0:T(8,128)(2,1)S(1)}, bf16[272,640]{1,0:T(8,128)(2,1)S(1)}, u32[]{:S(2)}, u32[]{:S(2)}) collective-permute-start(bf16[272,640]{1,0:T(8,128)(2,1)S(1)} %collective-permute-done.1.refs_3_), channel_id=1, source_target_pairs={{0,8},{8,16},{12,4},{16,24},{20,12},{24,32},{28,20},{32,40},{36,28... | collective-permute-start | bytes 1044488 | tf_op jit(solution)/shard_map/ppermute | solution.py:41
  25.6 13.1 %collective-permute-start.12 = (bf16[320,640]{1,0:T(8,128)(2,1)}, bf16[320,640]{1,0:T(8,128)(2,1)S(1)}, u32[]{:S(2)}, u32[]{:S(2)}) collective-permute-start(bf16[320,640]{1,0:T(8,128)(2,1)} %get-tuple-element.49), channel_id=1, source_target_pairs={{0,3},{1,0},{2,1},{3,2},{4,5},{5,6},{6,7},{7,4},{8,11},{9,8},{10,9... | collective-permute-start | bytes 1228808 | tf_op jit(solution)/shard_map/ppermute | solution.py:28
  28.7 10.0 %collective-permute-start.6 = (bf16[272,640]{1,0:T(8,128)(2,1)}, bf16[272,640]{1,0:T(8,128)(2,1)S(1)}, u32[]{:S(2)}, u32[]{:S(2)}) collective-permute-start(bf16[272,640]{1,0:T(8,128)(2,1)} %get-tuple-element.50.kv_in), channel_id=1, source_target_pairs={{4,24},{12,32},{20,40},{24,4},{28,48},{32,12},{36,56},{40,20},{44,... | collective-permute-start | bytes 1044488 | tf_op jit(solution)/shard_map/ppermute | solution.py:52
  30.6 1.9 %copy-start.2 = (bf16[1280,1280]{1,0:T(8,128)(2,1)S(1)}, bf16[1280,1280]{1,0:T(8,128)(2,1)}, u32[]{:S(2)}) copy-start(bf16[1280,1280]{1,0:T(8,128)(2,1)} %w_down_in.1) | copy-start | bytes 9830404
  32.5 1.1 copy-start.7
  33.6 1.0 copy-start.8
  34.6 6.3 %copy-start.10 = (s32[2]{0:T(128)S(1)}, s32[2]{0:T(128)}, u32[]{:S(2)}) copy-start(s32[2]{0:T(128)} %ids_ref.5) | copy-start | bytes 28
  34.6 25.7 %copy-start.3 = (bf16[1280,1280]{1,0:T(8,128)(2,1)S(1)}, bf16[1280,1280]{1,0:T(8,128)(2,1)}, u32[]{:S(2)}) copy-start(bf16[1280,1280]{1,0:T(8,128)(2,1)} %refs_8_.1) | copy-start | bytes 9830404
  35.3 25.0 %copy-start.1 = (bf16[320,1280]{1,0:T(8,128)(2,1)S(1)}, bf16[320,1280]{1,0:T(8,128)(2,1)}, u32[]{:S(2)}) copy-start(bf16[320,1280]{1,0:T(8,128)(2,1)} %w_out_ref.1) | copy-start | bytes 2457604
  35.3 25.0 %copy-start.4 = (bf16[256,1280]{1,0:T(8,128)(2,1)S(1)}, bf16[256,1280]{1,0:T(8,128)(2,1)}, u32[]{:S(2)}) copy-start(bf16[256,1280]{1,0:T(8,128)(2,1)} %refs_6_.1) | copy-start | bytes 1966084
  35.3 25.0 %copy-start.9 = (f32[1280]{0:T(1024)S(1)}, f32[1280]{0:T(1024)}, u32[]{:S(2)}) copy-start(f32[1280]{0:T(1024)} %refs_7_.1) | copy-start | bytes 15364
  35.3 3.9 %collective-permute-start.8 = (bf16[272,640]{1,0:T(8,128)(2,1)S(1)}, bf16[272,640]{1,0:T(8,128)(2,1)S(1)}, u32[]{:S(2)}, u32[]{:S(2)}) collective-permute-start(bf16[272,640]{1,0:T(8,128)(2,1)S(1)} %collective-permute-done.refs_1_), channel_id=1, source_target_pairs={{0,4},{4,0},{8,12},{12,8},{16,20},{20,16},{24,28},{28,24},{32,36},... | collective-permute-start | bytes 1044488 | tf_op jit(solution)/shard_map/ppermute | solution.py:46
  35.4 3.9 %collective-permute-start.9 = (bf16[272,640]{1,0:T(8,128)(2,1)S(1)}, bf16[272,640]{1,0:T(8,128)(2,1)S(1)}, u32[]{:S(2)}, u32[]{:S(2)}) collective-permute-start(bf16[272,640]{1,0:T(8,128)(2,1)S(1)} %get-tuple-element.54.refs_2_), channel_id=1, source_target_pairs={{0,4},{4,0},{8,12},{12,8},{16,20},{20,16},{24,28},{28,24},{32,36},... | collective-permute-start | bytes 1044488 | tf_op jit(solution)/shard_map/ppermute | solution.py:46
  35.9 3.8 %collective-permute-start.10 = (bf16[272,640]{1,0:T(8,128)(2,1)S(1)}, bf16[272,640]{1,0:T(8,128)(2,1)S(1)}, u32[]{:S(2)}, u32[]{:S(2)}) collective-permute-start(bf16[272,640]{1,0:T(8,128)(2,1)S(1)} %collective-permute-done.1.refs_3_), channel_id=1, source_target_pairs={{0,4},{4,0},{8,12},{12,8},{16,20},{20,16},{24,28},{28,24},{32,36},... | collective-permute-start | bytes 1044488 | tf_op jit(solution)/shard_map/ppermute | solution.py:46
  38.7 1.7 %collective-permute-start.7 = (bf16[272,640]{1,0:T(8,128)(2,1)S(1)}, bf16[272,640]{1,0:T(8,128)(2,1)S(1)}, u32[]{:S(2)}, u32[]{:S(2)}) collective-permute-start(bf16[272,640]{1,0:T(8,128)(2,1)S(1)} %collective-permute-done.2.refs_0_), channel_id=1, source_target_pairs={{0,4},{4,0},{8,12},{12,8},{16,20},{20,16},{24,28},{28,24},{32,36},... | collective-permute-start | bytes 1044488 | tf_op jit(solution)/shard_map/ppermute | solution.py:46
  38.7 2.2 %collective-permute-start.11 = (bf16[272,640]{1,0:T(8,128)(2,1)S(1)}, bf16[272,640]{1,0:T(8,128)(2,1)S(1)}, u32[]{:S(2)}, u32[]{:S(2)}) collective-permute-start(bf16[272,640]{1,0:T(8,128)(2,1)S(1)} %collective-permute-done.3.refs_4_), channel_id=1, source_target_pairs={{0,4},{4,0},{8,12},{12,8},{16,20},{20,16},{24,28},{28,24},{32,36},... | collective-permute-start | bytes 1044488 | tf_op jit(solution)/shard_map/ppermute | solution.py:46
  39.2 8.1 %collective-permute-start.13 = (bf16[320,640]{1,0:T(8,128)(2,1)S(1)}, bf16[320,640]{1,0:T(8,128)(2,1)S(1)}, u32[]{:S(2)}, u32[]{:S(2)}) collective-permute-start(bf16[320,640]{1,0:T(8,128)(2,1)S(1)} %collective-permute-done.12.refs_2_), channel_id=1, source_target_pairs={{0,4},{4,0},{8,12},{12,8},{16,20},{20,16},{24,28},{28,24},{32,36},... | collective-permute-start | bytes 1228808 | tf_op jit(solution)/shard_map/ppermute | solution.py:46
  39.3 8.0 %collective-permute-start.14 = (bf16[320,640]{1,0:T(8,128)(2,1)S(1)}, bf16[320,640]{1,0:T(8,128)(2,1)S(1)}, u32[]{:S(2)}, u32[]{:S(2)}) collective-permute-start(bf16[320,640]{1,0:T(8,128)(2,1)S(1)} %collective-permute-done.4.refs_1_), channel_id=1, source_target_pairs={{0,4},{4,0},{8,12},{12,8},{16,20},{20,16},{24,28},{28,24},{32,36},... | collective-permute-start | bytes 1228808 | tf_op jit(solution)/shard_map/ppermute | solution.py:46
  39.7 7.6 %collective-permute-start.15 = (bf16[320,640]{1,0:T(8,128)(2,1)S(1)}, bf16[320,640]{1,0:T(8,128)(2,1)S(1)}, u32[]{:S(2)}, u32[]{:S(2)}) collective-permute-start(bf16[320,640]{1,0:T(8,128)(2,1)S(1)} %collective-permute-done.5.refs_0_), channel_id=1, source_target_pairs={{0,4},{4,0},{8,12},{12,8},{16,20},{20,16},{24,28},{28,24},{32,36},... | collective-permute-start | bytes 1228808 | tf_op jit(solution)/shard_map/ppermute | solution.py:46
  47.3 13.0 %collective-permute-start.16 = (bf16[256,320]{1,0:T(8,128)(2,1)S(1)}, bf16[256,320]{1,0:T(8,128)(2,1)S(1)}, u32[]{:S(2)}, u32[]{:S(2)}) collective-permute-start(bf16[256,320]{1,0:T(8,128)(2,1)S(1)} %get-tuple-element.61.att0), channel_id=1, source_target_pairs={{0,1},{1,2},{2,3},{3,0},{4,7},{5,4},{6,5},{7,6},{8,9},{9,10},{10,1... | collective-permute-start | bytes 491528 | tf_op jit(solution)/shard_map/ppermute | solution.py:28
  47.4 12.9 %collective-permute-start.17 = (bf16[256,320]{1,0:T(8,128)(2,1)S(1)}, bf16[256,320]{1,0:T(8,128)(2,1)S(1)}, u32[]{:S(2)}, u32[]{:S(2)}) collective-permute-start(bf16[256,320]{1,0:T(8,128)(2,1)S(1)} %get-tuple-element.61.att0), channel_id=1, source_target_pairs={{0,2},{1,3},{2,0},{3,1},{4,6},{5,7},{6,4},{7,5},{8,10},{9,11},{10,... | collective-permute-start | bytes 491528 | tf_op jit(solution)/shard_map/ppermute | solution.py:22
  49.8 10.4 %collective-permute-start.18 = (bf16[256,320]{1,0:T(8,128)(2,1)S(1)}, bf16[256,320]{1,0:T(8,128)(2,1)S(1)}, u32[]{:S(2)}, u32[]{:S(2)}) collective-permute-start(bf16[256,320]{1,0:T(8,128)(2,1)S(1)} %get-tuple-element.61.att0), channel_id=1, source_target_pairs={{0,3},{1,0},{2,1},{3,2},{4,5},{5,6},{6,7},{7,4},{8,11},{9,8},{10,9... | collective-permute-start | bytes 491528 | tf_op jit(solution)/shard_map/ppermute | solution.py:28
  60.3 29.0 %copy-start.5 = (bf16[320,4096]{1,0:T(8,128)(2,1)S(1)}, bf16[320,4096]{1,0:T(8,128)(2,1)}, u32[]{:S(2)}) copy-start(bf16[320,4096]{1,0:T(8,128)(2,1)} %w_proj_ref.1) | copy-start | bytes 7864324
  60.3 29.0 %copy-start.6 = (bf16[3,1280,320]{1,2,0:T(8,128)(2,1)S(1)}, bf16[3,1280,320]{1,2,0:T(8,128)(2,1)}, u32[]{:S(2)}) copy-start(bf16[3,1280,320]{1,2,0:T(8,128)(2,1)} %param.17) | copy-start | bytes 7372804
  66.2 11.2 %collective-permute-start.19 = (bf16[656,128]{1,0:T(8,128)(2,1)S(1)}, bf16[656,128]{1,0:T(8,128)(2,1)S(1)}, u32[]{:S(2)}, u32[]{:S(2)}) collective-permute-start(bf16[656,128]{1,0:T(8,128)(2,1)S(1)} %get-tuple-element.68), channel_id=1, source_target_pairs={{0,1},{1,2},{2,3},{3,0},{4,5},{5,6},{6,7},{7,4},{8,9},{9,10},{10,1... | collective-permute-start | bytes 503816 | tf_op jit(solution)/shard_map/ppermute | solution.py:22
  66.3 11.1 %collective-permute-start.20 = (bf16[656,128]{1,0:T(8,128)(2,1)S(1)}, bf16[656,128]{1,0:T(8,128)(2,1)S(1)}, u32[]{:S(2)}, u32[]{:S(2)}) collective-permute-start(bf16[656,128]{1,0:T(8,128)(2,1)S(1)} %get-tuple-element.69), channel_id=1, source_target_pairs={{0,2},{1,3},{2,0},{3,1},{4,6},{5,7},{6,4},{7,5},{8,10},{9,11},{10,... | collective-permute-start | bytes 503816 | tf_op jit(solution)/shard_map/ppermute | solution.py:22
  68.7 9.4 %collective-permute-start.21 = (bf16[656,128]{1,0:T(8,128)(2,1)S(1)}, bf16[656,128]{1,0:T(8,128)(2,1)S(1)}, u32[]{:S(2)}, u32[]{:S(2)}) collective-permute-start(bf16[656,128]{1,0:T(8,128)(2,1)S(1)} %get-tuple-element.70), channel_id=1, source_target_pairs={{0,3},{1,0},{2,1},{3,2},{4,7},{5,4},{6,5},{7,6},{8,11},{9,8},{10,9... | collective-permute-start | bytes 503816 | tf_op jit(solution)/shard_map/ppermute | solution.py:22
  78.2 8.8 %collective-permute-start.22 = (bf16[64,1280]{1,0:T(8,128)(2,1)S(1)}, bf16[64,1280]{1,0:T(8,128)(2,1)S(1)}, u32[]{:S(2)}, u32[]{:S(2)}) collective-permute-start(bf16[64,1280]{1,0:T(8,128)(2,1)S(1)} %get-tuple-element.71.own), channel_id=1, source_target_pairs={{0,1},{1,2},{2,3},{3,0},{4,5},{5,6},{6,7},{7,4},{8,9},{9,10},{10,1... | collective-permute-start | bytes 491528 | tf_op jit(solution)/shard_map/ppermute | solution.py:22
  78.5 10.9 %collective-permute-start.23 = (bf16[64,1280]{1,0:T(8,128)(2,1)S(1)}, bf16[64,1280]{1,0:T(8,128)(2,1)S(1)}, u32[]{:S(2)}, u32[]{:S(2)}) collective-permute-start(bf16[64,1280]{1,0:T(8,128)(2,1)S(1)} %get-tuple-element.71.own), channel_id=1, source_target_pairs={{0,2},{1,3},{2,0},{3,1},{4,6},{5,7},{6,4},{7,5},{8,10},{9,11},{10,... | collective-permute-start | bytes 491528 | tf_op jit(solution)/shard_map/ppermute | solution.py:22
  82.0 7.3 %collective-permute-start.24 = (bf16[64,1280]{1,0:T(8,128)(2,1)S(1)}, bf16[64,1280]{1,0:T(8,128)(2,1)S(1)}, u32[]{:S(2)}, u32[]{:S(2)}) collective-permute-start(bf16[64,1280]{1,0:T(8,128)(2,1)S(1)} %get-tuple-element.71.own), channel_id=1, source_target_pairs={{0,3},{1,0},{2,1},{3,2},{4,7},{5,4},{6,5},{7,6},{8,11},{9,8},{10,9... | collective-permute-start | bytes 491528 | tf_op jit(solution)/shard_map/ppermute | solution.py:22
  82.0 4.9 %collective-permute-start.25 = (bf16[16,128]{1,0:T(8,128)(2,1)S(1)}, bf16[16,128]{1,0:T(8,128)(2,1)S(1)}, u32[]{:S(2)}, u32[]{:S(2)}) collective-permute-start(bf16[16,128]{1,0:T(8,128)(2,1)S(1)} %get-tuple-element.72), channel_id=1, source_target_pairs={{0,4},{4,8},{8,12},{12,16},{16,20},{20,24},{24,28},{28,32},{32,36}... | collective-permute-start | bytes 12296 | tf_op jit(solution)/shard_map/ppermute | solution.py:33
  93.6 8.6 %collective-permute-start.26 = (bf16[32,4096]{1,0:T(8,128)(2,1)S(1)}, bf16[32,4096]{1,0:T(8,128)(2,1)S(1)}, u32[]{:S(2)}, u32[]{:S(2)}) collective-permute-start(bf16[32,4096]{1,0:T(8,128)(2,1)S(1)} %get-tuple-element.74), channel_id=1, source_target_pairs={{0,1},{1,2},{2,3},{3,0},{4,5},{5,6},{6,7},{7,4},{8,9},{9,10},{10,1... | collective-permute-start | bytes 786440 | tf_op jit(solution)/shard_map/ppermute | solution.py:22
  94.0 14.7 %collective-permute-start.27 = (bf16[32,4096]{1,0:T(8,128)(2,1)S(1)}, bf16[32,4096]{1,0:T(8,128)(2,1)S(1)}, u32[]{:S(2)}, u32[]{:S(2)}) collective-permute-start(bf16[32,4096]{1,0:T(8,128)(2,1)S(1)} %get-tuple-element.75), channel_id=1, source_target_pairs={{0,2},{1,3},{2,0},{3,1},{4,6},{5,7},{6,4},{7,5},{8,10},{9,11},{10,... | collective-permute-start | bytes 786440 | tf_op jit(solution)/shard_map/ppermute | solution.py:22
  97.3 11.4 %collective-permute-start.28 = (bf16[32,4096]{1,0:T(8,128)(2,1)S(1)}, bf16[32,4096]{1,0:T(8,128)(2,1)S(1)}, u32[]{:S(2)}, u32[]{:S(2)}) collective-permute-start(bf16[32,4096]{1,0:T(8,128)(2,1)S(1)} %get-tuple-element.76), channel_id=1, source_target_pairs={{0,3},{1,0},{2,1},{3,2},{4,7},{5,4},{6,5},{7,6},{8,11},{9,8},{10,9... | collective-permute-start | bytes 786440 | tf_op jit(solution)/shard_map/ppermute | solution.py:22
